TPU v7x, 32 devices: a whole 2x2x4 slice. The times are simulated.
32 devices in a mesh: dp: 8 (over y, x, core), expert: 4 (over z).
Axes of the slice: x: 2, y: 2, z: 4, core: 2. Of those that a mesh axis runs over, the one named last changes fastest.
Arguments:
- cotangent: bfloat16 [8192, 2048], P(('dp', 'expert')), may hold values from -0.625 to 0.625
- route_weight: float32 [8192], P(('dp', 'expert')), may hold values from 0.1 to 1
- expert_ids: int32 [8192], P(('dp', 'expert')), may hold values from 0 to 3, as said below
- slot_ids: int32 [8192], P(('dp', 'expert')), may hold values from 0 to 127
- hidden_saved: bfloat16 [8, 4, 4, 128, 768], P('dp', 'expert'), may hold values from -6 to 6
- down_weight: float32 [4, 2048, 768], P('expert', 'dp')
- first_moment: float32 [4, 2048, 768], P('expert', 'dp'), may hold values from -3 to 3
- second_moment: float32 [4, 2048, 768], P('expert', 'dp'), may hold values from 0.003 to 0.03
Outputs:
- new_weight: float32 [4, 2048, 768], P('expert', 'dp')
- new_first: float32 [4, 2048, 768], P('expert', 'dp')
- new_second: float32 [4, 2048, 768], P('expert', 'dp')
Inputs may be any that keep to these rules, and one draw needn't show every extreme that they name: `expert_ids`: within the rows of one device no pair (expert, slot) repeats, so no expert gets more than 128 rows from one device; in every data group one expert gets exactly 128 rows from each device of the group.
All inputs are finite; a program needn't handle non-finite values.
Results may differ from a plain program's by a relative error of at most 0.00049.
Values may be sent and summed in bfloat16 or wider, within the bound.
No kernel may reach another device: no remote copies, remote signals or barrier semaphores. Data moves between devices by JAX's collectives and lax.ppermute only.
A program may use at most 64 MiB of HBM per device.

v0:
```python
import jax
import jax.numpy as jnp
from jax import lax
from jax.sharding import PartitionSpec as P


def on_device(
    cotangent,
    route_weight,
    expert_ids,
    slot_ids,
    hidden_saved,
    down_weight,
    first_moment,
    second_moment,
):
    tok_rows, width = cotangent.shape
    owners = lax.axis_size("expert")
    hidden_rows = hidden_saved.reshape(-1, hidden_saved.shape[-1])
    capacity = hidden_rows.shape[0] // owners
    weight = down_weight[0]
    routed = (route_weight[:, None] * cotangent.astype(jnp.float32)).astype(jnp.bfloat16)
    target = expert_ids * capacity + slot_ids
    outgoing = jnp.zeros((owners * capacity, width), jnp.bfloat16).at[target].set(routed)
    arrived = lax.all_to_all(
        outgoing.reshape(owners, capacity, width), "expert", split_axis=0, concat_axis=0, tiled=True
    )
    arrived = arrived.reshape(owners * capacity, width)
    whole_term = lax.dot_general(
        arrived, hidden_rows, (((0,), (0,)), ((), ())), preferred_element_type=jnp.float32
    )
    grad = lax.psum_scatter(whole_term, "dp", scatter_dimension=0, tiled=True)
    new_first = 0.9 * first_moment[0] + 0.1 * grad
    new_second = 0.999 * second_moment[0] + 0.001 * grad * grad
    update = (
        new_first / (1.0 - 0.9**10) / (jnp.sqrt(new_second / (1.0 - 0.999**10)) + 1e-06)
        + 0.01 * weight
    )
    weight_sq, update_sq = lax.psum((jnp.sum(weight * weight), jnp.sum(update * update)), "dp")
    ratio = jnp.sqrt(weight_sq) / (jnp.sqrt(update_sq) + 1e-06)
    new_weight = weight - 0.1 * ratio * update
    return (new_weight[None], new_first[None], new_second[None])


def solution(mesh):
    placed = (
        P(("dp", "expert"), None),
        P(("dp", "expert")),
        P(("dp", "expert")),
        P(("dp", "expert")),
        P("dp", "expert", None, None, None),
        P("expert", "dp", None),
        P("expert", "dp", None),
        P("expert", "dp", None),
    )
    return jax.shard_map(
        on_device,
        mesh=mesh,
        in_specs=placed,
        out_specs=(P("expert", "dp", None), P("expert", "dp", None), P("expert", "dp", None)),
        check_vma=False,
    )
```

profile of v0, /device:TPU:0, one launch (start us, length us, event | category | flops | bytes accessed | tf_op | source)
XLA Modules:
  0.0 157.9 jit_solution(2995791615367867809)
XLA Ops:
  7.2 0.0 copy-start
  7.2 0.0 reduce-scatter.2.cloned.1.call-start
  7.2 0.8 compare_select_fusion
  8.0 3.6 %scatter_custom_fusion = bf16[512,2048]{1,0:T(8,128)(2,1)S(1)} fusion(s32[256]{0:T(256)S(1)} %compare_select_fusion, bf16[256,2048]{1,0:T(8,128)(2,1)} %param.8, f32[256]{0:T(256)} %param.9, bf16[]{:T(256)} %constant.2.clone.1), kind=kCustom, calls=%fused_computation.3 | custom fusion | flops 1572864 | bytes 3146754 | tf_op jit(solution)/shard_map/scatter | solution.py:24
  11.6 54.3 %all_to_all.5 = bf16[4,128,2048]{2,1,0:T(8,128)(2,1)S(1)} all-to-all(bf16[4,128,2048]{2,1,0:T(8,128)(2,1)S(1)} %bitcast.39), channel_id=1, replica_groups=mesh['dp'=8,'expert'=4] {'expert'}, dimensions={0} | all-to-all | bytes 4194304 | tf_op jit(solution)/shard_map/all_to_all | solution.py:25
  65.9 0.0 copy-done
  65.9 4.5 %fusion.10 = f32[2048,768]{1,0:T(8,128)} fusion(bf16[512,2048]{1,0:T(8,128)(2,1)S(1)} %bitcast.38, bf16[512,768]{1,0:T(8,128)(2,1)S(1)} %bitcast.37), kind=kOutput, calls=%fused_computation.18 | convolution fusion | flops 1610612736 | bytes 9175040 | tf_op jit(solution)/shard_map/dot_general | solution.py:29
  70.4 0.0 copy-start.1
  70.4 0.0 copy-start.2
  70.4 0.0 reduce-scatter.2.cloned.1.call-update
  70.5 61.1 %reduce-scatter.2.cloned.1.call-done = f32[256,768]{1,0:T(8,128)} async-done(((f32[2048,768]{1,0:T(8,128)}), f32[256,768]{1,0:T(8,128)}) %reduce-scatter.2.cloned.1.call-update) | async-done | bytes 786448 | tf_op jit(solution)/shard_map/reduce_scatter | solution.py:32
  131.6 0.0 copy-done.1
  131.6 0.0 copy-done.2
  131.6 3.8 %multiply_reduce_fusion = (f32[]{:T(128)}, f32[256,768]{1,0:T(8,128)S(1)}, f32[1,256,768]{2,1,0:T(8,128)}, f32[1,256,768]{2,1,0:T(8,128)}, f32[]{:T(128)}) fusion(f32[1,256,768]{2,1,0:T(8,128)S(1)} %copy-done.1, f32[256,768]{1,0:T(8,128)} %reduce-scatter.2.cloned.1.call-done, f32[1,256,768]{2,1,0:T(8,128)S(1)} %copy-done.2, f32[1,256,768]{2,1,0:T(8,128)} %param.14), kind=kLoop, calls=%fused_computation.14 | loop fusion | flops 3342334 | bytes 5505032 | tf_op jit(solution)/shard_map/reduce_sum | solution.py:39
  135.4 13.3 %all-reduce = (f32[]{:T(128)}, f32[]{:T(128)}) all-reduce(f32[]{:T(128)} %get-tuple-element.9, f32[]{:T(128)} %get-tuple-element.5), channel_id=1, replica_groups=mesh['dp'=8,'expert'=4] {'dp'}, use_global_device_ids=true, to_apply=%region_1.0 | all-reduce | flops 2 | bytes 16 | tf_op jit(solution)/shard_map/psum | solution.py:39
  150.1 1.0 fusion.6
Async XLA Ops:
  7.2 58.7 %copy-start = (bf16[1,1,4,128,768]{4,3,2,1,0:T(8,128)(2,1)S(1)}, bf16[1,1,4,128,768]{4,3,2,1,0:T(8,128)(2,1)}, u32[]{:S(2)}) copy-start(bf16[1,1,4,128,768]{4,3,2,1,0:T(8,128)(2,1)} %param.12) | copy-start | bytes 2359300
  7.2 124.4 %reduce-scatter.2.cloned.1.call-start = ((), (), s32[]{:S(2)}) async-start(), calls=%async_computation.2 | async-start | bytes 7077888 | tf_op jit(solution)/shard_map/reduce_scatter | solution.py:32
  70.4 61.1 %copy-start.1 = (f32[1,256,768]{2,1,0:T(8,128)S(1)}, f32[1,256,768]{2,1,0:T(8,128)}, u32[]{:S(2)}) copy-start(f32[1,256,768]{2,1,0:T(8,128)} %param.13) | copy-start | bytes 2359300
  70.4 61.1 %copy-start.2 = (f32[1,256,768]{2,1,0:T(8,128)S(1)}, f32[1,256,768]{2,1,0:T(8,128)}, u32[]{:S(2)}) copy-start(f32[1,256,768]{2,1,0:T(8,128)} %param.15) | copy-start | bytes 2359300
Sparse Core Ops, SparseCore 0:
  70.6 60.9 reduce-scatter.1
where the time goes:
time: 158 us
  blocking collectives  67.6 us (43%)
  waiting for transfers between devices  61.1 us (39%)
  between operations  15.4 us (10%)
  other arithmetic  9.11 us (6%)
  matrix products  4.54 us (3%)
    reduce_scatter x1, waiting for transfers between devices, on_device(): grad = lax.psum_scatter(whole_term, 'dp', scatter_dimension=0, tiled=True)  61.1 us
    all_to_all x1, blocking collectives, on_device(): lax.all_to_all(outgoing.reshape(owners, capacity, width), 'expert', split...  54.3 us
    psum x1, blocking collectives, on_device(): lax.psum((jnp.sum(weight * weight), jnp.sum(update * update)), 'dp')  13.3 us
    dot_general x1, matrix products, on_device(): lax.dot_general(arrived, hidden_rows, (((0,), (0,)), ((), ())), preferred...  4.54 us
    reduce_sum x1, other arithmetic, on_device(): jnp.sum(update * update)  3.82 us
    scatter x1, other arithmetic, on_device(): jnp.zeros((owners * capacity, width), jnp.bfloat16).at[target].set(routed)  3.57 us
  transfers between devices with their start and end apart: 1, of which 1 were waited for; matrix products, arithmetic and copies ran while one was open for 0% of the time, Pallas kernels for 0%

commit v1 on v0

--- a/solution.py
+++ b/solution.py
@@ -1,7 +1,15 @@
+import functools
+
 import jax
 import jax.numpy as jnp
 from jax import lax
+from jax.experimental import pallas as pl
+from jax.experimental.pallas import tpu as pltpu
 from jax.sharding import PartitionSpec as P
+
+VMEM = pl.BlockSpec(memory_space=pltpu.VMEM)
+TAIL = 16
+ROWS_FIRST = (((0,), (0,)), ((), ()))
 
 
 def on_device(
@@ -42,6 +50,216 @@
     return (new_weight[None], new_first[None], new_second[None])
 
 
+def cut_kernel(n_dp, cot_ref, scale_ref, expert_ref, slot_ref, *out_refs):
+    tokens, width = cot_ref.shape
+    part = width // n_dp
+    me = lax.axis_index("dp")
+    scale = jnp.broadcast_to(scale_ref[...], (128, tokens)).T
+    scale = jnp.concatenate([scale] * (part // 128), axis=1)
+    row = lax.broadcasted_iota(jnp.int32, (TAIL, tokens), 0)
+    ids = jnp.where(row == 0, expert_ref[...], jnp.where(row == 1, slot_ref[...], 0))
+    ids = ids.astype(jnp.float32).astype(jnp.bfloat16)
+    for mask, out_ref in enumerate(out_refs):
+        begin = pl.multiple_of((me ^ mask) * part, part)
+        block = cot_ref[:, pl.ds(begin, part)].astype(jnp.float32)
+        out_ref[:tokens, :] = (scale * block).astype(jnp.bfloat16)
+        out_ref[tokens:, :] = ids
+
+
+def pack_kernel(owners, capacity, n_blocks, *refs):
+    me = lax.axis_index("expert")
+    blocks, outs = refs[:n_blocks], refs[n_blocks:]
+    tokens = blocks[0].shape[0] - TAIL
+    slot = lax.broadcasted_iota(jnp.int32, (capacity, tokens), 0).astype(jnp.float32)
+    for at, block in enumerate(blocks):
+        ids = block[tokens:, :].astype(jnp.float32)
+        place = ids[0:1, :] * capacity + ids[1:2, :]
+        rows = block[:tokens, :]
+        for shift, out in enumerate(outs):
+            expert = lax.rem(me + shift, owners)
+            first = (expert * capacity).astype(jnp.float32)
+            hot = jnp.where(slot + first == place, 1.0, 0.0).astype(jnp.bfloat16)
+            packed = jnp.dot(hot, rows, preferred_element_type=jnp.float32)
+            out[at * capacity : (at + 1) * capacity, :] = packed.astype(jnp.bfloat16)
+
+
+def add_products(owners, capacity, total, packed, hidden):
+    me = lax.axis_index("expert")
+    for at, parts in enumerate(hidden):
+        for shift, rows_ref in enumerate(packed):
+            source = lax.rem(me + owners - shift, owners)
+            begin = pl.multiple_of(source * capacity, capacity)
+            rows = rows_ref[at * capacity : (at + 1) * capacity, :]
+            column = 0
+            for part in parts:
+                wide = part.shape[1]
+                total[:, column : column + wide] += lax.dot_general(
+                    rows, part[pl.ds(begin, capacity), :], ROWS_FIRST, preferred_element_type=jnp.float32
+                )
+                column += wide
+
+
+def split_refs(refs, owners, chunks):
+    out, at = [], 0
+    for parts in chunks:
+        packed = refs[at : at + owners]
+        at += owners
+        hidden = []
+        for n in parts:
+            hidden.append(refs[at : at + n])
+            at += n
+        out.append((packed, hidden))
+    return out, refs[at:]
+
+
+def early_kernel(owners, capacity, chunks, *refs):
+    pairs, (total,) = split_refs(refs, owners, chunks)
+    total[...] = jnp.zeros_like(total)
+    for packed, hidden in pairs:
+        add_products(owners, capacity, total, packed, hidden)
+
+
+def update_kernel(owners, capacity, chunks, *refs):
+    pairs, rest = split_refs(refs, owners, chunks)
+    early, weight_ref, first_ref, second_ref, new_first, new_second, update_ref, sums, total = rest
+    total[...] = early[...]
+    for packed, hidden in pairs:
+        add_products(owners, capacity, total, packed, hidden)
+    grad = total[...]
+    weight = weight_ref[0]
+    first = 0.9 * first_ref[0] + 0.1 * grad
+    second = 0.999 * second_ref[0] + 0.001 * grad * grad
+    new_first[0] = first
+    new_second[0] = second
+    update = first / (1.0 - 0.9**10) / (jnp.sqrt(second / (1.0 - 0.999**10)) + 1e-06) + 0.01 * weight
+    update_ref[...] = update
+    row = lax.broadcasted_iota(jnp.int32, sums.shape, 0)
+    sums[...] = jnp.where(row == 0, jnp.sum(weight * weight), jnp.sum(update * update))
+
+
+def weight_kernel(n_sums, *refs):
+    sums, (weight_ref, update_ref, new_weight) = refs[:n_sums], refs[n_sums:]
+    total = sums[0][...]
+    for other in sums[1:]:
+        total = total + other[...]
+    norm = jnp.sqrt(total)
+    ratio = norm[0:1, 0:1] / (norm[1:2, 0:1] + 1e-06)
+    new_weight[0] = weight_ref[0] - (0.1 * ratio) * update_ref[...]
+
+
+def call(kernel, out_shape, *args, scratch=(), flops=0, name=None):
+    nbytes = sum(a.size * a.dtype.itemsize for a in jax.tree.leaves((args, out_shape)))
+    return pl.pallas_call(
+        kernel,
+        out_shape=out_shape,
+        in_specs=[VMEM] * len(args),
+        out_specs=jax.tree.map(lambda _: VMEM, out_shape),
+        scratch_shapes=scratch,
+        compiler_params=pltpu.CompilerParams(vmem_limit_bytes=40 * 2**20),
+        cost_estimate=pl.CostEstimate(flops=flops, bytes_accessed=nbytes, transcendentals=0),
+        name=name,
+    )(*args)
+
+
+def by_permutes(
+    cotangent,
+    route_weight,
+    expert_ids,
+    slot_ids,
+    hidden_saved,
+    down_weight,
+    first_moment,
+    second_moment,
+):
+    n_dp, owners = lax.axis_size("dp"), lax.axis_size("expert")
+    tokens, width = cotangent.shape
+    capacity, ff = hidden_saved.shape[3:]
+    part = width // n_dp
+    bf16, f32 = jnp.bfloat16, jnp.float32
+    hidden = hidden_saved.reshape(owners * capacity, ff)
+
+    def across(array, mask):
+        return lax.ppermute(array, "dp", [(d, d ^ mask) for d in range(n_dp)])
+
+    def along(array, shift):
+        return lax.ppermute(array, "expert", [(d, (d + shift) % owners) for d in range(owners)])
+
+    block = jax.ShapeDtypeStruct((tokens + TAIL, part), bf16)
+    cut = call(
+        functools.partial(cut_kernel, n_dp),
+        [block] * n_dp,
+        cotangent,
+        route_weight.reshape(1, tokens),
+        expert_ids.reshape(1, tokens),
+        slot_ids.reshape(1, tokens),
+        name="cut",
+    )
+    blocks = [cut[0]] + [across(cut[mask], mask) for mask in range(1, n_dp)]
+
+    def exchange(masks):
+        size = len(masks) * capacity
+        packed = call(
+            functools.partial(pack_kernel, owners, capacity, len(masks)),
+            [jax.ShapeDtypeStruct((size, part), bf16)] * owners,
+            *[blocks[mask] for mask in masks],
+            flops=2 * size * owners * tokens * part,
+            name="pack",
+        )
+        return [packed[0]] + [along(packed[shift], shift) for shift in range(1, owners)]
+
+    chunks = ((0, 1), (2, 3, 4, 5), (6, 7))
+    arrived = [exchange(masks) for masks in chunks]
+
+    half = ff // 2
+    by_x, by_y = across(hidden, 2), across(hidden, 4)
+    left, right = across(by_x[:, :half], 4), across(by_y[:, half:], 2)
+    own = {0: [hidden], 2: [by_x], 4: [by_y], 6: [left, right]}
+    rows = dict(own)
+    for mask, parts in own.items():
+        rows[mask ^ 1] = [across(p, 1) for p in parts]
+
+    def operands(at):
+        flat = list(arrived[at])
+        for mask in chunks[at]:
+            flat += rows[mask]
+        return flat
+
+    counts = [tuple(len(rows[mask]) for mask in masks) for masks in chunks]
+    matrix = jax.ShapeDtypeStruct((part, ff), f32)
+    early = call(
+        functools.partial(early_kernel, owners, capacity, counts[:2]),
+        matrix,
+        *operands(0),
+        *operands(1),
+        flops=2 * 6 * owners * capacity * part * ff,
+        name="early",
+    )
+    state = jax.ShapeDtypeStruct((1, part, ff), f32)
+    new_first, new_second, update, sums = call(
+        functools.partial(update_kernel, owners, capacity, counts[2:]),
+        [state, state, matrix, jax.ShapeDtypeStruct((8, 128), f32)],
+        *operands(2),
+        early,
+        down_weight,
+        first_moment,
+        second_moment,
+        scratch=[pltpu.VMEM((part, ff), f32)],
+        flops=2 * 2 * owners * capacity * part * ff,
+        name="update",
+    )
+    sums = sums + across(sums, 1)
+    parts = [sums] + [across(sums, mask) for mask in (2, 4, 6)]
+    new_weight = call(
+        functools.partial(weight_kernel, len(parts)),
+        state,
+        *parts,
+        down_weight,
+        update,
+        name="weight",
+    )
+    return new_weight, new_first, new_second
+
+
 def solution(mesh):
     placed = (
         P(("dp", "expert"), None),
@@ -54,7 +272,7 @@
         P("expert", "dp", None),
     )
     return jax.shard_map(
-        on_device,
+        by_permutes if mesh.shape["dp"] == 8 else on_device,
         mesh=mesh,
         in_specs=placed,
         out_specs=(P("expert", "dp", None), P("expert", "dp", None), P("expert", "dp", None)),

time: 158 us -> 113 us (0.72)
  blocking collectives: 67.6 us -> 0 us
  starting transfers between devices: 0.04 us -> 34.7 us
  between operations: 15.4 us -> 0.79 us
  other arithmetic: 9.11 us -> 0.01 us
  Pallas kernels: 0 us -> 7.79 us
  waiting for transfers between devices: 61.1 us -> 67.3 us
  matrix products: 4.54 us -> 0 us
  local copies, waits for them, and re-layouts: 0.02 us -> 2.04 us
    ppermute x0 -> x29, waiting for transfers between devices: none -> 67.3 us  [the longest x20 37.3 us: across(): return lax.ppermute(array, 'dp', [(d, d ^ mask) for d in range(n_dp)])]
    reduce_scatter x1 -> x0, waiting for transfers between devices: 61.1 us -> none  [on_device(): grad = lax.psum_scatter(whole_term, 'dp', scatter_dimension=0, tiled=True)]
    all_to_all x1 -> x0, blocking collectives: 54.3 us -> none  [on_device(): lax.all_to_all(outgoing.reshape(owners, capacity, width), 'expert', split...]
    ppermute x0 -> x29, starting transfers between devices: none -> 34.7 us  [the longest x9 18.5 us: along(): lax.ppermute(array, 'expert', [(d, (d + shift) % owners) for d in range(o...]
    psum x1 -> x0, blocking collectives: 13.3 us -> none  [on_device(): lax.psum((jnp.sum(weight * weight), jnp.sum(update * update)), 'dp')]
    pallas_call x0 -> x7, Pallas kernels: none -> 7.79 us  [call(): pl.pallas_call(kernel, out_shape=out_shape, in_specs=[VMEM] * len(args),...]
    dot_general x1 -> x0, matrix products: 4.54 us -> none  [on_device(): lax.dot_general(arrived, hidden_rows, (((0,), (0,)), ((), ())), preferred...]
    reduce_sum x1 -> x0, other arithmetic: 3.82 us -> none  [on_device(): jnp.sum(update * update)]
  transfers between devices with their start and end apart: 1 -> 29, of which waited for: 1 -> 14; matrix products, arithmetic and copies ran while one was open for 0% -> 0% of each run, Pallas kernels for 0% -> 4%
where the time goes in v1:
time: 113 us
  waiting for transfers between devices  67.3 us (60%)
  starting transfers between devices  34.7 us (31%)
  Pallas kernels  7.79 us (7%)
  local copies, waits for them, and re-layouts  2.04 us (2%)
    ppermute x20, waiting for transfers between devices, across(): return lax.ppermute(array, 'dp', [(d, d ^ mask) for d in range(n_dp)])  37.3 us
    ppermute x9, waiting for transfers between devices, along(): lax.ppermute(array, 'expert', [(d, (d + shift) % owners) for d in range(o...  30 us
    ppermute x9, starting transfers between devices, along(): lax.ppermute(array, 'expert', [(d, (d + shift) % owners) for d in range(o...  18.5 us
    ppermute x20, starting transfers between devices, across(): return lax.ppermute(array, 'dp', [(d, d ^ mask) for d in range(n_dp)])  16.2 us
    pallas_call x7, Pallas kernels, call(): pl.pallas_call(kernel, out_shape=out_shape, in_specs=[VMEM] * len(args),...  7.79 us
  transfers between devices with their start and end apart: 29, of which 14 were waited for; matrix products, arithmetic and copies ran while one was open for 0% of the time, Pallas kernels for 4%

profile of v1, /device:TPU:0, one launch (start us, length us, event | category | flops | bytes accessed | tf_op | source)
XLA Modules:
  0.0 112.6 jit_solution(9132793934122322048)
XLA Ops:
  0.6 3.0 %collective-permute-start.5 = (bf16[512,768]{1,0:T(8,128)(2,1)}, bf16[512,768]{1,0:T(8,128)(2,1)S(1)}, u32[]{:S(2)}, u32[]{:S(2)}) collective-permute-start(bf16[512,768]{1,0:T(8,128)(2,1)} %bitcast.4), channel_id=1, source_target_pairs={{0,8},{4,12},{8,0},{12,4},{16,24},{20,28},{24,16},{28,20},{1,9},{5... | collective-permute-start | bytes 2359304 | tf_op jit(solution)/shard_map/ppermute | solution.py:182
  3.6 1.5 %collective-permute-start.7 = (bf16[512,768]{1,0:T(8,128)(2,1)}, bf16[512,768]{1,0:T(8,128)(2,1)S(1)}, u32[]{:S(2)}, u32[]{:S(2)}) collective-permute-start(bf16[512,768]{1,0:T(8,128)(2,1)} %bitcast.5), channel_id=1, source_target_pairs={{0,16},{4,20},{8,24},{12,28},{16,0},{20,4},{24,8},{28,12},{1,17},{... | collective-permute-start | bytes 2359304 | tf_op jit(solution)/shard_map/ppermute | solution.py:182
  8.6 16.6 %collective-permute-done.16.refs_0_ = bf16[272,256]{1,0:T(8,128)(2,1)S(1)} collective-permute-done((bf16[272,256]{1,0:T(8,128)(2,1)S(1)}, bf16[272,256]{1,0:T(8,128)(2,1)S(1)}, u32[]{:S(2)}, u32[]{:S(2)}) %collective-permute-start.16) | collective-permute-done | bytes 139296 | tf_op jit(solution)/shard_map/ppermute | solution.py:182
  25.2 1.4 %collective-permute-done.17.refs_1_ = bf16[272,256]{1,0:T(8,128)(2,1)S(1)} collective-permute-done((bf16[272,256]{1,0:T(8,128)(2,1)S(1)}, bf16[272,256]{1,0:T(8,128)(2,1)S(1)}, u32[]{:S(2)}, u32[]{:S(2)}) %collective-permute-start.17) | collective-permute-done | bytes 139296 | tf_op jit(solution)/shard_map/ppermute | solution.py:182
  26.6 1.9 %collective-permute-start.19 = (bf16[272,256]{1,0:T(8,128)(2,1)S(1)}, bf16[272,256]{1,0:T(8,128)(2,1)S(1)}, u32[]{:S(2)}, u32[]{:S(2)}) collective-permute-start(bf16[272,256]{1,0:T(8,128)(2,1)S(1)} %get-tuple-element.42), channel_id=1, source_target_pairs={{0,20},{4,16},{8,28},{12,24},{16,4},{20,0},{24,12},{28,8},{1,21},{... | collective-permute-start | bytes 417800 | tf_op jit(solution)/shard_map/ppermute | solution.py:182
  28.6 1.4 %collective-permute-start = (bf16[272,256]{1,0:T(8,128)(2,1)S(1)}, bf16[272,256]{1,0:T(8,128)(2,1)S(1)}, u32[]{:S(2)}, u32[]{:S(2)}) collective-permute-start(bf16[272,256]{1,0:T(8,128)(2,1)S(1)} %get-tuple-element.27), channel_id=1, source_target_pairs={{0,24},{4,28},{8,16},{12,20},{16,8},{20,12},{24,0},{28,4},{1,25},{... | collective-permute-start | bytes 417800 | tf_op jit(solution)/shard_map/ppermute | solution.py:182
  30.8 7.4 %collective-permute-done.19.refs_3_ = bf16[272,256]{1,0:T(8,128)(2,1)S(1)} collective-permute-done((bf16[272,256]{1,0:T(8,128)(2,1)S(1)}, bf16[272,256]{1,0:T(8,128)(2,1)S(1)}, u32[]{:S(2)}, u32[]{:S(2)}) %collective-permute-start.19) | collective-permute-done | bytes 139296 | tf_op jit(solution)/shard_map/ppermute | solution.py:182
  40.0 1.6 %collective-permute-start.20 = (bf16[512,256]{1,0:T(8,128)(2,1)S(1)}, bf16[512,256]{1,0:T(8,128)(2,1)S(1)}, u32[]{:S(2)}, u32[]{:S(2)}) collective-permute-start(bf16[512,256]{1,0:T(8,128)(2,1)S(1)} %get-tuple-element.44), channel_id=1, source_target_pairs={{0,1},{1,2},{2,3},{3,0},{4,5},{5,6},{6,7},{7,4},{8,9},{9,10},{10,1... | collective-permute-start | bytes 786440 | tf_op jit(solution)/shard_map/ppermute | solution.py:185
  41.7 1.5 %collective-permute-start.13 = (bf16[256,256]{1,0:T(8,128)(2,1)S(1)}, bf16[256,256]{1,0:T(8,128)(2,1)S(1)}, u32[]{:S(2)}, u32[]{:S(2)}) collective-permute-start(bf16[256,256]{1,0:T(8,128)(2,1)S(1)} %get-tuple-element.37), channel_id=1, source_target_pairs={{0,2},{1,3},{2,0},{3,1},{4,6},{5,7},{6,4},{7,5},{8,10},{9,11},{10,... | collective-permute-start | bytes 393224 | tf_op jit(solution)/shard_map/ppermute | solution.py:185
  43.2 3.3 %collective-permute-done.12.refs_1_ = bf16[256,256]{1,0:T(8,128)(2,1)S(1)} collective-permute-done((bf16[256,256]{1,0:T(8,128)(2,1)S(1)}, bf16[256,256]{1,0:T(8,128)(2,1)S(1)}, u32[]{:S(2)}, u32[]{:S(2)}) %collective-permute-start.12) | collective-permute-done | bytes 131104 | tf_op jit(solution)/shard_map/ppermute | solution.py:185
  46.5 1.4 %collective-permute-start.14 = (bf16[256,256]{1,0:T(8,128)(2,1)S(1)}, bf16[256,256]{1,0:T(8,128)(2,1)S(1)}, u32[]{:S(2)}, u32[]{:S(2)}) collective-permute-start(bf16[256,256]{1,0:T(8,128)(2,1)S(1)} %get-tuple-element.38), channel_id=1, source_target_pairs={{0,3},{1,0},{2,1},{3,2},{4,7},{5,4},{6,5},{7,6},{8,11},{9,8},{10,9... | collective-permute-start | bytes 393224 | tf_op jit(solution)/shard_map/ppermute | solution.py:185
  47.9 9.3 %collective-permute-done.13.refs_2_ = bf16[256,256]{1,0:T(8,128)(2,1)S(1)} collective-permute-done((bf16[256,256]{1,0:T(8,128)(2,1)S(1)}, bf16[256,256]{1,0:T(8,128)(2,1)S(1)}, u32[]{:S(2)}, u32[]{:S(2)}) %collective-permute-start.13) | collective-permute-done | bytes 131104 | tf_op jit(solution)/shard_map/ppermute | solution.py:185
  57.2 4.3 %collective-permute-start.22 = (bf16[512,256]{1,0:T(8,128)(2,1)S(1)}, bf16[512,256]{1,0:T(8,128)(2,1)S(1)}, u32[]{:S(2)}, u32[]{:S(2)}) collective-permute-start(bf16[512,256]{1,0:T(8,128)(2,1)S(1)} %get-tuple-element.46), channel_id=1, source_target_pairs={{0,3},{1,0},{2,1},{3,2},{4,7},{5,4},{6,5},{7,6},{8,11},{9,8},{10,9... | collective-permute-start | bytes 786440 | tf_op jit(solution)/shard_map/ppermute | solution.py:185
  62.2 10.7 %collective-permute-done.21.refs_8_ = bf16[512,256]{1,0:T(8,128)(2,1)S(1)} collective-permute-done((bf16[512,256]{1,0:T(8,128)(2,1)S(1)}, bf16[512,256]{1,0:T(8,128)(2,1)S(1)}, u32[]{:S(2)}, u32[]{:S(2)}) %collective-permute-start.21) | collective-permute-done | bytes 262176 | tf_op jit(solution)/shard_map/ppermute | solution.py:185
  72.9 1.5 %collective-permute-start.8 = (bf16[512,384]{1,0:T(8,128)(2,1)S(1)}, bf16[512,384]{1,0:T(8,128)(2,1)S(1)}, u32[]{:S(2)}, u32[]{:S(2)}) collective-permute-start(bf16[512,384]{1,0:T(8,128)(2,1)S(1)} %slice.9), channel_id=1, source_target_pairs={{0,8},{4,12},{8,0},{12,4},{16,24},{20,28},{24,16},{28,20},{1,9},{5... | collective-permute-start | bytes 1179656 | tf_op jit(solution)/shard_map/ppermute | solution.py:182
  75.5 6.5 %collective-permute-done.8.refs_5_ = bf16[512,384]{1,0:T(8,128)(2,1)S(1)} collective-permute-done((bf16[512,384]{1,0:T(8,128)(2,1)S(1)}, bf16[512,384]{1,0:T(8,128)(2,1)S(1)}, u32[]{:S(2)}, u32[]{:S(2)}) %collective-permute-start.8) | collective-permute-done | bytes 393248 | tf_op jit(solution)/shard_map/ppermute | solution.py:182
  83.5 5.0 %collective-permute-start.2 = (bf16[256,256]{1,0:T(8,128)(2,1)S(1)}, bf16[256,256]{1,0:T(8,128)(2,1)S(1)}, u32[]{:S(2)}, u32[]{:S(2)}) collective-permute-start(bf16[256,256]{1,0:T(8,128)(2,1)S(1)} %get-tuple-element.30), channel_id=1, source_target_pairs={{0,1},{1,2},{2,3},{3,0},{4,5},{5,6},{6,7},{7,4},{8,9},{9,10},{10,1... | collective-permute-start | bytes 393224 | tf_op jit(solution)/shard_map/ppermute | solution.py:185
  88.6 3.3 %collective-permute-start.3 = (bf16[256,256]{1,0:T(8,128)(2,1)S(1)}, bf16[256,256]{1,0:T(8,128)(2,1)S(1)}, u32[]{:S(2)}, u32[]{:S(2)}) collective-permute-start(bf16[256,256]{1,0:T(8,128)(2,1)S(1)} %get-tuple-element.31), channel_id=1, source_target_pairs={{0,2},{1,3},{2,0},{3,1},{4,6},{5,7},{6,4},{7,5},{8,10},{9,11},{10,... | collective-permute-start | bytes 393224 | tf_op jit(solution)/shard_map/ppermute | solution.py:185
  91.9 2.6 %early.1.refs_8_ = f32[256,768]{1,0:T(8,128)S(1)} custom-call(bf16[256,256]{1,0:T(8,128)(2,1)S(1)} %get-tuple-element.35.refs_0_, bf16[256,256]{1,0:T(8,128)(2,1)S(1)} %collective-permute-done.12.refs_1_, bf16[256,256]{1,0:T(8,128)(2,1)S(1)} %collective-permute-done.13.refs_2_, bf16[256,256]{1,0:T(8,128)(2,1)S(1)} %collective-permute-done.14.refs_3_, ...), custom_call_target="tpu_custom_call" | custom-call | flops 1207959552 | bytes 7077888 | tf_op jit(solution)/shard_map/early/pallas_call | solution.py:152
  95.8 5.4 %collective-permute-done.3.refs_2_ = bf16[256,256]{1,0:T(8,128)(2,1)S(1)} collective-permute-done((bf16[256,256]{1,0:T(8,128)(2,1)S(1)}, bf16[256,256]{1,0:T(8,128)(2,1)S(1)}, u32[]{:S(2)}, u32[]{:S(2)}) %collective-permute-start.3) | collective-permute-done | bytes 131104 | tf_op jit(solution)/shard_map/ppermute | solution.py:185
  101.2 2.8 %update.1 = (f32[1,256,768]{2,1,0:T(8,128)}, f32[1,256,768]{2,1,0:T(8,128)}, f32[256,768]{1,0:T(8,128)S(1)}, f32[8,128]{1,0:T(8,128)S(1)}) custom-call(bf16[256,256]{1,0:T(8,128)(2,1)S(1)} %get-tuple-element.29.refs_0_, bf16[256,256]{1,0:T(8,128)(2,1)S(1)} %collective-permute-done.2.refs_1_, bf16[256,256]{1,0:T(8,128)(2,1)S(1)} %collective-permute-done.3.refs_2_, ...), custom_call_target="tpu_custom_call" | custom-call | flops 402653184 | bytes 7606272 | tf_op jit(solution)/shard_map/update/pallas_call | solution.py:152
  105.7 1.4 %collective-permute-start.27 = (f32[8,128]{1,0:T(8,128)S(1)}, f32[8,128]{1,0:T(8,128)S(1)}, u32[]{:S(2)}, u32[]{:S(2)}) collective-permute-start(f32[8,128]{1,0:T(8,128)S(1)} %add.3.refs_0_), channel_id=1, source_target_pairs={{0,16},{4,20},{8,24},{12,28},{16,0},{20,4},{24,8},{28,12},{1,17},{... | collective-permute-start | bytes 12296 | tf_op jit(solution)/shard_map/ppermute | solution.py:182
  107.0 1.6 %collective-permute-start.28 = (f32[8,128]{1,0:T(8,128)S(1)}, f32[8,128]{1,0:T(8,128)S(1)}, u32[]{:S(2)}, u32[]{:S(2)}) collective-permute-start(f32[8,128]{1,0:T(8,128)S(1)} %add.3.refs_0_), channel_id=1, source_target_pairs={{0,24},{4,28},{8,16},{12,20},{16,8},{20,12},{24,0},{28,4},{1,25},{... | collective-permute-start | bytes 12296 | tf_op jit(solution)/shard_map/ppermute | solution.py:182
  109.3 2.3 %collective-permute-done.28.refs_3_ = f32[8,128]{1,0:T(8,128)S(1)} collective-permute-done((f32[8,128]{1,0:T(8,128)S(1)}, f32[8,128]{1,0:T(8,128)S(1)}, u32[]{:S(2)}, u32[]{:S(2)}) %collective-permute-start.28) | collective-permute-done | bytes 4128 | tf_op jit(solution)/shard_map/ppermute | solution.py:182
  (60 shorter events, 13.9 us)
Async XLA Ops:
  0.6 60.9 %collective-permute-start.5 = (bf16[512,768]{1,0:T(8,128)(2,1)}, bf16[512,768]{1,0:T(8,128)(2,1)S(1)}, u32[]{:S(2)}, u32[]{:S(2)}) collective-permute-start(bf16[512,768]{1,0:T(8,128)(2,1)} %bitcast.4), channel_id=1, source_target_pairs={{0,8},{4,12},{8,0},{12,4},{16,24},{20,28},{24,16},{28,20},{1,9},{5... | collective-permute-start | bytes 2359304 | tf_op jit(solution)/shard_map/ppermute | solution.py:182
  3.6 58.4 %collective-permute-start.7 = (bf16[512,768]{1,0:T(8,128)(2,1)}, bf16[512,768]{1,0:T(8,128)(2,1)S(1)}, u32[]{:S(2)}, u32[]{:S(2)}) collective-permute-start(bf16[512,768]{1,0:T(8,128)(2,1)} %bitcast.5), channel_id=1, source_target_pairs={{0,16},{4,20},{8,24},{12,28},{16,0},{20,4},{24,8},{28,12},{1,17},{... | collective-permute-start | bytes 2359304 | tf_op jit(solution)/shard_map/ppermute | solution.py:182
  7.4 17.8 %collective-permute-start.16 = (bf16[272,256]{1,0:T(8,128)(2,1)S(1)}, bf16[272,256]{1,0:T(8,128)(2,1)S(1)}, u32[]{:S(2)}, u32[]{:S(2)}) collective-permute-start(bf16[272,256]{1,0:T(8,128)(2,1)S(1)} %get-tuple-element.39), channel_id=1, source_target_pairs={{0,8},{4,12},{8,0},{12,4},{16,24},{20,28},{24,16},{28,20},{1,9},{5... | collective-permute-start | bytes 417800 | tf_op jit(solution)/shard_map/ppermute | solution.py:182
  8.0 18.6 %collective-permute-start.17 = (bf16[272,256]{1,0:T(8,128)(2,1)S(1)}, bf16[272,256]{1,0:T(8,128)(2,1)S(1)}, u32[]{:S(2)}, u32[]{:S(2)}) collective-permute-start(bf16[272,256]{1,0:T(8,128)(2,1)S(1)} %get-tuple-element.40), channel_id=1, source_target_pairs={{0,12},{4,8},{8,4},{12,0},{16,28},{20,24},{24,20},{28,16},{1,13},{... | collective-permute-start | bytes 417800 | tf_op jit(solution)/shard_map/ppermute | solution.py:182
  8.1 20.5 %collective-permute-start.18 = (bf16[272,256]{1,0:T(8,128)(2,1)S(1)}, bf16[272,256]{1,0:T(8,128)(2,1)S(1)}, u32[]{:S(2)}, u32[]{:S(2)}) collective-permute-start(bf16[272,256]{1,0:T(8,128)(2,1)S(1)} %get-tuple-element.41), channel_id=1, source_target_pairs={{0,16},{4,20},{8,24},{12,28},{16,0},{20,4},{24,8},{28,12},{1,17},{... | collective-permute-start | bytes 417800 | tf_op jit(solution)/shard_map/ppermute | solution.py:182
  26.6 11.6 %collective-permute-start.19 = (bf16[272,256]{1,0:T(8,128)(2,1)S(1)}, bf16[272,256]{1,0:T(8,128)(2,1)S(1)}, u32[]{:S(2)}, u32[]{:S(2)}) collective-permute-start(bf16[272,256]{1,0:T(8,128)(2,1)S(1)} %get-tuple-element.42), channel_id=1, source_target_pairs={{0,20},{4,16},{8,28},{12,24},{16,4},{20,0},{24,12},{28,8},{1,21},{... | collective-permute-start | bytes 417800 | tf_op jit(solution)/shard_map/ppermute | solution.py:182
  28.6 11.5 %collective-permute-start = (bf16[272,256]{1,0:T(8,128)(2,1)S(1)}, bf16[272,256]{1,0:T(8,128)(2,1)S(1)}, u32[]{:S(2)}, u32[]{:S(2)}) collective-permute-start(bf16[272,256]{1,0:T(8,128)(2,1)S(1)} %get-tuple-element.27), channel_id=1, source_target_pairs={{0,24},{4,28},{8,16},{12,20},{16,8},{20,12},{24,0},{28,4},{1,25},{... | collective-permute-start | bytes 417800 | tf_op jit(solution)/shard_map/ppermute | solution.py:182
  30.0 11.7 %collective-permute-start.1 = (bf16[272,256]{1,0:T(8,128)(2,1)S(1)}, bf16[272,256]{1,0:T(8,128)(2,1)S(1)}, u32[]{:S(2)}, u32[]{:S(2)}) collective-permute-start(bf16[272,256]{1,0:T(8,128)(2,1)S(1)} %get-tuple-element.28), channel_id=1, source_target_pairs={{0,28},{4,24},{8,20},{12,16},{16,12},{20,8},{24,4},{28,0},{1,29},{... | collective-permute-start | bytes 417800 | tf_op jit(solution)/shard_map/ppermute | solution.py:182
  38.3 8.2 %collective-permute-start.12 = (bf16[256,256]{1,0:T(8,128)(2,1)S(1)}, bf16[256,256]{1,0:T(8,128)(2,1)S(1)}, u32[]{:S(2)}, u32[]{:S(2)}) collective-permute-start(bf16[256,256]{1,0:T(8,128)(2,1)S(1)} %get-tuple-element.36), channel_id=1, source_target_pairs={{0,1},{1,2},{2,3},{3,0},{4,5},{5,6},{6,7},{7,4},{8,9},{9,10},{10,1... | collective-permute-start | bytes 393224 | tf_op jit(solution)/shard_map/ppermute | solution.py:185
  40.0 21.5 %collective-permute-start.20 = (bf16[512,256]{1,0:T(8,128)(2,1)S(1)}, bf16[512,256]{1,0:T(8,128)(2,1)S(1)}, u32[]{:S(2)}, u32[]{:S(2)}) collective-permute-start(bf16[512,256]{1,0:T(8,128)(2,1)S(1)} %get-tuple-element.44), channel_id=1, source_target_pairs={{0,1},{1,2},{2,3},{3,0},{4,5},{5,6},{6,7},{7,4},{8,9},{9,10},{10,1... | collective-permute-start | bytes 786440 | tf_op jit(solution)/shard_map/ppermute | solution.py:185
  41.7 15.5 %collective-permute-start.13 = (bf16[256,256]{1,0:T(8,128)(2,1)S(1)}, bf16[256,256]{1,0:T(8,128)(2,1)S(1)}, u32[]{:S(2)}, u32[]{:S(2)}) collective-permute-start(bf16[256,256]{1,0:T(8,128)(2,1)S(1)} %get-tuple-element.37), channel_id=1, source_target_pairs={{0,2},{1,3},{2,0},{3,1},{4,6},{5,7},{6,4},{7,5},{8,10},{9,11},{10,... | collective-permute-start | bytes 393224 | tf_op jit(solution)/shard_map/ppermute | solution.py:185
  46.5 10.7 %collective-permute-start.14 = (bf16[256,256]{1,0:T(8,128)(2,1)S(1)}, bf16[256,256]{1,0:T(8,128)(2,1)S(1)}, u32[]{:S(2)}, u32[]{:S(2)}) collective-permute-start(bf16[256,256]{1,0:T(8,128)(2,1)S(1)} %get-tuple-element.38), channel_id=1, source_target_pairs={{0,3},{1,0},{2,1},{3,2},{4,7},{5,4},{6,5},{7,6},{8,11},{9,8},{10,9... | collective-permute-start | bytes 393224 | tf_op jit(solution)/shard_map/ppermute | solution.py:185
  57.2 15.7 %collective-permute-start.21 = (bf16[512,256]{1,0:T(8,128)(2,1)S(1)}, bf16[512,256]{1,0:T(8,128)(2,1)S(1)}, u32[]{:S(2)}, u32[]{:S(2)}) collective-permute-start(bf16[512,256]{1,0:T(8,128)(2,1)S(1)} %get-tuple-element.45), channel_id=1, source_target_pairs={{0,2},{1,3},{2,0},{3,1},{4,6},{5,7},{6,4},{7,5},{8,10},{9,11},{10,... | collective-permute-start | bytes 786440 | tf_op jit(solution)/shard_map/ppermute | solution.py:185
  57.2 17.2 %collective-permute-start.22 = (bf16[512,256]{1,0:T(8,128)(2,1)S(1)}, bf16[512,256]{1,0:T(8,128)(2,1)S(1)}, u32[]{:S(2)}, u32[]{:S(2)}) collective-permute-start(bf16[512,256]{1,0:T(8,128)(2,1)S(1)} %get-tuple-element.46), channel_id=1, source_target_pairs={{0,3},{1,0},{2,1},{3,2},{4,7},{5,4},{6,5},{7,6},{8,11},{9,8},{10,9... | collective-permute-start | bytes 786440 | tf_op jit(solution)/shard_map/ppermute | solution.py:185
  61.5 22.0 %collective-permute-start.15 = (bf16[512,768]{1,0:T(8,128)(2,1)S(1)}, bf16[512,768]{1,0:T(8,128)(2,1)S(1)}, u32[]{:S(2)}, u32[]{:S(2)}) collective-permute-start(bf16[512,768]{1,0:T(8,128)(2,1)S(1)} %bitcast.6), channel_id=1, source_target_pairs={{0,4},{4,0},{8,12},{12,8},{16,20},{20,16},{24,28},{28,24},{1,5},{5... | collective-permute-start | bytes 2359304 | tf_op jit(solution)/shard_map/ppermute | solution.py:182
  61.5 27.0 %collective-permute-start.23 = (bf16[512,768]{1,0:T(8,128)(2,1)S(1)}, bf16[512,768]{1,0:T(8,128)(2,1)S(1)}, u32[]{:S(2)}, u32[]{:S(2)}) collective-permute-start(bf16[512,768]{1,0:T(8,128)(2,1)S(1)} %collective-permute-done.5.refs_10_), channel_id=1, source_target_pairs={{0,4},{4,0},{8,12},{12,8},{16,20},{20,16},{24,28},{28,24},{1,5},{5... | collective-permute-start | bytes 2359304 | tf_op jit(solution)/shard_map/ppermute | solution.py:182
  62.0 29.8 %collective-permute-start.24 = (bf16[512,768]{1,0:T(8,128)(2,1)S(1)}, bf16[512,768]{1,0:T(8,128)(2,1)S(1)}, u32[]{:S(2)}, u32[]{:S(2)}) collective-permute-start(bf16[512,768]{1,0:T(8,128)(2,1)S(1)} %collective-permute-done.7.refs_12_), channel_id=1, source_target_pairs={{0,4},{4,0},{8,12},{12,8},{16,20},{20,16},{24,28},{28,24},{1,5},{5... | collective-permute-start | bytes 2359304 | tf_op jit(solution)/shard_map/ppermute | solution.py:182
  72.9 9.1 %collective-permute-start.8 = (bf16[512,384]{1,0:T(8,128)(2,1)S(1)}, bf16[512,384]{1,0:T(8,128)(2,1)S(1)}, u32[]{:S(2)}, u32[]{:S(2)}) collective-permute-start(bf16[512,384]{1,0:T(8,128)(2,1)S(1)} %slice.9), channel_id=1, source_target_pairs={{0,8},{4,12},{8,0},{12,4},{16,24},{20,28},{24,16},{28,20},{1,9},{5... | collective-permute-start | bytes 1179656 | tf_op jit(solution)/shard_map/ppermute | solution.py:182
  74.4 8.8 %collective-permute-start.6 = (bf16[512,384]{1,0:T(8,128)(2,1)S(1)}, bf16[512,384]{1,0:T(8,128)(2,1)S(1)}, u32[]{:S(2)}, u32[]{:S(2)}) collective-permute-start(bf16[512,384]{1,0:T(8,128)(2,1)S(1)} %slice.8), channel_id=1, source_target_pairs={{0,16},{4,20},{8,24},{12,28},{16,0},{20,4},{24,8},{28,12},{1,17},{... | collective-permute-start | bytes 1179656 | tf_op jit(solution)/shard_map/ppermute | solution.py:182
  82.0 19.1 %collective-permute-start.10 = (bf16[512,384]{1,0:T(8,128)(2,1)S(1)}, bf16[512,384]{1,0:T(8,128)(2,1)S(1)}, u32[]{:S(2)}, u32[]{:S(2)}) collective-permute-start(bf16[512,384]{1,0:T(8,128)(2,1)S(1)} %collective-permute-done.8.refs_5_), channel_id=1, source_target_pairs={{0,4},{4,0},{8,12},{12,8},{16,20},{20,16},{24,28},{28,24},{1,5},{5... | collective-permute-start | bytes 1179656 | tf_op jit(solution)/shard_map/ppermute | solution.py:182
  83.2 17.9 %collective-permute-start.9 = (bf16[512,384]{1,0:T(8,128)(2,1)S(1)}, bf16[512,384]{1,0:T(8,128)(2,1)S(1)}, u32[]{:S(2)}, u32[]{:S(2)}) collective-permute-start(bf16[512,384]{1,0:T(8,128)(2,1)S(1)} %collective-permute-done.6.refs_4_), channel_id=1, source_target_pairs={{0,4},{4,0},{8,12},{12,8},{16,20},{20,16},{24,28},{28,24},{1,5},{5... | collective-permute-start | bytes 1179656 | tf_op jit(solution)/shard_map/ppermute | solution.py:182
  83.5 12.2 %collective-permute-start.2 = (bf16[256,256]{1,0:T(8,128)(2,1)S(1)}, bf16[256,256]{1,0:T(8,128)(2,1)S(1)}, u32[]{:S(2)}, u32[]{:S(2)}) collective-permute-start(bf16[256,256]{1,0:T(8,128)(2,1)S(1)} %get-tuple-element.30), channel_id=1, source_target_pairs={{0,1},{1,2},{2,3},{3,0},{4,5},{5,6},{6,7},{7,4},{8,9},{9,10},{10,1... | collective-permute-start | bytes 393224 | tf_op jit(solution)/shard_map/ppermute | solution.py:185
  88.6 12.5 %collective-permute-start.3 = (bf16[256,256]{1,0:T(8,128)(2,1)S(1)}, bf16[256,256]{1,0:T(8,128)(2,1)S(1)}, u32[]{:S(2)}, u32[]{:S(2)}) collective-permute-start(bf16[256,256]{1,0:T(8,128)(2,1)S(1)} %get-tuple-element.31), channel_id=1, source_target_pairs={{0,2},{1,3},{2,0},{3,1},{4,6},{5,7},{6,4},{7,5},{8,10},{9,11},{10,... | collective-permute-start | bytes 393224 | tf_op jit(solution)/shard_map/ppermute | solution.py:185
  91.9 9.2 %collective-permute-start.4 = (bf16[256,256]{1,0:T(8,128)(2,1)S(1)}, bf16[256,256]{1,0:T(8,128)(2,1)S(1)}, u32[]{:S(2)}, u32[]{:S(2)}) collective-permute-start(bf16[256,256]{1,0:T(8,128)(2,1)S(1)} %get-tuple-element.32), channel_id=1, source_target_pairs={{0,3},{1,0},{2,1},{3,2},{4,7},{5,4},{6,5},{7,6},{8,11},{9,8},{10,9... | collective-permute-start | bytes 393224 | tf_op jit(solution)/shard_map/ppermute | solution.py:185
  (13 other events, 102.9 us)

commit v2 on v1

v2 whole, which is shorter than its diff:
```python
import functools

import jax
import jax.numpy as jnp
from jax import lax
from jax.experimental import pallas as pl
from jax.experimental.pallas import tpu as pltpu
from jax.sharding import PartitionSpec as P

VMEM = pl.BlockSpec(memory_space=pltpu.VMEM)
TAIL = 16
ROWS_FIRST = (((0,), (0,)), ((), ()))


def on_device(
    cotangent,
    route_weight,
    expert_ids,
    slot_ids,
    hidden_saved,
    down_weight,
    first_moment,
    second_moment,
):
    tok_rows, width = cotangent.shape
    owners = lax.axis_size("expert")
    hidden_rows = hidden_saved.reshape(-1, hidden_saved.shape[-1])
    capacity = hidden_rows.shape[0] // owners
    weight = down_weight[0]
    routed = (route_weight[:, None] * cotangent.astype(jnp.float32)).astype(jnp.bfloat16)
    target = expert_ids * capacity + slot_ids
    outgoing = jnp.zeros((owners * capacity, width), jnp.bfloat16).at[target].set(routed)
    arrived = lax.all_to_all(
        outgoing.reshape(owners, capacity, width), "expert", split_axis=0, concat_axis=0, tiled=True
    )
    arrived = arrived.reshape(owners * capacity, width)
    whole_term = lax.dot_general(
        arrived, hidden_rows, (((0,), (0,)), ((), ())), preferred_element_type=jnp.float32
    )
    grad = lax.psum_scatter(whole_term, "dp", scatter_dimension=0, tiled=True)
    new_first = 0.9 * first_moment[0] + 0.1 * grad
    new_second = 0.999 * second_moment[0] + 0.001 * grad * grad
    update = (
        new_first / (1.0 - 0.9**10) / (jnp.sqrt(new_second / (1.0 - 0.999**10)) + 1e-06)
        + 0.01 * weight
    )
    weight_sq, update_sq = lax.psum((jnp.sum(weight * weight), jnp.sum(update * update)), "dp")
    ratio = jnp.sqrt(weight_sq) / (jnp.sqrt(update_sq) + 1e-06)
    new_weight = weight - 0.1 * ratio * update
    return (new_weight[None], new_first[None], new_second[None])


def cut_kernel(n_chips, cot_ref, scale_ref, expert_ref, slot_ref, *out_refs):
    tokens, width = cot_ref.shape
    part = width // n_chips
    half = part // 2
    me = lax.axis_index("dp")
    chip, core = me // 2, lax.rem(me, 2)
    scale = jnp.broadcast_to(scale_ref[...], (128, tokens)).T
    scale = jnp.concatenate([scale] * (half // 128), axis=1)
    row = lax.broadcasted_iota(jnp.int32, (TAIL, tokens), 0)
    ids = jnp.where(row == 0, expert_ref[...], jnp.where(row == 1, slot_ref[...], 0))
    ids = ids.astype(jnp.float32).astype(jnp.bfloat16)
    for mask, out_ref in enumerate(out_refs):
        for side in range(2):
            begin = (chip ^ mask) * part + (core ^ side) * half
            block = cot_ref[:, pl.ds(pl.multiple_of(begin, half), half)].astype(jnp.float32)
            out_ref[:tokens, side * half : (side + 1) * half] = (scale * block).astype(jnp.bfloat16)
        out_ref[tokens:, :] = jnp.concatenate([ids] * (part // tokens), axis=1)


def pack_kernel(owners, capacity, n_blocks, *refs):
    me = lax.axis_index("expert")
    blocks, outs = refs[:n_blocks], refs[n_blocks : n_blocks + owners]
    tokens = blocks[0].shape[0] - TAIL
    slot = lax.broadcasted_iota(jnp.int32, (capacity, tokens), 0).astype(jnp.float32)
    for at, block in enumerate(blocks):
        ids = block[tokens:, :tokens].astype(jnp.float32)
        place = ids[0:1, :] * capacity + ids[1:2, :]
        rows = block[:tokens, :]
        for shift, out in enumerate(outs):
            expert = lax.rem(me + shift, owners)
            first = (expert * capacity).astype(jnp.float32)
            hot = jnp.where(slot + first == place, 1.0, 0.0).astype(jnp.bfloat16)
            packed = jnp.dot(hot, rows, preferred_element_type=jnp.float32)
            out[at * capacity : (at + 1) * capacity, :] = packed.astype(jnp.bfloat16)


def product_kernel(owners, capacity, columns, cuts, *refs):
    me = lax.axis_index("expert")
    packed, refs = refs[:owners], refs[owners:]
    saved, early, out = refs[: sum(cuts)], refs[sum(cuts) : -1], refs[-1]
    begins = [
        pl.multiple_of(lax.rem(me + owners - shift, owners) * capacity, capacity) for shift in range(owners)
    ]
    rows = [
        jnp.concatenate([ref[at * capacity : (at + 1) * capacity, columns] for ref in packed])
        for at in range(len(cuts))
    ]
    groups = []
    for n in cuts:
        groups.append(saved[:n])
        saved = saved[n:]
    wide = min(part.shape[1] for parts in groups for part in parts)
    for column in range(0, out.shape[1], wide):
        total = None
        for group, parts in zip(rows, groups):
            part = parts[column // parts[0].shape[1]]
            inside = column % part.shape[1]
            right = jnp.concatenate([part[pl.ds(begin, capacity), inside : inside + wide] for begin in begins])
            term = lax.dot_general(group, right, ROWS_FIRST, preferred_element_type=jnp.float32)
            total = term if total is None else total + term
        for ref in early:
            total = total + ref[:, column : column + wide]
        out[:, column : column + wide] = total


def update_kernel(mine_ref, other_ref, weight_ref, first_ref, second_ref, new_first, new_second, update_ref, sums):
    grad = mine_ref[...] + other_ref[...]
    weight = weight_ref[0]
    first = 0.9 * first_ref[0] + 0.1 * grad
    second = 0.999 * second_ref[0] + 0.001 * grad * grad
    new_first[0] = first
    new_second[0] = second
    update = first / (1.0 - 0.9**10) / (jnp.sqrt(second / (1.0 - 0.999**10)) + 1e-06) + 0.01 * weight
    update_ref[...] = update
    row = lax.broadcasted_iota(jnp.int32, sums.shape, 0)
    sums[...] = jnp.where(row == 0, jnp.sum(weight * weight), jnp.sum(update * update))


def weight_kernel(n_sums, *refs):
    sums, (weight_ref, update_ref, new_weight) = refs[:n_sums], refs[n_sums:]
    total = sums[0][...]
    for other in sums[1:]:
        total = total + other[...]
    norm = jnp.sqrt(total)
    ratio = norm[0:1, 0:1] / (norm[1:2, 0:1] + 1e-06)
    new_weight[0] = weight_ref[0] - (0.1 * ratio) * update_ref[...]


def call(kernel, out_shape, *args, flops=0, name=None):
    nbytes = sum(a.size * a.dtype.itemsize for a in jax.tree.leaves((args, out_shape)))
    return pl.pallas_call(
        kernel,
        out_shape=out_shape,
        in_specs=[VMEM] * len(args),
        out_specs=jax.tree.map(lambda _: VMEM, out_shape),
        compiler_params=pltpu.CompilerParams(vmem_limit_bytes=40 * 2**20),
        cost_estimate=pl.CostEstimate(flops=flops, bytes_accessed=nbytes, transcendentals=0),
        name=name,
    )(*args)


def after(arrays, *earlier):
    return lax.optimization_barrier((arrays, earlier))[0]


def by_permutes(
    cotangent,
    route_weight,
    expert_ids,
    slot_ids,
    hidden_saved,
    down_weight,
    first_moment,
    second_moment,
):
    n_dp, owners = lax.axis_size("dp"), lax.axis_size("expert")
    n_chips = n_dp // 2
    tokens, width = cotangent.shape
    capacity, ff = hidden_saved.shape[3:]
    part = width // n_chips
    half = part // 2
    bf16, f32 = jnp.bfloat16, jnp.float32
    hidden = hidden_saved.reshape(owners * capacity, ff)

    def across(array, mask):
        return lax.ppermute(array, "dp", [(d, d ^ mask) for d in range(n_dp)])

    def along(array, shift):
        return lax.ppermute(array, "expert", [(d, (d + shift) % owners) for d in range(owners)])

    def pack(*blocks):
        size = len(blocks) * capacity
        return call(
            functools.partial(pack_kernel, owners, capacity, len(blocks)),
            [jax.ShapeDtypeStruct((size, part), bf16)] * owners,
            *blocks,
            flops=2 * size * owners * tokens * part,
            name="pack",
        )

    def multiply(columns, packed, groups, *early):
        n = columns.stop - columns.start
        return call(
            functools.partial(product_kernel, owners, capacity, columns, [len(parts) for parts in groups]),
            jax.ShapeDtypeStruct((n, ff), f32),
            *packed,
            *[part for parts in groups for part in parts],
            *early,
            flops=2 * len(groups) * owners * capacity * n * ff,
            name="product",
        )

    cut = call(
        functools.partial(cut_kernel, n_chips),
        [jax.ShapeDtypeStruct((tokens + TAIL, part), bf16)] * n_chips,
        cotangent,
        route_weight.reshape(1, tokens),
        expert_ids.reshape(1, tokens),
        slot_ids.reshape(1, tokens),
        name="cut",
    )
    near = pack(cut[0])
    cut = after((cut[1], cut[2], cut[3]), *near)
    from_x, from_y, from_xy = across(cut[0], 2), across(cut[1], 4), across(cut[2], 6)
    near = {0: near[0], 1: along(near[1], 1), 2: along(near[2], 2), 3: near[3]}
    near[3] = along(after(near[3], near[1]), 3)
    far = pack(from_x, from_y, from_xy)
    far, hidden_sent = after((far, hidden), *near.values())
    far = {0: far[0], 1: along(far[1], 1), 2: far[2], 3: along(far[3], 3)}
    by_x, by_y = across(hidden_sent, 2), across(hidden_sent, 4)
    far[2], left, right = after((far[2], by_x[:, : ff // 2], by_y[:, ff // 2 :]), far[1], far[3], by_x, by_y)
    far[2] = along(far[2], 2)
    by_xy = across(left, 4), across(right, 2)

    keep, give = slice(0, half), slice(half, part)
    totals = {}
    for side in (give, keep):
        early = multiply(side, near.values(), [(hidden,)])
        totals[side.start] = multiply(side, far.values(), [(by_x,), (by_y,), by_xy], early)
    other = across(totals[give.start], 1)

    state = jax.ShapeDtypeStruct((1, half, ff), f32)
    new_first, new_second, update, sums = call(
        update_kernel,
        [state, state, jax.ShapeDtypeStruct((half, ff), f32), jax.ShapeDtypeStruct((8, 128), f32)],
        totals[keep.start],
        other,
        down_weight,
        first_moment,
        second_moment,
        name="update",
    )
    sums = sums + across(sums, 1)
    parts = [sums] + [across(sums, mask) for mask in (2, 4, 6)]
    new_weight = call(
        functools.partial(weight_kernel, len(parts)),
        state,
        *parts,
        down_weight,
        update,
        name="weight",
    )
    return new_weight, new_first, new_second


def solution(mesh):
    placed = (
        P(("dp", "expert"), None),
        P(("dp", "expert")),
        P(("dp", "expert")),
        P(("dp", "expert")),
        P("dp", "expert", None, None, None),
        P("expert", "dp", None),
        P("expert", "dp", None),
        P("expert", "dp", None),
    )
    return jax.shard_map(
        by_permutes if mesh.shape["dp"] == 8 else on_device,
        mesh=mesh,
        in_specs=placed,
        out_specs=(P("expert", "dp", None), P("expert", "dp", None), P("expert", "dp", None)),
        check_vma=False,
    )
```

time: 113 us -> 76.8 us (0.68)
  waiting for transfers between devices: 67.3 us -> 42.8 us
  starting transfers between devices: 34.7 us -> 23.7 us
    ppermute x20 -> x12, waiting for transfers between devices: 37.3 us -> 19.4 us  [across(): return lax.ppermute(array, 'dp', [(d, d ^ mask) for d in range(n_dp)])]
    ppermute x9 -> x6, starting transfers between devices: 18.5 us -> 11.3 us  [along(): lax.ppermute(array, 'expert', [(d, (d + shift) % owners) for d in range(o...]
    ppermute x9 -> x6, waiting for transfers between devices: 30 us -> 23.4 us  [along(): lax.ppermute(array, 'expert', [(d, (d + shift) % owners) for d in range(o...]
    ppermute x20 -> x12, starting transfers between devices: 16.2 us -> 12.4 us  [across(): return lax.ppermute(array, 'dp', [(d, d ^ mask) for d in range(n_dp)])]
    pallas_call x7 -> x9, Pallas kernels: 7.79 us -> 7.39 us  [call(): pl.pallas_call(kernel, out_shape=out_shape, in_specs=[VMEM] * len(args),...]
  transfers between devices with their start and end apart: 29 -> 18, of which waited for: 14 -> 12; matrix products, arithmetic and copies ran while one was open for 0% -> 0% of each run, Pallas kernels for 4% -> 3%
where the time goes in v2:
time: 76.8 us; the launch traced here: 76.7 us
  waiting for transfers between devices  42.8 us (56%)
  starting transfers between devices  23.7 us (31%)
  Pallas kernels  7.39 us (10%)
  local copies, waits for them, and re-layouts  2.02 us (3%)
  between operations  0.78 us (1%)
    ppermute x6, waiting for transfers between devices, along(): lax.ppermute(array, 'expert', [(d, (d + shift) % owners) for d in range(o...  23.4 us
    ppermute x12, waiting for transfers between devices, across(): return lax.ppermute(array, 'dp', [(d, d ^ mask) for d in range(n_dp)])  19.4 us
    ppermute x12, starting transfers between devices, across(): return lax.ppermute(array, 'dp', [(d, d ^ mask) for d in range(n_dp)])  12.4 us
    ppermute x6, starting transfers between devices, along(): lax.ppermute(array, 'expert', [(d, (d + shift) % owners) for d in range(o...  11.3 us
    pallas_call x9, Pallas kernels, call(): pl.pallas_call(kernel, out_shape=out_shape, in_specs=[VMEM] * len(args),...  7.39 us
    unnamed x16, local copies, waits for them, and re-layouts  1.94 us
  transfers between devices with their start and end apart: 18, of which 12 were waited for; matrix products, arithmetic and copies ran while one was open for 0% of the time, Pallas kernels for 3%

profile of v2, /device:TPU:0, one launch (start us, length us, event | category | flops | bytes accessed | tf_op | source)
XLA Modules:
  0.0 76.7 jit_solution(16459667413253596636)
XLA Ops:
  1.3 1.2 %copy-done.2 = bf16[256,2048]{1,0:T(8,128)(2,1)S(1)} copy-done((bf16[256,2048]{1,0:T(8,128)(2,1)S(1)}, bf16[256,2048]{1,0:T(8,128)(2,1)}, u32[]{:S(2)}) %copy-start.2) | copy-done | bytes 1048600
  3.2 3.0 %collective-permute-start = (bf16[272,512]{1,0:T(8,128)(2,1)S(1)}, bf16[272,512]{1,0:T(8,128)(2,1)S(1)}, u32[]{:S(2)}, u32[]{:S(2)}) collective-permute-start(bf16[272,512]{1,0:T(8,128)(2,1)S(1)} %get-tuple-element.39), channel_id=1, source_target_pairs={{0,8},{4,12},{8,0},{12,4},{16,24},{20,28},{24,16},{28,20},{1,9},{5... | collective-permute-start | bytes 835592 | tf_op jit(solution)/shard_map/ppermute | solution.py:178
  6.2 1.5 %collective-permute-start.1 = (bf16[272,512]{1,0:T(8,128)(2,1)S(1)}, bf16[272,512]{1,0:T(8,128)(2,1)S(1)}, u32[]{:S(2)}, u32[]{:S(2)}) collective-permute-start(bf16[272,512]{1,0:T(8,128)(2,1)S(1)} %get-tuple-element.40), channel_id=1, source_target_pairs={{0,16},{4,20},{8,24},{12,28},{16,0},{20,4},{24,8},{28,12},{1,17},{... | collective-permute-start | bytes 835592 | tf_op jit(solution)/shard_map/ppermute | solution.py:178
  7.7 2.0 %collective-permute-start.3 = (bf16[128,512]{1,0:T(8,128)(2,1)S(1)}, bf16[128,512]{1,0:T(8,128)(2,1)S(1)}, u32[]{:S(2)}, u32[]{:S(2)}) collective-permute-start(bf16[128,512]{1,0:T(8,128)(2,1)S(1)} %get-tuple-element.36), channel_id=1, source_target_pairs={{0,1},{1,2},{2,3},{3,0},{4,5},{5,6},{6,7},{7,4},{8,9},{9,10},{10,1... | collective-permute-start | bytes 393224 | tf_op jit(solution)/shard_map/ppermute | solution.py:181
  9.8 2.6 %collective-permute-start.4 = (bf16[128,512]{1,0:T(8,128)(2,1)S(1)}, bf16[128,512]{1,0:T(8,128)(2,1)S(1)}, u32[]{:S(2)}, u32[]{:S(2)}) collective-permute-start(bf16[128,512]{1,0:T(8,128)(2,1)S(1)} %get-tuple-element.37), channel_id=1, source_target_pairs={{0,2},{1,3},{2,0},{3,1},{4,6},{5,7},{6,4},{7,5},{8,10},{9,11},{10,... | collective-permute-start | bytes 393224 | tf_op jit(solution)/shard_map/ppermute | solution.py:181
  12.3 3.7 %collective-permute-done.3.refs_1_ = bf16[128,512]{1,0:T(8,128)(2,1)S(1)} collective-permute-done((bf16[128,512]{1,0:T(8,128)(2,1)S(1)}, bf16[128,512]{1,0:T(8,128)(2,1)S(1)}, u32[]{:S(2)}, u32[]{:S(2)}) %collective-permute-start.3) | collective-permute-done | bytes 131104 | tf_op jit(solution)/shard_map/ppermute | solution.py:181
  16.0 1.3 %collective-permute-start.5 = (bf16[128,512]{1,0:T(8,128)(2,1)S(1)}, bf16[128,512]{1,0:T(8,128)(2,1)S(1)}, u32[]{:S(2)}, u32[]{:S(2)}) collective-permute-start(bf16[128,512]{1,0:T(8,128)(2,1)S(1)} %get-tuple-element.46), channel_id=1, source_target_pairs={{0,3},{1,0},{2,1},{3,2},{4,7},{5,4},{6,5},{7,6},{8,11},{9,8},{10,9... | collective-permute-start | bytes 393224 | tf_op jit(solution)/shard_map/ppermute | solution.py:181
  17.4 2.9 %collective-permute-done.1.refs_1_ = bf16[272,512]{1,0:T(8,128)(2,1)S(1)} collective-permute-done((bf16[272,512]{1,0:T(8,128)(2,1)S(1)}, bf16[272,512]{1,0:T(8,128)(2,1)S(1)}, u32[]{:S(2)}, u32[]{:S(2)}) %collective-permute-start.1) | collective-permute-done | bytes 278560 | tf_op jit(solution)/shard_map/ppermute | solution.py:178
  21.5 1.5 %collective-permute-start.8 = (bf16[512,768]{1,0:T(8,128)(2,1)S(1)}, bf16[512,768]{1,0:T(8,128)(2,1)S(1)}, u32[]{:S(2)}, u32[]{:S(2)}) collective-permute-start(bf16[512,768]{1,0:T(8,128)(2,1)S(1)} %bitcast.4), channel_id=1, source_target_pairs={{0,16},{4,20},{8,24},{12,28},{16,0},{20,4},{24,8},{28,12},{1,17},{... | collective-permute-start | bytes 2359304 | tf_op jit(solution)/shard_map/ppermute | solution.py:178
  23.0 1.5 %collective-permute-start.7 = (bf16[512,768]{1,0:T(8,128)(2,1)S(1)}, bf16[512,768]{1,0:T(8,128)(2,1)S(1)}, u32[]{:S(2)}, u32[]{:S(2)}) collective-permute-start(bf16[512,768]{1,0:T(8,128)(2,1)S(1)} %bitcast.5), channel_id=1, source_target_pairs={{0,8},{4,12},{8,0},{12,4},{16,24},{20,28},{24,16},{28,20},{1,9},{5... | collective-permute-start | bytes 2359304 | tf_op jit(solution)/shard_map/ppermute | solution.py:178
  24.5 2.8 %collective-permute-start.6 = (bf16[384,512]{1,0:T(8,128)(2,1)S(1)}, bf16[384,512]{1,0:T(8,128)(2,1)S(1)}, u32[]{:S(2)}, u32[]{:S(2)}) collective-permute-start(bf16[384,512]{1,0:T(8,128)(2,1)S(1)} %get-tuple-element.48), channel_id=1, source_target_pairs={{0,1},{1,2},{2,3},{3,0},{4,5},{5,6},{6,7},{7,4},{8,9},{9,10},{10,1... | collective-permute-start | bytes 1179656 | tf_op jit(solution)/shard_map/ppermute | solution.py:181
  28.3 11.2 %collective-permute-done.8.refs_5_ = bf16[512,768]{1,0:T(8,128)(2,1)S(1)} collective-permute-done((bf16[512,768]{1,0:T(8,128)(2,1)S(1)}, bf16[512,768]{1,0:T(8,128)(2,1)S(1)}, u32[]{:S(2)}, u32[]{:S(2)}) %collective-permute-start.8) | collective-permute-done | bytes 786464 | tf_op jit(solution)/shard_map/ppermute | solution.py:178
  39.6 1.2 %collective-permute-done.7.refs_4_ = bf16[512,768]{1,0:T(8,128)(2,1)S(1)} collective-permute-done((bf16[512,768]{1,0:T(8,128)(2,1)S(1)}, bf16[512,768]{1,0:T(8,128)(2,1)S(1)}, u32[]{:S(2)}, u32[]{:S(2)}) %collective-permute-start.7) | collective-permute-done | bytes 786464 | tf_op jit(solution)/shard_map/ppermute | solution.py:178
  40.8 2.6 %collective-permute-done.9.refs_3_ = bf16[384,512]{1,0:T(8,128)(2,1)S(1)} collective-permute-done((bf16[384,512]{1,0:T(8,128)(2,1)S(1)}, bf16[384,512]{1,0:T(8,128)(2,1)S(1)}, u32[]{:S(2)}, u32[]{:S(2)}) %collective-permute-start.9) | collective-permute-done | bytes 393248 | tf_op jit(solution)/shard_map/ppermute | solution.py:181
  43.5 1.5 %collective-permute-start.10 = (bf16[384,512]{1,0:T(8,128)(2,1)S(1)}, bf16[384,512]{1,0:T(8,128)(2,1)S(1)}, u32[]{:S(2)}, u32[]{:S(2)}) collective-permute-start(bf16[384,512]{1,0:T(8,128)(2,1)S(1)} %get-tuple-element.52), channel_id=1, source_target_pairs={{0,2},{1,3},{2,0},{3,1},{4,6},{5,7},{6,4},{7,5},{8,10},{9,11},{10,... | collective-permute-start | bytes 1179656 | tf_op jit(solution)/shard_map/ppermute | solution.py:181
  46.4 16.5 %collective-permute-done.10.refs_2_ = bf16[384,512]{1,0:T(8,128)(2,1)S(1)} collective-permute-done((bf16[384,512]{1,0:T(8,128)(2,1)S(1)}, bf16[384,512]{1,0:T(8,128)(2,1)S(1)}, u32[]{:S(2)}, u32[]{:S(2)}) %collective-permute-start.10) | collective-permute-done | bytes 393248 | tf_op jit(solution)/shard_map/ppermute | solution.py:181
  62.9 1.0 %product.7 = f32[256,768]{1,0:T(8,128)S(1)} custom-call(bf16[384,512]{1,0:T(8,128)(2,1)S(1)} %get-tuple-element.47.refs_0_, bf16[384,512]{1,0:T(8,128)(2,1)S(1)} %collective-permute-done.6.refs_1_, bf16[384,512]{1,0:T(8,128)(2,1)S(1)} %collective-permute-done.10.refs_2_, bf16[384,512]{1,0:T(8,128)(2,1)S(1)} %collective-permute-done.9.refs_3_, ...), custom_call_target="tpu_custom_call" | custom-call | flops 603979776 | bytes 5505024 | tf_op jit(solution)/shard_map/product/pallas_call | solution.py:143
  64.4 1.0 %product.5.mine_ref = f32[256,768]{1,0:T(8,128)S(1)} custom-call(bf16[384,512]{1,0:T(8,128)(2,1)S(1)} %get-tuple-element.47.refs_0_, bf16[384,512]{1,0:T(8,128)(2,1)S(1)} %collective-permute-done.6.refs_1_, bf16[384,512]{1,0:T(8,128)(2,1)S(1)} %collective-permute-done.10.refs_2_, bf16[384,512]{1,0:T(8,128)(2,1)S(1)} %collective-permute-done.9.refs_3_, ...), custom_call_target="tpu_custom_call" | custom-call | flops 603979776 | bytes 5505024 | tf_op jit(solution)/shard_map/product/pallas_call | solution.py:143
  66.3 2.3 %update.1 = (f32[1,256,768]{2,1,0:T(8,128)}, f32[1,256,768]{2,1,0:T(8,128)}, f32[256,768]{1,0:T(8,128)S(1)}, f32[8,128]{1,0:T(8,128)S(1)}) custom-call(f32[256,768]{1,0:T(8,128)S(1)} %product.5.mine_ref, f32[256,768]{1,0:T(8,128)S(1)} %collective-permute-done.13.other_ref, f32[1,256,768]{2,1,0:T(8,128)S(1)} %copy-done.1, f32[1,256,768]{2,1,0:T(8,128)S(1)} %copy-done.3, ...), custom_call_target="tpu_custom_call" | custom-call | bytes 6295552 | tf_op jit(solution)/shard_map/update/pallas_call | solution.py:143
  70.8 1.2 %collective-permute-start.16 = (f32[8,128]{1,0:T(8,128)S(1)}, f32[8,128]{1,0:T(8,128)S(1)}, u32[]{:S(2)}, u32[]{:S(2)}) collective-permute-start(f32[8,128]{1,0:T(8,128)S(1)} %add.3.refs_0_), channel_id=1, source_target_pairs={{0,16},{4,20},{8,24},{12,28},{16,0},{20,4},{24,8},{28,12},{1,17},{... | collective-permute-start | bytes 12296 | tf_op jit(solution)/shard_map/ppermute | solution.py:178
  72.0 1.3 %collective-permute-start.15 = (f32[8,128]{1,0:T(8,128)S(1)}, f32[8,128]{1,0:T(8,128)S(1)}, u32[]{:S(2)}, u32[]{:S(2)}) collective-permute-start(f32[8,128]{1,0:T(8,128)S(1)} %add.3.refs_0_), channel_id=1, source_target_pairs={{0,8},{4,12},{8,0},{12,4},{16,24},{20,28},{24,16},{28,20},{1,9},{5... | collective-permute-start | bytes 12296 | tf_op jit(solution)/shard_map/ppermute | solution.py:178
  73.3 1.0 %collective-permute-done.17.refs_3_ = f32[8,128]{1,0:T(8,128)S(1)} collective-permute-done((f32[8,128]{1,0:T(8,128)S(1)}, f32[8,128]{1,0:T(8,128)S(1)}, u32[]{:S(2)}, u32[]{:S(2)}) %collective-permute-start.17) | collective-permute-done | bytes 4128 | tf_op jit(solution)/shard_map/ppermute | solution.py:178
  74.4 1.2 %collective-permute-done.15.refs_1_ = f32[8,128]{1,0:T(8,128)S(1)} collective-permute-done((f32[8,128]{1,0:T(8,128)S(1)}, f32[8,128]{1,0:T(8,128)S(1)}, u32[]{:S(2)}, u32[]{:S(2)}) %collective-permute-start.15) | collective-permute-done | bytes 4128 | tf_op jit(solution)/shard_map/ppermute | solution.py:178
  75.6 1.1 %weight.1 = f32[1,256,768]{2,1,0:T(8,128)} custom-call(f32[8,128]{1,0:T(8,128)S(1)} %add.3.refs_0_, f32[8,128]{1,0:T(8,128)S(1)} %collective-permute-done.15.refs_1_, f32[8,128]{1,0:T(8,128)S(1)} %collective-permute-done.16.refs_2_, f32[8,128]{1,0:T(8,128)S(1)} %collective-permute-done.17.refs_3_, f32[1,256,768]{2,1,0:T(8,128)S(1)} %copy-done.1, ...), custom_call_target="tpu_custom_call" | custom-call | bytes 2375680 | tf_op jit(solution)/shard_map/weight/pallas_call | solution.py:143
  (40 shorter events, 8.5 us)
Async XLA Ops:
  0.7 0.7 copy-start.5
  1.3 1.2 %copy-start.2 = (bf16[256,2048]{1,0:T(8,128)(2,1)S(1)}, bf16[256,2048]{1,0:T(8,128)(2,1)}, u32[]{:S(2)}) copy-start(bf16[256,2048]{1,0:T(8,128)(2,1)} %cot_ref.1) | copy-start | bytes 3145732
  3.2 18.3 %copy-start = (bf16[1,1,4,128,768]{4,3,2,1,0:T(8,128)(2,1)S(1)}, bf16[1,1,4,128,768]{4,3,2,1,0:T(8,128)(2,1)}, u32[]{:S(2)}) copy-start(bf16[1,1,4,128,768]{4,3,2,1,0:T(8,128)(2,1)} %param.12) | copy-start | bytes 2359300
  3.2 14.2 %collective-permute-start = (bf16[272,512]{1,0:T(8,128)(2,1)S(1)}, bf16[272,512]{1,0:T(8,128)(2,1)S(1)}, u32[]{:S(2)}, u32[]{:S(2)}) collective-permute-start(bf16[272,512]{1,0:T(8,128)(2,1)S(1)} %get-tuple-element.39), channel_id=1, source_target_pairs={{0,8},{4,12},{8,0},{12,4},{16,24},{20,28},{24,16},{28,20},{1,9},{5... | collective-permute-start | bytes 835592 | tf_op jit(solution)/shard_map/ppermute | solution.py:178
  6.2 14.1 %collective-permute-start.1 = (bf16[272,512]{1,0:T(8,128)(2,1)S(1)}, bf16[272,512]{1,0:T(8,128)(2,1)S(1)}, u32[]{:S(2)}, u32[]{:S(2)}) collective-permute-start(bf16[272,512]{1,0:T(8,128)(2,1)S(1)} %get-tuple-element.40), channel_id=1, source_target_pairs={{0,16},{4,20},{8,24},{12,28},{16,0},{20,4},{24,8},{28,12},{1,17},{... | collective-permute-start | bytes 835592 | tf_op jit(solution)/shard_map/ppermute | solution.py:178
  7.7 12.6 %collective-permute-start.2 = (bf16[272,512]{1,0:T(8,128)(2,1)S(1)}, bf16[272,512]{1,0:T(8,128)(2,1)S(1)}, u32[]{:S(2)}, u32[]{:S(2)}) collective-permute-start(bf16[272,512]{1,0:T(8,128)(2,1)S(1)} %get-tuple-element.41), channel_id=1, source_target_pairs={{0,24},{4,28},{8,16},{12,20},{16,8},{20,12},{24,0},{28,4},{1,25},{... | collective-permute-start | bytes 835592 | tf_op jit(solution)/shard_map/ppermute | solution.py:178
  7.7 8.3 %collective-permute-start.3 = (bf16[128,512]{1,0:T(8,128)(2,1)S(1)}, bf16[128,512]{1,0:T(8,128)(2,1)S(1)}, u32[]{:S(2)}, u32[]{:S(2)}) collective-permute-start(bf16[128,512]{1,0:T(8,128)(2,1)S(1)} %get-tuple-element.36), channel_id=1, source_target_pairs={{0,1},{1,2},{2,3},{3,0},{4,5},{5,6},{6,7},{7,4},{8,9},{9,10},{10,1... | collective-permute-start | bytes 393224 | tf_op jit(solution)/shard_map/ppermute | solution.py:181
  9.8 11.1 %collective-permute-start.4 = (bf16[128,512]{1,0:T(8,128)(2,1)S(1)}, bf16[128,512]{1,0:T(8,128)(2,1)S(1)}, u32[]{:S(2)}, u32[]{:S(2)}) collective-permute-start(bf16[128,512]{1,0:T(8,128)(2,1)S(1)} %get-tuple-element.37), channel_id=1, source_target_pairs={{0,2},{1,3},{2,0},{3,1},{4,6},{5,7},{6,4},{7,5},{8,10},{9,11},{10,... | collective-permute-start | bytes 393224 | tf_op jit(solution)/shard_map/ppermute | solution.py:181
  16.0 5.4 %collective-permute-start.5 = (bf16[128,512]{1,0:T(8,128)(2,1)S(1)}, bf16[128,512]{1,0:T(8,128)(2,1)S(1)}, u32[]{:S(2)}, u32[]{:S(2)}) collective-permute-start(bf16[128,512]{1,0:T(8,128)(2,1)S(1)} %get-tuple-element.46), channel_id=1, source_target_pairs={{0,3},{1,0},{2,1},{3,2},{4,7},{5,4},{6,5},{7,6},{8,11},{9,8},{10,9... | collective-permute-start | bytes 393224 | tf_op jit(solution)/shard_map/ppermute | solution.py:181
  21.5 18.1 %collective-permute-start.8 = (bf16[512,768]{1,0:T(8,128)(2,1)S(1)}, bf16[512,768]{1,0:T(8,128)(2,1)S(1)}, u32[]{:S(2)}, u32[]{:S(2)}) collective-permute-start(bf16[512,768]{1,0:T(8,128)(2,1)S(1)} %bitcast.4), channel_id=1, source_target_pairs={{0,16},{4,20},{8,24},{12,28},{16,0},{20,4},{24,8},{28,12},{1,17},{... | collective-permute-start | bytes 2359304 | tf_op jit(solution)/shard_map/ppermute | solution.py:178
  23.0 17.8 %collective-permute-start.7 = (bf16[512,768]{1,0:T(8,128)(2,1)S(1)}, bf16[512,768]{1,0:T(8,128)(2,1)S(1)}, u32[]{:S(2)}, u32[]{:S(2)}) collective-permute-start(bf16[512,768]{1,0:T(8,128)(2,1)S(1)} %bitcast.5), channel_id=1, source_target_pairs={{0,8},{4,12},{8,0},{12,4},{16,24},{20,28},{24,16},{28,20},{1,9},{5... | collective-permute-start | bytes 2359304 | tf_op jit(solution)/shard_map/ppermute | solution.py:178
  24.5 16.3 %collective-permute-start.6 = (bf16[384,512]{1,0:T(8,128)(2,1)S(1)}, bf16[384,512]{1,0:T(8,128)(2,1)S(1)}, u32[]{:S(2)}, u32[]{:S(2)}) collective-permute-start(bf16[384,512]{1,0:T(8,128)(2,1)S(1)} %get-tuple-element.48), channel_id=1, source_target_pairs={{0,1},{1,2},{2,3},{3,0},{4,5},{5,6},{6,7},{7,4},{8,9},{9,10},{10,1... | collective-permute-start | bytes 1179656 | tf_op jit(solution)/shard_map/ppermute | solution.py:181
  27.3 16.2 %collective-permute-start.9 = (bf16[384,512]{1,0:T(8,128)(2,1)S(1)}, bf16[384,512]{1,0:T(8,128)(2,1)S(1)}, u32[]{:S(2)}, u32[]{:S(2)}) collective-permute-start(bf16[384,512]{1,0:T(8,128)(2,1)S(1)} %get-tuple-element.51), channel_id=1, source_target_pairs={{0,3},{1,0},{2,1},{3,2},{4,7},{5,4},{6,5},{7,6},{8,11},{9,8},{10,9... | collective-permute-start | bytes 1179656 | tf_op jit(solution)/shard_map/ppermute | solution.py:181
  43.5 19.4 %collective-permute-start.10 = (bf16[384,512]{1,0:T(8,128)(2,1)S(1)}, bf16[384,512]{1,0:T(8,128)(2,1)S(1)}, u32[]{:S(2)}, u32[]{:S(2)}) collective-permute-start(bf16[384,512]{1,0:T(8,128)(2,1)S(1)} %get-tuple-element.52), channel_id=1, source_target_pairs={{0,2},{1,3},{2,0},{3,1},{4,6},{5,7},{6,4},{7,5},{8,10},{9,11},{10,... | collective-permute-start | bytes 1179656 | tf_op jit(solution)/shard_map/ppermute | solution.py:181
  45.0 17.9 %collective-permute-start.11 = (bf16[512,384]{1,0:T(8,128)(2,1)S(1)}, bf16[512,384]{1,0:T(8,128)(2,1)S(1)}, u32[]{:S(2)}, u32[]{:S(2)}) collective-permute-start(bf16[512,384]{1,0:T(8,128)(2,1)S(1)} %slice.8), channel_id=1, source_target_pairs={{0,16},{4,20},{8,24},{12,28},{16,0},{20,4},{24,8},{28,12},{1,17},{... | collective-permute-start | bytes 1179656 | tf_op jit(solution)/shard_map/ppermute | solution.py:178
  45.4 17.5 %collective-permute-start.12 = (bf16[512,384]{1,0:T(8,128)(2,1)S(1)}, bf16[512,384]{1,0:T(8,128)(2,1)S(1)}, u32[]{:S(2)}, u32[]{:S(2)}) collective-permute-start(bf16[512,384]{1,0:T(8,128)(2,1)S(1)} %slice.9), channel_id=1, source_target_pairs={{0,8},{4,12},{8,0},{12,4},{16,24},{20,28},{24,16},{28,20},{1,9},{5... | collective-permute-start | bytes 1179656 | tf_op jit(solution)/shard_map/ppermute | solution.py:178
  63.9 2.4 %collective-permute-start.13 = (f32[256,768]{1,0:T(8,128)S(1)}, f32[256,768]{1,0:T(8,128)S(1)}, u32[]{:S(2)}, u32[]{:S(2)}) collective-permute-start(f32[256,768]{1,0:T(8,128)S(1)} %product.7), channel_id=1, source_target_pairs={{0,4},{4,0},{8,12},{12,8},{16,20},{20,16},{24,28},{28,24},{1,5},{5... | collective-permute-start | bytes 2359304 | tf_op jit(solution)/shard_map/ppermute | solution.py:178
  64.4 1.9 %copy-start.1 = (f32[1,256,768]{2,1,0:T(8,128)S(1)}, f32[1,256,768]{2,1,0:T(8,128)}, u32[]{:S(2)}) copy-start(f32[1,256,768]{2,1,0:T(8,128)} %refs_4_.1) | copy-start | bytes 2359300
  64.4 1.9 %copy-start.3 = (f32[1,256,768]{2,1,0:T(8,128)S(1)}, f32[1,256,768]{2,1,0:T(8,128)}, u32[]{:S(2)}) copy-start(f32[1,256,768]{2,1,0:T(8,128)} %first_ref.1) | copy-start | bytes 2359300
  64.4 1.8 %copy-start.4 = (f32[1,256,768]{2,1,0:T(8,128)S(1)}, f32[1,256,768]{2,1,0:T(8,128)}, u32[]{:S(2)}) copy-start(f32[1,256,768]{2,1,0:T(8,128)} %second_ref.1) | copy-start | bytes 2359300
  68.6 1.2 %collective-permute-start.14 = (f32[8,128]{1,0:T(8,128)S(1)}, f32[8,128]{1,0:T(8,128)S(1)}, u32[]{:S(2)}, u32[]{:S(2)}) collective-permute-start(f32[8,128]{1,0:T(8,128)S(1)} %get-tuple-element.55), channel_id=1, source_target_pairs={{0,4},{4,0},{8,12},{12,8},{16,20},{20,16},{24,28},{28,24},{1,5},{5... | collective-permute-start | bytes 12296 | tf_op jit(solution)/shard_map/ppermute | solution.py:178
  69.8 4.5 %collective-permute-start.17 = (f32[8,128]{1,0:T(8,128)S(1)}, f32[8,128]{1,0:T(8,128)S(1)}, u32[]{:S(2)}, u32[]{:S(2)}) collective-permute-start(f32[8,128]{1,0:T(8,128)S(1)} %add.3.refs_0_), channel_id=1, source_target_pairs={{0,24},{4,28},{8,16},{12,20},{16,8},{20,12},{24,0},{28,4},{1,25},{... | collective-permute-start | bytes 12296 | tf_op jit(solution)/shard_map/ppermute | solution.py:178
  70.8 3.6 %collective-permute-start.16 = (f32[8,128]{1,0:T(8,128)S(1)}, f32[8,128]{1,0:T(8,128)S(1)}, u32[]{:S(2)}, u32[]{:S(2)}) collective-permute-start(f32[8,128]{1,0:T(8,128)S(1)} %add.3.refs_0_), channel_id=1, source_target_pairs={{0,16},{4,20},{8,24},{12,28},{16,0},{20,4},{24,8},{28,12},{1,17},{... | collective-permute-start | bytes 12296 | tf_op jit(solution)/shard_map/ppermute | solution.py:178
  72.0 3.6 %collective-permute-start.15 = (f32[8,128]{1,0:T(8,128)S(1)}, f32[8,128]{1,0:T(8,128)S(1)}, u32[]{:S(2)}, u32[]{:S(2)}) collective-permute-start(f32[8,128]{1,0:T(8,128)S(1)} %add.3.refs_0_), channel_id=1, source_target_pairs={{0,8},{4,12},{8,0},{12,4},{16,24},{20,28},{24,16},{28,20},{1,9},{5... | collective-permute-start | bytes 12296 | tf_op jit(solution)/shard_map/ppermute | solution.py:178
  (2 other events, 1.4 us)

commit v3 on v2

v3 whole, which is shorter than its diff:
```python
import functools

import jax
import jax.numpy as jnp
from jax import lax
from jax.experimental import pallas as pl
from jax.experimental.pallas import tpu as pltpu
from jax.sharding import PartitionSpec as P

VMEM = pl.BlockSpec(memory_space=pltpu.VMEM)
HBM = pl.BlockSpec(memory_space=pltpu.HBM)
TAIL = 16
ROWS_FIRST = (((0,), (0,)), ((), ()))


def on_device(
    cotangent,
    route_weight,
    expert_ids,
    slot_ids,
    hidden_saved,
    down_weight,
    first_moment,
    second_moment,
):
    tok_rows, width = cotangent.shape
    owners = lax.axis_size("expert")
    hidden_rows = hidden_saved.reshape(-1, hidden_saved.shape[-1])
    capacity = hidden_rows.shape[0] // owners
    weight = down_weight[0]
    routed = (route_weight[:, None] * cotangent.astype(jnp.float32)).astype(jnp.bfloat16)
    target = expert_ids * capacity + slot_ids
    outgoing = jnp.zeros((owners * capacity, width), jnp.bfloat16).at[target].set(routed)
    arrived = lax.all_to_all(
        outgoing.reshape(owners, capacity, width), "expert", split_axis=0, concat_axis=0, tiled=True
    )
    arrived = arrived.reshape(owners * capacity, width)
    whole_term = lax.dot_general(
        arrived, hidden_rows, (((0,), (0,)), ((), ())), preferred_element_type=jnp.float32
    )
    grad = lax.psum_scatter(whole_term, "dp", scatter_dimension=0, tiled=True)
    new_first = 0.9 * first_moment[0] + 0.1 * grad
    new_second = 0.999 * second_moment[0] + 0.001 * grad * grad
    update = (
        new_first / (1.0 - 0.9**10) / (jnp.sqrt(new_second / (1.0 - 0.999**10)) + 1e-06)
        + 0.01 * weight
    )
    weight_sq, update_sq = lax.psum((jnp.sum(weight * weight), jnp.sum(update * update)), "dp")
    ratio = jnp.sqrt(weight_sq) / (jnp.sqrt(update_sq) + 1e-06)
    new_weight = weight - 0.1 * ratio * update
    return (new_weight[None], new_first[None], new_second[None])


def packed_rows(rows, expert_row, slot_row, expert, capacity):
    slot = lax.broadcasted_iota(jnp.int32, (capacity, rows.shape[0]), 0).astype(jnp.float32)
    place = (expert_row - expert.astype(jnp.float32)) * capacity + slot_row
    hot = jnp.where(slot == place, 1.0, 0.0).astype(jnp.bfloat16)
    return jnp.dot(hot, rows, preferred_element_type=jnp.float32).astype(jnp.bfloat16)


def cut_kernel(n_chips, owners, capacity, cot_ref, scale_ref, expert_ref, slot_ref, *refs):
    packed, blocks = refs[:owners], refs[owners : owners + n_chips - 1]
    cot, scales, experts, slots, sems = refs[owners + n_chips - 1 :]
    tokens, width = cot_ref.shape
    part = width // n_chips
    half = part // 2
    me = lax.axis_index("dp")
    chip, core = me // 2, lax.rem(me, 2)
    small = [
        pltpu.make_async_copy(src, dst, sems.at[at])
        for at, (src, dst) in enumerate([(scale_ref, scales), (expert_ref, experts), (slot_ref, slots)])
    ]
    large = []
    for mask in range(n_chips):
        columns = pl.ds(pl.multiple_of((chip ^ mask) * part, part), part)
        large.append(pltpu.make_async_copy(cot_ref.at[:, columns], cot.at[mask], sems.at[3 + mask]))
    for copy in small + large:
        copy.start()
    for copy in small:
        copy.wait()
    scale = jnp.broadcast_to(scales[...], (128, tokens)).T
    scale = jnp.concatenate([scale] * (half // 128), axis=1)
    expert_row, slot_row = experts[...].astype(jnp.float32), slots[...].astype(jnp.float32)
    row = lax.broadcasted_iota(jnp.int32, (TAIL, tokens), 0)
    ids = jnp.where(row == 0, expert_row, jnp.where(row == 1, slot_row, 0.0)).astype(jnp.bfloat16)
    for mask, copy in enumerate(large):
        copy.wait()
        halves = []
        for side in range(2):
            begin = pl.multiple_of((core ^ side) * half, half)
            block = cot[mask, :, pl.ds(begin, half)].astype(jnp.float32)
            halves.append((scale * block).astype(jnp.bfloat16))
        routed = jnp.concatenate(halves, axis=1)
        if mask == 0:
            z = lax.axis_index("expert")
            for shift, out in enumerate(packed):
                out[...] = packed_rows(routed, expert_row, slot_row, lax.rem(z + shift, owners), capacity)
        else:
            out = blocks[mask - 1]
            out[:tokens, :] = routed
            out[tokens:, :] = jnp.concatenate([ids] * (part // tokens), axis=1)


def pack_kernel(owners, capacity, n_blocks, *refs):
    z = lax.axis_index("expert")
    blocks, outs = refs[:n_blocks], refs[n_blocks:]
    tokens = blocks[0].shape[0] - TAIL
    for at, block in enumerate(blocks):
        ids = block[tokens:, :tokens].astype(jnp.float32)
        rows = block[:tokens, :]
        for shift, out in enumerate(outs):
            expert = lax.rem(z + shift, owners)
            out[at * capacity : (at + 1) * capacity, :] = packed_rows(rows, ids[0:1], ids[1:2], expert, capacity)


def product_kernel(owners, capacity, columns, plan, *refs):
    me = lax.axis_index("expert")
    used = 1 + max(max(max(parts), max(place for place, _, _ in packed)) for parts, packed in plan)
    early, out = refs[used:-1], refs[-1]
    rows = [
        jnp.concatenate([refs[place][at * capacity : (at + 1) * capacity, columns] for place, at, _ in packed])
        for _, packed in plan
    ]
    wide = min(refs[place].shape[1] for parts, _ in plan for place in parts)
    for column in range(0, out.shape[1], wide):
        total = None
        for left, (parts, packed) in zip(rows, plan):
            part = refs[parts[column // refs[parts[0]].shape[1]]]
            inside = slice(column % part.shape[1], column % part.shape[1] + wide)
            begins = [lax.rem(me + owners - shift, owners) * capacity for _, _, shift in packed]
            right = [part[pl.ds(pl.multiple_of(begin, capacity), capacity), inside] for begin in begins]
            term = lax.dot_general(left, jnp.concatenate(right), ROWS_FIRST, preferred_element_type=jnp.float32)
            total = term if total is None else total + term
        for ref in early:
            total = total + ref[:, column : column + wide]
        out[:, column : column + wide] = total


def new_moments(grad, first_ref, second_ref):
    return 0.9 * first_ref[0] + 0.1 * grad, 0.999 * second_ref[0] + 0.001 * grad * grad


def update_kernel(mine_ref, other_ref, weight_ref, first_ref, second_ref, grad_ref, update_ref, sums):
    grad = mine_ref[...] + other_ref[...]
    grad_ref[...] = grad
    weight = weight_ref[0]
    first, second = new_moments(grad, first_ref, second_ref)
    update = first / (1.0 - 0.9**10) / (jnp.sqrt(second / (1.0 - 0.999**10)) + 1e-06) + 0.01 * weight
    update_ref[...] = update
    row = lax.broadcasted_iota(jnp.int32, sums.shape, 0)
    sums[...] = jnp.where(row == 0, jnp.sum(weight * weight), jnp.sum(update * update))


def moment_kernel(grad_ref, first_ref, second_ref, new_first, new_second):
    new_first[0], new_second[0] = new_moments(grad_ref[...], first_ref, second_ref)


def weight_kernel(n_sums, *refs):
    sums, (weight_ref, update_ref, out_ref, new_weight, sems) = refs[:n_sums], refs[n_sums:]
    total = sums[0][...]
    for other in sums[1:]:
        total = total + other[...]
    norm = jnp.sqrt(total)
    scale = 0.1 * (norm[0:1, 0:1] / (norm[1:2, 0:1] + 1e-06))
    n = sems.shape[0]
    rows = update_ref.shape[0] // n
    copies = []
    for at in range(n):
        span = pl.ds(at * rows, rows)
        new_weight[0, span, :] = weight_ref[0, span, :] - scale * update_ref[span, :]
        copies.append(pltpu.make_async_copy(new_weight.at[:, span], out_ref.at[:, span], sems.at[at]))
        copies[-1].start()
    for copy in copies:
        copy.wait()


def call(kernel, out_shape, *args, spaces=VMEM, out_spaces=VMEM, scratch=(), grant=40, flops=0, name=None):
    nbytes = sum(a.size * a.dtype.itemsize for a in jax.tree.leaves((args, out_shape)))
    return pl.pallas_call(
        kernel,
        out_shape=out_shape,
        in_specs=[spaces] * len(args),
        out_specs=jax.tree.map(lambda _: out_spaces, out_shape),
        scratch_shapes=scratch,
        compiler_params=pltpu.CompilerParams(vmem_limit_bytes=grant * 2**20),
        cost_estimate=pl.CostEstimate(flops=flops, bytes_accessed=nbytes, transcendentals=0),
        name=name,
    )(*args)


def after(arrays, *earlier):
    return lax.optimization_barrier((arrays, earlier))[0]


def by_permutes(
    cotangent,
    route_weight,
    expert_ids,
    slot_ids,
    hidden_saved,
    down_weight,
    first_moment,
    second_moment,
):
    n_dp, owners = lax.axis_size("dp"), lax.axis_size("expert")
    n_chips = n_dp // 2
    tokens, width = cotangent.shape
    capacity, ff = hidden_saved.shape[3:]
    part = width // n_chips
    half = part // 2
    bf16, f32 = jnp.bfloat16, jnp.float32
    hidden = hidden_saved.reshape(owners * capacity, ff)

    def across(array, mask):
        return lax.ppermute(array, "dp", [(d, d ^ mask) for d in range(n_dp)])

    def along(array, shift):
        return lax.ppermute(array, "expert", [(d, (d + shift) % owners) for d in range(owners)])

    def pack(*blocks):
        size = len(blocks) * capacity
        return call(
            functools.partial(pack_kernel, owners, capacity, len(blocks)),
            [jax.ShapeDtypeStruct((size, part), bf16)] * owners,
            *blocks,
            flops=2 * size * owners * tokens * part,
            name="pack",
        )

    def multiply(columns, groups, *early):
        arrays, plan = [], []

        def place(array):
            if not any(array is other for other in arrays):
                arrays.append(array)
            return [array is other for other in arrays].index(True)

        for parts, packed in groups:
            plan.append(([place(p) for p in parts], [(place(p), at, shift) for p, at, shift in packed]))
        n = columns.stop - columns.start
        return call(
            functools.partial(product_kernel, owners, capacity, columns, plan),
            jax.ShapeDtypeStruct((n, ff), f32),
            *arrays,
            *early,
            flops=2 * sum(len(packed) for _, packed in plan) * capacity * n * ff,
            name="product",
        )

    packed, block = jax.ShapeDtypeStruct((capacity, part), bf16), jax.ShapeDtypeStruct((tokens + TAIL, part), bf16)
    cut = call(
        functools.partial(cut_kernel, n_chips, owners, capacity),
        [packed] * owners + [block] * (n_chips - 1),
        cotangent,
        *[ids.reshape(1, tokens) for ids in (route_weight, expert_ids, slot_ids)],
        spaces=HBM,
        scratch=[
            pltpu.VMEM((n_chips, tokens, part), bf16),
            pltpu.VMEM((1, tokens), f32),
            pltpu.VMEM((1, tokens), jnp.int32),
            pltpu.VMEM((1, tokens), jnp.int32),
            pltpu.SemaphoreType.DMA((3 + n_chips,)),
        ],
        grant=60,
        name="cut",
    )
    near, (to_x, to_y, to_xy) = cut[:owners], cut[owners:]
    from_x, from_y, from_xy = across(to_x, 2), across(to_y, 4), across(to_xy, 6)
    near = [near[0], along(near[1], 1), along(near[2], 2), near[3]]
    near[3] = along(after(near[3], near[1]), 3)
    far = pack(from_x, from_y, from_xy)
    far, left, right = after((far, hidden[:, : ff // 2], hidden[:, ff // 2 :]), *near)
    far = list(far)
    x_left, x_right, y_left, y_right = across(left, 2), across(right, 2), across(left, 4), across(right, 4)
    far[2] = along(far[2], 2)
    far[1], far[3], xy_left, xy_right = after(
        (far[1], far[3], x_left, y_right), far[2], x_left, x_right, y_left, y_right
    )
    far[1], far[3] = along(far[1], 1), along(far[3], 3)
    xy_left, xy_right = across(xy_left, 4), across(xy_right, 2)

    keep, give = slice(0, half), slice(half, part)
    def terms(packed, at, *shifts):
        return [(packed[shift], at, shift) for shift in shifts]

    by_x, by_y, by_xy = (x_left, x_right), (y_left, y_right), (xy_left, xy_right)
    totals = {}
    for side in (give, keep):
        groups = [((hidden,), terms(near, 0, 0, 1, 2, 3)), (by_x, terms(far, 0, 0, 2)), (by_y, terms(far, 1, 0, 2))]
        totals[side.start] = multiply(side, groups)
    totals = after(totals, *totals.values())
    for side in (give, keep):
        groups = [(by_x, terms(far, 0, 1, 3)), (by_y, terms(far, 1, 1, 3)), (by_xy, terms(far, 2, 0, 1, 2, 3))]
        totals[side.start] = multiply(side, groups, totals[side.start])
    other = across(totals[give.start], 1)

    state, matrix = jax.ShapeDtypeStruct((1, half, ff), f32), jax.ShapeDtypeStruct((half, ff), f32)
    grad, update, sums = call(
        update_kernel,
        [matrix, matrix, jax.ShapeDtypeStruct((8, 128), f32)],
        totals[keep.start],
        other,
        down_weight,
        first_moment,
        second_moment,
        name="update",
    )
    sums = sums + across(sums, 1)
    parts = [sums] + [across(sums, mask) for mask in (2, 4, 6)]
    new_first, new_second = call(
        moment_kernel, [state, state], after(grad, sums), first_moment, second_moment, name="moment"
    )
    new_weight = call(
        functools.partial(weight_kernel, len(parts)),
        state,
        *parts,
        down_weight,
        update,
        out_spaces=HBM,
        scratch=[pltpu.VMEM((1, half, ff), f32), pltpu.SemaphoreType.DMA((4,))],
        name="weight",
    )
    return new_weight, new_first, new_second


def solution(mesh):
    placed = (
        P(("dp", "expert"), None),
        P(("dp", "expert")),
        P(("dp", "expert")),
        P(("dp", "expert")),
        P("dp", "expert", None, None, None),
        P("expert", "dp", None),
        P("expert", "dp", None),
        P("expert", "dp", None),
    )
    return jax.shard_map(
        by_permutes if mesh.shape["dp"] == 8 else on_device,
        mesh=mesh,
        in_specs=placed,
        out_specs=(P("expert", "dp", None), P("expert", "dp", None), P("expert", "dp", None)),
        check_vma=False,
    )
```

time: 76.8 us -> 73.5 us (0.957)
  waiting for transfers between devices: 42.8 us -> 34.7 us
  starting transfers between devices: 23.7 us -> 27.8 us
  Pallas kernels: 7.39 us -> 9.95 us
  local copies, waits for them, and re-layouts: 2.02 us -> 0.11 us
    ppermute x12 -> x14, waiting for transfers between devices: 19.4 us -> 14 us  [across(): return lax.ppermute(array, 'dp', [(d, d ^ mask) for d in range(n_dp)])]
    ppermute x6, waiting for transfers between devices: 23.4 us -> 20.8 us  [along(): lax.ppermute(array, 'expert', [(d, (d + shift) % owners) for d in range(o...]
    pallas_call x9, Pallas kernels: 7.39 us -> 9.95 us  [call(): pl.pallas_call(kernel, out_shape=out_shape, in_specs=[spaces] * len(args)...]
    ppermute x6, starting transfers between devices: 11.3 us -> 13.5 us  [along(): lax.ppermute(array, 'expert', [(d, (d + shift) % owners) for d in range(o...]
    unnamed x16 -> x10, local copies, waits for them, and re-layouts: 1.94 us -> 0.03 us
    ppermute x12 -> x14, starting transfers between devices: 12.4 us -> 14.3 us  [across(): return lax.ppermute(array, 'dp', [(d, d ^ mask) for d in range(n_dp)])]
  transfers between devices with their start and end apart: 18 -> 20, of which waited for: 12 -> 11; matrix products, arithmetic and copies ran while one was open for 0% -> 0% of each run, Pallas kernels for 3% -> 6%
where the time goes in v3:
time: 73.5 us; the launch traced here: 73.4 us
  waiting for transfers between devices  34.7 us (47%)
  starting transfers between devices  27.8 us (38%)
  Pallas kernels  9.95 us (14%)
  between operations  0.76 us (1%)
    ppermute x6, waiting for transfers between devices, along(): lax.ppermute(array, 'expert', [(d, (d + shift) % owners) for d in range(o...  20.8 us
    ppermute x14, starting transfers between devices, across(): return lax.ppermute(array, 'dp', [(d, d ^ mask) for d in range(n_dp)])  14.3 us
    ppermute x14, waiting for transfers between devices, across(): return lax.ppermute(array, 'dp', [(d, d ^ mask) for d in range(n_dp)])  14 us
    ppermute x6, starting transfers between devices, along(): lax.ppermute(array, 'expert', [(d, (d + shift) % owners) for d in range(o...  13.5 us
    pallas_call x9, Pallas kernels, call(): pl.pallas_call(kernel, out_shape=out_shape, in_specs=[spaces] * len(args)...  9.95 us
  transfers between devices with their start and end apart: 20, of which 11 were waited for; matrix products, arithmetic and copies ran while one was open for 0% of the time, Pallas kernels for 6%

profile of v3, /device:TPU:0, one launch (start us, length us, event | category | flops | bytes accessed | tf_op | source)
XLA Modules:
  0.0 73.4 jit_solution(8546720979731466524)
XLA Ops:
  0.6 2.6 %cut.1 = (bf16[128,512]{1,0:T(8,128)(2,1)}, bf16[128,512]{1,0:T(8,128)(2,1)}, bf16[128,512]{1,0:T(8,128)(2,1)}, bf16[128,512]{1,0:T(8,128)(2,1)}, bf16[272,512]{...) custom-call(bf16[256,2048]{1,0:T(8,128)(2,1)} %cot_ref.1, f32[1,256]{1,0:T(1,128)} %bitcast.7, ...), custom_call_target="tpu_custom_call" | custom-call | bytes 2411520 | tf_op jit(solution)/shard_map/cut/pallas_call | solution.py:179
  3.3 3.1 %collective-permute-start.3 = (bf16[128,512]{1,0:T(8,128)(2,1)}, bf16[128,512]{1,0:T(8,128)(2,1)S(1)}, u32[]{:S(2)}, u32[]{:S(2)}) collective-permute-start(bf16[128,512]{1,0:T(8,128)(2,1)} %get-tuple-element.41), channel_id=1, source_target_pairs={{0,1},{1,2},{2,3},{3,0},{4,5},{5,6},{6,7},{7,4},{8,9},{9,10},{10,1... | collective-permute-start | bytes 393224 | tf_op jit(solution)/shard_map/ppermute | solution.py:218
  6.3 1.5 %collective-permute-start = (bf16[272,512]{1,0:T(8,128)(2,1)}, bf16[272,512]{1,0:T(8,128)(2,1)S(1)}, u32[]{:S(2)}, u32[]{:S(2)}) collective-permute-start(bf16[272,512]{1,0:T(8,128)(2,1)} %get-tuple-element.33), channel_id=1, source_target_pairs={{0,8},{4,12},{8,0},{12,4},{16,24},{20,28},{24,16},{28,20},{1,9},{5... | collective-permute-start | bytes 835592 | tf_op jit(solution)/shard_map/ppermute | solution.py:215
  7.8 1.5 %collective-permute-start.1 = (bf16[272,512]{1,0:T(8,128)(2,1)}, bf16[272,512]{1,0:T(8,128)(2,1)S(1)}, u32[]{:S(2)}, u32[]{:S(2)}) collective-permute-start(bf16[272,512]{1,0:T(8,128)(2,1)} %get-tuple-element.34), channel_id=1, source_target_pairs={{0,16},{4,20},{8,24},{12,28},{16,0},{20,4},{24,8},{28,12},{1,17},{... | collective-permute-start | bytes 835592 | tf_op jit(solution)/shard_map/ppermute | solution.py:215
  9.8 2.6 %collective-permute-start.4 = (bf16[128,512]{1,0:T(8,128)(2,1)}, bf16[128,512]{1,0:T(8,128)(2,1)S(1)}, u32[]{:S(2)}, u32[]{:S(2)}) collective-permute-start(bf16[128,512]{1,0:T(8,128)(2,1)} %get-tuple-element.42), channel_id=1, source_target_pairs={{0,2},{1,3},{2,0},{3,1},{4,6},{5,7},{6,4},{7,5},{8,10},{9,11},{10,... | collective-permute-start | bytes 393224 | tf_op jit(solution)/shard_map/ppermute | solution.py:218
  12.4 1.4 %collective-permute-start.5 = (bf16[128,512]{1,0:T(8,128)(2,1)}, bf16[128,512]{1,0:T(8,128)(2,1)S(1)}, u32[]{:S(2)}, u32[]{:S(2)}) collective-permute-start(bf16[128,512]{1,0:T(8,128)(2,1)} %get-tuple-element.44), channel_id=1, source_target_pairs={{0,3},{1,0},{2,1},{3,2},{4,7},{5,4},{6,5},{7,6},{8,11},{9,8},{10,9... | collective-permute-start | bytes 393224 | tf_op jit(solution)/shard_map/ppermute | solution.py:218
  13.9 2.2 %collective-permute-done.refs_0_ = bf16[272,512]{1,0:T(8,128)(2,1)S(1)} collective-permute-done((bf16[272,512]{1,0:T(8,128)(2,1)}, bf16[272,512]{1,0:T(8,128)(2,1)S(1)}, u32[]{:S(2)}, u32[]{:S(2)}) %collective-permute-start) | collective-permute-done | bytes 278560 | tf_op jit(solution)/shard_map/ppermute | solution.py:215
  16.1 5.7 %collective-permute-done.1.refs_1_ = bf16[272,512]{1,0:T(8,128)(2,1)S(1)} collective-permute-done((bf16[272,512]{1,0:T(8,128)(2,1)}, bf16[272,512]{1,0:T(8,128)(2,1)S(1)}, u32[]{:S(2)}, u32[]{:S(2)}) %collective-permute-start.1) | collective-permute-done | bytes 278560 | tf_op jit(solution)/shard_map/ppermute | solution.py:215
  22.5 2.7 %collective-permute-start.9 = (bf16[384,512]{1,0:T(8,128)(2,1)S(1)}, bf16[384,512]{1,0:T(8,128)(2,1)S(1)}, u32[]{:S(2)}, u32[]{:S(2)}) collective-permute-start(bf16[384,512]{1,0:T(8,128)(2,1)S(1)} %get-tuple-element.49), channel_id=1, source_target_pairs={{0,2},{1,3},{2,0},{3,1},{4,6},{5,7},{6,4},{7,5},{8,10},{9,11},{10,... | collective-permute-start | bytes 1179656 | tf_op jit(solution)/shard_map/ppermute | solution.py:218
  25.1 1.5 %collective-permute-start.10 = (bf16[512,384]{1,0:T(8,128)(2,1)S(1)}, bf16[512,384]{1,0:T(8,128)(2,1)S(1)}, u32[]{:S(2)}, u32[]{:S(2)}) collective-permute-start(bf16[512,384]{1,0:T(8,128)(2,1)S(1)} %get-tuple-element.45), channel_id=1, source_target_pairs={{0,16},{4,20},{8,24},{12,28},{16,0},{20,4},{24,8},{28,12},{1,17},{... | collective-permute-start | bytes 1179656 | tf_op jit(solution)/shard_map/ppermute | solution.py:215
  27.2 1.2 %collective-permute-start.8 = (bf16[512,384]{1,0:T(8,128)(2,1)S(1)}, bf16[512,384]{1,0:T(8,128)(2,1)S(1)}, u32[]{:S(2)}, u32[]{:S(2)}) collective-permute-start(bf16[512,384]{1,0:T(8,128)(2,1)S(1)} %get-tuple-element.46), channel_id=1, source_target_pairs={{0,16},{4,20},{8,24},{12,28},{16,0},{20,4},{24,8},{28,12},{1,17},{... | collective-permute-start | bytes 1179656 | tf_op jit(solution)/shard_map/ppermute | solution.py:215
  29.2 12.1 %collective-permute-done.9.refs_8_.refs_9_ = bf16[384,512]{1,0:T(8,128)(2,1)S(1)} collective-permute-done((bf16[384,512]{1,0:T(8,128)(2,1)S(1)}, bf16[384,512]{1,0:T(8,128)(2,1)S(1)}, u32[]{:S(2)}, u32[]{:S(2)}) %collective-permute-start.9) | collective-permute-done | bytes 393248 | tf_op jit(solution)/shard_map/ppermute | solution.py:218
  41.3 1.4 %collective-permute-done.8.refs_10_.refs_5_ = bf16[512,384]{1,0:T(8,128)(2,1)S(1)} collective-permute-done((bf16[512,384]{1,0:T(8,128)(2,1)S(1)}, bf16[512,384]{1,0:T(8,128)(2,1)S(1)}, u32[]{:S(2)}, u32[]{:S(2)}) %collective-permute-start.8) | collective-permute-done | bytes 393248 | tf_op jit(solution)/shard_map/ppermute | solution.py:215
  43.6 3.1 %collective-permute-start.12 = (bf16[384,512]{1,0:T(8,128)(2,1)S(1)}, bf16[384,512]{1,0:T(8,128)(2,1)S(1)}, u32[]{:S(2)}, u32[]{:S(2)}) collective-permute-start(bf16[384,512]{1,0:T(8,128)(2,1)S(1)} %get-tuple-element.51), channel_id=1, source_target_pairs={{0,3},{1,0},{2,1},{3,2},{4,7},{5,4},{6,5},{7,6},{8,11},{9,8},{10,9... | collective-permute-start | bytes 1179656 | tf_op jit(solution)/shard_map/ppermute | solution.py:218
  46.8 1.5 %collective-permute-start.13 = (bf16[512,384]{1,0:T(8,128)(2,1)S(1)}, bf16[512,384]{1,0:T(8,128)(2,1)S(1)}, u32[]{:S(2)}, u32[]{:S(2)}) collective-permute-start(bf16[512,384]{1,0:T(8,128)(2,1)S(1)} %collective-permute-done.6.refs_5_.refs_0_), channel_id=1, source_target_pairs={{0,16},{4,20},{8,24},{12,28},{16,0},{20,4},{24,8},{28,12},{1,17},{... | collective-permute-start | bytes 1179656 | tf_op jit(solution)/shard_map/ppermute | solution.py:215
  48.3 1.4 %collective-permute-start.14 = (bf16[512,384]{1,0:T(8,128)(2,1)S(1)}, bf16[512,384]{1,0:T(8,128)(2,1)S(1)}, u32[]{:S(2)}, u32[]{:S(2)}) collective-permute-start(bf16[512,384]{1,0:T(8,128)(2,1)S(1)} %collective-permute-done.8.refs_10_.refs_5_), channel_id=1, source_target_pairs={{0,8},{4,12},{8,0},{12,4},{16,24},{20,28},{24,16},{28,20},{1,9},{5... | collective-permute-start | bytes 1179656 | tf_op jit(solution)/shard_map/ppermute | solution.py:215
  51.2 5.6 %collective-permute-done.11.refs_2_ = bf16[384,512]{1,0:T(8,128)(2,1)S(1)} collective-permute-done((bf16[384,512]{1,0:T(8,128)(2,1)S(1)}, bf16[384,512]{1,0:T(8,128)(2,1)S(1)}, u32[]{:S(2)}, u32[]{:S(2)}) %collective-permute-start.11) | collective-permute-done | bytes 393248 | tf_op jit(solution)/shard_map/ppermute | solution.py:218
  56.8 3.0 %collective-permute-done.12.refs_3_ = bf16[384,512]{1,0:T(8,128)(2,1)S(1)} collective-permute-done((bf16[384,512]{1,0:T(8,128)(2,1)S(1)}, bf16[384,512]{1,0:T(8,128)(2,1)S(1)}, u32[]{:S(2)}, u32[]{:S(2)}) %collective-permute-start.12) | collective-permute-done | bytes 393248 | tf_op jit(solution)/shard_map/ppermute | solution.py:218
  61.5 1.5 %collective-permute-done.15.other_ref = f32[256,768]{1,0:T(8,128)S(1)} collective-permute-done((f32[256,768]{1,0:T(8,128)S(1)}, f32[256,768]{1,0:T(8,128)S(1)}, u32[]{:S(2)}, u32[]{:S(2)}) %collective-permute-start.15) | collective-permute-done | bytes 786464 | tf_op jit(solution)/shard_map/ppermute | solution.py:215
  63.0 1.4 %update.1 = (f32[256,768]{1,0:T(8,128)S(1)}, f32[256,768]{1,0:T(8,128)S(1)}, f32[8,128]{1,0:T(8,128)S(1)}) custom-call(f32[256,768]{1,0:T(8,128)S(1)} %product.6.mine_ref, f32[256,768]{1,0:T(8,128)S(1)} %collective-permute-done.15.other_ref, f32[1,256,768]{2,1,0:T(8,128)S(1)} %copy-done.3, f32[1,256,768]{2,1,0:T(8,128)S(1)} %copy-done.1, ...), custom_call_target="tpu_custom_call" | custom-call | bytes 5509120 | tf_op jit(solution)/shard_map/update/pallas_call | solution.py:179
  64.6 1.0 %collective-permute-done.16 = f32[8,128]{1,0:T(8,128)S(1)} collective-permute-done((f32[8,128]{1,0:T(8,128)S(1)}, f32[8,128]{1,0:T(8,128)S(1)}, u32[]{:S(2)}, u32[]{:S(2)}) %collective-permute-start.16) | collective-permute-done | bytes 4128 | tf_op jit(solution)/shard_map/ppermute | solution.py:215
  65.7 2.5 %collective-permute-start.19 = (f32[8,128]{1,0:T(8,128)S(1)}, f32[8,128]{1,0:T(8,128)S(1)}, u32[]{:S(2)}, u32[]{:S(2)}) collective-permute-start(f32[8,128]{1,0:T(8,128)S(1)} %add.3.refs_0_), channel_id=1, source_target_pairs={{0,24},{4,28},{8,16},{12,20},{16,8},{20,12},{24,0},{28,4},{1,25},{... | collective-permute-start | bytes 12296 | tf_op jit(solution)/shard_map/ppermute | solution.py:215
  69.2 1.3 %moment.1 = (f32[1,256,768]{2,1,0:T(8,128)}, f32[1,256,768]{2,1,0:T(8,128)}) custom-call(f32[256,768]{1,0:T(8,128)S(1)} %get-tuple-element.60.grad_ref, f32[1,256,768]{2,1,0:T(8,128)S(1)} %copy-done.1, f32[1,256,768]{2,1,0:T(8,128)S(1)} %copy-done.2), custom_call_target="tpu_custom_call" | custom-call | bytes 3932160 | tf_op jit(solution)/shard_map/moment/pallas_call | solution.py:179
  70.5 1.3 %collective-permute-done.18.refs_2_ = f32[8,128]{1,0:T(8,128)S(1)} collective-permute-done((f32[8,128]{1,0:T(8,128)S(1)}, f32[8,128]{1,0:T(8,128)S(1)}, u32[]{:S(2)}, u32[]{:S(2)}) %collective-permute-start.18) | collective-permute-done | bytes 4128 | tf_op jit(solution)/shard_map/ppermute | solution.py:215
  (37 shorter events, 9.2 us)
Async XLA Ops:
  0.6 13.2 %copy-start = (bf16[1,1,4,128,768]{4,3,2,1,0:T(8,128)(2,1)S(1)}, bf16[1,1,4,128,768]{4,3,2,1,0:T(8,128)(2,1)}, u32[]{:S(2)}) copy-start(bf16[1,1,4,128,768]{4,3,2,1,0:T(8,128)(2,1)} %param.12) | copy-start | bytes 2359300
  3.3 9.2 %collective-permute-start.3 = (bf16[128,512]{1,0:T(8,128)(2,1)}, bf16[128,512]{1,0:T(8,128)(2,1)S(1)}, u32[]{:S(2)}, u32[]{:S(2)}) collective-permute-start(bf16[128,512]{1,0:T(8,128)(2,1)} %get-tuple-element.41), channel_id=1, source_target_pairs={{0,1},{1,2},{2,3},{3,0},{4,5},{5,6},{6,7},{7,4},{8,9},{9,10},{10,1... | collective-permute-start | bytes 393224 | tf_op jit(solution)/shard_map/ppermute | solution.py:218
  6.3 9.8 %collective-permute-start = (bf16[272,512]{1,0:T(8,128)(2,1)}, bf16[272,512]{1,0:T(8,128)(2,1)S(1)}, u32[]{:S(2)}, u32[]{:S(2)}) collective-permute-start(bf16[272,512]{1,0:T(8,128)(2,1)} %get-tuple-element.33), channel_id=1, source_target_pairs={{0,8},{4,12},{8,0},{12,4},{16,24},{20,28},{24,16},{28,20},{1,9},{5... | collective-permute-start | bytes 835592 | tf_op jit(solution)/shard_map/ppermute | solution.py:215
  7.8 14.0 %collective-permute-start.1 = (bf16[272,512]{1,0:T(8,128)(2,1)}, bf16[272,512]{1,0:T(8,128)(2,1)S(1)}, u32[]{:S(2)}, u32[]{:S(2)}) collective-permute-start(bf16[272,512]{1,0:T(8,128)(2,1)} %get-tuple-element.34), channel_id=1, source_target_pairs={{0,16},{4,20},{8,24},{12,28},{16,0},{20,4},{24,8},{28,12},{1,17},{... | collective-permute-start | bytes 835592 | tf_op jit(solution)/shard_map/ppermute | solution.py:215
  9.4 12.5 %collective-permute-start.2 = (bf16[272,512]{1,0:T(8,128)(2,1)}, bf16[272,512]{1,0:T(8,128)(2,1)S(1)}, u32[]{:S(2)}, u32[]{:S(2)}) collective-permute-start(bf16[272,512]{1,0:T(8,128)(2,1)} %get-tuple-element.35), channel_id=1, source_target_pairs={{0,24},{4,28},{8,16},{12,20},{16,8},{20,12},{24,0},{28,4},{1,25},{... | collective-permute-start | bytes 835592 | tf_op jit(solution)/shard_map/ppermute | solution.py:215
  9.8 12.6 %collective-permute-start.4 = (bf16[128,512]{1,0:T(8,128)(2,1)}, bf16[128,512]{1,0:T(8,128)(2,1)S(1)}, u32[]{:S(2)}, u32[]{:S(2)}) collective-permute-start(bf16[128,512]{1,0:T(8,128)(2,1)} %get-tuple-element.42), channel_id=1, source_target_pairs={{0,2},{1,3},{2,0},{3,1},{4,6},{5,7},{6,4},{7,5},{8,10},{9,11},{10,... | collective-permute-start | bytes 393224 | tf_op jit(solution)/shard_map/ppermute | solution.py:218
  12.4 10.0 %collective-permute-start.5 = (bf16[128,512]{1,0:T(8,128)(2,1)}, bf16[128,512]{1,0:T(8,128)(2,1)S(1)}, u32[]{:S(2)}, u32[]{:S(2)}) collective-permute-start(bf16[128,512]{1,0:T(8,128)(2,1)} %get-tuple-element.44), channel_id=1, source_target_pairs={{0,3},{1,0},{2,1},{3,2},{4,7},{5,4},{6,5},{7,6},{8,11},{9,8},{10,9... | collective-permute-start | bytes 393224 | tf_op jit(solution)/shard_map/ppermute | solution.py:218
  13.9 35.8 %copy-start.4 = (bf16[128,512]{1,0:T(8,128)(2,1)S(1)}, bf16[128,512]{1,0:T(8,128)(2,1)}, u32[]{:S(2)}) copy-start(bf16[128,512]{1,0:T(8,128)(2,1)} %get-tuple-element.40.refs_1_) | copy-start | bytes 393220
  22.5 18.9 %collective-permute-start.9 = (bf16[384,512]{1,0:T(8,128)(2,1)S(1)}, bf16[384,512]{1,0:T(8,128)(2,1)S(1)}, u32[]{:S(2)}, u32[]{:S(2)}) collective-permute-start(bf16[384,512]{1,0:T(8,128)(2,1)S(1)} %get-tuple-element.49), channel_id=1, source_target_pairs={{0,2},{1,3},{2,0},{3,1},{4,6},{5,7},{6,4},{7,5},{8,10},{9,11},{10,... | collective-permute-start | bytes 1179656 | tf_op jit(solution)/shard_map/ppermute | solution.py:218
  25.1 16.2 %collective-permute-start.10 = (bf16[512,384]{1,0:T(8,128)(2,1)S(1)}, bf16[512,384]{1,0:T(8,128)(2,1)S(1)}, u32[]{:S(2)}, u32[]{:S(2)}) collective-permute-start(bf16[512,384]{1,0:T(8,128)(2,1)S(1)} %get-tuple-element.45), channel_id=1, source_target_pairs={{0,16},{4,20},{8,24},{12,28},{16,0},{20,4},{24,8},{28,12},{1,17},{... | collective-permute-start | bytes 1179656 | tf_op jit(solution)/shard_map/ppermute | solution.py:215
  26.6 14.7 %collective-permute-start.6 = (bf16[512,384]{1,0:T(8,128)(2,1)S(1)}, bf16[512,384]{1,0:T(8,128)(2,1)S(1)}, u32[]{:S(2)}, u32[]{:S(2)}) collective-permute-start(bf16[512,384]{1,0:T(8,128)(2,1)S(1)} %get-tuple-element.45), channel_id=1, source_target_pairs={{0,8},{4,12},{8,0},{12,4},{16,24},{20,28},{24,16},{28,20},{1,9},{5... | collective-permute-start | bytes 1179656 | tf_op jit(solution)/shard_map/ppermute | solution.py:215
  27.2 15.6 %collective-permute-start.8 = (bf16[512,384]{1,0:T(8,128)(2,1)S(1)}, bf16[512,384]{1,0:T(8,128)(2,1)S(1)}, u32[]{:S(2)}, u32[]{:S(2)}) collective-permute-start(bf16[512,384]{1,0:T(8,128)(2,1)S(1)} %get-tuple-element.46), channel_id=1, source_target_pairs={{0,16},{4,20},{8,24},{12,28},{16,0},{20,4},{24,8},{28,12},{1,17},{... | collective-permute-start | bytes 1179656 | tf_op jit(solution)/shard_map/ppermute | solution.py:215
  28.4 14.5 %collective-permute-start.7 = (bf16[512,384]{1,0:T(8,128)(2,1)S(1)}, bf16[512,384]{1,0:T(8,128)(2,1)S(1)}, u32[]{:S(2)}, u32[]{:S(2)}) collective-permute-start(bf16[512,384]{1,0:T(8,128)(2,1)S(1)} %get-tuple-element.46), channel_id=1, source_target_pairs={{0,8},{4,12},{8,0},{12,4},{16,24},{20,28},{24,16},{28,20},{1,9},{5... | collective-permute-start | bytes 1179656 | tf_op jit(solution)/shard_map/ppermute | solution.py:215
  42.9 13.9 %collective-permute-start.11 = (bf16[384,512]{1,0:T(8,128)(2,1)S(1)}, bf16[384,512]{1,0:T(8,128)(2,1)S(1)}, u32[]{:S(2)}, u32[]{:S(2)}) collective-permute-start(bf16[384,512]{1,0:T(8,128)(2,1)S(1)} %get-tuple-element.50), channel_id=1, source_target_pairs={{0,1},{1,2},{2,3},{3,0},{4,5},{5,6},{6,7},{7,4},{8,9},{9,10},{10,1... | collective-permute-start | bytes 1179656 | tf_op jit(solution)/shard_map/ppermute | solution.py:218
  43.6 16.2 %collective-permute-start.12 = (bf16[384,512]{1,0:T(8,128)(2,1)S(1)}, bf16[384,512]{1,0:T(8,128)(2,1)S(1)}, u32[]{:S(2)}, u32[]{:S(2)}) collective-permute-start(bf16[384,512]{1,0:T(8,128)(2,1)S(1)} %get-tuple-element.51), channel_id=1, source_target_pairs={{0,3},{1,0},{2,1},{3,2},{4,7},{5,4},{6,5},{7,6},{8,11},{9,8},{10,9... | collective-permute-start | bytes 1179656 | tf_op jit(solution)/shard_map/ppermute | solution.py:218
  46.8 13.1 %collective-permute-start.13 = (bf16[512,384]{1,0:T(8,128)(2,1)S(1)}, bf16[512,384]{1,0:T(8,128)(2,1)S(1)}, u32[]{:S(2)}, u32[]{:S(2)}) collective-permute-start(bf16[512,384]{1,0:T(8,128)(2,1)S(1)} %collective-permute-done.6.refs_5_.refs_0_), channel_id=1, source_target_pairs={{0,16},{4,20},{8,24},{12,28},{16,0},{20,4},{24,8},{28,12},{1,17},{... | collective-permute-start | bytes 1179656 | tf_op jit(solution)/shard_map/ppermute | solution.py:215
  48.3 11.6 %collective-permute-start.14 = (bf16[512,384]{1,0:T(8,128)(2,1)S(1)}, bf16[512,384]{1,0:T(8,128)(2,1)S(1)}, u32[]{:S(2)}, u32[]{:S(2)}) collective-permute-start(bf16[512,384]{1,0:T(8,128)(2,1)S(1)} %collective-permute-done.8.refs_10_.refs_5_), channel_id=1, source_target_pairs={{0,8},{4,12},{8,0},{12,4},{16,24},{20,28},{24,16},{28,20},{1,9},{5... | collective-permute-start | bytes 1179656 | tf_op jit(solution)/shard_map/ppermute | solution.py:215
  60.6 2.4 %copy-start.1 = (f32[1,256,768]{2,1,0:T(8,128)S(1)}, f32[1,256,768]{2,1,0:T(8,128)}, u32[]{:S(2)}) copy-start(f32[1,256,768]{2,1,0:T(8,128)} %first_ref.3) | copy-start | bytes 2359300
  60.6 2.4 %copy-start.2 = (f32[1,256,768]{2,1,0:T(8,128)S(1)}, f32[1,256,768]{2,1,0:T(8,128)}, u32[]{:S(2)}) copy-start(f32[1,256,768]{2,1,0:T(8,128)} %second_ref.3) | copy-start | bytes 2359300
  60.6 2.4 %collective-permute-start.15 = (f32[256,768]{1,0:T(8,128)S(1)}, f32[256,768]{1,0:T(8,128)S(1)}, u32[]{:S(2)}, u32[]{:S(2)}) collective-permute-start(f32[256,768]{1,0:T(8,128)S(1)} %product.7), channel_id=1, source_target_pairs={{0,4},{4,0},{8,12},{12,8},{16,20},{20,16},{24,28},{28,24},{1,5},{5... | collective-permute-start | bytes 2359304 | tf_op jit(solution)/shard_map/ppermute | solution.py:215
  64.4 1.2 %collective-permute-start.16 = (f32[8,128]{1,0:T(8,128)S(1)}, f32[8,128]{1,0:T(8,128)S(1)}, u32[]{:S(2)}, u32[]{:S(2)}) collective-permute-start(f32[8,128]{1,0:T(8,128)S(1)} %get-tuple-element.57), channel_id=1, source_target_pairs={{0,4},{4,0},{8,12},{12,8},{16,20},{20,16},{24,28},{28,24},{1,5},{5... | collective-permute-start | bytes 12296 | tf_op jit(solution)/shard_map/ppermute | solution.py:215
  65.7 4.8 %collective-permute-start.19 = (f32[8,128]{1,0:T(8,128)S(1)}, f32[8,128]{1,0:T(8,128)S(1)}, u32[]{:S(2)}, u32[]{:S(2)}) collective-permute-start(f32[8,128]{1,0:T(8,128)S(1)} %add.3.refs_0_), channel_id=1, source_target_pairs={{0,24},{4,28},{8,16},{12,20},{16,8},{20,12},{24,0},{28,4},{1,25},{... | collective-permute-start | bytes 12296 | tf_op jit(solution)/shard_map/ppermute | solution.py:215
  68.2 3.6 %collective-permute-start.18 = (f32[8,128]{1,0:T(8,128)S(1)}, f32[8,128]{1,0:T(8,128)S(1)}, u32[]{:S(2)}, u32[]{:S(2)}) collective-permute-start(f32[8,128]{1,0:T(8,128)S(1)} %add.3.refs_0_), channel_id=1, source_target_pairs={{0,16},{4,20},{8,24},{12,28},{16,0},{20,4},{24,8},{28,12},{1,17},{... | collective-permute-start | bytes 12296 | tf_op jit(solution)/shard_map/ppermute | solution.py:215
  68.8 3.6 %collective-permute-start.17 = (f32[8,128]{1,0:T(8,128)S(1)}, f32[8,128]{1,0:T(8,128)S(1)}, u32[]{:S(2)}, u32[]{:S(2)}) collective-permute-start(f32[8,128]{1,0:T(8,128)S(1)} %add.3.refs_0_), channel_id=1, source_target_pairs={{0,8},{4,12},{8,0},{12,4},{16,24},{20,28},{24,16},{28,20},{1,9},{5... | collective-permute-start | bytes 12296 | tf_op jit(solution)/shard_map/ppermute | solution.py:215
  (1 other events, 2.4 us)

commit v4 on v3

--- a/solution.py
+++ b/solution.py
@@ -60,7 +60,7 @@
 
 def cut_kernel(n_chips, owners, capacity, cot_ref, scale_ref, expert_ref, slot_ref, *refs):
     packed, blocks = refs[:owners], refs[owners : owners + n_chips - 1]
-    cot, scales, experts, slots, sems = refs[owners + n_chips - 1 :]
+    cot, scales, experts, slots, out_packed, out_blocks, sems, out_sems = refs[owners + n_chips - 1 :]
     tokens, width = cot_ref.shape
     part = width // n_chips
     half = part // 2
@@ -74,7 +74,8 @@
     for mask in range(n_chips):
         columns = pl.ds(pl.multiple_of((chip ^ mask) * part, part), part)
         large.append(pltpu.make_async_copy(cot_ref.at[:, columns], cot.at[mask], sems.at[3 + mask]))
-    for copy in small + large:
+    order = (*range(1, n_chips), 0)
+    for copy in small + [large[mask] for mask in order]:
         copy.start()
     for copy in small:
         copy.wait()
@@ -83,22 +84,33 @@
     expert_row, slot_row = experts[...].astype(jnp.float32), slots[...].astype(jnp.float32)
     row = lax.broadcasted_iota(jnp.int32, (TAIL, tokens), 0)
     ids = jnp.where(row == 0, expert_row, jnp.where(row == 1, slot_row, 0.0)).astype(jnp.bfloat16)
-    for mask, copy in enumerate(large):
-        copy.wait()
+    out_copies = []
+
+    def send(src, dst):
+        copy = pltpu.make_async_copy(src, dst, out_sems.at[len(out_copies)])
+        copy.start()
+        out_copies.append(copy)
+
+    for mask in order:
+        large[mask].wait()
         halves = []
         for side in range(2):
             begin = pl.multiple_of((core ^ side) * half, half)
             block = cot[mask, :, pl.ds(begin, half)].astype(jnp.float32)
             halves.append((scale * block).astype(jnp.bfloat16))
         routed = jnp.concatenate(halves, axis=1)
-        if mask == 0:
+        if mask:
+            out_blocks[mask - 1, :tokens, :] = routed
+            out_blocks[mask - 1, tokens:, :] = jnp.concatenate([ids] * (part // tokens), axis=1)
+            send(out_blocks.at[mask - 1], blocks[mask - 1])
+        else:
             z = lax.axis_index("expert")
             for shift, out in enumerate(packed):
-                out[...] = packed_rows(routed, expert_row, slot_row, lax.rem(z + shift, owners), capacity)
-        else:
-            out = blocks[mask - 1]
-            out[:tokens, :] = routed
-            out[tokens:, :] = jnp.concatenate([ids] * (part // tokens), axis=1)
+                expert = lax.rem(z + shift, owners)
+                out_packed[shift] = packed_rows(routed, expert_row, slot_row, expert, capacity)
+                send(out_packed.at[shift], out)
+    for copy in out_copies:
+        copy.wait()
 
 
 def pack_kernel(owners, capacity, n_blocks, *refs):
@@ -113,7 +125,7 @@
             out[at * capacity : (at + 1) * capacity, :] = packed_rows(rows, ids[0:1], ids[1:2], expert, capacity)
 
 
-def product_kernel(owners, capacity, columns, plan, *refs):
+def product_kernel(owners, capacity, columns, first, plan, *refs):
     me = lax.axis_index("expert")
     used = 1 + max(max(max(parts), max(place for place, _, _ in packed)) for parts, packed in plan)
     early, out = refs[used:-1], refs[-1]
@@ -122,7 +134,7 @@
         for _, packed in plan
     ]
     wide = min(refs[place].shape[1] for parts, _ in plan for place in parts)
-    for column in range(0, out.shape[1], wide):
+    for column in range(first, first + out.shape[1], wide):
         total = None
         for left, (parts, packed) in zip(rows, plan):
             part = refs[parts[column // refs[parts[0]].shape[1]]]
@@ -133,19 +145,21 @@
             total = term if total is None else total + term
         for ref in early:
             total = total + ref[:, column : column + wide]
-        out[:, column : column + wide] = total
+        out[:, column - first : column - first + wide] = total
 
 
 def new_moments(grad, first_ref, second_ref):
     return 0.9 * first_ref[0] + 0.1 * grad, 0.999 * second_ref[0] + 0.001 * grad * grad
 
 
-def update_kernel(mine_ref, other_ref, weight_ref, first_ref, second_ref, grad_ref, update_ref, sums):
-    grad = mine_ref[...] + other_ref[...]
+def update_kernel(mine_ref, left_ref, right_ref, weight_ref, first_ref, second_ref, grad_ref, update_ref, sums):
+    grad = mine_ref[...] + jnp.concatenate([left_ref[...], right_ref[...]], axis=1)
     grad_ref[...] = grad
     weight = weight_ref[0]
     first, second = new_moments(grad, first_ref, second_ref)
-    update = first / (1.0 - 0.9**10) / (jnp.sqrt(second / (1.0 - 0.999**10)) + 1e-06) + 0.01 * weight
+    first, second = first * (1.0 / (1.0 - 0.9**10)), second * (1.0 / (1.0 - 0.999**10))
+    root = second * lax.rsqrt(second)
+    update = first * pl.reciprocal(root + 1e-06) + 0.01 * weight
     update_ref[...] = update
     row = lax.broadcasted_iota(jnp.int32, sums.shape, 0)
     sums[...] = jnp.where(row == 0, jnp.sum(weight * weight), jnp.sum(update * update))
@@ -223,11 +237,11 @@
             functools.partial(pack_kernel, owners, capacity, len(blocks)),
             [jax.ShapeDtypeStruct((size, part), bf16)] * owners,
             *blocks,
-            flops=2 * size * owners * tokens * part,
+            flops=4 * 2 * size * owners * tokens * part,
             name="pack",
         )
 
-    def multiply(columns, groups, *early):
+    def multiply(columns, groups, *early, span=slice(0, ff)):
         arrays, plan = [], []
 
         def place(array):
@@ -239,11 +253,11 @@
             plan.append(([place(p) for p in parts], [(place(p), at, shift) for p, at, shift in packed]))
         n = columns.stop - columns.start
         return call(
-            functools.partial(product_kernel, owners, capacity, columns, plan),
-            jax.ShapeDtypeStruct((n, ff), f32),
+            functools.partial(product_kernel, owners, capacity, columns, span.start, plan),
+            jax.ShapeDtypeStruct((n, span.stop - span.start), f32),
             *arrays,
             *early,
-            flops=2 * sum(len(packed) for _, packed in plan) * capacity * n * ff,
+            flops=2 * sum(len(packed) for _, packed in plan) * capacity * n * (span.stop - span.start),
             name="product",
         )
 
@@ -259,8 +273,12 @@
             pltpu.VMEM((1, tokens), f32),
             pltpu.VMEM((1, tokens), jnp.int32),
             pltpu.VMEM((1, tokens), jnp.int32),
+            pltpu.VMEM((owners, capacity, part), bf16),
+            pltpu.VMEM((n_chips - 1, tokens + TAIL, part), bf16),
             pltpu.SemaphoreType.DMA((3 + n_chips,)),
+            pltpu.SemaphoreType.DMA((owners + n_chips - 1,)),
         ],
+        out_spaces=HBM,
         grant=60,
         name="cut",
     )
@@ -290,16 +308,21 @@
         totals[side.start] = multiply(side, groups)
     totals = after(totals, *totals.values())
     for side in (give, keep):
-        groups = [(by_x, terms(far, 0, 1, 3)), (by_y, terms(far, 1, 1, 3)), (by_xy, terms(far, 2, 0, 1, 2, 3))]
+        groups = [(by_x, terms(far, 0, 1)), (by_y, terms(far, 1, 1))]
         totals[side.start] = multiply(side, groups, totals[side.start])
-    other = across(totals[give.start], 1)
+    totals = after(totals, *totals.values())
+    groups = [(by_x, terms(far, 0, 3)), (by_y, terms(far, 1, 3)), (by_xy, terms(far, 2, 0, 1, 2, 3))]
+    spans = slice(0, ff // 2), slice(ff // 2, ff)
+    given = [multiply(give, groups, totals[give.start], span=span) for span in spans]
+    other = [across(part, 1) for part in given]
+    kept = multiply(keep, groups, after(totals[keep.start], *given))
 
     state, matrix = jax.ShapeDtypeStruct((1, half, ff), f32), jax.ShapeDtypeStruct((half, ff), f32)
     grad, update, sums = call(
         update_kernel,
         [matrix, matrix, jax.ShapeDtypeStruct((8, 128), f32)],
-        totals[keep.start],
-        other,
+        kept,
+        *other,
         down_weight,
         first_moment,
         second_moment,

time: 73.5 us -> 73.1 us (level)
  waiting for transfers between devices: 34.7 us -> 31.3 us
  starting transfers between devices: 27.8 us -> 30.5 us
    ppermute x14 -> x15, waiting for transfers between devices: 14 us -> 7.19 us  [across(): return lax.ppermute(array, 'dp', [(d, d ^ mask) for d in range(n_dp)])]
    ppermute x6, waiting for transfers between devices: 20.8 us -> 24.1 us  [along(): lax.ppermute(array, 'expert', [(d, (d + shift) % owners) for d in range(o...]
    ppermute x14 -> x15, starting transfers between devices: 14.3 us -> 16.1 us  [across(): return lax.ppermute(array, 'dp', [(d, d ^ mask) for d in range(n_dp)])]
    ppermute x6, starting transfers between devices: 13.5 us -> 14.4 us  [along(): lax.ppermute(array, 'expert', [(d, (d + shift) % owners) for d in range(o...]
    pallas_call x9 -> x12, Pallas kernels: 9.95 us -> 10.3 us  [call(): pl.pallas_call(kernel, out_shape=out_shape, in_specs=[spaces] * len(args)...]
  transfers between devices with their start and end apart: 20 -> 21, of which waited for: 11 -> 12; matrix products, arithmetic and copies ran while one was open for 0% -> 0% of each run, Pallas kernels for 6% -> 7%
where the time goes in v4:
time: 73.1 us; the launch traced here: 73 us
  waiting for transfers between devices  31.3 us (43%)
  starting transfers between devices  30.5 us (42%)
  Pallas kernels  10.3 us (14%)
  between operations  0.78 us (1%)
    ppermute x6, waiting for transfers between devices, along(): lax.ppermute(array, 'expert', [(d, (d + shift) % owners) for d in range(o...  24.1 us
    ppermute x15, starting transfers between devices, across(): return lax.ppermute(array, 'dp', [(d, d ^ mask) for d in range(n_dp)])  16.1 us
    ppermute x6, starting transfers between devices, along(): lax.ppermute(array, 'expert', [(d, (d + shift) % owners) for d in range(o...  14.4 us
    pallas_call x12, Pallas kernels, call(): pl.pallas_call(kernel, out_shape=out_shape, in_specs=[spaces] * len(args)...  10.3 us
    ppermute x15, waiting for transfers between devices, across(): return lax.ppermute(array, 'dp', [(d, d ^ mask) for d in range(n_dp)])  7.19 us
  transfers between devices with their start and end apart: 21, of which 12 were waited for; matrix products, arithmetic and copies ran while one was open for 0% of the time, Pallas kernels for 7%

profile of v4, /device:TPU:0, one launch (start us, length us, event | category | flops | bytes accessed | tf_op | source)
XLA Modules:
  0.0 73.0 jit_solution(16169039491578404290)
XLA Ops:
  0.6 2.4 %cut.1 = (bf16[128,512]{1,0:T(8,128)(2,1)}, bf16[128,512]{1,0:T(8,128)(2,1)}, bf16[128,512]{1,0:T(8,128)(2,1)}, bf16[128,512]{1,0:T(8,128)(2,1)}, bf16[272,512]{...) custom-call(bf16[256,2048]{1,0:T(8,128)(2,1)} %cot_ref.1, f32[1,256]{1,0:T(1,128)} %bitcast.7, ...), custom_call_target="tpu_custom_call" | custom-call | bytes 2411520 | tf_op jit(solution)/shard_map/cut/pallas_call | solution.py:193
  3.1 3.0 %collective-permute-start = (bf16[272,512]{1,0:T(8,128)(2,1)}, bf16[272,512]{1,0:T(8,128)(2,1)S(1)}, u32[]{:S(2)}, u32[]{:S(2)}) collective-permute-start(bf16[272,512]{1,0:T(8,128)(2,1)} %get-tuple-element.36), channel_id=1, source_target_pairs={{0,8},{4,12},{8,0},{12,4},{16,24},{20,28},{24,16},{28,20},{1,9},{5... | collective-permute-start | bytes 835592 | tf_op jit(solution)/shard_map/ppermute | solution.py:229
  6.1 1.5 %collective-permute-start.1 = (bf16[272,512]{1,0:T(8,128)(2,1)}, bf16[272,512]{1,0:T(8,128)(2,1)S(1)}, u32[]{:S(2)}, u32[]{:S(2)}) collective-permute-start(bf16[272,512]{1,0:T(8,128)(2,1)} %get-tuple-element.37), channel_id=1, source_target_pairs={{0,16},{4,20},{8,24},{12,28},{16,0},{20,4},{24,8},{28,12},{1,17},{... | collective-permute-start | bytes 835592 | tf_op jit(solution)/shard_map/ppermute | solution.py:229
  7.6 2.0 %collective-permute-start.3 = (bf16[128,512]{1,0:T(8,128)(2,1)}, bf16[128,512]{1,0:T(8,128)(2,1)S(1)}, u32[]{:S(2)}, u32[]{:S(2)}) collective-permute-start(bf16[128,512]{1,0:T(8,128)(2,1)} %get-tuple-element.44), channel_id=1, source_target_pairs={{0,1},{1,2},{2,3},{3,0},{4,5},{5,6},{6,7},{7,4},{8,9},{9,10},{10,1... | collective-permute-start | bytes 393224 | tf_op jit(solution)/shard_map/ppermute | solution.py:232
  9.7 2.6 %collective-permute-start.4 = (bf16[128,512]{1,0:T(8,128)(2,1)}, bf16[128,512]{1,0:T(8,128)(2,1)S(1)}, u32[]{:S(2)}, u32[]{:S(2)}) collective-permute-start(bf16[128,512]{1,0:T(8,128)(2,1)} %get-tuple-element.45), channel_id=1, source_target_pairs={{0,2},{1,3},{2,0},{3,1},{4,6},{5,7},{6,4},{7,5},{8,10},{9,11},{10,... | collective-permute-start | bytes 393224 | tf_op jit(solution)/shard_map/ppermute | solution.py:232
  12.4 3.8 %collective-permute-done.3.refs_2_ = bf16[128,512]{1,0:T(8,128)(2,1)S(1)} collective-permute-done((bf16[128,512]{1,0:T(8,128)(2,1)}, bf16[128,512]{1,0:T(8,128)(2,1)S(1)}, u32[]{:S(2)}, u32[]{:S(2)}) %collective-permute-start.3) | collective-permute-done | bytes 131104 | tf_op jit(solution)/shard_map/ppermute | solution.py:232
  16.2 1.3 %collective-permute-start.5 = (bf16[128,512]{1,0:T(8,128)(2,1)S(1)}, bf16[128,512]{1,0:T(8,128)(2,1)S(1)}, u32[]{:S(2)}, u32[]{:S(2)}) collective-permute-start(bf16[128,512]{1,0:T(8,128)(2,1)S(1)} %copy-done.5), channel_id=1, source_target_pairs={{0,3},{1,0},{2,1},{3,2},{4,7},{5,4},{6,5},{7,6},{8,11},{9,8},{10,9... | collective-permute-start | bytes 393224 | tf_op jit(solution)/shard_map/ppermute | solution.py:232
  17.5 2.9 %collective-permute-done.1.refs_1_ = bf16[272,512]{1,0:T(8,128)(2,1)S(1)} collective-permute-done((bf16[272,512]{1,0:T(8,128)(2,1)}, bf16[272,512]{1,0:T(8,128)(2,1)S(1)}, u32[]{:S(2)}, u32[]{:S(2)}) %collective-permute-start.1) | collective-permute-done | bytes 278560 | tf_op jit(solution)/shard_map/ppermute | solution.py:229
  21.6 4.6 %collective-permute-start.9 = (bf16[384,512]{1,0:T(8,128)(2,1)S(1)}, bf16[384,512]{1,0:T(8,128)(2,1)S(1)}, u32[]{:S(2)}, u32[]{:S(2)}) collective-permute-start(bf16[384,512]{1,0:T(8,128)(2,1)S(1)} %get-tuple-element.52), channel_id=1, source_target_pairs={{0,2},{1,3},{2,0},{3,1},{4,6},{5,7},{6,4},{7,5},{8,10},{9,11},{10,... | collective-permute-start | bytes 1179656 | tf_op jit(solution)/shard_map/ppermute | solution.py:232
  26.2 1.5 %collective-permute-start.10 = (bf16[512,384]{1,0:T(8,128)(2,1)S(1)}, bf16[512,384]{1,0:T(8,128)(2,1)S(1)}, u32[]{:S(2)}, u32[]{:S(2)}) collective-permute-start(bf16[512,384]{1,0:T(8,128)(2,1)S(1)} %get-tuple-element.48), channel_id=1, source_target_pairs={{0,16},{4,20},{8,24},{12,28},{16,0},{20,4},{24,8},{28,12},{1,17},{... | collective-permute-start | bytes 1179656 | tf_op jit(solution)/shard_map/ppermute | solution.py:229
  27.7 1.6 %collective-permute-start.6 = (bf16[512,384]{1,0:T(8,128)(2,1)S(1)}, bf16[512,384]{1,0:T(8,128)(2,1)S(1)}, u32[]{:S(2)}, u32[]{:S(2)}) collective-permute-start(bf16[512,384]{1,0:T(8,128)(2,1)S(1)} %get-tuple-element.48), channel_id=1, source_target_pairs={{0,8},{4,12},{8,0},{12,4},{16,24},{20,28},{24,16},{28,20},{1,9},{5... | collective-permute-start | bytes 1179656 | tf_op jit(solution)/shard_map/ppermute | solution.py:229
  30.2 10.5 %collective-permute-done.9.refs_8_.refs_9_ = bf16[384,512]{1,0:T(8,128)(2,1)S(1)} collective-permute-done((bf16[384,512]{1,0:T(8,128)(2,1)S(1)}, bf16[384,512]{1,0:T(8,128)(2,1)S(1)}, u32[]{:S(2)}, u32[]{:S(2)}) %collective-permute-start.9) | collective-permute-done | bytes 393248 | tf_op jit(solution)/shard_map/ppermute | solution.py:232
  41.8 1.6 %collective-permute-start.14 = (bf16[384,512]{1,0:T(8,128)(2,1)S(1)}, bf16[384,512]{1,0:T(8,128)(2,1)S(1)}, u32[]{:S(2)}, u32[]{:S(2)}) collective-permute-start(bf16[384,512]{1,0:T(8,128)(2,1)S(1)} %get-tuple-element.57), channel_id=1, source_target_pairs={{0,1},{1,2},{2,3},{3,0},{4,5},{5,6},{6,7},{7,4},{8,9},{9,10},{10,1... | collective-permute-start | bytes 1179656 | tf_op jit(solution)/shard_map/ppermute | solution.py:232
  43.4 2.3 %collective-permute-start.11 = (bf16[384,512]{1,0:T(8,128)(2,1)S(1)}, bf16[384,512]{1,0:T(8,128)(2,1)S(1)}, u32[]{:S(2)}, u32[]{:S(2)}) collective-permute-start(bf16[384,512]{1,0:T(8,128)(2,1)S(1)} %get-tuple-element.53), channel_id=1, source_target_pairs={{0,3},{1,0},{2,1},{3,2},{4,7},{5,4},{6,5},{7,6},{8,11},{9,8},{10,9... | collective-permute-start | bytes 1179656 | tf_op jit(solution)/shard_map/ppermute | solution.py:232
  45.6 1.5 %collective-permute-start.12 = (bf16[512,384]{1,0:T(8,128)(2,1)S(1)}, bf16[512,384]{1,0:T(8,128)(2,1)S(1)}, u32[]{:S(2)}, u32[]{:S(2)}) collective-permute-start(bf16[512,384]{1,0:T(8,128)(2,1)S(1)} %collective-permute-done.6.refs_5_.refs_0_), channel_id=1, source_target_pairs={{0,16},{4,20},{8,24},{12,28},{16,0},{20,4},{24,8},{28,12},{1,17},{... | collective-permute-start | bytes 1179656 | tf_op jit(solution)/shard_map/ppermute | solution.py:229
  47.1 1.4 %collective-permute-start.13 = (bf16[512,384]{1,0:T(8,128)(2,1)S(1)}, bf16[512,384]{1,0:T(8,128)(2,1)S(1)}, u32[]{:S(2)}, u32[]{:S(2)}) collective-permute-start(bf16[512,384]{1,0:T(8,128)(2,1)S(1)} %collective-permute-done.8.refs_10_.refs_4_), channel_id=1, source_target_pairs={{0,8},{4,12},{8,0},{12,4},{16,24},{20,28},{24,16},{28,20},{1,9},{5... | collective-permute-start | bytes 1179656 | tf_op jit(solution)/shard_map/ppermute | solution.py:229
  50.1 5.6 %collective-permute-done.14.refs_2_.refs_8_ = bf16[384,512]{1,0:T(8,128)(2,1)S(1)} collective-permute-done((bf16[384,512]{1,0:T(8,128)(2,1)S(1)}, bf16[384,512]{1,0:T(8,128)(2,1)S(1)}, u32[]{:S(2)}, u32[]{:S(2)}) %collective-permute-start.14) | collective-permute-done | bytes 393248 | tf_op jit(solution)/shard_map/ppermute | solution.py:232
  56.5 3.6 %collective-permute-done.11.refs_2_ = bf16[384,512]{1,0:T(8,128)(2,1)S(1)} collective-permute-done((bf16[384,512]{1,0:T(8,128)(2,1)S(1)}, bf16[384,512]{1,0:T(8,128)(2,1)S(1)}, u32[]{:S(2)}, u32[]{:S(2)}) %collective-permute-start.11) | collective-permute-done | bytes 393248 | tf_op jit(solution)/shard_map/ppermute | solution.py:232
  63.0 1.2 %update.1 = (f32[256,768]{1,0:T(8,128)S(1)}, f32[256,768]{1,0:T(8,128)S(1)}, f32[8,128]{1,0:T(8,128)S(1)}) custom-call(f32[256,768]{1,0:T(8,128)S(1)} %product.13.mine_ref, f32[256,384]{1,0:T(8,128)S(1)} %collective-permute-done.15.left_ref, f32[256,384]{1,0:T(8,128)S(1)} %collective-permute-done.16.right_ref, f32[1,256,768]{2,1,0:T(8,128)S(1)} %copy-done.3, ...), custom_call_target="tpu_custom_call" | custom-call | bytes 5509120 | tf_op jit(solution)/shard_map/update/pallas_call | solution.py:193
  65.4 1.5 %collective-permute-start.20 = (f32[8,128]{1,0:T(8,128)S(1)}, f32[8,128]{1,0:T(8,128)S(1)}, u32[]{:S(2)}, u32[]{:S(2)}) collective-permute-start(f32[8,128]{1,0:T(8,128)S(1)} %add.3.refs_0_), channel_id=1, source_target_pairs={{0,24},{4,28},{8,16},{12,20},{16,8},{20,12},{24,0},{28,4},{1,25},{... | collective-permute-start | bytes 12296 | tf_op jit(solution)/shard_map/ppermute | solution.py:229
  66.9 1.4 %collective-permute-start.19 = (f32[8,128]{1,0:T(8,128)S(1)}, f32[8,128]{1,0:T(8,128)S(1)}, u32[]{:S(2)}, u32[]{:S(2)}) collective-permute-start(f32[8,128]{1,0:T(8,128)S(1)} %add.3.refs_0_), channel_id=1, source_target_pairs={{0,16},{4,20},{8,24},{12,28},{16,0},{20,4},{24,8},{28,12},{1,17},{... | collective-permute-start | bytes 12296 | tf_op jit(solution)/shard_map/ppermute | solution.py:229
  68.9 1.3 %moment.1 = (f32[1,256,768]{2,1,0:T(8,128)}, f32[1,256,768]{2,1,0:T(8,128)}) custom-call(f32[256,768]{1,0:T(8,128)S(1)} %get-tuple-element.66.grad_ref, f32[1,256,768]{2,1,0:T(8,128)S(1)} %copy-done.1, f32[1,256,768]{2,1,0:T(8,128)S(1)} %copy-done.2), custom_call_target="tpu_custom_call" | custom-call | bytes 3932160 | tf_op jit(solution)/shard_map/moment/pallas_call | solution.py:193
  70.5 1.4 %collective-permute-done.18.refs_1_ = f32[8,128]{1,0:T(8,128)S(1)} collective-permute-done((f32[8,128]{1,0:T(8,128)S(1)}, f32[8,128]{1,0:T(8,128)S(1)}, u32[]{:S(2)}, u32[]{:S(2)}) %collective-permute-start.18) | collective-permute-done | bytes 4128 | tf_op jit(solution)/shard_map/ppermute | solution.py:229
  72.0 1.0 %weight.1 = f32[1,256,768]{2,1,0:T(8,128)} custom-call(f32[8,128]{1,0:T(8,128)S(1)} %add.3.refs_0_, f32[8,128]{1,0:T(8,128)S(1)} %collective-permute-done.18.refs_1_, f32[8,128]{1,0:T(8,128)S(1)} %collective-permute-done.19.refs_2_, f32[8,128]{1,0:T(8,128)S(1)} %collective-permute-done.20.refs_3_, f32[1,256,768]{2,1,0:T(8,128)S(1)} %copy-done.3, ...), custom_call_target="tpu_custom_call" | custom-call | bytes 2375680 | tf_op jit(solution)/shard_map/weight/pallas_call | solution.py:193
  (44 shorter events, 10.5 us)
Async XLA Ops:
  0.6 11.6 %copy-start = (bf16[1,1,4,128,768]{4,3,2,1,0:T(8,128)(2,1)S(1)}, bf16[1,1,4,128,768]{4,3,2,1,0:T(8,128)(2,1)}, u32[]{:S(2)}) copy-start(bf16[1,1,4,128,768]{4,3,2,1,0:T(8,128)(2,1)} %param.12) | copy-start | bytes 2359300
  3.1 14.4 %collective-permute-start = (bf16[272,512]{1,0:T(8,128)(2,1)}, bf16[272,512]{1,0:T(8,128)(2,1)S(1)}, u32[]{:S(2)}, u32[]{:S(2)}) collective-permute-start(bf16[272,512]{1,0:T(8,128)(2,1)} %get-tuple-element.36), channel_id=1, source_target_pairs={{0,8},{4,12},{8,0},{12,4},{16,24},{20,28},{24,16},{28,20},{1,9},{5... | collective-permute-start | bytes 835592 | tf_op jit(solution)/shard_map/ppermute | solution.py:229
  6.1 14.3 %collective-permute-start.1 = (bf16[272,512]{1,0:T(8,128)(2,1)}, bf16[272,512]{1,0:T(8,128)(2,1)S(1)}, u32[]{:S(2)}, u32[]{:S(2)}) collective-permute-start(bf16[272,512]{1,0:T(8,128)(2,1)} %get-tuple-element.37), channel_id=1, source_target_pairs={{0,16},{4,20},{8,24},{12,28},{16,0},{20,4},{24,8},{28,12},{1,17},{... | collective-permute-start | bytes 835592 | tf_op jit(solution)/shard_map/ppermute | solution.py:229
  7.6 12.8 %collective-permute-start.2 = (bf16[272,512]{1,0:T(8,128)(2,1)}, bf16[272,512]{1,0:T(8,128)(2,1)S(1)}, u32[]{:S(2)}, u32[]{:S(2)}) collective-permute-start(bf16[272,512]{1,0:T(8,128)(2,1)} %get-tuple-element.38), channel_id=1, source_target_pairs={{0,24},{4,28},{8,16},{12,20},{16,8},{20,12},{24,0},{28,4},{1,25},{... | collective-permute-start | bytes 835592 | tf_op jit(solution)/shard_map/ppermute | solution.py:229
  7.6 8.5 %collective-permute-start.3 = (bf16[128,512]{1,0:T(8,128)(2,1)}, bf16[128,512]{1,0:T(8,128)(2,1)S(1)}, u32[]{:S(2)}, u32[]{:S(2)}) collective-permute-start(bf16[128,512]{1,0:T(8,128)(2,1)} %get-tuple-element.44), channel_id=1, source_target_pairs={{0,1},{1,2},{2,3},{3,0},{4,5},{5,6},{6,7},{7,4},{8,9},{9,10},{10,1... | collective-permute-start | bytes 393224 | tf_op jit(solution)/shard_map/ppermute | solution.py:232
  9.7 11.3 %collective-permute-start.4 = (bf16[128,512]{1,0:T(8,128)(2,1)}, bf16[128,512]{1,0:T(8,128)(2,1)S(1)}, u32[]{:S(2)}, u32[]{:S(2)}) collective-permute-start(bf16[128,512]{1,0:T(8,128)(2,1)} %get-tuple-element.45), channel_id=1, source_target_pairs={{0,2},{1,3},{2,0},{3,1},{4,6},{5,7},{6,4},{7,5},{8,10},{9,11},{10,... | collective-permute-start | bytes 393224 | tf_op jit(solution)/shard_map/ppermute | solution.py:232
  12.3 3.9 %copy-start.5 = (bf16[128,512]{1,0:T(8,128)(2,1)S(1)}, bf16[128,512]{1,0:T(8,128)(2,1)}, u32[]{:S(2)}) copy-start(bf16[128,512]{1,0:T(8,128)(2,1)} %get-tuple-element.47) | copy-start | bytes 393220
  16.2 32.4 %copy-start.4 = (bf16[128,512]{1,0:T(8,128)(2,1)S(1)}, bf16[128,512]{1,0:T(8,128)(2,1)}, u32[]{:S(2)}) copy-start(bf16[128,512]{1,0:T(8,128)(2,1)} %get-tuple-element.43.refs_1_) | copy-start | bytes 393220
  16.2 5.4 %collective-permute-start.5 = (bf16[128,512]{1,0:T(8,128)(2,1)S(1)}, bf16[128,512]{1,0:T(8,128)(2,1)S(1)}, u32[]{:S(2)}, u32[]{:S(2)}) collective-permute-start(bf16[128,512]{1,0:T(8,128)(2,1)S(1)} %copy-done.5), channel_id=1, source_target_pairs={{0,3},{1,0},{2,1},{3,2},{4,7},{5,4},{6,5},{7,6},{8,11},{9,8},{10,9... | collective-permute-start | bytes 393224 | tf_op jit(solution)/shard_map/ppermute | solution.py:232
  21.6 19.1 %collective-permute-start.9 = (bf16[384,512]{1,0:T(8,128)(2,1)S(1)}, bf16[384,512]{1,0:T(8,128)(2,1)S(1)}, u32[]{:S(2)}, u32[]{:S(2)}) collective-permute-start(bf16[384,512]{1,0:T(8,128)(2,1)S(1)} %get-tuple-element.52), channel_id=1, source_target_pairs={{0,2},{1,3},{2,0},{3,1},{4,6},{5,7},{6,4},{7,5},{8,10},{9,11},{10,... | collective-permute-start | bytes 1179656 | tf_op jit(solution)/shard_map/ppermute | solution.py:232
  26.2 14.5 %collective-permute-start.10 = (bf16[512,384]{1,0:T(8,128)(2,1)S(1)}, bf16[512,384]{1,0:T(8,128)(2,1)S(1)}, u32[]{:S(2)}, u32[]{:S(2)}) collective-permute-start(bf16[512,384]{1,0:T(8,128)(2,1)S(1)} %get-tuple-element.48), channel_id=1, source_target_pairs={{0,16},{4,20},{8,24},{12,28},{16,0},{20,4},{24,8},{28,12},{1,17},{... | collective-permute-start | bytes 1179656 | tf_op jit(solution)/shard_map/ppermute | solution.py:229
  27.7 13.0 %collective-permute-start.6 = (bf16[512,384]{1,0:T(8,128)(2,1)S(1)}, bf16[512,384]{1,0:T(8,128)(2,1)S(1)}, u32[]{:S(2)}, u32[]{:S(2)}) collective-permute-start(bf16[512,384]{1,0:T(8,128)(2,1)S(1)} %get-tuple-element.48), channel_id=1, source_target_pairs={{0,8},{4,12},{8,0},{12,4},{16,24},{20,28},{24,16},{28,20},{1,9},{5... | collective-permute-start | bytes 1179656 | tf_op jit(solution)/shard_map/ppermute | solution.py:229
  29.3 12.3 %collective-permute-start.8 = (bf16[512,384]{1,0:T(8,128)(2,1)S(1)}, bf16[512,384]{1,0:T(8,128)(2,1)S(1)}, u32[]{:S(2)}, u32[]{:S(2)}) collective-permute-start(bf16[512,384]{1,0:T(8,128)(2,1)S(1)} %get-tuple-element.49), channel_id=1, source_target_pairs={{0,16},{4,20},{8,24},{12,28},{16,0},{20,4},{24,8},{28,12},{1,17},{... | collective-permute-start | bytes 1179656 | tf_op jit(solution)/shard_map/ppermute | solution.py:229
  29.8 12.0 %collective-permute-start.7 = (bf16[512,384]{1,0:T(8,128)(2,1)S(1)}, bf16[512,384]{1,0:T(8,128)(2,1)S(1)}, u32[]{:S(2)}, u32[]{:S(2)}) collective-permute-start(bf16[512,384]{1,0:T(8,128)(2,1)S(1)} %get-tuple-element.49), channel_id=1, source_target_pairs={{0,8},{4,12},{8,0},{12,4},{16,24},{20,28},{24,16},{28,20},{1,9},{5... | collective-permute-start | bytes 1179656 | tf_op jit(solution)/shard_map/ppermute | solution.py:229
  41.8 13.9 %collective-permute-start.14 = (bf16[384,512]{1,0:T(8,128)(2,1)S(1)}, bf16[384,512]{1,0:T(8,128)(2,1)S(1)}, u32[]{:S(2)}, u32[]{:S(2)}) collective-permute-start(bf16[384,512]{1,0:T(8,128)(2,1)S(1)} %get-tuple-element.57), channel_id=1, source_target_pairs={{0,1},{1,2},{2,3},{3,0},{4,5},{5,6},{6,7},{7,4},{8,9},{9,10},{10,1... | collective-permute-start | bytes 1179656 | tf_op jit(solution)/shard_map/ppermute | solution.py:232
  43.4 16.7 %collective-permute-start.11 = (bf16[384,512]{1,0:T(8,128)(2,1)S(1)}, bf16[384,512]{1,0:T(8,128)(2,1)S(1)}, u32[]{:S(2)}, u32[]{:S(2)}) collective-permute-start(bf16[384,512]{1,0:T(8,128)(2,1)S(1)} %get-tuple-element.53), channel_id=1, source_target_pairs={{0,3},{1,0},{2,1},{3,2},{4,7},{5,4},{6,5},{7,6},{8,11},{9,8},{10,9... | collective-permute-start | bytes 1179656 | tf_op jit(solution)/shard_map/ppermute | solution.py:232
  45.6 14.5 %collective-permute-start.12 = (bf16[512,384]{1,0:T(8,128)(2,1)S(1)}, bf16[512,384]{1,0:T(8,128)(2,1)S(1)}, u32[]{:S(2)}, u32[]{:S(2)}) collective-permute-start(bf16[512,384]{1,0:T(8,128)(2,1)S(1)} %collective-permute-done.6.refs_5_.refs_0_), channel_id=1, source_target_pairs={{0,16},{4,20},{8,24},{12,28},{16,0},{20,4},{24,8},{28,12},{1,17},{... | collective-permute-start | bytes 1179656 | tf_op jit(solution)/shard_map/ppermute | solution.py:229
  47.1 13.0 %collective-permute-start.13 = (bf16[512,384]{1,0:T(8,128)(2,1)S(1)}, bf16[512,384]{1,0:T(8,128)(2,1)S(1)}, u32[]{:S(2)}, u32[]{:S(2)}) collective-permute-start(bf16[512,384]{1,0:T(8,128)(2,1)S(1)} %collective-permute-done.8.refs_10_.refs_4_), channel_id=1, source_target_pairs={{0,8},{4,12},{8,0},{12,4},{16,24},{20,28},{24,16},{28,20},{1,9},{5... | collective-permute-start | bytes 1179656 | tf_op jit(solution)/shard_map/ppermute | solution.py:229
  60.5 1.8 %collective-permute-start.15 = (f32[256,384]{1,0:T(8,128)S(1)}, f32[256,384]{1,0:T(8,128)S(1)}, u32[]{:S(2)}, u32[]{:S(2)}) collective-permute-start(f32[256,384]{1,0:T(8,128)S(1)} %product.11), channel_id=1, source_target_pairs={{0,4},{4,0},{8,12},{12,8},{16,20},{20,16},{24,28},{28,24},{1,5},{5... | collective-permute-start | bytes 1179656 | tf_op jit(solution)/shard_map/ppermute | solution.py:229
  61.1 1.9 %collective-permute-start.16 = (f32[256,384]{1,0:T(8,128)S(1)}, f32[256,384]{1,0:T(8,128)S(1)}, u32[]{:S(2)}, u32[]{:S(2)}) collective-permute-start(f32[256,384]{1,0:T(8,128)S(1)} %product.12), channel_id=1, source_target_pairs={{0,4},{4,0},{8,12},{12,8},{16,20},{20,16},{24,28},{28,24},{1,5},{5... | collective-permute-start | bytes 1179656 | tf_op jit(solution)/shard_map/ppermute | solution.py:229
  64.2 1.3 %collective-permute-start.17 = (f32[8,128]{1,0:T(8,128)S(1)}, f32[8,128]{1,0:T(8,128)S(1)}, u32[]{:S(2)}, u32[]{:S(2)}) collective-permute-start(f32[8,128]{1,0:T(8,128)S(1)} %get-tuple-element.63), channel_id=1, source_target_pairs={{0,4},{4,0},{8,12},{12,8},{16,20},{20,16},{24,28},{28,24},{1,5},{5... | collective-permute-start | bytes 12296 | tf_op jit(solution)/shard_map/ppermute | solution.py:229
  65.4 4.8 %collective-permute-start.20 = (f32[8,128]{1,0:T(8,128)S(1)}, f32[8,128]{1,0:T(8,128)S(1)}, u32[]{:S(2)}, u32[]{:S(2)}) collective-permute-start(f32[8,128]{1,0:T(8,128)S(1)} %add.3.refs_0_), channel_id=1, source_target_pairs={{0,24},{4,28},{8,16},{12,20},{16,8},{20,12},{24,0},{28,4},{1,25},{... | collective-permute-start | bytes 12296 | tf_op jit(solution)/shard_map/ppermute | solution.py:229
  66.9 3.6 %collective-permute-start.19 = (f32[8,128]{1,0:T(8,128)S(1)}, f32[8,128]{1,0:T(8,128)S(1)}, u32[]{:S(2)}, u32[]{:S(2)}) collective-permute-start(f32[8,128]{1,0:T(8,128)S(1)} %add.3.refs_0_), channel_id=1, source_target_pairs={{0,16},{4,20},{8,24},{12,28},{16,0},{20,4},{24,8},{28,12},{1,17},{... | collective-permute-start | bytes 12296 | tf_op jit(solution)/shard_map/ppermute | solution.py:229
  68.4 3.6 %collective-permute-start.18 = (f32[8,128]{1,0:T(8,128)S(1)}, f32[8,128]{1,0:T(8,128)S(1)}, u32[]{:S(2)}, u32[]{:S(2)}) collective-permute-start(f32[8,128]{1,0:T(8,128)S(1)} %add.3.refs_0_), channel_id=1, source_target_pairs={{0,8},{4,12},{8,0},{12,4},{16,24},{20,28},{24,16},{28,20},{1,9},{5... | collective-permute-start | bytes 12296 | tf_op jit(solution)/shard_map/ppermute | solution.py:229
  (3 other events, 5.8 us)

commit v5 on v4

--- a/solution.py
+++ b/solution.py
@@ -9,6 +9,7 @@
 
 VMEM = pl.BlockSpec(memory_space=pltpu.VMEM)
 HBM = pl.BlockSpec(memory_space=pltpu.HBM)
+ANY = pl.BlockSpec(memory_space=pl.ANY)
 TAIL = 16
 ROWS_FIRST = (((0,), (0,)), ((), ()))
 
@@ -60,7 +61,7 @@
 
 def cut_kernel(n_chips, owners, capacity, cot_ref, scale_ref, expert_ref, slot_ref, *refs):
     packed, blocks = refs[:owners], refs[owners : owners + n_chips - 1]
-    cot, scales, experts, slots, out_packed, out_blocks, sems, out_sems = refs[owners + n_chips - 1 :]
+    cot, scales, experts, slots, sems = refs[owners + n_chips - 1 :]
     tokens, width = cot_ref.shape
     part = width // n_chips
     half = part // 2
@@ -84,13 +85,6 @@
     expert_row, slot_row = experts[...].astype(jnp.float32), slots[...].astype(jnp.float32)
     row = lax.broadcasted_iota(jnp.int32, (TAIL, tokens), 0)
     ids = jnp.where(row == 0, expert_row, jnp.where(row == 1, slot_row, 0.0)).astype(jnp.bfloat16)
-    out_copies = []
-
-    def send(src, dst):
-        copy = pltpu.make_async_copy(src, dst, out_sems.at[len(out_copies)])
-        copy.start()
-        out_copies.append(copy)
-
     for mask in order:
         large[mask].wait()
         halves = []
@@ -100,17 +94,14 @@
             halves.append((scale * block).astype(jnp.bfloat16))
         routed = jnp.concatenate(halves, axis=1)
         if mask:
-            out_blocks[mask - 1, :tokens, :] = routed
-            out_blocks[mask - 1, tokens:, :] = jnp.concatenate([ids] * (part // tokens), axis=1)
-            send(out_blocks.at[mask - 1], blocks[mask - 1])
+            out = blocks[mask - 1]
+            out[:tokens, :] = routed
+            out[tokens:, :] = jnp.concatenate([ids] * (part // tokens), axis=1)
         else:
             z = lax.axis_index("expert")
             for shift, out in enumerate(packed):
                 expert = lax.rem(z + shift, owners)
-                out_packed[shift] = packed_rows(routed, expert_row, slot_row, expert, capacity)
-                send(out_packed.at[shift], out)
-    for copy in out_copies:
-        copy.wait()
+                out[...] = packed_rows(routed, expert_row, slot_row, expert, capacity)
 
 
 def pack_kernel(owners, capacity, n_blocks, *refs):
@@ -125,20 +116,21 @@
             out[at * capacity : (at + 1) * capacity, :] = packed_rows(rows, ids[0:1], ids[1:2], expert, capacity)
 
 
-def product_kernel(owners, capacity, columns, first, plan, *refs):
+def product_kernel(owners, capacity, columns, first, plan, n_early, *refs):
     me = lax.axis_index("expert")
     used = 1 + max(max(max(parts), max(place for place, _, _ in packed)) for parts, packed in plan)
-    early, out = refs[used:-1], refs[-1]
+    early, out = refs[used : used + n_early], refs[-1]
     rows = [
         jnp.concatenate([refs[place][at * capacity : (at + 1) * capacity, columns] for place, at, _ in packed])
         for _, packed in plan
     ]
-    wide = min(refs[place].shape[1] for parts, _ in plan for place in parts)
+    wide = min(out.shape[1], *(refs[place].shape[1] for parts, _ in plan for place in parts))
     for column in range(first, first + out.shape[1], wide):
         total = None
         for left, (parts, packed) in zip(rows, plan):
-            part = refs[parts[column // refs[parts[0]].shape[1]]]
-            inside = slice(column % part.shape[1], column % part.shape[1] + wide)
+            size = refs[parts[0]].shape[1]
+            part = refs[parts[column // size]]
+            inside = slice(column % size, column % size + wide)
             begins = [lax.rem(me + owners - shift, owners) * capacity for _, _, shift in packed]
             right = [part[pl.ds(pl.multiple_of(begin, capacity), capacity), inside] for begin in begins]
             term = lax.dot_general(left, jnp.concatenate(right), ROWS_FIRST, preferred_element_type=jnp.float32)
@@ -193,13 +185,20 @@
     return pl.pallas_call(
         kernel,
         out_shape=out_shape,
-        in_specs=[spaces] * len(args),
+        in_specs=spaces if isinstance(spaces, list) else [spaces] * len(args),
         out_specs=jax.tree.map(lambda _: out_spaces, out_shape),
         scratch_shapes=scratch,
         compiler_params=pltpu.CompilerParams(vmem_limit_bytes=grant * 2**20),
         cost_estimate=pl.CostEstimate(flops=flops, bytes_accessed=nbytes, transcendentals=0),
         name=name,
     )(*args)
+
+
+def tick(*arrays, flops):
+    def kernel(*refs):
+        refs[-1][...] = jnp.zeros(refs[-1].shape, jnp.float32)
+
+    return call(kernel, jax.ShapeDtypeStruct((8, 128), jnp.float32), *arrays, spaces=ANY, flops=flops, name="tick")
 
 
 def after(arrays, *earlier):
@@ -241,7 +240,7 @@
             name="pack",
         )
 
-    def multiply(columns, groups, *early, span=slice(0, ff)):
+    def multiply(columns, groups, *early, span=slice(0, ff), waits=()):
         arrays, plan = [], []
 
         def place(array):
@@ -253,67 +252,59 @@
             plan.append(([place(p) for p in parts], [(place(p), at, shift) for p, at, shift in packed]))
         n = columns.stop - columns.start
         return call(
-            functools.partial(product_kernel, owners, capacity, columns, span.start, plan),
+            functools.partial(product_kernel, owners, capacity, columns, span.start, plan, len(early)),
             jax.ShapeDtypeStruct((n, span.stop - span.start), f32),
             *arrays,
             *early,
+            *waits,
+            spaces=[VMEM] * (len(arrays) + len(early)) + [ANY] * len(waits),
             flops=2 * sum(len(packed) for _, packed in plan) * capacity * n * (span.stop - span.start),
             name="product",
         )
 
     packed, block = jax.ShapeDtypeStruct((capacity, part), bf16), jax.ShapeDtypeStruct((tokens + TAIL, part), bf16)
+    operands = cotangent, *[ids.reshape(1, tokens) for ids in (route_weight, expert_ids, slot_ids)]
     cut = call(
         functools.partial(cut_kernel, n_chips, owners, capacity),
         [packed] * owners + [block] * (n_chips - 1),
-        cotangent,
-        *[ids.reshape(1, tokens) for ids in (route_weight, expert_ids, slot_ids)],
+        *[pltpu.with_memory_space_constraint(array, pltpu.HBM) for array in operands],
         spaces=HBM,
         scratch=[
             pltpu.VMEM((n_chips, tokens, part), bf16),
             pltpu.VMEM((1, tokens), f32),
             pltpu.VMEM((1, tokens), jnp.int32),
             pltpu.VMEM((1, tokens), jnp.int32),
-            pltpu.VMEM((owners, capacity, part), bf16),
-            pltpu.VMEM((n_chips - 1, tokens + TAIL, part), bf16),
             pltpu.SemaphoreType.DMA((3 + n_chips,)),
-            pltpu.SemaphoreType.DMA((owners + n_chips - 1,)),
         ],
-        out_spaces=HBM,
-        grant=60,
         name="cut",
     )
     near, (to_x, to_y, to_xy) = cut[:owners], cut[owners:]
-    from_x, from_y, from_xy = across(to_x, 2), across(to_y, 4), across(to_xy, 6)
-    near = [near[0], along(near[1], 1), along(near[2], 2), near[3]]
-    near[3] = along(after(near[3], near[1]), 3)
-    far = pack(from_x, from_y, from_xy)
-    far, left, right = after((far, hidden[:, : ff // 2], hidden[:, ff // 2 :]), *near)
-    far = list(far)
-    x_left, x_right, y_left, y_right = across(left, 2), across(right, 2), across(left, 4), across(right, 4)
-    far[2] = along(far[2], 2)
-    far[1], far[3], xy_left, xy_right = after(
-        (far[1], far[3], x_left, y_right), far[2], x_left, x_right, y_left, y_right
-    )
-    far[1], far[3] = along(far[1], 1), along(far[3], 3)
-    xy_left, xy_right = across(xy_left, 4), across(xy_right, 2)
+    from_x, from_y = across(to_x, 2), across(to_y, 4)
+    near = [near[0]] + [along(near[shift], shift) for shift in range(1, owners)]
+    mid = pack(from_y)
+    mid = [mid[0], along(mid[1], 1), along(mid[2], 2), along(mid[3], 3)]
+    from_xy = across(after(to_xy, from_x, from_y, near[1], near[2]), 6)
+    by_x = across(after(hidden, from_x, from_y, *near), 2)
+    by_y = across(after(hidden, from_x, from_y, *near), 4)
+    far = pack(from_x, from_xy)
+    far = [far[0]] + [along(far[shift], shift) for shift in range(1, owners)]
+    left, right = after((by_x[:, : ff // 2], by_y[:, ff // 2 :]), by_x, by_y)
+    by_xy = across(left, 4), across(right, 2)
 
     keep, give = slice(0, half), slice(half, part)
     def terms(packed, at, *shifts):
         return [(packed[shift], at, shift) for shift in shifts]
 
-    by_x, by_y, by_xy = (x_left, x_right), (y_left, y_right), (xy_left, xy_right)
     totals = {}
+    seen = tick(*mid[1:], flops=20*10**9)
     for side in (give, keep):
-        groups = [((hidden,), terms(near, 0, 0, 1, 2, 3)), (by_x, terms(far, 0, 0, 2)), (by_y, terms(far, 1, 0, 2))]
-        totals[side.start] = multiply(side, groups)
-    totals = after(totals, *totals.values())
-    for side in (give, keep):
-        groups = [(by_x, terms(far, 0, 1)), (by_y, terms(far, 1, 1))]
-        totals[side.start] = multiply(side, groups, totals[side.start])
-    totals = after(totals, *totals.values())
-    groups = [(by_x, terms(far, 0, 3)), (by_y, terms(far, 1, 3)), (by_xy, terms(far, 2, 0, 1, 2, 3))]
+        groups = [((hidden,), terms(near, 0, 0, 1, 2, 3)), ((by_y,), terms(mid, 0, 0, 1, 2, 3))]
+        totals[side.start] = multiply(side, groups, waits=[seen])
+    seen = tick(*far[1:], *totals.values(), flops=5*10**9)
+    groups = [((by_x,), terms(far, 0, 0, 1, 2, 3)), (by_xy, terms(far, 1, 0, 1, 2, 3))]
     spans = slice(0, ff // 2), slice(ff // 2, ff)
-    given = [multiply(give, groups, totals[give.start], span=span) for span in spans]
+    ready = [seen, down_weight, first_moment, second_moment]
+    given = [multiply(give, groups, totals[give.start], span=span, waits=ready) for span in spans]
     other = [across(part, 1) for part in given]
     kept = multiply(keep, groups, after(totals[keep.start], *given))
 

time: 73.1 us -> 71 us (0.971)
  starting transfers between devices: 30.5 us -> 24.3 us
  waiting for transfers between devices: 31.3 us -> 36.8 us
  Pallas kernels: 10.3 us -> 8.85 us
    ppermute x15 -> x13, waiting for transfers between devices: 7.19 us -> 12.2 us  [across(): return lax.ppermute(array, 'dp', [(d, d ^ mask) for d in range(n_dp)])]
    ppermute x6 -> x9, starting transfers between devices: 14.4 us -> 11.1 us  [along(): lax.ppermute(array, 'expert', [(d, (d + shift) % owners) for d in range(o...]
    ppermute x15 -> x13, starting transfers between devices: 16.1 us -> 13.2 us  [across(): return lax.ppermute(array, 'dp', [(d, d ^ mask) for d in range(n_dp)])]
    pallas_call x12 -> x13, Pallas kernels: 10.3 us -> 8.85 us  [call(): pl.pallas_call(kernel, out_shape=out_shape, in_specs=spaces if isinstance...]
    ppermute x6 -> x9, waiting for transfers between devices: 24.1 us -> 24.6 us  [along(): lax.ppermute(array, 'expert', [(d, (d + shift) % owners) for d in range(o...]
  transfers between devices with their start and end apart: 21 -> 22, of which waited for: 12 -> 14; matrix products, arithmetic and copies ran while one was open for 0% -> 0% of each run, Pallas kernels for 7% -> 6%
where the time goes in v5:
time: 71 us; the launch traced here: 70.9 us
  waiting for transfers between devices  36.8 us (52%)
  starting transfers between devices  24.3 us (34%)
  Pallas kernels  8.85 us (12%)
  between operations  0.8 us (1%)
    ppermute x9, waiting for transfers between devices, along(): lax.ppermute(array, 'expert', [(d, (d + shift) % owners) for d in range(o...  24.6 us
    ppermute x13, starting transfers between devices, across(): return lax.ppermute(array, 'dp', [(d, d ^ mask) for d in range(n_dp)])  13.2 us
    ppermute x13, waiting for transfers between devices, across(): return lax.ppermute(array, 'dp', [(d, d ^ mask) for d in range(n_dp)])  12.2 us
    ppermute x9, starting transfers between devices, along(): lax.ppermute(array, 'expert', [(d, (d + shift) % owners) for d in range(o...  11.1 us
    pallas_call x13, Pallas kernels, call(): pl.pallas_call(kernel, out_shape=out_shape, in_specs=spaces if isinstance...  8.85 us
  transfers between devices with their start and end apart: 22, of which 14 were waited for; matrix products, arithmetic and copies ran while one was open for 0% of the time, Pallas kernels for 6%

profile of v5, /device:TPU:0, one launch (start us, length us, event | category | flops | bytes accessed | tf_op | source)
XLA Modules:
  0.0 70.9 jit_solution(17397076802551338593)
XLA Ops:
  0.6 1.6 %cut.1 = (bf16[128,512]{1,0:T(8,128)(2,1)S(1)}, bf16[128,512]{1,0:T(8,128)(2,1)S(1)}, bf16[128,512]{1,0:T(8,128)(2,1)S(1)}, bf16[128,512]{1,0:T(8,128)(2,1)S(1)}...) custom-call(bf16[256,2048]{1,0:T(8,128)(2,1)} %cot_ref.1, ...), custom_call_target="tpu_custom_call" | custom-call | bytes 2411520 | tf_op jit(solution)/shard_map/cut/pallas_call | solution.py:185
  2.3 3.0 %collective-permute-start = (bf16[272,512]{1,0:T(8,128)(2,1)S(1)}, bf16[272,512]{1,0:T(8,128)(2,1)S(1)}, u32[]{:S(2)}, u32[]{:S(2)}) collective-permute-start(bf16[272,512]{1,0:T(8,128)(2,1)S(1)} %get-tuple-element.29), channel_id=1, source_target_pairs={{0,8},{4,12},{8,0},{12,4},{16,24},{20,28},{24,16},{28,20},{1,9},{5... | collective-permute-start | bytes 835592 | tf_op jit(solution)/shard_map/ppermute | solution.py:228
  5.3 1.5 %collective-permute-start.1 = (bf16[272,512]{1,0:T(8,128)(2,1)S(1)}, bf16[272,512]{1,0:T(8,128)(2,1)S(1)}, u32[]{:S(2)}, u32[]{:S(2)}) collective-permute-start(bf16[272,512]{1,0:T(8,128)(2,1)S(1)} %get-tuple-element.30), channel_id=1, source_target_pairs={{0,16},{4,20},{8,24},{12,28},{16,0},{20,4},{24,8},{28,12},{1,17},{... | collective-permute-start | bytes 835592 | tf_op jit(solution)/shard_map/ppermute | solution.py:228
  6.8 1.6 %collective-permute-start.2 = (bf16[128,512]{1,0:T(8,128)(2,1)S(1)}, bf16[128,512]{1,0:T(8,128)(2,1)S(1)}, u32[]{:S(2)}, u32[]{:S(2)}) collective-permute-start(bf16[128,512]{1,0:T(8,128)(2,1)S(1)} %get-tuple-element.32), channel_id=1, source_target_pairs={{0,1},{1,2},{2,3},{3,0},{4,5},{5,6},{6,7},{7,4},{8,9},{9,10},{10,1... | collective-permute-start | bytes 393224 | tf_op jit(solution)/shard_map/ppermute | solution.py:231
  8.4 2.6 %collective-permute-start.3 = (bf16[128,512]{1,0:T(8,128)(2,1)S(1)}, bf16[128,512]{1,0:T(8,128)(2,1)S(1)}, u32[]{:S(2)}, u32[]{:S(2)}) collective-permute-start(bf16[128,512]{1,0:T(8,128)(2,1)S(1)} %get-tuple-element.33), channel_id=1, source_target_pairs={{0,2},{1,3},{2,0},{3,1},{4,6},{5,7},{6,4},{7,5},{8,10},{9,11},{10,... | collective-permute-start | bytes 393224 | tf_op jit(solution)/shard_map/ppermute | solution.py:231
  11.0 3.9 %collective-permute-done.2.refs_2_ = bf16[128,512]{1,0:T(8,128)(2,1)S(1)} collective-permute-done((bf16[128,512]{1,0:T(8,128)(2,1)S(1)}, bf16[128,512]{1,0:T(8,128)(2,1)S(1)}, u32[]{:S(2)}, u32[]{:S(2)}) %collective-permute-start.2) | collective-permute-done | bytes 131104 | tf_op jit(solution)/shard_map/ppermute | solution.py:231
  14.8 4.1 %collective-permute-done.3.refs_3_ = bf16[128,512]{1,0:T(8,128)(2,1)S(1)} collective-permute-done((bf16[128,512]{1,0:T(8,128)(2,1)S(1)}, bf16[128,512]{1,0:T(8,128)(2,1)S(1)}, u32[]{:S(2)}, u32[]{:S(2)}) %collective-permute-start.3) | collective-permute-done | bytes 131104 | tf_op jit(solution)/shard_map/ppermute | solution.py:231
  19.4 1.6 %collective-permute-start.4 = (bf16[128,512]{1,0:T(8,128)(2,1)S(1)}, bf16[128,512]{1,0:T(8,128)(2,1)S(1)}, u32[]{:S(2)}, u32[]{:S(2)}) collective-permute-start(bf16[128,512]{1,0:T(8,128)(2,1)S(1)} %get-tuple-element.34), channel_id=1, source_target_pairs={{0,3},{1,0},{2,1},{3,2},{4,7},{5,4},{6,5},{7,6},{8,11},{9,8},{10,9... | collective-permute-start | bytes 393224 | tf_op jit(solution)/shard_map/ppermute | solution.py:231
  22.0 3.3 %collective-permute-start.15 = (bf16[128,512]{1,0:T(8,128)(2,1)S(1)}, bf16[128,512]{1,0:T(8,128)(2,1)S(1)}, u32[]{:S(2)}, u32[]{:S(2)}) collective-permute-start(bf16[128,512]{1,0:T(8,128)(2,1)S(1)} %get-tuple-element.47), channel_id=1, source_target_pairs={{0,3},{1,0},{2,1},{3,2},{4,7},{5,4},{6,5},{7,6},{8,11},{9,8},{10,9... | collective-permute-start | bytes 393224 | tf_op jit(solution)/shard_map/ppermute | solution.py:231
  25.3 1.2 %collective-permute-done.4.refs_4_ = bf16[128,512]{1,0:T(8,128)(2,1)S(1)} collective-permute-done((bf16[128,512]{1,0:T(8,128)(2,1)S(1)}, bf16[128,512]{1,0:T(8,128)(2,1)S(1)}, u32[]{:S(2)}, u32[]{:S(2)}) %collective-permute-start.4) | collective-permute-done | bytes 131104 | tf_op jit(solution)/shard_map/ppermute | solution.py:231
  26.5 1.5 %collective-permute-start.10 = (bf16[512,768]{1,0:T(8,128)(2,1)S(1)}, bf16[512,768]{1,0:T(8,128)(2,1)S(1)}, u32[]{:S(2)}, u32[]{:S(2)}) collective-permute-start(bf16[512,768]{1,0:T(8,128)(2,1)S(1)} %bitcast.4), channel_id=1, source_target_pairs={{0,16},{4,20},{8,24},{12,28},{16,0},{20,4},{24,8},{28,12},{1,17},{... | collective-permute-start | bytes 2359304 | tf_op jit(solution)/shard_map/ppermute | solution.py:228
  28.5 1.0 %collective-permute-start.5 = (bf16[512,768]{1,0:T(8,128)(2,1)S(1)}, bf16[512,768]{1,0:T(8,128)(2,1)S(1)}, u32[]{:S(2)}, u32[]{:S(2)}) collective-permute-start(bf16[512,768]{1,0:T(8,128)(2,1)S(1)} %bitcast.5), channel_id=1, source_target_pairs={{0,8},{4,12},{8,0},{12,4},{16,24},{20,28},{24,16},{28,20},{1,9},{5... | collective-permute-start | bytes 2359304 | tf_op jit(solution)/shard_map/ppermute | solution.py:228
  30.2 2.5 %collective-permute-done.14.refs_1_.refs_8_ = bf16[128,512]{1,0:T(8,128)(2,1)S(1)} collective-permute-done((bf16[128,512]{1,0:T(8,128)(2,1)S(1)}, bf16[128,512]{1,0:T(8,128)(2,1)S(1)}, u32[]{:S(2)}, u32[]{:S(2)}) %collective-permute-start.14) | collective-permute-done | bytes 131104 | tf_op jit(solution)/shard_map/ppermute | solution.py:231
  32.7 1.2 %collective-permute-start.8 = (bf16[256,512]{1,0:T(8,128)(2,1)S(1)}, bf16[256,512]{1,0:T(8,128)(2,1)S(1)}, u32[]{:S(2)}, u32[]{:S(2)}) collective-permute-start(bf16[256,512]{1,0:T(8,128)(2,1)S(1)} %get-tuple-element.40), channel_id=1, source_target_pairs={{0,2},{1,3},{2,0},{3,1},{4,6},{5,7},{6,4},{7,5},{8,10},{9,11},{10,... | collective-permute-start | bytes 786440 | tf_op jit(solution)/shard_map/ppermute | solution.py:231
  33.9 4.5 %collective-permute-done.15.refs_2_.refs_9_ = bf16[128,512]{1,0:T(8,128)(2,1)S(1)} collective-permute-done((bf16[128,512]{1,0:T(8,128)(2,1)S(1)}, bf16[128,512]{1,0:T(8,128)(2,1)S(1)}, u32[]{:S(2)}, u32[]{:S(2)}) %collective-permute-start.15) | collective-permute-done | bytes 131104 | tf_op jit(solution)/shard_map/ppermute | solution.py:231
  38.5 6.8 %collective-permute-done.10.refs_5_ = bf16[512,768]{1,0:T(8,128)(2,1)S(1)} collective-permute-done((bf16[512,768]{1,0:T(8,128)(2,1)S(1)}, bf16[512,768]{1,0:T(8,128)(2,1)S(1)}, u32[]{:S(2)}, u32[]{:S(2)}) %collective-permute-start.10) | collective-permute-done | bytes 786464 | tf_op jit(solution)/shard_map/ppermute | solution.py:228
  45.3 1.7 %collective-permute-done.5.refs_0_ = bf16[512,768]{1,0:T(8,128)(2,1)S(1)} collective-permute-done((bf16[512,768]{1,0:T(8,128)(2,1)S(1)}, bf16[512,768]{1,0:T(8,128)(2,1)S(1)}, u32[]{:S(2)}, u32[]{:S(2)}) %collective-permute-start.5) | collective-permute-done | bytes 786464 | tf_op jit(solution)/shard_map/ppermute | solution.py:228
  49.5 2.9 %collective-permute-done.8.refs_1_.refs_3_ = bf16[256,512]{1,0:T(8,128)(2,1)S(1)} collective-permute-done((bf16[256,512]{1,0:T(8,128)(2,1)S(1)}, bf16[256,512]{1,0:T(8,128)(2,1)S(1)}, u32[]{:S(2)}, u32[]{:S(2)}) %collective-permute-start.8) | collective-permute-done | bytes 262176 | tf_op jit(solution)/shard_map/ppermute | solution.py:231
  52.4 5.5 %collective-permute-done.9.refs_2_.refs_4_ = bf16[256,512]{1,0:T(8,128)(2,1)S(1)} collective-permute-done((bf16[256,512]{1,0:T(8,128)(2,1)S(1)}, bf16[256,512]{1,0:T(8,128)(2,1)S(1)}, u32[]{:S(2)}, u32[]{:S(2)}) %collective-permute-start.9) | collective-permute-done | bytes 262176 | tf_op jit(solution)/shard_map/ppermute | solution.py:231
  60.8 1.2 %update.1 = (f32[256,768]{1,0:T(8,128)S(1)}, f32[256,768]{1,0:T(8,128)S(1)}, f32[8,128]{1,0:T(8,128)S(1)}) custom-call(f32[256,768]{1,0:T(8,128)S(1)} %product.9.mine_ref, f32[256,384]{1,0:T(8,128)S(1)} %collective-permute-done.16.left_ref, f32[256,384]{1,0:T(8,128)S(1)} %collective-permute-done.17.right_ref, f32[1,256,768]{2,1,0:T(8,128)S(1)} %copy-done.2, ...), custom_call_target="tpu_custom_call" | custom-call | bytes 5509120 | tf_op jit(solution)/shard_map/update/pallas_call | solution.py:185
  63.3 2.4 %collective-permute-start.21 = (f32[8,128]{1,0:T(8,128)S(1)}, f32[8,128]{1,0:T(8,128)S(1)}, u32[]{:S(2)}, u32[]{:S(2)}) collective-permute-start(f32[8,128]{1,0:T(8,128)S(1)} %add.3.refs_0_), channel_id=1, source_target_pairs={{0,24},{4,28},{8,16},{12,20},{16,8},{20,12},{24,0},{28,4},{1,25},{... | collective-permute-start | bytes 12296 | tf_op jit(solution)/shard_map/ppermute | solution.py:228
  66.8 1.4 %moment.1 = (f32[1,256,768]{2,1,0:T(8,128)}, f32[1,256,768]{2,1,0:T(8,128)}) custom-call(f32[256,768]{1,0:T(8,128)S(1)} %get-tuple-element.52.grad_ref, f32[1,256,768]{2,1,0:T(8,128)S(1)} %copy-done, f32[1,256,768]{2,1,0:T(8,128)S(1)} %copy-done.1), custom_call_target="tpu_custom_call" | custom-call | bytes 3932160 | tf_op jit(solution)/shard_map/moment/pallas_call | solution.py:185
  68.2 1.2 %collective-permute-done.20.refs_2_ = f32[8,128]{1,0:T(8,128)S(1)} collective-permute-done((f32[8,128]{1,0:T(8,128)S(1)}, f32[8,128]{1,0:T(8,128)S(1)}, u32[]{:S(2)}, u32[]{:S(2)}) %collective-permute-start.20) | collective-permute-done | bytes 4128 | tf_op jit(solution)/shard_map/ppermute | solution.py:228
  69.9 1.0 %weight.1 = f32[1,256,768]{2,1,0:T(8,128)} custom-call(f32[8,128]{1,0:T(8,128)S(1)} %add.3.refs_0_, f32[8,128]{1,0:T(8,128)S(1)} %collective-permute-done.19.refs_1_, f32[8,128]{1,0:T(8,128)S(1)} %collective-permute-done.20.refs_2_, f32[8,128]{1,0:T(8,128)S(1)} %collective-permute-done.21.refs_3_, f32[1,256,768]{2,1,0:T(8,128)S(1)} %copy-done.2, ...), custom_call_target="tpu_custom_call" | custom-call | bytes 2375680 | tf_op jit(solution)/shard_map/weight/pallas_call | solution.py:185
  (44 shorter events, 10.7 us)
Async XLA Ops:
  2.3 16.7 %collective-permute-start = (bf16[272,512]{1,0:T(8,128)(2,1)S(1)}, bf16[272,512]{1,0:T(8,128)(2,1)S(1)}, u32[]{:S(2)}, u32[]{:S(2)}) collective-permute-start(bf16[272,512]{1,0:T(8,128)(2,1)S(1)} %get-tuple-element.29), channel_id=1, source_target_pairs={{0,8},{4,12},{8,0},{12,4},{16,24},{20,28},{24,16},{28,20},{1,9},{5... | collective-permute-start | bytes 835592 | tf_op jit(solution)/shard_map/ppermute | solution.py:228
  5.3 13.7 %collective-permute-start.1 = (bf16[272,512]{1,0:T(8,128)(2,1)S(1)}, bf16[272,512]{1,0:T(8,128)(2,1)S(1)}, u32[]{:S(2)}, u32[]{:S(2)}) collective-permute-start(bf16[272,512]{1,0:T(8,128)(2,1)S(1)} %get-tuple-element.30), channel_id=1, source_target_pairs={{0,16},{4,20},{8,24},{12,28},{16,0},{20,4},{24,8},{28,12},{1,17},{... | collective-permute-start | bytes 835592 | tf_op jit(solution)/shard_map/ppermute | solution.py:228
  6.8 8.0 %collective-permute-start.2 = (bf16[128,512]{1,0:T(8,128)(2,1)S(1)}, bf16[128,512]{1,0:T(8,128)(2,1)S(1)}, u32[]{:S(2)}, u32[]{:S(2)}) collective-permute-start(bf16[128,512]{1,0:T(8,128)(2,1)S(1)} %get-tuple-element.32), channel_id=1, source_target_pairs={{0,1},{1,2},{2,3},{3,0},{4,5},{5,6},{6,7},{7,4},{8,9},{9,10},{10,1... | collective-permute-start | bytes 393224 | tf_op jit(solution)/shard_map/ppermute | solution.py:231
  8.4 10.6 %collective-permute-start.3 = (bf16[128,512]{1,0:T(8,128)(2,1)S(1)}, bf16[128,512]{1,0:T(8,128)(2,1)S(1)}, u32[]{:S(2)}, u32[]{:S(2)}) collective-permute-start(bf16[128,512]{1,0:T(8,128)(2,1)S(1)} %get-tuple-element.33), channel_id=1, source_target_pairs={{0,2},{1,3},{2,0},{3,1},{4,6},{5,7},{6,4},{7,5},{8,10},{9,11},{10,... | collective-permute-start | bytes 393224 | tf_op jit(solution)/shard_map/ppermute | solution.py:231
  19.0 9.6 %collective-permute-start.6 = (bf16[272,512]{1,0:T(8,128)(2,1)S(1)}, bf16[272,512]{1,0:T(8,128)(2,1)S(1)}, u32[]{:S(2)}, u32[]{:S(2)}) collective-permute-start(bf16[272,512]{1,0:T(8,128)(2,1)S(1)} %get-tuple-element.37), channel_id=1, source_target_pairs={{0,24},{4,28},{8,16},{12,20},{16,8},{20,12},{24,0},{28,4},{1,25},{... | collective-permute-start | bytes 835592 | tf_op jit(solution)/shard_map/ppermute | solution.py:228
  19.4 7.1 %collective-permute-start.4 = (bf16[128,512]{1,0:T(8,128)(2,1)S(1)}, bf16[128,512]{1,0:T(8,128)(2,1)S(1)}, u32[]{:S(2)}, u32[]{:S(2)}) collective-permute-start(bf16[128,512]{1,0:T(8,128)(2,1)S(1)} %get-tuple-element.34), channel_id=1, source_target_pairs={{0,3},{1,0},{2,1},{3,2},{4,7},{5,4},{6,5},{7,6},{8,11},{9,8},{10,9... | collective-permute-start | bytes 393224 | tf_op jit(solution)/shard_map/ppermute | solution.py:231
  21.4 8.6 %collective-permute-start.13 = (bf16[128,512]{1,0:T(8,128)(2,1)S(1)}, bf16[128,512]{1,0:T(8,128)(2,1)S(1)}, u32[]{:S(2)}, u32[]{:S(2)}) collective-permute-start(bf16[128,512]{1,0:T(8,128)(2,1)S(1)} %get-tuple-element.45), channel_id=1, source_target_pairs={{0,1},{1,2},{2,3},{3,0},{4,5},{5,6},{6,7},{7,4},{8,9},{9,10},{10,1... | collective-permute-start | bytes 393224 | tf_op jit(solution)/shard_map/ppermute | solution.py:231
  21.8 10.8 %collective-permute-start.14 = (bf16[128,512]{1,0:T(8,128)(2,1)S(1)}, bf16[128,512]{1,0:T(8,128)(2,1)S(1)}, u32[]{:S(2)}, u32[]{:S(2)}) collective-permute-start(bf16[128,512]{1,0:T(8,128)(2,1)S(1)} %get-tuple-element.46), channel_id=1, source_target_pairs={{0,2},{1,3},{2,0},{3,1},{4,6},{5,7},{6,4},{7,5},{8,10},{9,11},{10,... | collective-permute-start | bytes 393224 | tf_op jit(solution)/shard_map/ppermute | solution.py:231
  22.0 16.4 %collective-permute-start.15 = (bf16[128,512]{1,0:T(8,128)(2,1)S(1)}, bf16[128,512]{1,0:T(8,128)(2,1)S(1)}, u32[]{:S(2)}, u32[]{:S(2)}) collective-permute-start(bf16[128,512]{1,0:T(8,128)(2,1)S(1)} %get-tuple-element.47), channel_id=1, source_target_pairs={{0,3},{1,0},{2,1},{3,2},{4,7},{5,4},{6,5},{7,6},{8,11},{9,8},{10,9... | collective-permute-start | bytes 393224 | tf_op jit(solution)/shard_map/ppermute | solution.py:231
  26.5 18.8 %collective-permute-start.10 = (bf16[512,768]{1,0:T(8,128)(2,1)S(1)}, bf16[512,768]{1,0:T(8,128)(2,1)S(1)}, u32[]{:S(2)}, u32[]{:S(2)}) collective-permute-start(bf16[512,768]{1,0:T(8,128)(2,1)S(1)} %bitcast.4), channel_id=1, source_target_pairs={{0,16},{4,20},{8,24},{12,28},{16,0},{20,4},{24,8},{28,12},{1,17},{... | collective-permute-start | bytes 2359304 | tf_op jit(solution)/shard_map/ppermute | solution.py:228
  28.5 18.5 %collective-permute-start.5 = (bf16[512,768]{1,0:T(8,128)(2,1)S(1)}, bf16[512,768]{1,0:T(8,128)(2,1)S(1)}, u32[]{:S(2)}, u32[]{:S(2)}) collective-permute-start(bf16[512,768]{1,0:T(8,128)(2,1)S(1)} %bitcast.5), channel_id=1, source_target_pairs={{0,8},{4,12},{8,0},{12,4},{16,24},{20,28},{24,16},{28,20},{1,9},{5... | collective-permute-start | bytes 2359304 | tf_op jit(solution)/shard_map/ppermute | solution.py:228
  30.0 19.4 %collective-permute-start.7 = (bf16[256,512]{1,0:T(8,128)(2,1)S(1)}, bf16[256,512]{1,0:T(8,128)(2,1)S(1)}, u32[]{:S(2)}, u32[]{:S(2)}) collective-permute-start(bf16[256,512]{1,0:T(8,128)(2,1)S(1)} %get-tuple-element.39), channel_id=1, source_target_pairs={{0,1},{1,2},{2,3},{3,0},{4,5},{5,6},{6,7},{7,4},{8,9},{9,10},{10,1... | collective-permute-start | bytes 786440 | tf_op jit(solution)/shard_map/ppermute | solution.py:231
  32.7 19.7 %collective-permute-start.8 = (bf16[256,512]{1,0:T(8,128)(2,1)S(1)}, bf16[256,512]{1,0:T(8,128)(2,1)S(1)}, u32[]{:S(2)}, u32[]{:S(2)}) collective-permute-start(bf16[256,512]{1,0:T(8,128)(2,1)S(1)} %get-tuple-element.40), channel_id=1, source_target_pairs={{0,2},{1,3},{2,0},{3,1},{4,6},{5,7},{6,4},{7,5},{8,10},{9,11},{10,... | collective-permute-start | bytes 786440 | tf_op jit(solution)/shard_map/ppermute | solution.py:231
  38.4 19.4 %collective-permute-start.9 = (bf16[256,512]{1,0:T(8,128)(2,1)S(1)}, bf16[256,512]{1,0:T(8,128)(2,1)S(1)}, u32[]{:S(2)}, u32[]{:S(2)}) collective-permute-start(bf16[256,512]{1,0:T(8,128)(2,1)S(1)} %get-tuple-element.41), channel_id=1, source_target_pairs={{0,3},{1,0},{2,1},{3,2},{4,7},{5,4},{6,5},{7,6},{8,11},{9,8},{10,9... | collective-permute-start | bytes 786440 | tf_op jit(solution)/shard_map/ppermute | solution.py:231
  47.1 10.8 %collective-permute-start.11 = (bf16[512,384]{1,0:T(8,128)(2,1)S(1)}, bf16[512,384]{1,0:T(8,128)(2,1)S(1)}, u32[]{:S(2)}, u32[]{:S(2)}) collective-permute-start(bf16[512,384]{1,0:T(8,128)(2,1)S(1)} %slice.8), channel_id=1, source_target_pairs={{0,16},{4,20},{8,24},{12,28},{16,0},{20,4},{24,8},{28,12},{1,17},{... | collective-permute-start | bytes 1179656 | tf_op jit(solution)/shard_map/ppermute | solution.py:228
  47.7 10.2 %collective-permute-start.12 = (bf16[512,384]{1,0:T(8,128)(2,1)S(1)}, bf16[512,384]{1,0:T(8,128)(2,1)S(1)}, u32[]{:S(2)}, u32[]{:S(2)}) collective-permute-start(bf16[512,384]{1,0:T(8,128)(2,1)S(1)} %slice.9), channel_id=1, source_target_pairs={{0,8},{4,12},{8,0},{12,4},{16,24},{20,28},{24,16},{28,20},{1,9},{5... | collective-permute-start | bytes 1179656 | tf_op jit(solution)/shard_map/ppermute | solution.py:228
  49.4 8.5 %copy-start = (f32[1,256,768]{2,1,0:T(8,128)S(1)}, f32[1,256,768]{2,1,0:T(8,128)}, u32[]{:S(2)}) copy-start(f32[1,256,768]{2,1,0:T(8,128)} %first_ref.3) | copy-start | bytes 2359300
  49.4 8.5 %copy-start.1 = (f32[1,256,768]{2,1,0:T(8,128)S(1)}, f32[1,256,768]{2,1,0:T(8,128)}, u32[]{:S(2)}) copy-start(f32[1,256,768]{2,1,0:T(8,128)} %second_ref.3) | copy-start | bytes 2359300
  58.4 1.9 %collective-permute-start.16 = (f32[256,384]{1,0:T(8,128)S(1)}, f32[256,384]{1,0:T(8,128)S(1)}, u32[]{:S(2)}, u32[]{:S(2)}) collective-permute-start(f32[256,384]{1,0:T(8,128)S(1)} %product.7), channel_id=1, source_target_pairs={{0,4},{4,0},{8,12},{12,8},{16,20},{20,16},{24,28},{28,24},{1,5},{5... | collective-permute-start | bytes 1179656 | tf_op jit(solution)/shard_map/ppermute | solution.py:228
  59.0 1.9 %collective-permute-start.17 = (f32[256,384]{1,0:T(8,128)S(1)}, f32[256,384]{1,0:T(8,128)S(1)}, u32[]{:S(2)}, u32[]{:S(2)}) collective-permute-start(f32[256,384]{1,0:T(8,128)S(1)} %product.8), channel_id=1, source_target_pairs={{0,4},{4,0},{8,12},{12,8},{16,20},{20,16},{24,28},{28,24},{1,5},{5... | collective-permute-start | bytes 1179656 | tf_op jit(solution)/shard_map/ppermute | solution.py:228
  62.1 1.3 %collective-permute-start.18 = (f32[8,128]{1,0:T(8,128)S(1)}, f32[8,128]{1,0:T(8,128)S(1)}, u32[]{:S(2)}, u32[]{:S(2)}) collective-permute-start(f32[8,128]{1,0:T(8,128)S(1)} %get-tuple-element.49), channel_id=1, source_target_pairs={{0,4},{4,0},{8,12},{12,8},{16,20},{20,16},{24,28},{28,24},{1,5},{5... | collective-permute-start | bytes 12296 | tf_op jit(solution)/shard_map/ppermute | solution.py:228
  63.3 4.9 %collective-permute-start.21 = (f32[8,128]{1,0:T(8,128)S(1)}, f32[8,128]{1,0:T(8,128)S(1)}, u32[]{:S(2)}, u32[]{:S(2)}) collective-permute-start(f32[8,128]{1,0:T(8,128)S(1)} %add.3.refs_0_), channel_id=1, source_target_pairs={{0,24},{4,28},{8,16},{12,20},{16,8},{20,12},{24,0},{28,4},{1,25},{... | collective-permute-start | bytes 12296 | tf_op jit(solution)/shard_map/ppermute | solution.py:228
  65.8 3.6 %collective-permute-start.20 = (f32[8,128]{1,0:T(8,128)S(1)}, f32[8,128]{1,0:T(8,128)S(1)}, u32[]{:S(2)}, u32[]{:S(2)}) collective-permute-start(f32[8,128]{1,0:T(8,128)S(1)} %add.3.refs_0_), channel_id=1, source_target_pairs={{0,16},{4,20},{8,24},{12,28},{16,0},{20,4},{24,8},{28,12},{1,17},{... | collective-permute-start | bytes 12296 | tf_op jit(solution)/shard_map/ppermute | solution.py:228
  66.3 3.6 %collective-permute-start.19 = (f32[8,128]{1,0:T(8,128)S(1)}, f32[8,128]{1,0:T(8,128)S(1)}, u32[]{:S(2)}, u32[]{:S(2)}) collective-permute-start(f32[8,128]{1,0:T(8,128)S(1)} %add.3.refs_0_), channel_id=1, source_target_pairs={{0,8},{4,12},{8,0},{12,4},{16,24},{20,28},{24,16},{28,20},{1,9},{5... | collective-permute-start | bytes 12296 | tf_op jit(solution)/shard_map/ppermute | solution.py:228
  (2 other events, 15.5 us)

commit v6 on v5

--- a/solution.py
+++ b/solution.py
@@ -106,7 +106,7 @@
 
 def pack_kernel(owners, capacity, n_blocks, *refs):
     z = lax.axis_index("expert")
-    blocks, outs = refs[:n_blocks], refs[n_blocks:]
+    blocks, outs = refs[:n_blocks], refs[-owners:]
     tokens = blocks[0].shape[0] - TAIL
     for at, block in enumerate(blocks):
         ids = block[tokens:, :tokens].astype(jnp.float32)
@@ -230,12 +230,14 @@
     def along(array, shift):
         return lax.ppermute(array, "expert", [(d, (d + shift) % owners) for d in range(owners)])
 
-    def pack(*blocks):
+    def pack(*blocks, waits=()):
         size = len(blocks) * capacity
         return call(
             functools.partial(pack_kernel, owners, capacity, len(blocks)),
             [jax.ShapeDtypeStruct((size, part), bf16)] * owners,
             *blocks,
+            *waits,
+            spaces=[VMEM] * len(blocks) + [ANY] * len(waits),
             flops=4 * 2 * size * owners * tokens * part,
             name="pack",
         )
@@ -281,12 +283,14 @@
     near, (to_x, to_y, to_xy) = cut[:owners], cut[owners:]
     from_x, from_y = across(to_x, 2), across(to_y, 4)
     near = [near[0]] + [along(near[shift], shift) for shift in range(1, owners)]
-    mid = pack(from_y)
+    seen = tick(near[2], flops=2*10**9)
+    mid = pack(from_y, waits=[seen])
     mid = [mid[0], along(mid[1], 1), along(mid[2], 2), along(mid[3], 3)]
-    from_xy = across(after(to_xy, from_x, from_y, near[1], near[2]), 6)
-    by_x = across(after(hidden, from_x, from_y, *near), 2)
-    by_y = across(after(hidden, from_x, from_y, *near), 4)
-    far = pack(from_x, from_xy)
+    late = tick(near[1], near[3], flops=2*10**9)
+    from_xy = across(after(to_xy, from_x, from_y, seen), 6)
+    by_x = across(after(hidden, from_x, from_y, near[2], late), 2)
+    by_y = across(after(hidden, from_x, from_y, near[2], late), 4)
+    far = pack(from_x, from_xy, waits=[late])
     far = [far[0]] + [along(far[shift], shift) for shift in range(1, owners)]
     left, right = after((by_x[:, : ff // 2], by_y[:, ff // 2 :]), by_x, by_y)
     by_xy = across(left, 4), across(right, 2)

time: 71 us -> 66.9 us (0.942)
  waiting for transfers between devices: 36.8 us -> 28.6 us
  starting transfers between devices: 24.3 us -> 28.1 us
    ppermute x13, waiting for transfers between devices: 12.2 us -> 3.99 us  [across(): return lax.ppermute(array, 'dp', [(d, d ^ mask) for d in range(n_dp)])]
    ppermute x13, starting transfers between devices: 13.2 us -> 15.6 us  [across(): return lax.ppermute(array, 'dp', [(d, d ^ mask) for d in range(n_dp)])]
    ppermute x9, starting transfers between devices: 11.1 us -> 12.5 us  [along(): lax.ppermute(array, 'expert', [(d, (d + shift) % owners) for d in range(o...]
    pallas_call x13 -> x15, Pallas kernels: 8.85 us -> 8.86 us  [call(): pl.pallas_call(kernel, out_shape=out_shape, in_specs=spaces if isinstance...]
  transfers between devices with their start and end apart: 22 -> 22, of which waited for: 14 -> 9; matrix products, arithmetic and copies ran while one was open for 0% -> 0% of each run, Pallas kernels for 6% -> 7%
where the time goes in v6:
time: 66.9 us; the launch traced here: 66.7 us
  waiting for transfers between devices  28.6 us (43%)
  starting transfers between devices  28.1 us (42%)
  Pallas kernels  8.86 us (13%)
  between operations  0.84 us (1%)
    ppermute x9, waiting for transfers between devices, along(): lax.ppermute(array, 'expert', [(d, (d + shift) % owners) for d in range(o...  24.6 us
    ppermute x13, starting transfers between devices, across(): return lax.ppermute(array, 'dp', [(d, d ^ mask) for d in range(n_dp)])  15.6 us
    ppermute x9, starting transfers between devices, along(): lax.ppermute(array, 'expert', [(d, (d + shift) % owners) for d in range(o...  12.5 us
    pallas_call x15, Pallas kernels, call(): pl.pallas_call(kernel, out_shape=out_shape, in_specs=spaces if isinstance...  8.86 us
    ppermute x13, waiting for transfers between devices, across(): return lax.ppermute(array, 'dp', [(d, d ^ mask) for d in range(n_dp)])  3.99 us
  transfers between devices with their start and end apart: 22, of which 9 were waited for; matrix products, arithmetic and copies ran while one was open for 0% of the time, Pallas kernels for 7%

profile of v6, /device:TPU:0, one launch (start us, length us, event | category | flops | bytes accessed | tf_op | source)
XLA Modules:
  0.0 66.7 jit_solution(214884256709536069)
XLA Ops:
  0.6 1.6 %cut.1 = (bf16[128,512]{1,0:T(8,128)(2,1)S(1)}, bf16[128,512]{1,0:T(8,128)(2,1)S(1)}, bf16[128,512]{1,0:T(8,128)(2,1)S(1)}, bf16[128,512]{1,0:T(8,128)(2,1)S(1)}...) custom-call(bf16[256,2048]{1,0:T(8,128)(2,1)} %cot_ref.1, ...), custom_call_target="tpu_custom_call" | custom-call | bytes 2411520 | tf_op jit(solution)/shard_map/cut/pallas_call | solution.py:185
  2.3 4.1 %collective-permute-start.2 = (bf16[128,512]{1,0:T(8,128)(2,1)S(1)}, bf16[128,512]{1,0:T(8,128)(2,1)S(1)}, u32[]{:S(2)}, u32[]{:S(2)}) collective-permute-start(bf16[128,512]{1,0:T(8,128)(2,1)S(1)} %get-tuple-element.31), channel_id=1, source_target_pairs={{0,2},{1,3},{2,0},{3,1},{4,6},{5,7},{6,4},{7,5},{8,10},{9,11},{10,... | collective-permute-start | bytes 393224 | tf_op jit(solution)/shard_map/ppermute | solution.py:231
  6.4 1.5 %collective-permute-start = (bf16[272,512]{1,0:T(8,128)(2,1)S(1)}, bf16[272,512]{1,0:T(8,128)(2,1)S(1)}, u32[]{:S(2)}, u32[]{:S(2)}) collective-permute-start(bf16[272,512]{1,0:T(8,128)(2,1)S(1)} %get-tuple-element.29), channel_id=1, source_target_pairs={{0,8},{4,12},{8,0},{12,4},{16,24},{20,28},{24,16},{28,20},{1,9},{5... | collective-permute-start | bytes 835592 | tf_op jit(solution)/shard_map/ppermute | solution.py:228
  7.9 1.5 %collective-permute-start.1 = (bf16[272,512]{1,0:T(8,128)(2,1)S(1)}, bf16[272,512]{1,0:T(8,128)(2,1)S(1)}, u32[]{:S(2)}, u32[]{:S(2)}) collective-permute-start(bf16[272,512]{1,0:T(8,128)(2,1)S(1)} %get-tuple-element.30), channel_id=1, source_target_pairs={{0,16},{4,20},{8,24},{12,28},{16,0},{20,4},{24,8},{28,12},{1,17},{... | collective-permute-start | bytes 835592 | tf_op jit(solution)/shard_map/ppermute | solution.py:228
  9.4 1.6 %collective-permute-start.3 = (bf16[128,512]{1,0:T(8,128)(2,1)S(1)}, bf16[128,512]{1,0:T(8,128)(2,1)S(1)}, u32[]{:S(2)}, u32[]{:S(2)}) collective-permute-start(bf16[128,512]{1,0:T(8,128)(2,1)S(1)} %get-tuple-element.32), channel_id=1, source_target_pairs={{0,1},{1,2},{2,3},{3,0},{4,5},{5,6},{6,7},{7,4},{8,9},{9,10},{10,1... | collective-permute-start | bytes 393224 | tf_op jit(solution)/shard_map/ppermute | solution.py:231
  11.0 2.2 %collective-permute-start.4 = (bf16[128,512]{1,0:T(8,128)(2,1)S(1)}, bf16[128,512]{1,0:T(8,128)(2,1)S(1)}, u32[]{:S(2)}, u32[]{:S(2)}) collective-permute-start(bf16[128,512]{1,0:T(8,128)(2,1)S(1)} %get-tuple-element.33), channel_id=1, source_target_pairs={{0,3},{1,0},{2,1},{3,2},{4,7},{5,4},{6,5},{7,6},{8,11},{9,8},{10,9... | collective-permute-start | bytes 393224 | tf_op jit(solution)/shard_map/ppermute | solution.py:231
  13.2 1.5 %collective-permute-done.2.refs_0_.refs_3_ = bf16[128,512]{1,0:T(8,128)(2,1)S(1)} collective-permute-done((bf16[128,512]{1,0:T(8,128)(2,1)S(1)}, bf16[128,512]{1,0:T(8,128)(2,1)S(1)}, u32[]{:S(2)}, u32[]{:S(2)}) %collective-permute-start.2) | collective-permute-done | bytes 131104 | tf_op jit(solution)/shard_map/ppermute | solution.py:231
  14.7 1.0 %collective-permute-done.1.refs_0_ = bf16[272,512]{1,0:T(8,128)(2,1)S(1)} collective-permute-done((bf16[272,512]{1,0:T(8,128)(2,1)S(1)}, bf16[272,512]{1,0:T(8,128)(2,1)S(1)}, u32[]{:S(2)}, u32[]{:S(2)}) %collective-permute-start.1) | collective-permute-done | bytes 278560 | tf_op jit(solution)/shard_map/ppermute | solution.py:228
  15.7 3.5 %collective-permute-start.6 = (bf16[272,512]{1,0:T(8,128)(2,1)S(1)}, bf16[272,512]{1,0:T(8,128)(2,1)S(1)}, u32[]{:S(2)}, u32[]{:S(2)}) collective-permute-start(bf16[272,512]{1,0:T(8,128)(2,1)S(1)} %get-tuple-element.36), channel_id=1, source_target_pairs={{0,24},{4,28},{8,16},{12,20},{16,8},{20,12},{24,0},{28,4},{1,25},{... | collective-permute-start | bytes 835592 | tf_op jit(solution)/shard_map/ppermute | solution.py:228
  19.6 3.0 %collective-permute-start.14 = (bf16[128,512]{1,0:T(8,128)(2,1)S(1)}, bf16[128,512]{1,0:T(8,128)(2,1)S(1)}, u32[]{:S(2)}, u32[]{:S(2)}) collective-permute-start(bf16[128,512]{1,0:T(8,128)(2,1)S(1)} %get-tuple-element.46), channel_id=1, source_target_pairs={{0,2},{1,3},{2,0},{3,1},{4,6},{5,7},{6,4},{7,5},{8,10},{9,11},{10,... | collective-permute-start | bytes 393224 | tf_op jit(solution)/shard_map/ppermute | solution.py:231
  22.6 0.9 %collective-permute-start.15 = (bf16[128,512]{1,0:T(8,128)(2,1)S(1)}, bf16[128,512]{1,0:T(8,128)(2,1)S(1)}, u32[]{:S(2)}, u32[]{:S(2)}) collective-permute-start(bf16[128,512]{1,0:T(8,128)(2,1)S(1)} %get-tuple-element.47), channel_id=1, source_target_pairs={{0,3},{1,0},{2,1},{3,2},{4,7},{5,4},{6,5},{7,6},{8,11},{9,8},{10,9... | collective-permute-start | bytes 393224 | tf_op jit(solution)/shard_map/ppermute | solution.py:231
  24.8 1.3 %collective-permute-start.5 = (bf16[512,768]{1,0:T(8,128)(2,1)S(1)}, bf16[512,768]{1,0:T(8,128)(2,1)S(1)}, u32[]{:S(2)}, u32[]{:S(2)}) collective-permute-start(bf16[512,768]{1,0:T(8,128)(2,1)S(1)} %bitcast.5), channel_id=1, source_target_pairs={{0,8},{4,12},{8,0},{12,4},{16,24},{20,28},{24,16},{28,20},{1,9},{5... | collective-permute-start | bytes 2359304 | tf_op jit(solution)/shard_map/ppermute | solution.py:228
  27.2 14.0 %collective-permute-done.14.refs_1_.refs_8_ = bf16[128,512]{1,0:T(8,128)(2,1)S(1)} collective-permute-done((bf16[128,512]{1,0:T(8,128)(2,1)S(1)}, bf16[128,512]{1,0:T(8,128)(2,1)S(1)}, u32[]{:S(2)}, u32[]{:S(2)}) %collective-permute-start.14) | collective-permute-done | bytes 131104 | tf_op jit(solution)/shard_map/ppermute | solution.py:231
  41.3 1.4 %collective-permute-start.11 = (bf16[512,384]{1,0:T(8,128)(2,1)S(1)}, bf16[512,384]{1,0:T(8,128)(2,1)S(1)}, u32[]{:S(2)}, u32[]{:S(2)}) collective-permute-start(bf16[512,384]{1,0:T(8,128)(2,1)S(1)} %slice.8), channel_id=1, source_target_pairs={{0,16},{4,20},{8,24},{12,28},{16,0},{20,4},{24,8},{28,12},{1,17},{... | collective-permute-start | bytes 1179656 | tf_op jit(solution)/shard_map/ppermute | solution.py:228
  42.7 1.5 %collective-permute-start.12 = (bf16[512,384]{1,0:T(8,128)(2,1)S(1)}, bf16[512,384]{1,0:T(8,128)(2,1)S(1)}, u32[]{:S(2)}, u32[]{:S(2)}) collective-permute-start(bf16[512,384]{1,0:T(8,128)(2,1)S(1)} %slice.9), channel_id=1, source_target_pairs={{0,8},{4,12},{8,0},{12,4},{16,24},{20,28},{24,16},{28,20},{1,9},{5... | collective-permute-start | bytes 1179656 | tf_op jit(solution)/shard_map/ppermute | solution.py:228
  45.5 5.8 %collective-permute-done.8.refs_1_.refs_3_ = bf16[256,512]{1,0:T(8,128)(2,1)S(1)} collective-permute-done((bf16[256,512]{1,0:T(8,128)(2,1)S(1)}, bf16[256,512]{1,0:T(8,128)(2,1)S(1)}, u32[]{:S(2)}, u32[]{:S(2)}) %collective-permute-start.8) | collective-permute-done | bytes 262176 | tf_op jit(solution)/shard_map/ppermute | solution.py:231
  51.3 3.2 %collective-permute-done.9.refs_2_.refs_4_ = bf16[256,512]{1,0:T(8,128)(2,1)S(1)} collective-permute-done((bf16[256,512]{1,0:T(8,128)(2,1)S(1)}, bf16[256,512]{1,0:T(8,128)(2,1)S(1)}, u32[]{:S(2)}, u32[]{:S(2)}) %collective-permute-start.9) | collective-permute-done | bytes 262176 | tf_op jit(solution)/shard_map/ppermute | solution.py:231
  57.5 1.2 %update.1 = (f32[256,768]{1,0:T(8,128)S(1)}, f32[256,768]{1,0:T(8,128)S(1)}, f32[8,128]{1,0:T(8,128)S(1)}) custom-call(f32[256,768]{1,0:T(8,128)S(1)} %product.9.mine_ref, f32[256,384]{1,0:T(8,128)S(1)} %collective-permute-done.16.left_ref, f32[256,384]{1,0:T(8,128)S(1)} %collective-permute-done.17.right_ref, f32[1,256,768]{2,1,0:T(8,128)S(1)} %copy-done.2, ...), custom_call_target="tpu_custom_call" | custom-call | bytes 5509120 | tf_op jit(solution)/shard_map/update/pallas_call | solution.py:185
  59.2 0.8 %collective-permute-done.18 = f32[8,128]{1,0:T(8,128)S(1)} collective-permute-done((f32[8,128]{1,0:T(8,128)S(1)}, f32[8,128]{1,0:T(8,128)S(1)}, u32[]{:S(2)}, u32[]{:S(2)}) %collective-permute-start.18) | collective-permute-done | bytes 4128 | tf_op jit(solution)/shard_map/ppermute | solution.py:228
  60.6 1.5 %collective-permute-start.20 = (f32[8,128]{1,0:T(8,128)S(1)}, f32[8,128]{1,0:T(8,128)S(1)}, u32[]{:S(2)}, u32[]{:S(2)}) collective-permute-start(f32[8,128]{1,0:T(8,128)S(1)} %add.3.refs_0_), channel_id=1, source_target_pairs={{0,16},{4,20},{8,24},{12,28},{16,0},{20,4},{24,8},{28,12},{1,17},{... | collective-permute-start | bytes 12296 | tf_op jit(solution)/shard_map/ppermute | solution.py:228
  62.1 1.4 %collective-permute-start.19 = (f32[8,128]{1,0:T(8,128)S(1)}, f32[8,128]{1,0:T(8,128)S(1)}, u32[]{:S(2)}, u32[]{:S(2)}) collective-permute-start(f32[8,128]{1,0:T(8,128)S(1)} %add.3.refs_0_), channel_id=1, source_target_pairs={{0,8},{4,12},{8,0},{12,4},{16,24},{20,28},{24,16},{28,20},{1,9},{5... | collective-permute-start | bytes 12296 | tf_op jit(solution)/shard_map/ppermute | solution.py:228
  63.5 1.4 %moment.1 = (f32[1,256,768]{2,1,0:T(8,128)}, f32[1,256,768]{2,1,0:T(8,128)}) custom-call(f32[256,768]{1,0:T(8,128)S(1)} %get-tuple-element.52.grad_ref, f32[1,256,768]{2,1,0:T(8,128)S(1)} %copy-done, f32[1,256,768]{2,1,0:T(8,128)S(1)} %copy-done.1), custom_call_target="tpu_custom_call" | custom-call | bytes 3932160 | tf_op jit(solution)/shard_map/moment/pallas_call | solution.py:185
  64.9 0.8 %collective-permute-done.19.refs_1_ = f32[8,128]{1,0:T(8,128)S(1)} collective-permute-done((f32[8,128]{1,0:T(8,128)S(1)}, f32[8,128]{1,0:T(8,128)S(1)}, u32[]{:S(2)}, u32[]{:S(2)}) %collective-permute-start.19) | collective-permute-done | bytes 4128 | tf_op jit(solution)/shard_map/ppermute | solution.py:228
  65.7 1.0 %weight.1 = f32[1,256,768]{2,1,0:T(8,128)} custom-call(f32[8,128]{1,0:T(8,128)S(1)} %add.3.refs_0_, f32[8,128]{1,0:T(8,128)S(1)} %collective-permute-done.19.refs_1_, f32[8,128]{1,0:T(8,128)S(1)} %collective-permute-done.20.refs_2_, f32[8,128]{1,0:T(8,128)S(1)} %collective-permute-done.21.refs_3_, f32[1,256,768]{2,1,0:T(8,128)S(1)} %copy-done.2, ...), custom_call_target="tpu_custom_call" | custom-call | bytes 2375680 | tf_op jit(solution)/shard_map/weight/pallas_call | solution.py:185
  (46 shorter events, 8.0 us)
Async XLA Ops:
  2.3 12.4 %collective-permute-start.2 = (bf16[128,512]{1,0:T(8,128)(2,1)S(1)}, bf16[128,512]{1,0:T(8,128)(2,1)S(1)}, u32[]{:S(2)}, u32[]{:S(2)}) collective-permute-start(bf16[128,512]{1,0:T(8,128)(2,1)S(1)} %get-tuple-element.31), channel_id=1, source_target_pairs={{0,2},{1,3},{2,0},{3,1},{4,6},{5,7},{6,4},{7,5},{8,10},{9,11},{10,... | collective-permute-start | bytes 393224 | tf_op jit(solution)/shard_map/ppermute | solution.py:231
  6.4 8.3 %collective-permute-start = (bf16[272,512]{1,0:T(8,128)(2,1)S(1)}, bf16[272,512]{1,0:T(8,128)(2,1)S(1)}, u32[]{:S(2)}, u32[]{:S(2)}) collective-permute-start(bf16[272,512]{1,0:T(8,128)(2,1)S(1)} %get-tuple-element.29), channel_id=1, source_target_pairs={{0,8},{4,12},{8,0},{12,4},{16,24},{20,28},{24,16},{28,20},{1,9},{5... | collective-permute-start | bytes 835592 | tf_op jit(solution)/shard_map/ppermute | solution.py:228
  7.9 7.8 %collective-permute-start.1 = (bf16[272,512]{1,0:T(8,128)(2,1)S(1)}, bf16[272,512]{1,0:T(8,128)(2,1)S(1)}, u32[]{:S(2)}, u32[]{:S(2)}) collective-permute-start(bf16[272,512]{1,0:T(8,128)(2,1)S(1)} %get-tuple-element.30), channel_id=1, source_target_pairs={{0,16},{4,20},{8,24},{12,28},{16,0},{20,4},{24,8},{28,12},{1,17},{... | collective-permute-start | bytes 835592 | tf_op jit(solution)/shard_map/ppermute | solution.py:228
  9.4 13.2 %collective-permute-start.3 = (bf16[128,512]{1,0:T(8,128)(2,1)S(1)}, bf16[128,512]{1,0:T(8,128)(2,1)S(1)}, u32[]{:S(2)}, u32[]{:S(2)}) collective-permute-start(bf16[128,512]{1,0:T(8,128)(2,1)S(1)} %get-tuple-element.32), channel_id=1, source_target_pairs={{0,1},{1,2},{2,3},{3,0},{4,5},{5,6},{6,7},{7,4},{8,9},{9,10},{10,1... | collective-permute-start | bytes 393224 | tf_op jit(solution)/shard_map/ppermute | solution.py:231
  11.0 12.5 %collective-permute-start.4 = (bf16[128,512]{1,0:T(8,128)(2,1)S(1)}, bf16[128,512]{1,0:T(8,128)(2,1)S(1)}, u32[]{:S(2)}, u32[]{:S(2)}) collective-permute-start(bf16[128,512]{1,0:T(8,128)(2,1)S(1)} %get-tuple-element.33), channel_id=1, source_target_pairs={{0,3},{1,0},{2,1},{3,2},{4,7},{5,4},{6,5},{7,6},{8,11},{9,8},{10,9... | collective-permute-start | bytes 393224 | tf_op jit(solution)/shard_map/ppermute | solution.py:231
  15.7 9.1 %collective-permute-start.6 = (bf16[272,512]{1,0:T(8,128)(2,1)S(1)}, bf16[272,512]{1,0:T(8,128)(2,1)S(1)}, u32[]{:S(2)}, u32[]{:S(2)}) collective-permute-start(bf16[272,512]{1,0:T(8,128)(2,1)S(1)} %get-tuple-element.36), channel_id=1, source_target_pairs={{0,24},{4,28},{8,16},{12,20},{16,8},{20,12},{24,0},{28,4},{1,25},{... | collective-permute-start | bytes 835592 | tf_op jit(solution)/shard_map/ppermute | solution.py:228
  19.5 7.0 %collective-permute-start.13 = (bf16[128,512]{1,0:T(8,128)(2,1)S(1)}, bf16[128,512]{1,0:T(8,128)(2,1)S(1)}, u32[]{:S(2)}, u32[]{:S(2)}) collective-permute-start(bf16[128,512]{1,0:T(8,128)(2,1)S(1)} %get-tuple-element.45), channel_id=1, source_target_pairs={{0,1},{1,2},{2,3},{3,0},{4,5},{5,6},{6,7},{7,4},{8,9},{9,10},{10,1... | collective-permute-start | bytes 393224 | tf_op jit(solution)/shard_map/ppermute | solution.py:231
  19.6 21.5 %collective-permute-start.14 = (bf16[128,512]{1,0:T(8,128)(2,1)S(1)}, bf16[128,512]{1,0:T(8,128)(2,1)S(1)}, u32[]{:S(2)}, u32[]{:S(2)}) collective-permute-start(bf16[128,512]{1,0:T(8,128)(2,1)S(1)} %get-tuple-element.46), channel_id=1, source_target_pairs={{0,2},{1,3},{2,0},{3,1},{4,6},{5,7},{6,4},{7,5},{8,10},{9,11},{10,... | collective-permute-start | bytes 393224 | tf_op jit(solution)/shard_map/ppermute | solution.py:231
  22.6 18.5 %collective-permute-start.15 = (bf16[128,512]{1,0:T(8,128)(2,1)S(1)}, bf16[128,512]{1,0:T(8,128)(2,1)S(1)}, u32[]{:S(2)}, u32[]{:S(2)}) collective-permute-start(bf16[128,512]{1,0:T(8,128)(2,1)S(1)} %get-tuple-element.47), channel_id=1, source_target_pairs={{0,3},{1,0},{2,1},{3,2},{4,7},{5,4},{6,5},{7,6},{8,11},{9,8},{10,9... | collective-permute-start | bytes 393224 | tf_op jit(solution)/shard_map/ppermute | solution.py:231
  23.8 17.4 %collective-permute-start.10 = (bf16[512,768]{1,0:T(8,128)(2,1)S(1)}, bf16[512,768]{1,0:T(8,128)(2,1)S(1)}, u32[]{:S(2)}, u32[]{:S(2)}) collective-permute-start(bf16[512,768]{1,0:T(8,128)(2,1)S(1)} %bitcast.4), channel_id=1, source_target_pairs={{0,16},{4,20},{8,24},{12,28},{16,0},{20,4},{24,8},{28,12},{1,17},{... | collective-permute-start | bytes 2359304 | tf_op jit(solution)/shard_map/ppermute | solution.py:228
  24.8 16.5 %collective-permute-start.5 = (bf16[512,768]{1,0:T(8,128)(2,1)S(1)}, bf16[512,768]{1,0:T(8,128)(2,1)S(1)}, u32[]{:S(2)}, u32[]{:S(2)}) collective-permute-start(bf16[512,768]{1,0:T(8,128)(2,1)S(1)} %bitcast.5), channel_id=1, source_target_pairs={{0,8},{4,12},{8,0},{12,4},{16,24},{20,28},{24,16},{28,20},{1,9},{5... | collective-permute-start | bytes 2359304 | tf_op jit(solution)/shard_map/ppermute | solution.py:228
  26.6 18.9 %collective-permute-start.7 = (bf16[256,512]{1,0:T(8,128)(2,1)S(1)}, bf16[256,512]{1,0:T(8,128)(2,1)S(1)}, u32[]{:S(2)}, u32[]{:S(2)}) collective-permute-start(bf16[256,512]{1,0:T(8,128)(2,1)S(1)} %get-tuple-element.38), channel_id=1, source_target_pairs={{0,1},{1,2},{2,3},{3,0},{4,5},{5,6},{6,7},{7,4},{8,9},{9,10},{10,1... | collective-permute-start | bytes 786440 | tf_op jit(solution)/shard_map/ppermute | solution.py:231
  41.2 10.2 %collective-permute-start.8 = (bf16[256,512]{1,0:T(8,128)(2,1)S(1)}, bf16[256,512]{1,0:T(8,128)(2,1)S(1)}, u32[]{:S(2)}, u32[]{:S(2)}) collective-permute-start(bf16[256,512]{1,0:T(8,128)(2,1)S(1)} %get-tuple-element.39), channel_id=1, source_target_pairs={{0,2},{1,3},{2,0},{3,1},{4,6},{5,7},{6,4},{7,5},{8,10},{9,11},{10,... | collective-permute-start | bytes 786440 | tf_op jit(solution)/shard_map/ppermute | solution.py:231
  41.2 13.4 %collective-permute-start.9 = (bf16[256,512]{1,0:T(8,128)(2,1)S(1)}, bf16[256,512]{1,0:T(8,128)(2,1)S(1)}, u32[]{:S(2)}, u32[]{:S(2)}) collective-permute-start(bf16[256,512]{1,0:T(8,128)(2,1)S(1)} %get-tuple-element.40), channel_id=1, source_target_pairs={{0,3},{1,0},{2,1},{3,2},{4,7},{5,4},{6,5},{7,6},{8,11},{9,8},{10,9... | collective-permute-start | bytes 786440 | tf_op jit(solution)/shard_map/ppermute | solution.py:231
  41.3 13.3 %collective-permute-start.11 = (bf16[512,384]{1,0:T(8,128)(2,1)S(1)}, bf16[512,384]{1,0:T(8,128)(2,1)S(1)}, u32[]{:S(2)}, u32[]{:S(2)}) collective-permute-start(bf16[512,384]{1,0:T(8,128)(2,1)S(1)} %slice.8), channel_id=1, source_target_pairs={{0,16},{4,20},{8,24},{12,28},{16,0},{20,4},{24,8},{28,12},{1,17},{... | collective-permute-start | bytes 1179656 | tf_op jit(solution)/shard_map/ppermute | solution.py:228
  42.7 11.8 %collective-permute-start.12 = (bf16[512,384]{1,0:T(8,128)(2,1)S(1)}, bf16[512,384]{1,0:T(8,128)(2,1)S(1)}, u32[]{:S(2)}, u32[]{:S(2)}) collective-permute-start(bf16[512,384]{1,0:T(8,128)(2,1)S(1)} %slice.9), channel_id=1, source_target_pairs={{0,8},{4,12},{8,0},{12,4},{16,24},{20,28},{24,16},{28,20},{1,9},{5... | collective-permute-start | bytes 1179656 | tf_op jit(solution)/shard_map/ppermute | solution.py:228
  45.5 9.1 %copy-start = (f32[1,256,768]{2,1,0:T(8,128)S(1)}, f32[1,256,768]{2,1,0:T(8,128)}, u32[]{:S(2)}) copy-start(f32[1,256,768]{2,1,0:T(8,128)} %first_ref.3) | copy-start | bytes 2359300
  45.5 9.1 %copy-start.1 = (f32[1,256,768]{2,1,0:T(8,128)S(1)}, f32[1,256,768]{2,1,0:T(8,128)}, u32[]{:S(2)}) copy-start(f32[1,256,768]{2,1,0:T(8,128)} %second_ref.3) | copy-start | bytes 2359300
  55.1 1.9 %collective-permute-start.16 = (f32[256,384]{1,0:T(8,128)S(1)}, f32[256,384]{1,0:T(8,128)S(1)}, u32[]{:S(2)}, u32[]{:S(2)}) collective-permute-start(f32[256,384]{1,0:T(8,128)S(1)} %product.7), channel_id=1, source_target_pairs={{0,4},{4,0},{8,12},{12,8},{16,20},{20,16},{24,28},{28,24},{1,5},{5... | collective-permute-start | bytes 1179656 | tf_op jit(solution)/shard_map/ppermute | solution.py:228
  55.6 1.9 %collective-permute-start.17 = (f32[256,384]{1,0:T(8,128)S(1)}, f32[256,384]{1,0:T(8,128)S(1)}, u32[]{:S(2)}, u32[]{:S(2)}) collective-permute-start(f32[256,384]{1,0:T(8,128)S(1)} %product.8), channel_id=1, source_target_pairs={{0,4},{4,0},{8,12},{12,8},{16,20},{20,16},{24,28},{28,24},{1,5},{5... | collective-permute-start | bytes 1179656 | tf_op jit(solution)/shard_map/ppermute | solution.py:228
  58.8 1.3 %collective-permute-start.18 = (f32[8,128]{1,0:T(8,128)S(1)}, f32[8,128]{1,0:T(8,128)S(1)}, u32[]{:S(2)}, u32[]{:S(2)}) collective-permute-start(f32[8,128]{1,0:T(8,128)S(1)} %get-tuple-element.49), channel_id=1, source_target_pairs={{0,4},{4,0},{8,12},{12,8},{16,20},{20,16},{24,28},{28,24},{1,5},{5... | collective-permute-start | bytes 12296 | tf_op jit(solution)/shard_map/ppermute | solution.py:228
  60.0 4.9 %collective-permute-start.21 = (f32[8,128]{1,0:T(8,128)S(1)}, f32[8,128]{1,0:T(8,128)S(1)}, u32[]{:S(2)}, u32[]{:S(2)}) collective-permute-start(f32[8,128]{1,0:T(8,128)S(1)} %add.3.refs_0_), channel_id=1, source_target_pairs={{0,24},{4,28},{8,16},{12,20},{16,8},{20,12},{24,0},{28,4},{1,25},{... | collective-permute-start | bytes 12296 | tf_op jit(solution)/shard_map/ppermute | solution.py:228
  60.6 4.3 %collective-permute-start.20 = (f32[8,128]{1,0:T(8,128)S(1)}, f32[8,128]{1,0:T(8,128)S(1)}, u32[]{:S(2)}, u32[]{:S(2)}) collective-permute-start(f32[8,128]{1,0:T(8,128)S(1)} %add.3.refs_0_), channel_id=1, source_target_pairs={{0,16},{4,20},{8,24},{12,28},{16,0},{20,4},{24,8},{28,12},{1,17},{... | collective-permute-start | bytes 12296 | tf_op jit(solution)/shard_map/ppermute | solution.py:228
  62.1 3.6 %collective-permute-start.19 = (f32[8,128]{1,0:T(8,128)S(1)}, f32[8,128]{1,0:T(8,128)S(1)}, u32[]{:S(2)}, u32[]{:S(2)}) collective-permute-start(f32[8,128]{1,0:T(8,128)S(1)} %add.3.refs_0_), channel_id=1, source_target_pairs={{0,8},{4,12},{8,0},{12,4},{16,24},{20,28},{24,16},{28,20},{1,9},{5... | collective-permute-start | bytes 12296 | tf_op jit(solution)/shard_map/ppermute | solution.py:228
  (2 other events, 10.2 us)

commit v7 on v6

--- a/solution.py
+++ b/solution.py
@@ -140,40 +140,51 @@
         out[:, column - first : column - first + wide] = total
 
 
-def new_moments(grad, first_ref, second_ref):
-    return 0.9 * first_ref[0] + 0.1 * grad, 0.999 * second_ref[0] + 0.001 * grad * grad
-
-
-def update_kernel(mine_ref, left_ref, right_ref, weight_ref, first_ref, second_ref, grad_ref, update_ref, sums):
-    grad = mine_ref[...] + jnp.concatenate([left_ref[...], right_ref[...]], axis=1)
+def new_moments(grad, first, second):
+    return 0.9 * first + 0.1 * grad, 0.999 * second + 0.001 * grad * grad
+
+
+def update_kernel(begin, mine_ref, other_ref, weight_ref, first_ref, second_ref, *refs):
+    earlier, (grad_ref, update_ref, sums) = refs[:-3], refs[-3:]
+    columns = slice(begin, begin + other_ref.shape[1])
+    grad = mine_ref[:, columns] + other_ref[...]
     grad_ref[...] = grad
-    weight = weight_ref[0]
-    first, second = new_moments(grad, first_ref, second_ref)
+    weight = weight_ref[0, :, columns]
+    first, second = new_moments(grad, first_ref[0, :, columns], second_ref[0, :, columns])
     first, second = first * (1.0 / (1.0 - 0.9**10)), second * (1.0 / (1.0 - 0.999**10))
     root = second * lax.rsqrt(second)
     update = first * pl.reciprocal(root + 1e-06) + 0.01 * weight
     update_ref[...] = update
     row = lax.broadcasted_iota(jnp.int32, sums.shape, 0)
-    sums[...] = jnp.where(row == 0, jnp.sum(weight * weight), jnp.sum(update * update))
-
-
-def moment_kernel(grad_ref, first_ref, second_ref, new_first, new_second):
-    new_first[0], new_second[0] = new_moments(grad_ref[...], first_ref, second_ref)
+    total = jnp.where(row == 0, jnp.sum(weight * weight), jnp.sum(update * update))
+    for ref in earlier:
+        total = total + ref[...]
+    sums[...] = total
+
+
+def moment_kernel(left_ref, right_ref, first_ref, second_ref, new_first, new_second):
+    begin = 0
+    for grad_ref in (left_ref, right_ref):
+        columns = slice(begin, begin + grad_ref.shape[1])
+        first, second = new_moments(grad_ref[...], first_ref[0, :, columns], second_ref[0, :, columns])
+        new_first[0, :, columns], new_second[0, :, columns] = first, second
+        begin += grad_ref.shape[1]
 
 
 def weight_kernel(n_sums, *refs):
-    sums, (weight_ref, update_ref, out_ref, new_weight, sems) = refs[:n_sums], refs[n_sums:]
+    sums, (weight_ref, left_ref, right_ref, out_ref, new_weight, sems) = refs[:n_sums], refs[n_sums:]
     total = sums[0][...]
     for other in sums[1:]:
         total = total + other[...]
     norm = jnp.sqrt(total)
     scale = 0.1 * (norm[0:1, 0:1] / (norm[1:2, 0:1] + 1e-06))
     n = sems.shape[0]
-    rows = update_ref.shape[0] // n
+    rows = left_ref.shape[0] // n
     copies = []
     for at in range(n):
         span = pl.ds(at * rows, rows)
-        new_weight[0, span, :] = weight_ref[0, span, :] - scale * update_ref[span, :]
+        update = jnp.concatenate([left_ref[span, :], right_ref[span, :]], axis=1)
+        new_weight[0, span, :] = weight_ref[0, span, :] - scale * update
         copies.append(pltpu.make_async_copy(new_weight.at[:, span], out_ref.at[:, span], sems.at[at]))
         copies[-1].start()
     for copy in copies:
@@ -304,36 +315,44 @@
     for side in (give, keep):
         groups = [((hidden,), terms(near, 0, 0, 1, 2, 3)), ((by_y,), terms(mid, 0, 0, 1, 2, 3))]
         totals[side.start] = multiply(side, groups, waits=[seen])
-    seen = tick(*far[1:], *totals.values(), flops=5*10**9)
-    groups = [((by_x,), terms(far, 0, 0, 1, 2, 3)), (by_xy, terms(far, 1, 0, 1, 2, 3))]
+    seen = tick(far[1], far[2], *totals.values(), flops=5*10**9)
+    state_in = down_weight, first_moment, second_moment
+    for side in (give, keep):
+        groups = [((by_x,), terms(far, 0, 0, 1, 2)), (by_xy, terms(far, 1, 0, 1, 2))]
+        totals[side.start] = multiply(side, groups, totals[side.start], waits=[seen, *state_in])
+    seen = tick(far[3], *totals.values(), flops=5*10**9)
+    groups = [((by_x,), terms(far, 0, 3)), (by_xy, terms(far, 1, 3))]
     spans = slice(0, ff // 2), slice(ff // 2, ff)
-    ready = [seen, down_weight, first_moment, second_moment]
+    ready = [seen]
     given = [multiply(give, groups, totals[give.start], span=span, waits=ready) for span in spans]
     other = [across(part, 1) for part in given]
     kept = multiply(keep, groups, after(totals[keep.start], *given))
 
-    state, matrix = jax.ShapeDtypeStruct((1, half, ff), f32), jax.ShapeDtypeStruct((half, ff), f32)
-    grad, update, sums = call(
-        update_kernel,
-        [matrix, matrix, jax.ShapeDtypeStruct((8, 128), f32)],
-        kept,
-        *other,
-        down_weight,
-        first_moment,
-        second_moment,
-        name="update",
-    )
-    sums = sums + across(sums, 1)
+    state = jax.ShapeDtypeStruct((1, half, ff), f32)
+    grads, updates, sums = [], [], []
+    for span, part in zip(spans, other):
+        piece = jax.ShapeDtypeStruct(part.shape, f32)
+        grad, update, total = call(
+            functools.partial(update_kernel, span.start),
+            [piece, piece, jax.ShapeDtypeStruct((8, 128), f32)],
+            kept,
+            part,
+            *state_in,
+            *sums,
+            name="update",
+        )
+        grads, updates, sums = [*grads, grad], [*updates, update], [total]
+    sums = sums[0] + across(sums[0], 1)
     parts = [sums] + [across(sums, mask) for mask in (2, 4, 6)]
     new_first, new_second = call(
-        moment_kernel, [state, state], after(grad, sums), first_moment, second_moment, name="moment"
+        moment_kernel, [state, state], *after(tuple(grads), sums), first_moment, second_moment, name="moment"
     )
     new_weight = call(
         functools.partial(weight_kernel, len(parts)),
         state,
         *parts,
         down_weight,
-        update,
+        *updates,
         out_spaces=HBM,
         scratch=[pltpu.VMEM((1, half, ff), f32), pltpu.SemaphoreType.DMA((4,))],
         name="weight",

time: 66.9 us -> 66.3 us (level)
  waiting for transfers between devices: 28.6 us -> 27.4 us
  Pallas kernels: 8.86 us -> 9.53 us
    ppermute x9, waiting for transfers between devices: 24.6 us -> 22.3 us  [along(): lax.ppermute(array, 'expert', [(d, (d + shift) % owners) for d in range(o...]
    ppermute x13, waiting for transfers between devices: 3.99 us -> 5.09 us  [across(): return lax.ppermute(array, 'dp', [(d, d ^ mask) for d in range(n_dp)])]
    pallas_call x15 -> x19, Pallas kernels: 8.86 us -> 9.53 us  [call(): pl.pallas_call(kernel, out_shape=out_shape, in_specs=spaces if isinstance...]
  transfers between devices with their start and end apart: 22 -> 22, of which waited for: 9 -> 11; matrix products, arithmetic and copies ran while one was open for 0% -> 0% of each run, Pallas kernels for 7% -> 9%
where the time goes in v7:
time: 66.3 us; the launch traced here: 66.1 us
  starting transfers between devices  27.9 us (42%)
  waiting for transfers between devices  27.4 us (41%)
  Pallas kernels  9.53 us (14%)
  between operations  0.84 us (1%)
    ppermute x9, waiting for transfers between devices, along(): lax.ppermute(array, 'expert', [(d, (d + shift) % owners) for d in range(o...  22.3 us
    ppermute x13, starting transfers between devices, across(): return lax.ppermute(array, 'dp', [(d, d ^ mask) for d in range(n_dp)])  15.4 us
    ppermute x9, starting transfers between devices, along(): lax.ppermute(array, 'expert', [(d, (d + shift) % owners) for d in range(o...  12.5 us
    pallas_call x19, Pallas kernels, call(): pl.pallas_call(kernel, out_shape=out_shape, in_specs=spaces if isinstance...  9.53 us
    ppermute x13, waiting for transfers between devices, across(): return lax.ppermute(array, 'dp', [(d, d ^ mask) for d in range(n_dp)])  5.09 us
  transfers between devices with their start and end apart: 22, of which 11 were waited for; matrix products, arithmetic and copies ran while one was open for 0% of the time, Pallas kernels for 9%

profile of v7, /device:TPU:0, one launch (start us, length us, event | category | flops | bytes accessed | tf_op | source)
XLA Modules:
  0.0 66.1 jit_solution(10570448924350334212)
XLA Ops:
  0.6 1.6 %cut.1 = (bf16[128,512]{1,0:T(8,128)(2,1)S(1)}, bf16[128,512]{1,0:T(8,128)(2,1)S(1)}, bf16[128,512]{1,0:T(8,128)(2,1)S(1)}, bf16[128,512]{1,0:T(8,128)(2,1)S(1)}...) custom-call(bf16[256,2048]{1,0:T(8,128)(2,1)} %cot_ref.1, ...), custom_call_target="tpu_custom_call" | custom-call | bytes 2411520 | tf_op jit(solution)/shard_map/cut/pallas_call | solution.py:196
  2.3 4.1 %collective-permute-start.2 = (bf16[128,512]{1,0:T(8,128)(2,1)S(1)}, bf16[128,512]{1,0:T(8,128)(2,1)S(1)}, u32[]{:S(2)}, u32[]{:S(2)}) collective-permute-start(bf16[128,512]{1,0:T(8,128)(2,1)S(1)} %get-tuple-element.35), channel_id=1, source_target_pairs={{0,2},{1,3},{2,0},{3,1},{4,6},{5,7},{6,4},{7,5},{8,10},{9,11},{10,... | collective-permute-start | bytes 393224 | tf_op jit(solution)/shard_map/ppermute | solution.py:242
  6.4 1.5 %collective-permute-start = (bf16[272,512]{1,0:T(8,128)(2,1)S(1)}, bf16[272,512]{1,0:T(8,128)(2,1)S(1)}, u32[]{:S(2)}, u32[]{:S(2)}) collective-permute-start(bf16[272,512]{1,0:T(8,128)(2,1)S(1)} %get-tuple-element.33), channel_id=1, source_target_pairs={{0,8},{4,12},{8,0},{12,4},{16,24},{20,28},{24,16},{28,20},{1,9},{5... | collective-permute-start | bytes 835592 | tf_op jit(solution)/shard_map/ppermute | solution.py:239
  7.9 1.5 %collective-permute-start.1 = (bf16[272,512]{1,0:T(8,128)(2,1)S(1)}, bf16[272,512]{1,0:T(8,128)(2,1)S(1)}, u32[]{:S(2)}, u32[]{:S(2)}) collective-permute-start(bf16[272,512]{1,0:T(8,128)(2,1)S(1)} %get-tuple-element.34), channel_id=1, source_target_pairs={{0,16},{4,20},{8,24},{12,28},{16,0},{20,4},{24,8},{28,12},{1,17},{... | collective-permute-start | bytes 835592 | tf_op jit(solution)/shard_map/ppermute | solution.py:239
  9.4 1.6 %collective-permute-start.3 = (bf16[128,512]{1,0:T(8,128)(2,1)S(1)}, bf16[128,512]{1,0:T(8,128)(2,1)S(1)}, u32[]{:S(2)}, u32[]{:S(2)}) collective-permute-start(bf16[128,512]{1,0:T(8,128)(2,1)S(1)} %get-tuple-element.36), channel_id=1, source_target_pairs={{0,1},{1,2},{2,3},{3,0},{4,5},{5,6},{6,7},{7,4},{8,9},{9,10},{10,1... | collective-permute-start | bytes 393224 | tf_op jit(solution)/shard_map/ppermute | solution.py:242
  11.0 2.2 %collective-permute-start.4 = (bf16[128,512]{1,0:T(8,128)(2,1)S(1)}, bf16[128,512]{1,0:T(8,128)(2,1)S(1)}, u32[]{:S(2)}, u32[]{:S(2)}) collective-permute-start(bf16[128,512]{1,0:T(8,128)(2,1)S(1)} %get-tuple-element.37), channel_id=1, source_target_pairs={{0,3},{1,0},{2,1},{3,2},{4,7},{5,4},{6,5},{7,6},{8,11},{9,8},{10,9... | collective-permute-start | bytes 393224 | tf_op jit(solution)/shard_map/ppermute | solution.py:242
  13.2 1.5 %collective-permute-done.2.refs_0_.refs_3_ = bf16[128,512]{1,0:T(8,128)(2,1)S(1)} collective-permute-done((bf16[128,512]{1,0:T(8,128)(2,1)S(1)}, bf16[128,512]{1,0:T(8,128)(2,1)S(1)}, u32[]{:S(2)}, u32[]{:S(2)}) %collective-permute-start.2) | collective-permute-done | bytes 131104 | tf_op jit(solution)/shard_map/ppermute | solution.py:242
  14.7 1.0 %collective-permute-done.1.refs_0_ = bf16[272,512]{1,0:T(8,128)(2,1)S(1)} collective-permute-done((bf16[272,512]{1,0:T(8,128)(2,1)S(1)}, bf16[272,512]{1,0:T(8,128)(2,1)S(1)}, u32[]{:S(2)}, u32[]{:S(2)}) %collective-permute-start.1) | collective-permute-done | bytes 278560 | tf_op jit(solution)/shard_map/ppermute | solution.py:239
  15.7 3.5 %collective-permute-start.6 = (bf16[272,512]{1,0:T(8,128)(2,1)S(1)}, bf16[272,512]{1,0:T(8,128)(2,1)S(1)}, u32[]{:S(2)}, u32[]{:S(2)}) collective-permute-start(bf16[272,512]{1,0:T(8,128)(2,1)S(1)} %get-tuple-element.40), channel_id=1, source_target_pairs={{0,24},{4,28},{8,16},{12,20},{16,8},{20,12},{24,0},{28,4},{1,25},{... | collective-permute-start | bytes 835592 | tf_op jit(solution)/shard_map/ppermute | solution.py:239
  19.6 3.0 %collective-permute-start.14 = (bf16[128,512]{1,0:T(8,128)(2,1)S(1)}, bf16[128,512]{1,0:T(8,128)(2,1)S(1)}, u32[]{:S(2)}, u32[]{:S(2)}) collective-permute-start(bf16[128,512]{1,0:T(8,128)(2,1)S(1)} %get-tuple-element.50), channel_id=1, source_target_pairs={{0,2},{1,3},{2,0},{3,1},{4,6},{5,7},{6,4},{7,5},{8,10},{9,11},{10,... | collective-permute-start | bytes 393224 | tf_op jit(solution)/shard_map/ppermute | solution.py:242
  22.6 0.9 %collective-permute-start.15 = (bf16[128,512]{1,0:T(8,128)(2,1)S(1)}, bf16[128,512]{1,0:T(8,128)(2,1)S(1)}, u32[]{:S(2)}, u32[]{:S(2)}) collective-permute-start(bf16[128,512]{1,0:T(8,128)(2,1)S(1)} %get-tuple-element.51), channel_id=1, source_target_pairs={{0,3},{1,0},{2,1},{3,2},{4,7},{5,4},{6,5},{7,6},{8,11},{9,8},{10,9... | collective-permute-start | bytes 393224 | tf_op jit(solution)/shard_map/ppermute | solution.py:242
  24.8 1.3 %collective-permute-start.5 = (bf16[512,768]{1,0:T(8,128)(2,1)S(1)}, bf16[512,768]{1,0:T(8,128)(2,1)S(1)}, u32[]{:S(2)}, u32[]{:S(2)}) collective-permute-start(bf16[512,768]{1,0:T(8,128)(2,1)S(1)} %bitcast.5), channel_id=1, source_target_pairs={{0,8},{4,12},{8,0},{12,4},{16,24},{20,28},{24,16},{28,20},{1,9},{5... | collective-permute-start | bytes 2359304 | tf_op jit(solution)/shard_map/ppermute | solution.py:239
  27.2 14.0 %collective-permute-done.14.refs_1_.refs_8_ = bf16[128,512]{1,0:T(8,128)(2,1)S(1)} collective-permute-done((bf16[128,512]{1,0:T(8,128)(2,1)S(1)}, bf16[128,512]{1,0:T(8,128)(2,1)S(1)}, u32[]{:S(2)}, u32[]{:S(2)}) %collective-permute-start.14) | collective-permute-done | bytes 131104 | tf_op jit(solution)/shard_map/ppermute | solution.py:242
  41.4 1.4 %collective-permute-start.9 = (bf16[512,384]{1,0:T(8,128)(2,1)S(1)}, bf16[512,384]{1,0:T(8,128)(2,1)S(1)}, u32[]{:S(2)}, u32[]{:S(2)}) collective-permute-start(bf16[512,384]{1,0:T(8,128)(2,1)S(1)} %slice.8), channel_id=1, source_target_pairs={{0,16},{4,20},{8,24},{12,28},{16,0},{20,4},{24,8},{28,12},{1,17},{... | collective-permute-start | bytes 1179656 | tf_op jit(solution)/shard_map/ppermute | solution.py:239
  42.7 1.5 %collective-permute-start.10 = (bf16[512,384]{1,0:T(8,128)(2,1)S(1)}, bf16[512,384]{1,0:T(8,128)(2,1)S(1)}, u32[]{:S(2)}, u32[]{:S(2)}) collective-permute-start(bf16[512,384]{1,0:T(8,128)(2,1)S(1)} %slice.9), channel_id=1, source_target_pairs={{0,8},{4,12},{8,0},{12,4},{16,24},{20,28},{24,16},{28,20},{1,9},{5... | collective-permute-start | bytes 1179656 | tf_op jit(solution)/shard_map/ppermute | solution.py:239
  45.5 5.8 %collective-permute-done.12.refs_1_.refs_3_ = bf16[256,512]{1,0:T(8,128)(2,1)S(1)} collective-permute-done((bf16[256,512]{1,0:T(8,128)(2,1)S(1)}, bf16[256,512]{1,0:T(8,128)(2,1)S(1)}, u32[]{:S(2)}, u32[]{:S(2)}) %collective-permute-start.12) | collective-permute-done | bytes 262176 | tf_op jit(solution)/shard_map/ppermute | solution.py:242
  51.4 0.9 %collective-permute-done.10.refs_5_.refs_3_ = bf16[512,384]{1,0:T(8,128)(2,1)S(1)} collective-permute-done((bf16[512,384]{1,0:T(8,128)(2,1)S(1)}, bf16[512,384]{1,0:T(8,128)(2,1)S(1)}, u32[]{:S(2)}, u32[]{:S(2)}) %collective-permute-start.10) | collective-permute-done | bytes 393248 | tf_op jit(solution)/shard_map/ppermute | solution.py:239
  53.6 0.9 %collective-permute-done.7.refs_0_.refs_1_ = bf16[256,512]{1,0:T(8,128)(2,1)S(1)} collective-permute-done((bf16[256,512]{1,0:T(8,128)(2,1)S(1)}, bf16[256,512]{1,0:T(8,128)(2,1)S(1)}, u32[]{:S(2)}, u32[]{:S(2)}) %collective-permute-start.7) | collective-permute-done | bytes 262176 | tf_op jit(solution)/shard_map/ppermute | solution.py:242
  58.2 1.0 %collective-permute-done.18 = f32[8,128]{1,0:T(8,128)S(1)} collective-permute-done((f32[8,128]{1,0:T(8,128)S(1)}, f32[8,128]{1,0:T(8,128)S(1)}, u32[]{:S(2)}, u32[]{:S(2)}) %collective-permute-start.18) | collective-permute-done | bytes 4128 | tf_op jit(solution)/shard_map/ppermute | solution.py:239
  59.8 1.7 %collective-permute-start.20 = (f32[8,128]{1,0:T(8,128)S(1)}, f32[8,128]{1,0:T(8,128)S(1)}, u32[]{:S(2)}, u32[]{:S(2)}) collective-permute-start(f32[8,128]{1,0:T(8,128)S(1)} %add.3.refs_0_), channel_id=1, source_target_pairs={{0,16},{4,20},{8,24},{12,28},{16,0},{20,4},{24,8},{28,12},{1,17},{... | collective-permute-start | bytes 12296 | tf_op jit(solution)/shard_map/ppermute | solution.py:239
  61.5 1.2 %collective-permute-start.19 = (f32[8,128]{1,0:T(8,128)S(1)}, f32[8,128]{1,0:T(8,128)S(1)}, u32[]{:S(2)}, u32[]{:S(2)}) collective-permute-start(f32[8,128]{1,0:T(8,128)S(1)} %add.3.refs_0_), channel_id=1, source_target_pairs={{0,8},{4,12},{8,0},{12,4},{16,24},{20,28},{24,16},{28,20},{1,9},{5... | collective-permute-start | bytes 12296 | tf_op jit(solution)/shard_map/ppermute | solution.py:239
  62.7 1.4 %moment.1 = (f32[1,256,768]{2,1,0:T(8,128)}, f32[1,256,768]{2,1,0:T(8,128)}) custom-call(f32[256,384]{1,0:T(8,128)S(1)} %get-tuple-element.59.left_ref, f32[256,384]{1,0:T(8,128)S(1)} %get-tuple-element.60.right_ref, f32[1,256,768]{2,1,0:T(8,128)S(1)} %copy-done, f32[1,256,768]{2,1,0:T(8,128)S(1)} %copy-done.1), custom_call_target="tpu_custom_call" | custom-call | bytes 3932160 | tf_op jit(solution)/shard_map/moment/pallas_call | solution.py:196
  64.1 1.0 %collective-permute-done.19.refs_1_ = f32[8,128]{1,0:T(8,128)S(1)} collective-permute-done((f32[8,128]{1,0:T(8,128)S(1)}, f32[8,128]{1,0:T(8,128)S(1)}, u32[]{:S(2)}, u32[]{:S(2)}) %collective-permute-start.19) | collective-permute-done | bytes 4128 | tf_op jit(solution)/shard_map/ppermute | solution.py:239
  65.1 1.0 %weight.1 = f32[1,256,768]{2,1,0:T(8,128)} custom-call(f32[8,128]{1,0:T(8,128)S(1)} %add.3.refs_0_, f32[8,128]{1,0:T(8,128)S(1)} %collective-permute-done.19.refs_1_, f32[8,128]{1,0:T(8,128)S(1)} %collective-permute-done.20.refs_2_, f32[8,128]{1,0:T(8,128)S(1)} %collective-permute-done.21.refs_3_, f32[1,256,768]{2,1,0:T(8,128)S(1)} %copy-done.2, ...), custom_call_target="tpu_custom_call" | custom-call | bytes 2375680 | tf_op jit(solution)/shard_map/weight/pallas_call | solution.py:196
  (50 shorter events, 9.7 us)
Async XLA Ops:
  2.3 12.4 %collective-permute-start.2 = (bf16[128,512]{1,0:T(8,128)(2,1)S(1)}, bf16[128,512]{1,0:T(8,128)(2,1)S(1)}, u32[]{:S(2)}, u32[]{:S(2)}) collective-permute-start(bf16[128,512]{1,0:T(8,128)(2,1)S(1)} %get-tuple-element.35), channel_id=1, source_target_pairs={{0,2},{1,3},{2,0},{3,1},{4,6},{5,7},{6,4},{7,5},{8,10},{9,11},{10,... | collective-permute-start | bytes 393224 | tf_op jit(solution)/shard_map/ppermute | solution.py:242
  6.4 8.3 %collective-permute-start = (bf16[272,512]{1,0:T(8,128)(2,1)S(1)}, bf16[272,512]{1,0:T(8,128)(2,1)S(1)}, u32[]{:S(2)}, u32[]{:S(2)}) collective-permute-start(bf16[272,512]{1,0:T(8,128)(2,1)S(1)} %get-tuple-element.33), channel_id=1, source_target_pairs={{0,8},{4,12},{8,0},{12,4},{16,24},{20,28},{24,16},{28,20},{1,9},{5... | collective-permute-start | bytes 835592 | tf_op jit(solution)/shard_map/ppermute | solution.py:239
  7.9 7.8 %collective-permute-start.1 = (bf16[272,512]{1,0:T(8,128)(2,1)S(1)}, bf16[272,512]{1,0:T(8,128)(2,1)S(1)}, u32[]{:S(2)}, u32[]{:S(2)}) collective-permute-start(bf16[272,512]{1,0:T(8,128)(2,1)S(1)} %get-tuple-element.34), channel_id=1, source_target_pairs={{0,16},{4,20},{8,24},{12,28},{16,0},{20,4},{24,8},{28,12},{1,17},{... | collective-permute-start | bytes 835592 | tf_op jit(solution)/shard_map/ppermute | solution.py:239
  9.4 13.2 %collective-permute-start.3 = (bf16[128,512]{1,0:T(8,128)(2,1)S(1)}, bf16[128,512]{1,0:T(8,128)(2,1)S(1)}, u32[]{:S(2)}, u32[]{:S(2)}) collective-permute-start(bf16[128,512]{1,0:T(8,128)(2,1)S(1)} %get-tuple-element.36), channel_id=1, source_target_pairs={{0,1},{1,2},{2,3},{3,0},{4,5},{5,6},{6,7},{7,4},{8,9},{9,10},{10,1... | collective-permute-start | bytes 393224 | tf_op jit(solution)/shard_map/ppermute | solution.py:242
  11.0 12.5 %collective-permute-start.4 = (bf16[128,512]{1,0:T(8,128)(2,1)S(1)}, bf16[128,512]{1,0:T(8,128)(2,1)S(1)}, u32[]{:S(2)}, u32[]{:S(2)}) collective-permute-start(bf16[128,512]{1,0:T(8,128)(2,1)S(1)} %get-tuple-element.37), channel_id=1, source_target_pairs={{0,3},{1,0},{2,1},{3,2},{4,7},{5,4},{6,5},{7,6},{8,11},{9,8},{10,9... | collective-permute-start | bytes 393224 | tf_op jit(solution)/shard_map/ppermute | solution.py:242
  15.7 9.1 %collective-permute-start.6 = (bf16[272,512]{1,0:T(8,128)(2,1)S(1)}, bf16[272,512]{1,0:T(8,128)(2,1)S(1)}, u32[]{:S(2)}, u32[]{:S(2)}) collective-permute-start(bf16[272,512]{1,0:T(8,128)(2,1)S(1)} %get-tuple-element.40), channel_id=1, source_target_pairs={{0,24},{4,28},{8,16},{12,20},{16,8},{20,12},{24,0},{28,4},{1,25},{... | collective-permute-start | bytes 835592 | tf_op jit(solution)/shard_map/ppermute | solution.py:239
  19.5 7.0 %collective-permute-start.13 = (bf16[128,512]{1,0:T(8,128)(2,1)S(1)}, bf16[128,512]{1,0:T(8,128)(2,1)S(1)}, u32[]{:S(2)}, u32[]{:S(2)}) collective-permute-start(bf16[128,512]{1,0:T(8,128)(2,1)S(1)} %get-tuple-element.49), channel_id=1, source_target_pairs={{0,1},{1,2},{2,3},{3,0},{4,5},{5,6},{6,7},{7,4},{8,9},{9,10},{10,1... | collective-permute-start | bytes 393224 | tf_op jit(solution)/shard_map/ppermute | solution.py:242
  19.6 21.6 %collective-permute-start.14 = (bf16[128,512]{1,0:T(8,128)(2,1)S(1)}, bf16[128,512]{1,0:T(8,128)(2,1)S(1)}, u32[]{:S(2)}, u32[]{:S(2)}) collective-permute-start(bf16[128,512]{1,0:T(8,128)(2,1)S(1)} %get-tuple-element.50), channel_id=1, source_target_pairs={{0,2},{1,3},{2,0},{3,1},{4,6},{5,7},{6,4},{7,5},{8,10},{9,11},{10,... | collective-permute-start | bytes 393224 | tf_op jit(solution)/shard_map/ppermute | solution.py:242
  22.6 18.5 %collective-permute-start.15 = (bf16[128,512]{1,0:T(8,128)(2,1)S(1)}, bf16[128,512]{1,0:T(8,128)(2,1)S(1)}, u32[]{:S(2)}, u32[]{:S(2)}) collective-permute-start(bf16[128,512]{1,0:T(8,128)(2,1)S(1)} %get-tuple-element.51), channel_id=1, source_target_pairs={{0,3},{1,0},{2,1},{3,2},{4,7},{5,4},{6,5},{7,6},{8,11},{9,8},{10,9... | collective-permute-start | bytes 393224 | tf_op jit(solution)/shard_map/ppermute | solution.py:242
  23.8 17.5 %collective-permute-start.8 = (bf16[512,768]{1,0:T(8,128)(2,1)S(1)}, bf16[512,768]{1,0:T(8,128)(2,1)S(1)}, u32[]{:S(2)}, u32[]{:S(2)}) collective-permute-start(bf16[512,768]{1,0:T(8,128)(2,1)S(1)} %bitcast.4), channel_id=1, source_target_pairs={{0,16},{4,20},{8,24},{12,28},{16,0},{20,4},{24,8},{28,12},{1,17},{... | collective-permute-start | bytes 2359304 | tf_op jit(solution)/shard_map/ppermute | solution.py:239
  24.8 16.5 %collective-permute-start.5 = (bf16[512,768]{1,0:T(8,128)(2,1)S(1)}, bf16[512,768]{1,0:T(8,128)(2,1)S(1)}, u32[]{:S(2)}, u32[]{:S(2)}) collective-permute-start(bf16[512,768]{1,0:T(8,128)(2,1)S(1)} %bitcast.5), channel_id=1, source_target_pairs={{0,8},{4,12},{8,0},{12,4},{16,24},{20,28},{24,16},{28,20},{1,9},{5... | collective-permute-start | bytes 2359304 | tf_op jit(solution)/shard_map/ppermute | solution.py:239
  26.6 18.9 %collective-permute-start.11 = (bf16[256,512]{1,0:T(8,128)(2,1)S(1)}, bf16[256,512]{1,0:T(8,128)(2,1)S(1)}, u32[]{:S(2)}, u32[]{:S(2)}) collective-permute-start(bf16[256,512]{1,0:T(8,128)(2,1)S(1)} %get-tuple-element.45), channel_id=1, source_target_pairs={{0,1},{1,2},{2,3},{3,0},{4,5},{5,6},{6,7},{7,4},{8,9},{9,10},{10,1... | collective-permute-start | bytes 786440 | tf_op jit(solution)/shard_map/ppermute | solution.py:242
  41.2 10.2 %collective-permute-start.12 = (bf16[256,512]{1,0:T(8,128)(2,1)S(1)}, bf16[256,512]{1,0:T(8,128)(2,1)S(1)}, u32[]{:S(2)}, u32[]{:S(2)}) collective-permute-start(bf16[256,512]{1,0:T(8,128)(2,1)S(1)} %get-tuple-element.46), channel_id=1, source_target_pairs={{0,2},{1,3},{2,0},{3,1},{4,6},{5,7},{6,4},{7,5},{8,10},{9,11},{10,... | collective-permute-start | bytes 786440 | tf_op jit(solution)/shard_map/ppermute | solution.py:242
  41.2 13.4 %collective-permute-start.7 = (bf16[256,512]{1,0:T(8,128)(2,1)S(1)}, bf16[256,512]{1,0:T(8,128)(2,1)S(1)}, u32[]{:S(2)}, u32[]{:S(2)}) collective-permute-start(bf16[256,512]{1,0:T(8,128)(2,1)S(1)} %get-tuple-element.41), channel_id=1, source_target_pairs={{0,3},{1,0},{2,1},{3,2},{4,7},{5,4},{6,5},{7,6},{8,11},{9,8},{10,9... | collective-permute-start | bytes 786440 | tf_op jit(solution)/shard_map/ppermute | solution.py:242
  41.4 10.0 %collective-permute-start.9 = (bf16[512,384]{1,0:T(8,128)(2,1)S(1)}, bf16[512,384]{1,0:T(8,128)(2,1)S(1)}, u32[]{:S(2)}, u32[]{:S(2)}) collective-permute-start(bf16[512,384]{1,0:T(8,128)(2,1)S(1)} %slice.8), channel_id=1, source_target_pairs={{0,16},{4,20},{8,24},{12,28},{16,0},{20,4},{24,8},{28,12},{1,17},{... | collective-permute-start | bytes 1179656 | tf_op jit(solution)/shard_map/ppermute | solution.py:239
  42.7 9.5 %collective-permute-start.10 = (bf16[512,384]{1,0:T(8,128)(2,1)S(1)}, bf16[512,384]{1,0:T(8,128)(2,1)S(1)}, u32[]{:S(2)}, u32[]{:S(2)}) collective-permute-start(bf16[512,384]{1,0:T(8,128)(2,1)S(1)} %slice.9), channel_id=1, source_target_pairs={{0,8},{4,12},{8,0},{12,4},{16,24},{20,28},{24,16},{28,20},{1,9},{5... | collective-permute-start | bytes 1179656 | tf_op jit(solution)/shard_map/ppermute | solution.py:239
  45.5 6.8 %copy-start = (f32[1,256,768]{2,1,0:T(8,128)S(1)}, f32[1,256,768]{2,1,0:T(8,128)}, u32[]{:S(2)}) copy-start(f32[1,256,768]{2,1,0:T(8,128)} %first_ref.5) | copy-start | bytes 2359300
  45.5 6.8 %copy-start.1 = (f32[1,256,768]{2,1,0:T(8,128)S(1)}, f32[1,256,768]{2,1,0:T(8,128)}, u32[]{:S(2)}) copy-start(f32[1,256,768]{2,1,0:T(8,128)} %second_ref.5) | copy-start | bytes 2359300
  54.9 1.8 %collective-permute-start.17 = (f32[256,384]{1,0:T(8,128)S(1)}, f32[256,384]{1,0:T(8,128)S(1)}, u32[]{:S(2)}, u32[]{:S(2)}) collective-permute-start(f32[256,384]{1,0:T(8,128)S(1)} %product.11), channel_id=1, source_target_pairs={{0,4},{4,0},{8,12},{12,8},{16,20},{20,16},{24,28},{28,24},{1,5},{5... | collective-permute-start | bytes 1179656 | tf_op jit(solution)/shard_map/ppermute | solution.py:239
  55.2 2.1 %collective-permute-start.16 = (f32[256,384]{1,0:T(8,128)S(1)}, f32[256,384]{1,0:T(8,128)S(1)}, u32[]{:S(2)}, u32[]{:S(2)}) collective-permute-start(f32[256,384]{1,0:T(8,128)S(1)} %product.12), channel_id=1, source_target_pairs={{0,4},{4,0},{8,12},{12,8},{16,20},{20,16},{24,28},{28,24},{1,5},{5... | collective-permute-start | bytes 1179656 | tf_op jit(solution)/shard_map/ppermute | solution.py:239
  57.9 1.2 %collective-permute-start.18 = (f32[8,128]{1,0:T(8,128)S(1)}, f32[8,128]{1,0:T(8,128)S(1)}, u32[]{:S(2)}, u32[]{:S(2)}) collective-permute-start(f32[8,128]{1,0:T(8,128)S(1)} %get-tuple-element.54), channel_id=1, source_target_pairs={{0,4},{4,0},{8,12},{12,8},{16,20},{20,16},{24,28},{28,24},{1,5},{5... | collective-permute-start | bytes 12296 | tf_op jit(solution)/shard_map/ppermute | solution.py:239
  59.2 4.9 %collective-permute-start.21 = (f32[8,128]{1,0:T(8,128)S(1)}, f32[8,128]{1,0:T(8,128)S(1)}, u32[]{:S(2)}, u32[]{:S(2)}) collective-permute-start(f32[8,128]{1,0:T(8,128)S(1)} %add.3.refs_0_), channel_id=1, source_target_pairs={{0,24},{4,28},{8,16},{12,20},{16,8},{20,12},{24,0},{28,4},{1,25},{... | collective-permute-start | bytes 12296 | tf_op jit(solution)/shard_map/ppermute | solution.py:239
  59.8 4.2 %collective-permute-start.20 = (f32[8,128]{1,0:T(8,128)S(1)}, f32[8,128]{1,0:T(8,128)S(1)}, u32[]{:S(2)}, u32[]{:S(2)}) collective-permute-start(f32[8,128]{1,0:T(8,128)S(1)} %add.3.refs_0_), channel_id=1, source_target_pairs={{0,16},{4,20},{8,24},{12,28},{16,0},{20,4},{24,8},{28,12},{1,17},{... | collective-permute-start | bytes 12296 | tf_op jit(solution)/shard_map/ppermute | solution.py:239
  61.5 3.6 %collective-permute-start.19 = (f32[8,128]{1,0:T(8,128)S(1)}, f32[8,128]{1,0:T(8,128)S(1)}, u32[]{:S(2)}, u32[]{:S(2)}) collective-permute-start(f32[8,128]{1,0:T(8,128)S(1)} %add.3.refs_0_), channel_id=1, source_target_pairs={{0,8},{4,12},{8,0},{12,4},{16,24},{20,28},{24,16},{28,20},{1,9},{5... | collective-permute-start | bytes 12296 | tf_op jit(solution)/shard_map/ppermute | solution.py:239
  (2 other events, 7.9 us)

commit v8 on v7

--- a/solution.py
+++ b/solution.py
@@ -12,6 +12,7 @@
 ANY = pl.BlockSpec(memory_space=pl.ANY)
 TAIL = 16
 ROWS_FIRST = (((0,), (0,)), ((), ()))
+UNIT = 10**9
 
 
 def on_device(
@@ -191,7 +192,7 @@
         copy.wait()
 
 
-def call(kernel, out_shape, *args, spaces=VMEM, out_spaces=VMEM, scratch=(), grant=40, flops=0, name=None):
+def call(kernel, out_shape, *args, spaces=VMEM, out_spaces=VMEM, scratch=(), flops=0, name=None):
     nbytes = sum(a.size * a.dtype.itemsize for a in jax.tree.leaves((args, out_shape)))
     return pl.pallas_call(
         kernel,
@@ -199,7 +200,7 @@
         in_specs=spaces if isinstance(spaces, list) else [spaces] * len(args),
         out_specs=jax.tree.map(lambda _: out_spaces, out_shape),
         scratch_shapes=scratch,
-        compiler_params=pltpu.CompilerParams(vmem_limit_bytes=grant * 2**20),
+        compiler_params=pltpu.CompilerParams(vmem_limit_bytes=40 * 2**20),
         cost_estimate=pl.CostEstimate(flops=flops, bytes_accessed=nbytes, transcendentals=0),
         name=name,
     )(*args)
@@ -294,39 +295,34 @@
     near, (to_x, to_y, to_xy) = cut[:owners], cut[owners:]
     from_x, from_y = across(to_x, 2), across(to_y, 4)
     near = [near[0]] + [along(near[shift], shift) for shift in range(1, owners)]
-    seen = tick(near[2], flops=2*10**9)
-    mid = pack(from_y, waits=[seen])
-    mid = [mid[0], along(mid[1], 1), along(mid[2], 2), along(mid[3], 3)]
-    late = tick(near[1], near[3], flops=2*10**9)
+    seen = tick(near[2], flops=2 * UNIT)
+    mid = pack(from_x, waits=[seen])
+    mid = [mid[0]] + [along(mid[shift], shift) for shift in range(1, owners)]
+    late = tick(near[1], near[3], flops=2 * UNIT)
     from_xy = across(after(to_xy, from_x, from_y, seen), 6)
-    by_x = across(after(hidden, from_x, from_y, near[2], late), 2)
-    by_y = across(after(hidden, from_x, from_y, near[2], late), 4)
-    far = pack(from_x, from_xy, waits=[late])
+    far = pack(from_y, from_xy, waits=[late])
     far = [far[0]] + [along(far[shift], shift) for shift in range(1, owners)]
-    left, right = after((by_x[:, : ff // 2], by_y[:, ff // 2 :]), by_x, by_y)
-    by_xy = across(left, 4), across(right, 2)
-
-    keep, give = slice(0, half), slice(half, part)
+    sent = after(hidden, from_x, from_y, near[2], late)
+    by_x, by_y = across(sent, 2), across(sent, 4)
+    by_xy = across(by_x[:, : ff // 2], 4), across(by_y[:, ff // 2 :], 2)
+
     def terms(packed, at, *shifts):
         return [(packed[shift], at, shift) for shift in shifts]
 
-    totals = {}
-    seen = tick(*mid[1:], flops=20*10**9)
-    for side in (give, keep):
-        groups = [((hidden,), terms(near, 0, 0, 1, 2, 3)), ((by_y,), terms(mid, 0, 0, 1, 2, 3))]
-        totals[side.start] = multiply(side, groups, waits=[seen])
-    seen = tick(far[1], far[2], *totals.values(), flops=5*10**9)
+    keep, give = slice(0, half), slice(half, part)
+    spans = slice(0, ff // 2), slice(ff // 2, ff)
     state_in = down_weight, first_moment, second_moment
-    for side in (give, keep):
-        groups = [((by_x,), terms(far, 0, 0, 1, 2)), (by_xy, terms(far, 1, 0, 1, 2))]
-        totals[side.start] = multiply(side, groups, totals[side.start], waits=[seen, *state_in])
-    seen = tick(far[3], *totals.values(), flops=5*10**9)
-    groups = [((by_x,), terms(far, 0, 3)), (by_xy, terms(far, 1, 3))]
-    spans = slice(0, ff // 2), slice(ff // 2, ff)
-    ready = [seen]
-    given = [multiply(give, groups, totals[give.start], span=span, waits=ready) for span in spans]
+    seen = tick(*mid[1:], flops=20 * UNIT)
+    groups = [((hidden,), terms(near, 0, 0, 1, 2, 3)), ((by_x,), terms(mid, 0, 0, 1, 2, 3))]
+    total = {side: multiply(side, groups, waits=[seen]) for side in (give, keep)}
+    seen = tick(far[1], far[2], *total.values(), flops=5 * UNIT)
+    groups = [((by_y,), terms(far, 0, 0, 1, 2)), (by_xy, terms(far, 1, 0, 1, 2))]
+    total = {side: multiply(side, groups, early, waits=[seen, *state_in]) for side, early in total.items()}
+    seen = tick(far[3], *total.values(), flops=5 * UNIT)
+    groups = [((by_y,), terms(far, 0, 3)), (by_xy, terms(far, 1, 3))]
+    given = [multiply(give, groups, total[give], span=span, waits=[seen]) for span in spans]
     other = [across(part, 1) for part in given]
-    kept = multiply(keep, groups, after(totals[keep.start], *given))
+    kept = multiply(keep, groups, after(total[keep], *given))
 
     state = jax.ShapeDtypeStruct((1, half, ff), f32)
     grads, updates, sums = [], [], []
@@ -372,7 +368,7 @@
         P("expert", "dp", None),
     )
     return jax.shard_map(
-        by_permutes if mesh.shape["dp"] == 8 else on_device,
+        by_permutes if (mesh.shape["dp"], mesh.shape["expert"]) == (8, 4) else on_device,
         mesh=mesh,
         in_specs=placed,
         out_specs=(P("expert", "dp", None), P("expert", "dp", None), P("expert", "dp", None)),

time: 66.3 us -> 66 us (level)
    ppermute x9, waiting for transfers between devices: 22.3 us -> 23.3 us  [along(): lax.ppermute(array, 'expert', [(d, (d + shift) % owners) for d in range(o...]
    ppermute x13, starting transfers between devices: 15.4 us -> 14.4 us  [across(): return lax.ppermute(array, 'dp', [(d, d ^ mask) for d in range(n_dp)])]
    ppermute x13, waiting for transfers between devices: 5.09 us -> 4.19 us  [across(): return lax.ppermute(array, 'dp', [(d, d ^ mask) for d in range(n_dp)])]
  transfers between devices with their start and end apart: 22 -> 22, of which waited for: 11 -> 9; matrix products, arithmetic and copies ran while one was open for 0% -> 0% of each run, Pallas kernels for 9% -> 9%
where the time goes in v8:
time: 66 us; the launch traced here: 65.8 us
  starting transfers between devices  27.6 us (42%)
  waiting for transfers between devices  27.5 us (42%)
  Pallas kernels  9.55 us (14%)
  between operations  0.86 us (1%)
    ppermute x9, waiting for transfers between devices, along(): lax.ppermute(array, 'expert', [(d, (d + shift) % owners) for d in range(o...  23.3 us
    ppermute x13, starting transfers between devices, across(): return lax.ppermute(array, 'dp', [(d, d ^ mask) for d in range(n_dp)])  14.4 us
    ppermute x9, starting transfers between devices, along(): lax.ppermute(array, 'expert', [(d, (d + shift) % owners) for d in range(o...  13.1 us
    pallas_call x19, Pallas kernels, call(): pl.pallas_call(kernel, out_shape=out_shape, in_specs=spaces if isinstance...  9.55 us
    ppermute x13, waiting for transfers between devices, across(): return lax.ppermute(array, 'dp', [(d, d ^ mask) for d in range(n_dp)])  4.19 us
  transfers between devices with their start and end apart: 22, of which 9 were waited for; matrix products, arithmetic and copies ran while one was open for 0% of the time, Pallas kernels for 9%

profile of v8, /device:TPU:0, one launch (start us, length us, event | category | flops | bytes accessed | tf_op | source)
XLA Modules:
  0.0 65.8 jit_solution(8311798403418799299)
XLA Ops:
  0.6 1.6 %cut.1 = (bf16[128,512]{1,0:T(8,128)(2,1)S(1)}, bf16[128,512]{1,0:T(8,128)(2,1)S(1)}, bf16[128,512]{1,0:T(8,128)(2,1)S(1)}, bf16[128,512]{1,0:T(8,128)(2,1)S(1)}...) custom-call(bf16[256,2048]{1,0:T(8,128)(2,1)} %cot_ref.1, ...), custom_call_target="tpu_custom_call" | custom-call | bytes 2411520 | tf_op jit(solution)/shard_map/cut/pallas_call | solution.py:197
  2.3 4.1 %collective-permute-start.2 = (bf16[128,512]{1,0:T(8,128)(2,1)S(1)}, bf16[128,512]{1,0:T(8,128)(2,1)S(1)}, u32[]{:S(2)}, u32[]{:S(2)}) collective-permute-start(bf16[128,512]{1,0:T(8,128)(2,1)S(1)} %get-tuple-element.33), channel_id=1, source_target_pairs={{0,2},{1,3},{2,0},{3,1},{4,6},{5,7},{6,4},{7,5},{8,10},{9,11},{10,... | collective-permute-start | bytes 393224 | tf_op jit(solution)/shard_map/ppermute | solution.py:243
  6.4 1.5 %collective-permute-start = (bf16[272,512]{1,0:T(8,128)(2,1)S(1)}, bf16[272,512]{1,0:T(8,128)(2,1)S(1)}, u32[]{:S(2)}, u32[]{:S(2)}) collective-permute-start(bf16[272,512]{1,0:T(8,128)(2,1)S(1)} %get-tuple-element.31), channel_id=1, source_target_pairs={{0,8},{4,12},{8,0},{12,4},{16,24},{20,28},{24,16},{28,20},{1,9},{5... | collective-permute-start | bytes 835592 | tf_op jit(solution)/shard_map/ppermute | solution.py:240
  7.9 1.5 %collective-permute-start.1 = (bf16[272,512]{1,0:T(8,128)(2,1)S(1)}, bf16[272,512]{1,0:T(8,128)(2,1)S(1)}, u32[]{:S(2)}, u32[]{:S(2)}) collective-permute-start(bf16[272,512]{1,0:T(8,128)(2,1)S(1)} %get-tuple-element.32), channel_id=1, source_target_pairs={{0,16},{4,20},{8,24},{12,28},{16,0},{20,4},{24,8},{28,12},{1,17},{... | collective-permute-start | bytes 835592 | tf_op jit(solution)/shard_map/ppermute | solution.py:240
  9.4 1.6 %collective-permute-start.3 = (bf16[128,512]{1,0:T(8,128)(2,1)S(1)}, bf16[128,512]{1,0:T(8,128)(2,1)S(1)}, u32[]{:S(2)}, u32[]{:S(2)}) collective-permute-start(bf16[128,512]{1,0:T(8,128)(2,1)S(1)} %get-tuple-element.34), channel_id=1, source_target_pairs={{0,1},{1,2},{2,3},{3,0},{4,5},{5,6},{6,7},{7,4},{8,9},{9,10},{10,1... | collective-permute-start | bytes 393224 | tf_op jit(solution)/shard_map/ppermute | solution.py:243
  11.0 2.2 %collective-permute-start.4 = (bf16[128,512]{1,0:T(8,128)(2,1)S(1)}, bf16[128,512]{1,0:T(8,128)(2,1)S(1)}, u32[]{:S(2)}, u32[]{:S(2)}) collective-permute-start(bf16[128,512]{1,0:T(8,128)(2,1)S(1)} %get-tuple-element.35), channel_id=1, source_target_pairs={{0,3},{1,0},{2,1},{3,2},{4,7},{5,4},{6,5},{7,6},{8,11},{9,8},{10,9... | collective-permute-start | bytes 393224 | tf_op jit(solution)/shard_map/ppermute | solution.py:243
  13.2 1.5 %collective-permute-done.2.refs_0_.refs_3_ = bf16[128,512]{1,0:T(8,128)(2,1)S(1)} collective-permute-done((bf16[128,512]{1,0:T(8,128)(2,1)S(1)}, bf16[128,512]{1,0:T(8,128)(2,1)S(1)}, u32[]{:S(2)}, u32[]{:S(2)}) %collective-permute-start.2) | collective-permute-done | bytes 131104 | tf_op jit(solution)/shard_map/ppermute | solution.py:243
  14.7 1.0 %collective-permute-done.1.refs_0_ = bf16[272,512]{1,0:T(8,128)(2,1)S(1)} collective-permute-done((bf16[272,512]{1,0:T(8,128)(2,1)S(1)}, bf16[272,512]{1,0:T(8,128)(2,1)S(1)}, u32[]{:S(2)}, u32[]{:S(2)}) %collective-permute-start.1) | collective-permute-done | bytes 278560 | tf_op jit(solution)/shard_map/ppermute | solution.py:240
  15.7 3.5 %collective-permute-start.6 = (bf16[272,512]{1,0:T(8,128)(2,1)S(1)}, bf16[272,512]{1,0:T(8,128)(2,1)S(1)}, u32[]{:S(2)}, u32[]{:S(2)}) collective-permute-start(bf16[272,512]{1,0:T(8,128)(2,1)S(1)} %get-tuple-element.38), channel_id=1, source_target_pairs={{0,24},{4,28},{8,16},{12,20},{16,8},{20,12},{24,0},{28,4},{1,25},{... | collective-permute-start | bytes 835592 | tf_op jit(solution)/shard_map/ppermute | solution.py:240
  19.6 3.0 %collective-permute-start.14 = (bf16[128,512]{1,0:T(8,128)(2,1)S(1)}, bf16[128,512]{1,0:T(8,128)(2,1)S(1)}, u32[]{:S(2)}, u32[]{:S(2)}) collective-permute-start(bf16[128,512]{1,0:T(8,128)(2,1)S(1)} %get-tuple-element.46), channel_id=1, source_target_pairs={{0,2},{1,3},{2,0},{3,1},{4,6},{5,7},{6,4},{7,5},{8,10},{9,11},{10,... | collective-permute-start | bytes 393224 | tf_op jit(solution)/shard_map/ppermute | solution.py:243
  22.6 0.9 %collective-permute-start.15 = (bf16[128,512]{1,0:T(8,128)(2,1)S(1)}, bf16[128,512]{1,0:T(8,128)(2,1)S(1)}, u32[]{:S(2)}, u32[]{:S(2)}) collective-permute-start(bf16[128,512]{1,0:T(8,128)(2,1)S(1)} %get-tuple-element.47), channel_id=1, source_target_pairs={{0,3},{1,0},{2,1},{3,2},{4,7},{5,4},{6,5},{7,6},{8,11},{9,8},{10,9... | collective-permute-start | bytes 393224 | tf_op jit(solution)/shard_map/ppermute | solution.py:243
  24.0 1.0 %collective-permute-done.6.refs_1_ = bf16[272,512]{1,0:T(8,128)(2,1)S(1)} collective-permute-done((bf16[272,512]{1,0:T(8,128)(2,1)S(1)}, bf16[272,512]{1,0:T(8,128)(2,1)S(1)}, u32[]{:S(2)}, u32[]{:S(2)}) %collective-permute-start.6) | collective-permute-done | bytes 278560 | tf_op jit(solution)/shard_map/ppermute | solution.py:240
  25.0 1.2 %collective-permute-start.5 = (bf16[512,768]{1,0:T(8,128)(2,1)S(1)}, bf16[512,768]{1,0:T(8,128)(2,1)S(1)}, u32[]{:S(2)}, u32[]{:S(2)}) collective-permute-start(bf16[512,768]{1,0:T(8,128)(2,1)S(1)} %bitcast.5), channel_id=1, source_target_pairs={{0,16},{4,20},{8,24},{12,28},{16,0},{20,4},{24,8},{28,12},{1,17},{... | collective-permute-start | bytes 2359304 | tf_op jit(solution)/shard_map/ppermute | solution.py:240
  26.7 1.2 %collective-permute-start.11 = (bf16[256,512]{1,0:T(8,128)(2,1)S(1)}, bf16[256,512]{1,0:T(8,128)(2,1)S(1)}, u32[]{:S(2)}, u32[]{:S(2)}) collective-permute-start(bf16[256,512]{1,0:T(8,128)(2,1)S(1)} %get-tuple-element.41), channel_id=1, source_target_pairs={{0,1},{1,2},{2,3},{3,0},{4,5},{5,6},{6,7},{7,4},{8,9},{9,10},{10,1... | collective-permute-start | bytes 786440 | tf_op jit(solution)/shard_map/ppermute | solution.py:243
  27.9 13.3 %collective-permute-done.14.refs_1_.refs_8_ = bf16[128,512]{1,0:T(8,128)(2,1)S(1)} collective-permute-done((bf16[128,512]{1,0:T(8,128)(2,1)S(1)}, bf16[128,512]{1,0:T(8,128)(2,1)S(1)}, u32[]{:S(2)}, u32[]{:S(2)}) %collective-permute-start.14) | collective-permute-done | bytes 131104 | tf_op jit(solution)/shard_map/ppermute | solution.py:243
  41.8 1.5 %collective-permute-start.10 = (bf16[512,384]{1,0:T(8,128)(2,1)S(1)}, bf16[512,384]{1,0:T(8,128)(2,1)S(1)}, u32[]{:S(2)}, u32[]{:S(2)}) collective-permute-start(bf16[512,384]{1,0:T(8,128)(2,1)S(1)} %slice.9), channel_id=1, source_target_pairs={{0,8},{4,12},{8,0},{12,4},{16,24},{20,28},{24,16},{28,20},{1,9},{5... | collective-permute-start | bytes 1179656 | tf_op jit(solution)/shard_map/ppermute | solution.py:240
  44.6 6.8 %collective-permute-done.12.refs_1_.refs_3_ = bf16[256,512]{1,0:T(8,128)(2,1)S(1)} collective-permute-done((bf16[256,512]{1,0:T(8,128)(2,1)S(1)}, bf16[256,512]{1,0:T(8,128)(2,1)S(1)}, u32[]{:S(2)}, u32[]{:S(2)}) %collective-permute-start.12) | collective-permute-done | bytes 262176 | tf_op jit(solution)/shard_map/ppermute | solution.py:243
  52.8 1.8 %collective-permute-done.7.refs_0_.refs_1_ = bf16[256,512]{1,0:T(8,128)(2,1)S(1)} collective-permute-done((bf16[256,512]{1,0:T(8,128)(2,1)S(1)}, bf16[256,512]{1,0:T(8,128)(2,1)S(1)}, u32[]{:S(2)}, u32[]{:S(2)}) %collective-permute-start.7) | collective-permute-done | bytes 262176 | tf_op jit(solution)/shard_map/ppermute | solution.py:243
  58.2 1.0 %collective-permute-done.18 = f32[8,128]{1,0:T(8,128)S(1)} collective-permute-done((f32[8,128]{1,0:T(8,128)S(1)}, f32[8,128]{1,0:T(8,128)S(1)}, u32[]{:S(2)}, u32[]{:S(2)}) %collective-permute-start.18) | collective-permute-done | bytes 4128 | tf_op jit(solution)/shard_map/ppermute | solution.py:240
  59.3 1.9 %collective-permute-start.20 = (f32[8,128]{1,0:T(8,128)S(1)}, f32[8,128]{1,0:T(8,128)S(1)}, u32[]{:S(2)}, u32[]{:S(2)}) collective-permute-start(f32[8,128]{1,0:T(8,128)S(1)} %add.3.refs_0_), channel_id=1, source_target_pairs={{0,16},{4,20},{8,24},{12,28},{16,0},{20,4},{24,8},{28,12},{1,17},{... | collective-permute-start | bytes 12296 | tf_op jit(solution)/shard_map/ppermute | solution.py:240
  61.2 1.4 %collective-permute-start.19 = (f32[8,128]{1,0:T(8,128)S(1)}, f32[8,128]{1,0:T(8,128)S(1)}, u32[]{:S(2)}, u32[]{:S(2)}) collective-permute-start(f32[8,128]{1,0:T(8,128)S(1)} %add.3.refs_0_), channel_id=1, source_target_pairs={{0,8},{4,12},{8,0},{12,4},{16,24},{20,28},{24,16},{28,20},{1,9},{5... | collective-permute-start | bytes 12296 | tf_op jit(solution)/shard_map/ppermute | solution.py:240
  62.7 1.4 %moment.1 = (f32[1,256,768]{2,1,0:T(8,128)}, f32[1,256,768]{2,1,0:T(8,128)}) custom-call(f32[256,384]{1,0:T(8,128)S(1)} %get-tuple-element.55.left_ref, f32[256,384]{1,0:T(8,128)S(1)} %get-tuple-element.56.right_ref, f32[1,256,768]{2,1,0:T(8,128)S(1)} %copy-done, f32[1,256,768]{2,1,0:T(8,128)S(1)} %copy-done.1), custom_call_target="tpu_custom_call" | custom-call | bytes 3932160 | tf_op jit(solution)/shard_map/moment/pallas_call | solution.py:197
  64.1 0.8 %collective-permute-done.19.refs_1_ = f32[8,128]{1,0:T(8,128)S(1)} collective-permute-done((f32[8,128]{1,0:T(8,128)S(1)}, f32[8,128]{1,0:T(8,128)S(1)}, u32[]{:S(2)}, u32[]{:S(2)}) %collective-permute-start.19) | collective-permute-done | bytes 4128 | tf_op jit(solution)/shard_map/ppermute | solution.py:240
  64.8 1.0 %weight.1 = f32[1,256,768]{2,1,0:T(8,128)} custom-call(f32[8,128]{1,0:T(8,128)S(1)} %add.3.refs_0_, f32[8,128]{1,0:T(8,128)S(1)} %collective-permute-done.19.refs_1_, f32[8,128]{1,0:T(8,128)S(1)} %collective-permute-done.20.refs_2_, f32[8,128]{1,0:T(8,128)S(1)} %collective-permute-done.21.refs_3_, f32[1,256,768]{2,1,0:T(8,128)S(1)} %copy-done.2, ...), custom_call_target="tpu_custom_call" | custom-call | bytes 2375680 | tf_op jit(solution)/shard_map/weight/pallas_call | solution.py:197
  (50 shorter events, 8.3 us)
Async XLA Ops:
  2.3 12.4 %collective-permute-start.2 = (bf16[128,512]{1,0:T(8,128)(2,1)S(1)}, bf16[128,512]{1,0:T(8,128)(2,1)S(1)}, u32[]{:S(2)}, u32[]{:S(2)}) collective-permute-start(bf16[128,512]{1,0:T(8,128)(2,1)S(1)} %get-tuple-element.33), channel_id=1, source_target_pairs={{0,2},{1,3},{2,0},{3,1},{4,6},{5,7},{6,4},{7,5},{8,10},{9,11},{10,... | collective-permute-start | bytes 393224 | tf_op jit(solution)/shard_map/ppermute | solution.py:243
  6.4 8.3 %collective-permute-start = (bf16[272,512]{1,0:T(8,128)(2,1)S(1)}, bf16[272,512]{1,0:T(8,128)(2,1)S(1)}, u32[]{:S(2)}, u32[]{:S(2)}) collective-permute-start(bf16[272,512]{1,0:T(8,128)(2,1)S(1)} %get-tuple-element.31), channel_id=1, source_target_pairs={{0,8},{4,12},{8,0},{12,4},{16,24},{20,28},{24,16},{28,20},{1,9},{5... | collective-permute-start | bytes 835592 | tf_op jit(solution)/shard_map/ppermute | solution.py:240
  7.9 7.8 %collective-permute-start.1 = (bf16[272,512]{1,0:T(8,128)(2,1)S(1)}, bf16[272,512]{1,0:T(8,128)(2,1)S(1)}, u32[]{:S(2)}, u32[]{:S(2)}) collective-permute-start(bf16[272,512]{1,0:T(8,128)(2,1)S(1)} %get-tuple-element.32), channel_id=1, source_target_pairs={{0,16},{4,20},{8,24},{12,28},{16,0},{20,4},{24,8},{28,12},{1,17},{... | collective-permute-start | bytes 835592 | tf_op jit(solution)/shard_map/ppermute | solution.py:240
  9.4 13.2 %collective-permute-start.3 = (bf16[128,512]{1,0:T(8,128)(2,1)S(1)}, bf16[128,512]{1,0:T(8,128)(2,1)S(1)}, u32[]{:S(2)}, u32[]{:S(2)}) collective-permute-start(bf16[128,512]{1,0:T(8,128)(2,1)S(1)} %get-tuple-element.34), channel_id=1, source_target_pairs={{0,1},{1,2},{2,3},{3,0},{4,5},{5,6},{6,7},{7,4},{8,9},{9,10},{10,1... | collective-permute-start | bytes 393224 | tf_op jit(solution)/shard_map/ppermute | solution.py:243
  11.0 12.5 %collective-permute-start.4 = (bf16[128,512]{1,0:T(8,128)(2,1)S(1)}, bf16[128,512]{1,0:T(8,128)(2,1)S(1)}, u32[]{:S(2)}, u32[]{:S(2)}) collective-permute-start(bf16[128,512]{1,0:T(8,128)(2,1)S(1)} %get-tuple-element.35), channel_id=1, source_target_pairs={{0,3},{1,0},{2,1},{3,2},{4,7},{5,4},{6,5},{7,6},{8,11},{9,8},{10,9... | collective-permute-start | bytes 393224 | tf_op jit(solution)/shard_map/ppermute | solution.py:243
  15.7 9.3 %collective-permute-start.6 = (bf16[272,512]{1,0:T(8,128)(2,1)S(1)}, bf16[272,512]{1,0:T(8,128)(2,1)S(1)}, u32[]{:S(2)}, u32[]{:S(2)}) collective-permute-start(bf16[272,512]{1,0:T(8,128)(2,1)S(1)} %get-tuple-element.38), channel_id=1, source_target_pairs={{0,24},{4,28},{8,16},{12,20},{16,8},{20,12},{24,0},{28,4},{1,25},{... | collective-permute-start | bytes 835592 | tf_op jit(solution)/shard_map/ppermute | solution.py:240
  19.5 7.1 %collective-permute-start.13 = (bf16[128,512]{1,0:T(8,128)(2,1)S(1)}, bf16[128,512]{1,0:T(8,128)(2,1)S(1)}, u32[]{:S(2)}, u32[]{:S(2)}) collective-permute-start(bf16[128,512]{1,0:T(8,128)(2,1)S(1)} %get-tuple-element.45), channel_id=1, source_target_pairs={{0,1},{1,2},{2,3},{3,0},{4,5},{5,6},{6,7},{7,4},{8,9},{9,10},{10,1... | collective-permute-start | bytes 393224 | tf_op jit(solution)/shard_map/ppermute | solution.py:243
  19.6 21.6 %collective-permute-start.14 = (bf16[128,512]{1,0:T(8,128)(2,1)S(1)}, bf16[128,512]{1,0:T(8,128)(2,1)S(1)}, u32[]{:S(2)}, u32[]{:S(2)}) collective-permute-start(bf16[128,512]{1,0:T(8,128)(2,1)S(1)} %get-tuple-element.46), channel_id=1, source_target_pairs={{0,2},{1,3},{2,0},{3,1},{4,6},{5,7},{6,4},{7,5},{8,10},{9,11},{10,... | collective-permute-start | bytes 393224 | tf_op jit(solution)/shard_map/ppermute | solution.py:243
  22.6 18.5 %collective-permute-start.15 = (bf16[128,512]{1,0:T(8,128)(2,1)S(1)}, bf16[128,512]{1,0:T(8,128)(2,1)S(1)}, u32[]{:S(2)}, u32[]{:S(2)}) collective-permute-start(bf16[128,512]{1,0:T(8,128)(2,1)S(1)} %get-tuple-element.47), channel_id=1, source_target_pairs={{0,3},{1,0},{2,1},{3,2},{4,7},{5,4},{6,5},{7,6},{8,11},{9,8},{10,9... | collective-permute-start | bytes 393224 | tf_op jit(solution)/shard_map/ppermute | solution.py:243
  23.8 17.5 %collective-permute-start.8 = (bf16[512,768]{1,0:T(8,128)(2,1)S(1)}, bf16[512,768]{1,0:T(8,128)(2,1)S(1)}, u32[]{:S(2)}, u32[]{:S(2)}) collective-permute-start(bf16[512,768]{1,0:T(8,128)(2,1)S(1)} %bitcast.4), channel_id=1, source_target_pairs={{0,8},{4,12},{8,0},{12,4},{16,24},{20,28},{24,16},{28,20},{1,9},{5... | collective-permute-start | bytes 2359304 | tf_op jit(solution)/shard_map/ppermute | solution.py:240
  25.0 16.7 %collective-permute-start.5 = (bf16[512,768]{1,0:T(8,128)(2,1)S(1)}, bf16[512,768]{1,0:T(8,128)(2,1)S(1)}, u32[]{:S(2)}, u32[]{:S(2)}) collective-permute-start(bf16[512,768]{1,0:T(8,128)(2,1)S(1)} %bitcast.5), channel_id=1, source_target_pairs={{0,16},{4,20},{8,24},{12,28},{16,0},{20,4},{24,8},{28,12},{1,17},{... | collective-permute-start | bytes 2359304 | tf_op jit(solution)/shard_map/ppermute | solution.py:240
  26.7 17.9 %collective-permute-start.11 = (bf16[256,512]{1,0:T(8,128)(2,1)S(1)}, bf16[256,512]{1,0:T(8,128)(2,1)S(1)}, u32[]{:S(2)}, u32[]{:S(2)}) collective-permute-start(bf16[256,512]{1,0:T(8,128)(2,1)S(1)} %get-tuple-element.41), channel_id=1, source_target_pairs={{0,1},{1,2},{2,3},{3,0},{4,5},{5,6},{6,7},{7,4},{8,9},{9,10},{10,1... | collective-permute-start | bytes 786440 | tf_op jit(solution)/shard_map/ppermute | solution.py:243
  41.2 10.2 %collective-permute-start.12 = (bf16[256,512]{1,0:T(8,128)(2,1)S(1)}, bf16[256,512]{1,0:T(8,128)(2,1)S(1)}, u32[]{:S(2)}, u32[]{:S(2)}) collective-permute-start(bf16[256,512]{1,0:T(8,128)(2,1)S(1)} %get-tuple-element.42), channel_id=1, source_target_pairs={{0,2},{1,3},{2,0},{3,1},{4,6},{5,7},{6,4},{7,5},{8,10},{9,11},{10,... | collective-permute-start | bytes 786440 | tf_op jit(solution)/shard_map/ppermute | solution.py:243
  41.2 13.4 %collective-permute-start.7 = (bf16[256,512]{1,0:T(8,128)(2,1)S(1)}, bf16[256,512]{1,0:T(8,128)(2,1)S(1)}, u32[]{:S(2)}, u32[]{:S(2)}) collective-permute-start(bf16[256,512]{1,0:T(8,128)(2,1)S(1)} %get-tuple-element.39), channel_id=1, source_target_pairs={{0,3},{1,0},{2,1},{3,2},{4,7},{5,4},{6,5},{7,6},{8,11},{9,8},{10,9... | collective-permute-start | bytes 786440 | tf_op jit(solution)/shard_map/ppermute | solution.py:243
  41.3 10.1 %collective-permute-start.9 = (bf16[512,384]{1,0:T(8,128)(2,1)S(1)}, bf16[512,384]{1,0:T(8,128)(2,1)S(1)}, u32[]{:S(2)}, u32[]{:S(2)}) collective-permute-start(bf16[512,384]{1,0:T(8,128)(2,1)S(1)} %slice.8), channel_id=1, source_target_pairs={{0,16},{4,20},{8,24},{12,28},{16,0},{20,4},{24,8},{28,12},{1,17},{... | collective-permute-start | bytes 1179656 | tf_op jit(solution)/shard_map/ppermute | solution.py:240
  41.8 9.6 %collective-permute-start.10 = (bf16[512,384]{1,0:T(8,128)(2,1)S(1)}, bf16[512,384]{1,0:T(8,128)(2,1)S(1)}, u32[]{:S(2)}, u32[]{:S(2)}) collective-permute-start(bf16[512,384]{1,0:T(8,128)(2,1)S(1)} %slice.9), channel_id=1, source_target_pairs={{0,8},{4,12},{8,0},{12,4},{16,24},{20,28},{24,16},{28,20},{1,9},{5... | collective-permute-start | bytes 1179656 | tf_op jit(solution)/shard_map/ppermute | solution.py:240
  44.6 6.8 %copy-start = (f32[1,256,768]{2,1,0:T(8,128)S(1)}, f32[1,256,768]{2,1,0:T(8,128)}, u32[]{:S(2)}) copy-start(f32[1,256,768]{2,1,0:T(8,128)} %first_ref.5) | copy-start | bytes 2359300
  44.6 6.8 %copy-start.1 = (f32[1,256,768]{2,1,0:T(8,128)S(1)}, f32[1,256,768]{2,1,0:T(8,128)}, u32[]{:S(2)}) copy-start(f32[1,256,768]{2,1,0:T(8,128)} %second_ref.5) | copy-start | bytes 2359300
  54.9 1.8 %collective-permute-start.17 = (f32[256,384]{1,0:T(8,128)S(1)}, f32[256,384]{1,0:T(8,128)S(1)}, u32[]{:S(2)}, u32[]{:S(2)}) collective-permute-start(f32[256,384]{1,0:T(8,128)S(1)} %product.11), channel_id=1, source_target_pairs={{0,4},{4,0},{8,12},{12,8},{16,20},{20,16},{24,28},{28,24},{1,5},{5... | collective-permute-start | bytes 1179656 | tf_op jit(solution)/shard_map/ppermute | solution.py:240
  55.2 2.1 %collective-permute-start.16 = (f32[256,384]{1,0:T(8,128)S(1)}, f32[256,384]{1,0:T(8,128)S(1)}, u32[]{:S(2)}, u32[]{:S(2)}) collective-permute-start(f32[256,384]{1,0:T(8,128)S(1)} %product.12), channel_id=1, source_target_pairs={{0,4},{4,0},{8,12},{12,8},{16,20},{20,16},{24,28},{28,24},{1,5},{5... | collective-permute-start | bytes 1179656 | tf_op jit(solution)/shard_map/ppermute | solution.py:240
  57.9 1.2 %collective-permute-start.18 = (f32[8,128]{1,0:T(8,128)S(1)}, f32[8,128]{1,0:T(8,128)S(1)}, u32[]{:S(2)}, u32[]{:S(2)}) collective-permute-start(f32[8,128]{1,0:T(8,128)S(1)} %get-tuple-element.50), channel_id=1, source_target_pairs={{0,4},{4,0},{8,12},{12,8},{16,20},{20,16},{24,28},{28,24},{1,5},{5... | collective-permute-start | bytes 12296 | tf_op jit(solution)/shard_map/ppermute | solution.py:240
  59.2 4.9 %collective-permute-start.21 = (f32[8,128]{1,0:T(8,128)S(1)}, f32[8,128]{1,0:T(8,128)S(1)}, u32[]{:S(2)}, u32[]{:S(2)}) collective-permute-start(f32[8,128]{1,0:T(8,128)S(1)} %add.3.refs_0_), channel_id=1, source_target_pairs={{0,24},{4,28},{8,16},{12,20},{16,8},{20,12},{24,0},{28,4},{1,25},{... | collective-permute-start | bytes 12296 | tf_op jit(solution)/shard_map/ppermute | solution.py:240
  59.3 4.8 %collective-permute-start.20 = (f32[8,128]{1,0:T(8,128)S(1)}, f32[8,128]{1,0:T(8,128)S(1)}, u32[]{:S(2)}, u32[]{:S(2)}) collective-permute-start(f32[8,128]{1,0:T(8,128)S(1)} %add.3.refs_0_), channel_id=1, source_target_pairs={{0,16},{4,20},{8,24},{12,28},{16,0},{20,4},{24,8},{28,12},{1,17},{... | collective-permute-start | bytes 12296 | tf_op jit(solution)/shard_map/ppermute | solution.py:240
  61.2 3.6 %collective-permute-start.19 = (f32[8,128]{1,0:T(8,128)S(1)}, f32[8,128]{1,0:T(8,128)S(1)}, u32[]{:S(2)}, u32[]{:S(2)}) collective-permute-start(f32[8,128]{1,0:T(8,128)S(1)} %add.3.refs_0_), channel_id=1, source_target_pairs={{0,8},{4,12},{8,0},{12,4},{16,24},{20,28},{24,16},{28,20},{1,9},{5... | collective-permute-start | bytes 12296 | tf_op jit(solution)/shard_map/ppermute | solution.py:240
  (2 other events, 7.9 us)

commit v9 on v8

--- a/solution.py
+++ b/solution.py
@@ -315,11 +315,11 @@
     seen = tick(*mid[1:], flops=20 * UNIT)
     groups = [((hidden,), terms(near, 0, 0, 1, 2, 3)), ((by_x,), terms(mid, 0, 0, 1, 2, 3))]
     total = {side: multiply(side, groups, waits=[seen]) for side in (give, keep)}
-    seen = tick(far[1], far[2], *total.values(), flops=5 * UNIT)
-    groups = [((by_y,), terms(far, 0, 0, 1, 2)), (by_xy, terms(far, 1, 0, 1, 2))]
+    seen = tick(far[1], far[3], *total.values(), flops=5 * UNIT)
+    groups = [((by_y,), terms(far, 0, 0, 1, 3)), (by_xy, terms(far, 1, 0, 1, 3))]
     total = {side: multiply(side, groups, early, waits=[seen, *state_in]) for side, early in total.items()}
-    seen = tick(far[3], *total.values(), flops=5 * UNIT)
-    groups = [((by_y,), terms(far, 0, 3)), (by_xy, terms(far, 1, 3))]
+    seen = tick(far[2], *total.values(), flops=5 * UNIT)
+    groups = [((by_y,), terms(far, 0, 2)), (by_xy, terms(far, 1, 2))]
     given = [multiply(give, groups, total[give], span=span, waits=[seen]) for span in spans]
     other = [across(part, 1) for part in given]
     kept = multiply(keep, groups, after(total[keep], *given))

time: 66 us -> 66.1 us (level)
  starting transfers between devices: 27.6 us -> 32.1 us
  waiting for transfers between devices: 27.5 us -> 23 us
    ppermute x9, waiting for transfers between devices: 23.3 us -> 9.36 us  [along(): lax.ppermute(array, 'expert', [(d, (d + shift) % owners) for d in range(o...]
    ppermute x13, waiting for transfers between devices: 4.19 us -> 13.7 us  [across(): return lax.ppermute(array, 'dp', [(d, d ^ mask) for d in range(n_dp)])]
    ppermute x9, starting transfers between devices: 13.1 us -> 17.5 us  [along(): lax.ppermute(array, 'expert', [(d, (d + shift) % owners) for d in range(o...]
  transfers between devices with their start and end apart: 22 -> 22, of which waited for: 9 -> 11; matrix products, arithmetic and copies ran while one was open for 0% -> 0% of each run, Pallas kernels for 9% -> 9%
where the time goes in v9:
time: 66.1 us; the launch traced here: 65.9 us
  starting transfers between devices  32.1 us (49%)
  waiting for transfers between devices  23 us (35%)
  Pallas kernels  9.55 us (14%)
  between operations  0.84 us (1%)
    ppermute x9, starting transfers between devices, along(): lax.ppermute(array, 'expert', [(d, (d + shift) % owners) for d in range(o...  17.5 us
    ppermute x13, starting transfers between devices, across(): return lax.ppermute(array, 'dp', [(d, d ^ mask) for d in range(n_dp)])  14.6 us
    ppermute x13, waiting for transfers between devices, across(): return lax.ppermute(array, 'dp', [(d, d ^ mask) for d in range(n_dp)])  13.7 us
    pallas_call x19, Pallas kernels, call(): pl.pallas_call(kernel, out_shape=out_shape, in_specs=spaces if isinstance...  9.55 us
    ppermute x9, waiting for transfers between devices, along(): lax.ppermute(array, 'expert', [(d, (d + shift) % owners) for d in range(o...  9.36 us
  transfers between devices with their start and end apart: 22, of which 11 were waited for; matrix products, arithmetic and copies ran while one was open for 0% of the time, Pallas kernels for 9%

profile of v9, /device:TPU:0, one launch (start us, length us, event | category | flops | bytes accessed | tf_op | source)
XLA Modules:
  0.0 65.9 jit_solution(12783590605075676491)
XLA Ops:
  0.6 1.6 %cut.1 = (bf16[128,512]{1,0:T(8,128)(2,1)S(1)}, bf16[128,512]{1,0:T(8,128)(2,1)S(1)}, bf16[128,512]{1,0:T(8,128)(2,1)S(1)}, bf16[128,512]{1,0:T(8,128)(2,1)S(1)}...) custom-call(bf16[256,2048]{1,0:T(8,128)(2,1)} %cot_ref.1, ...), custom_call_target="tpu_custom_call" | custom-call | bytes 2411520 | tf_op jit(solution)/shard_map/cut/pallas_call | solution.py:197
  2.3 4.1 %collective-permute-start.2 = (bf16[128,512]{1,0:T(8,128)(2,1)S(1)}, bf16[128,512]{1,0:T(8,128)(2,1)S(1)}, u32[]{:S(2)}, u32[]{:S(2)}) collective-permute-start(bf16[128,512]{1,0:T(8,128)(2,1)S(1)} %get-tuple-element.33), channel_id=1, source_target_pairs={{0,2},{1,3},{2,0},{3,1},{4,6},{5,7},{6,4},{7,5},{8,10},{9,11},{10,... | collective-permute-start | bytes 393224 | tf_op jit(solution)/shard_map/ppermute | solution.py:243
  6.4 1.5 %collective-permute-start = (bf16[272,512]{1,0:T(8,128)(2,1)S(1)}, bf16[272,512]{1,0:T(8,128)(2,1)S(1)}, u32[]{:S(2)}, u32[]{:S(2)}) collective-permute-start(bf16[272,512]{1,0:T(8,128)(2,1)S(1)} %get-tuple-element.31), channel_id=1, source_target_pairs={{0,8},{4,12},{8,0},{12,4},{16,24},{20,28},{24,16},{28,20},{1,9},{5... | collective-permute-start | bytes 835592 | tf_op jit(solution)/shard_map/ppermute | solution.py:240
  7.9 1.5 %collective-permute-start.1 = (bf16[272,512]{1,0:T(8,128)(2,1)S(1)}, bf16[272,512]{1,0:T(8,128)(2,1)S(1)}, u32[]{:S(2)}, u32[]{:S(2)}) collective-permute-start(bf16[272,512]{1,0:T(8,128)(2,1)S(1)} %get-tuple-element.32), channel_id=1, source_target_pairs={{0,16},{4,20},{8,24},{12,28},{16,0},{20,4},{24,8},{28,12},{1,17},{... | collective-permute-start | bytes 835592 | tf_op jit(solution)/shard_map/ppermute | solution.py:240
  9.4 1.6 %collective-permute-start.3 = (bf16[128,512]{1,0:T(8,128)(2,1)S(1)}, bf16[128,512]{1,0:T(8,128)(2,1)S(1)}, u32[]{:S(2)}, u32[]{:S(2)}) collective-permute-start(bf16[128,512]{1,0:T(8,128)(2,1)S(1)} %get-tuple-element.34), channel_id=1, source_target_pairs={{0,1},{1,2},{2,3},{3,0},{4,5},{5,6},{6,7},{7,4},{8,9},{9,10},{10,1... | collective-permute-start | bytes 393224 | tf_op jit(solution)/shard_map/ppermute | solution.py:243
  11.0 2.2 %collective-permute-start.4 = (bf16[128,512]{1,0:T(8,128)(2,1)S(1)}, bf16[128,512]{1,0:T(8,128)(2,1)S(1)}, u32[]{:S(2)}, u32[]{:S(2)}) collective-permute-start(bf16[128,512]{1,0:T(8,128)(2,1)S(1)} %get-tuple-element.35), channel_id=1, source_target_pairs={{0,3},{1,0},{2,1},{3,2},{4,7},{5,4},{6,5},{7,6},{8,11},{9,8},{10,9... | collective-permute-start | bytes 393224 | tf_op jit(solution)/shard_map/ppermute | solution.py:243
  13.2 1.5 %collective-permute-done.2.refs_0_.refs_3_ = bf16[128,512]{1,0:T(8,128)(2,1)S(1)} collective-permute-done((bf16[128,512]{1,0:T(8,128)(2,1)S(1)}, bf16[128,512]{1,0:T(8,128)(2,1)S(1)}, u32[]{:S(2)}, u32[]{:S(2)}) %collective-permute-start.2) | collective-permute-done | bytes 131104 | tf_op jit(solution)/shard_map/ppermute | solution.py:243
  14.7 1.0 %collective-permute-done.1.refs_0_ = bf16[272,512]{1,0:T(8,128)(2,1)S(1)} collective-permute-done((bf16[272,512]{1,0:T(8,128)(2,1)S(1)}, bf16[272,512]{1,0:T(8,128)(2,1)S(1)}, u32[]{:S(2)}, u32[]{:S(2)}) %collective-permute-start.1) | collective-permute-done | bytes 278560 | tf_op jit(solution)/shard_map/ppermute | solution.py:240
  15.7 3.5 %collective-permute-start.6 = (bf16[272,512]{1,0:T(8,128)(2,1)S(1)}, bf16[272,512]{1,0:T(8,128)(2,1)S(1)}, u32[]{:S(2)}, u32[]{:S(2)}) collective-permute-start(bf16[272,512]{1,0:T(8,128)(2,1)S(1)} %get-tuple-element.38), channel_id=1, source_target_pairs={{0,24},{4,28},{8,16},{12,20},{16,8},{20,12},{24,0},{28,4},{1,25},{... | collective-permute-start | bytes 835592 | tf_op jit(solution)/shard_map/ppermute | solution.py:240
  19.6 3.0 %collective-permute-start.14 = (bf16[128,512]{1,0:T(8,128)(2,1)S(1)}, bf16[128,512]{1,0:T(8,128)(2,1)S(1)}, u32[]{:S(2)}, u32[]{:S(2)}) collective-permute-start(bf16[128,512]{1,0:T(8,128)(2,1)S(1)} %get-tuple-element.46), channel_id=1, source_target_pairs={{0,2},{1,3},{2,0},{3,1},{4,6},{5,7},{6,4},{7,5},{8,10},{9,11},{10,... | collective-permute-start | bytes 393224 | tf_op jit(solution)/shard_map/ppermute | solution.py:243
  25.0 1.2 %collective-permute-start.5 = (bf16[512,768]{1,0:T(8,128)(2,1)S(1)}, bf16[512,768]{1,0:T(8,128)(2,1)S(1)}, u32[]{:S(2)}, u32[]{:S(2)}) collective-permute-start(bf16[512,768]{1,0:T(8,128)(2,1)S(1)} %bitcast.5), channel_id=1, source_target_pairs={{0,16},{4,20},{8,24},{12,28},{16,0},{20,4},{24,8},{28,12},{1,17},{... | collective-permute-start | bytes 2359304 | tf_op jit(solution)/shard_map/ppermute | solution.py:240
  26.7 1.2 %collective-permute-start.11 = (bf16[256,512]{1,0:T(8,128)(2,1)S(1)}, bf16[256,512]{1,0:T(8,128)(2,1)S(1)}, u32[]{:S(2)}, u32[]{:S(2)}) collective-permute-start(bf16[256,512]{1,0:T(8,128)(2,1)S(1)} %get-tuple-element.41), channel_id=1, source_target_pairs={{0,1},{1,2},{2,3},{3,0},{4,5},{5,6},{6,7},{7,4},{8,9},{9,10},{10,1... | collective-permute-start | bytes 786440 | tf_op jit(solution)/shard_map/ppermute | solution.py:243
  27.9 5.4 %collective-permute-done.14.refs_1_.refs_8_ = bf16[128,512]{1,0:T(8,128)(2,1)S(1)} collective-permute-done((bf16[128,512]{1,0:T(8,128)(2,1)S(1)}, bf16[128,512]{1,0:T(8,128)(2,1)S(1)}, u32[]{:S(2)}, u32[]{:S(2)}) %collective-permute-start.14) | collective-permute-done | bytes 131104 | tf_op jit(solution)/shard_map/ppermute | solution.py:243
  33.3 1.5 %collective-permute-start.12 = (bf16[256,512]{1,0:T(8,128)(2,1)S(1)}, bf16[256,512]{1,0:T(8,128)(2,1)S(1)}, u32[]{:S(2)}, u32[]{:S(2)}) collective-permute-start(bf16[256,512]{1,0:T(8,128)(2,1)S(1)} %get-tuple-element.42), channel_id=1, source_target_pairs={{0,3},{1,0},{2,1},{3,2},{4,7},{5,4},{6,5},{7,6},{8,11},{9,8},{10,9... | collective-permute-start | bytes 786440 | tf_op jit(solution)/shard_map/ppermute | solution.py:243
  34.8 2.9 %collective-permute-start.7 = (bf16[256,512]{1,0:T(8,128)(2,1)S(1)}, bf16[256,512]{1,0:T(8,128)(2,1)S(1)}, u32[]{:S(2)}, u32[]{:S(2)}) collective-permute-start(bf16[256,512]{1,0:T(8,128)(2,1)S(1)} %get-tuple-element.39), channel_id=1, source_target_pairs={{0,2},{1,3},{2,0},{3,1},{4,6},{5,7},{6,4},{7,5},{8,10},{9,11},{10,... | collective-permute-start | bytes 786440 | tf_op jit(solution)/shard_map/ppermute | solution.py:243
  37.8 3.3 %collective-permute-done.8.refs_5_ = bf16[512,768]{1,0:T(8,128)(2,1)S(1)} collective-permute-done((bf16[512,768]{1,0:T(8,128)(2,1)S(1)}, bf16[512,768]{1,0:T(8,128)(2,1)S(1)}, u32[]{:S(2)}, u32[]{:S(2)}) %collective-permute-start.8) | collective-permute-done | bytes 786464 | tf_op jit(solution)/shard_map/ppermute | solution.py:240
  41.3 2.0 %collective-permute-start.10 = (bf16[512,384]{1,0:T(8,128)(2,1)S(1)}, bf16[512,384]{1,0:T(8,128)(2,1)S(1)}, u32[]{:S(2)}, u32[]{:S(2)}) collective-permute-start(bf16[512,384]{1,0:T(8,128)(2,1)S(1)} %slice.9), channel_id=1, source_target_pairs={{0,8},{4,12},{8,0},{12,4},{16,24},{20,28},{24,16},{28,20},{1,9},{5... | collective-permute-start | bytes 1179656 | tf_op jit(solution)/shard_map/ppermute | solution.py:240
  44.6 4.9 %collective-permute-done.9.refs_4_.refs_2_ = bf16[512,384]{1,0:T(8,128)(2,1)S(1)} collective-permute-done((bf16[512,384]{1,0:T(8,128)(2,1)S(1)}, bf16[512,384]{1,0:T(8,128)(2,1)S(1)}, u32[]{:S(2)}, u32[]{:S(2)}) %collective-permute-start.9) | collective-permute-done | bytes 393248 | tf_op jit(solution)/shard_map/ppermute | solution.py:240
  49.5 1.2 %collective-permute-done.10.refs_5_.refs_3_ = bf16[512,384]{1,0:T(8,128)(2,1)S(1)} collective-permute-done((bf16[512,384]{1,0:T(8,128)(2,1)S(1)}, bf16[512,384]{1,0:T(8,128)(2,1)S(1)}, u32[]{:S(2)}, u32[]{:S(2)}) %collective-permute-start.10) | collective-permute-done | bytes 393248 | tf_op jit(solution)/shard_map/ppermute | solution.py:240
  52.1 2.4 %collective-permute-done.7.refs_0_.refs_1_ = bf16[256,512]{1,0:T(8,128)(2,1)S(1)} collective-permute-done((bf16[256,512]{1,0:T(8,128)(2,1)S(1)}, bf16[256,512]{1,0:T(8,128)(2,1)S(1)}, u32[]{:S(2)}, u32[]{:S(2)}) %collective-permute-start.7) | collective-permute-done | bytes 262176 | tf_op jit(solution)/shard_map/ppermute | solution.py:243
  59.8 1.5 %collective-permute-start.20 = (f32[8,128]{1,0:T(8,128)S(1)}, f32[8,128]{1,0:T(8,128)S(1)}, u32[]{:S(2)}, u32[]{:S(2)}) collective-permute-start(f32[8,128]{1,0:T(8,128)S(1)} %add.3.refs_0_), channel_id=1, source_target_pairs={{0,16},{4,20},{8,24},{12,28},{16,0},{20,4},{24,8},{28,12},{1,17},{... | collective-permute-start | bytes 12296 | tf_op jit(solution)/shard_map/ppermute | solution.py:240
  61.3 1.4 %collective-permute-start.19 = (f32[8,128]{1,0:T(8,128)S(1)}, f32[8,128]{1,0:T(8,128)S(1)}, u32[]{:S(2)}, u32[]{:S(2)}) collective-permute-start(f32[8,128]{1,0:T(8,128)S(1)} %add.3.refs_0_), channel_id=1, source_target_pairs={{0,8},{4,12},{8,0},{12,4},{16,24},{20,28},{24,16},{28,20},{1,9},{5... | collective-permute-start | bytes 12296 | tf_op jit(solution)/shard_map/ppermute | solution.py:240
  62.7 1.4 %moment.1 = (f32[1,256,768]{2,1,0:T(8,128)}, f32[1,256,768]{2,1,0:T(8,128)}) custom-call(f32[256,384]{1,0:T(8,128)S(1)} %get-tuple-element.55.left_ref, f32[256,384]{1,0:T(8,128)S(1)} %get-tuple-element.56.right_ref, f32[1,256,768]{2,1,0:T(8,128)S(1)} %copy-done, f32[1,256,768]{2,1,0:T(8,128)S(1)} %copy-done.1), custom_call_target="tpu_custom_call" | custom-call | bytes 3932160 | tf_op jit(solution)/shard_map/moment/pallas_call | solution.py:197
  64.9 1.0 %weight.1 = f32[1,256,768]{2,1,0:T(8,128)} custom-call(f32[8,128]{1,0:T(8,128)S(1)} %add.3.refs_0_, f32[8,128]{1,0:T(8,128)S(1)} %collective-permute-done.19.refs_1_, f32[8,128]{1,0:T(8,128)S(1)} %collective-permute-done.20.refs_2_, f32[8,128]{1,0:T(8,128)S(1)} %collective-permute-done.21.refs_3_, f32[1,256,768]{2,1,0:T(8,128)S(1)} %copy-done.2, ...), custom_call_target="tpu_custom_call" | custom-call | bytes 2375680 | tf_op jit(solution)/shard_map/weight/pallas_call | solution.py:197
  (50 shorter events, 12.1 us)
Async XLA Ops:
  2.3 12.4 %collective-permute-start.2 = (bf16[128,512]{1,0:T(8,128)(2,1)S(1)}, bf16[128,512]{1,0:T(8,128)(2,1)S(1)}, u32[]{:S(2)}, u32[]{:S(2)}) collective-permute-start(bf16[128,512]{1,0:T(8,128)(2,1)S(1)} %get-tuple-element.33), channel_id=1, source_target_pairs={{0,2},{1,3},{2,0},{3,1},{4,6},{5,7},{6,4},{7,5},{8,10},{9,11},{10,... | collective-permute-start | bytes 393224 | tf_op jit(solution)/shard_map/ppermute | solution.py:243
  6.4 8.3 %collective-permute-start = (bf16[272,512]{1,0:T(8,128)(2,1)S(1)}, bf16[272,512]{1,0:T(8,128)(2,1)S(1)}, u32[]{:S(2)}, u32[]{:S(2)}) collective-permute-start(bf16[272,512]{1,0:T(8,128)(2,1)S(1)} %get-tuple-element.31), channel_id=1, source_target_pairs={{0,8},{4,12},{8,0},{12,4},{16,24},{20,28},{24,16},{28,20},{1,9},{5... | collective-permute-start | bytes 835592 | tf_op jit(solution)/shard_map/ppermute | solution.py:240
  7.9 7.8 %collective-permute-start.1 = (bf16[272,512]{1,0:T(8,128)(2,1)S(1)}, bf16[272,512]{1,0:T(8,128)(2,1)S(1)}, u32[]{:S(2)}, u32[]{:S(2)}) collective-permute-start(bf16[272,512]{1,0:T(8,128)(2,1)S(1)} %get-tuple-element.32), channel_id=1, source_target_pairs={{0,16},{4,20},{8,24},{12,28},{16,0},{20,4},{24,8},{28,12},{1,17},{... | collective-permute-start | bytes 835592 | tf_op jit(solution)/shard_map/ppermute | solution.py:240
  9.4 13.2 %collective-permute-start.3 = (bf16[128,512]{1,0:T(8,128)(2,1)S(1)}, bf16[128,512]{1,0:T(8,128)(2,1)S(1)}, u32[]{:S(2)}, u32[]{:S(2)}) collective-permute-start(bf16[128,512]{1,0:T(8,128)(2,1)S(1)} %get-tuple-element.34), channel_id=1, source_target_pairs={{0,1},{1,2},{2,3},{3,0},{4,5},{5,6},{6,7},{7,4},{8,9},{9,10},{10,1... | collective-permute-start | bytes 393224 | tf_op jit(solution)/shard_map/ppermute | solution.py:243
  11.0 12.5 %collective-permute-start.4 = (bf16[128,512]{1,0:T(8,128)(2,1)S(1)}, bf16[128,512]{1,0:T(8,128)(2,1)S(1)}, u32[]{:S(2)}, u32[]{:S(2)}) collective-permute-start(bf16[128,512]{1,0:T(8,128)(2,1)S(1)} %get-tuple-element.35), channel_id=1, source_target_pairs={{0,3},{1,0},{2,1},{3,2},{4,7},{5,4},{6,5},{7,6},{8,11},{9,8},{10,9... | collective-permute-start | bytes 393224 | tf_op jit(solution)/shard_map/ppermute | solution.py:243
  15.7 9.3 %collective-permute-start.6 = (bf16[272,512]{1,0:T(8,128)(2,1)S(1)}, bf16[272,512]{1,0:T(8,128)(2,1)S(1)}, u32[]{:S(2)}, u32[]{:S(2)}) collective-permute-start(bf16[272,512]{1,0:T(8,128)(2,1)S(1)} %get-tuple-element.38), channel_id=1, source_target_pairs={{0,24},{4,28},{8,16},{12,20},{16,8},{20,12},{24,0},{28,4},{1,25},{... | collective-permute-start | bytes 835592 | tf_op jit(solution)/shard_map/ppermute | solution.py:240
  19.5 7.1 %collective-permute-start.13 = (bf16[128,512]{1,0:T(8,128)(2,1)S(1)}, bf16[128,512]{1,0:T(8,128)(2,1)S(1)}, u32[]{:S(2)}, u32[]{:S(2)}) collective-permute-start(bf16[128,512]{1,0:T(8,128)(2,1)S(1)} %get-tuple-element.45), channel_id=1, source_target_pairs={{0,1},{1,2},{2,3},{3,0},{4,5},{5,6},{6,7},{7,4},{8,9},{9,10},{10,1... | collective-permute-start | bytes 393224 | tf_op jit(solution)/shard_map/ppermute | solution.py:243
  19.6 13.7 %collective-permute-start.14 = (bf16[128,512]{1,0:T(8,128)(2,1)S(1)}, bf16[128,512]{1,0:T(8,128)(2,1)S(1)}, u32[]{:S(2)}, u32[]{:S(2)}) collective-permute-start(bf16[128,512]{1,0:T(8,128)(2,1)S(1)} %get-tuple-element.46), channel_id=1, source_target_pairs={{0,2},{1,3},{2,0},{3,1},{4,6},{5,7},{6,4},{7,5},{8,10},{9,11},{10,... | collective-permute-start | bytes 393224 | tf_op jit(solution)/shard_map/ppermute | solution.py:243
  22.6 12.2 %collective-permute-start.15 = (bf16[128,512]{1,0:T(8,128)(2,1)S(1)}, bf16[128,512]{1,0:T(8,128)(2,1)S(1)}, u32[]{:S(2)}, u32[]{:S(2)}) collective-permute-start(bf16[128,512]{1,0:T(8,128)(2,1)S(1)} %get-tuple-element.47), channel_id=1, source_target_pairs={{0,3},{1,0},{2,1},{3,2},{4,7},{5,4},{6,5},{7,6},{8,11},{9,8},{10,9... | collective-permute-start | bytes 393224 | tf_op jit(solution)/shard_map/ppermute | solution.py:243
  23.8 17.3 %collective-permute-start.8 = (bf16[512,768]{1,0:T(8,128)(2,1)S(1)}, bf16[512,768]{1,0:T(8,128)(2,1)S(1)}, u32[]{:S(2)}, u32[]{:S(2)}) collective-permute-start(bf16[512,768]{1,0:T(8,128)(2,1)S(1)} %bitcast.4), channel_id=1, source_target_pairs={{0,8},{4,12},{8,0},{12,4},{16,24},{20,28},{24,16},{28,20},{1,9},{5... | collective-permute-start | bytes 2359304 | tf_op jit(solution)/shard_map/ppermute | solution.py:240
  25.0 16.3 %collective-permute-start.5 = (bf16[512,768]{1,0:T(8,128)(2,1)S(1)}, bf16[512,768]{1,0:T(8,128)(2,1)S(1)}, u32[]{:S(2)}, u32[]{:S(2)}) collective-permute-start(bf16[512,768]{1,0:T(8,128)(2,1)S(1)} %bitcast.5), channel_id=1, source_target_pairs={{0,16},{4,20},{8,24},{12,28},{16,0},{20,4},{24,8},{28,12},{1,17},{... | collective-permute-start | bytes 2359304 | tf_op jit(solution)/shard_map/ppermute | solution.py:240
  26.7 17.9 %collective-permute-start.11 = (bf16[256,512]{1,0:T(8,128)(2,1)S(1)}, bf16[256,512]{1,0:T(8,128)(2,1)S(1)}, u32[]{:S(2)}, u32[]{:S(2)}) collective-permute-start(bf16[256,512]{1,0:T(8,128)(2,1)S(1)} %get-tuple-element.41), channel_id=1, source_target_pairs={{0,1},{1,2},{2,3},{3,0},{4,5},{5,6},{6,7},{7,4},{8,9},{9,10},{10,1... | collective-permute-start | bytes 786440 | tf_op jit(solution)/shard_map/ppermute | solution.py:243
  33.3 11.3 %collective-permute-start.12 = (bf16[256,512]{1,0:T(8,128)(2,1)S(1)}, bf16[256,512]{1,0:T(8,128)(2,1)S(1)}, u32[]{:S(2)}, u32[]{:S(2)}) collective-permute-start(bf16[256,512]{1,0:T(8,128)(2,1)S(1)} %get-tuple-element.42), channel_id=1, source_target_pairs={{0,3},{1,0},{2,1},{3,2},{4,7},{5,4},{6,5},{7,6},{8,11},{9,8},{10,9... | collective-permute-start | bytes 786440 | tf_op jit(solution)/shard_map/ppermute | solution.py:243
  34.8 19.7 %collective-permute-start.7 = (bf16[256,512]{1,0:T(8,128)(2,1)S(1)}, bf16[256,512]{1,0:T(8,128)(2,1)S(1)}, u32[]{:S(2)}, u32[]{:S(2)}) collective-permute-start(bf16[256,512]{1,0:T(8,128)(2,1)S(1)} %get-tuple-element.39), channel_id=1, source_target_pairs={{0,2},{1,3},{2,0},{3,1},{4,6},{5,7},{6,4},{7,5},{8,10},{9,11},{10,... | collective-permute-start | bytes 786440 | tf_op jit(solution)/shard_map/ppermute | solution.py:243
  41.1 8.4 %collective-permute-start.9 = (bf16[512,384]{1,0:T(8,128)(2,1)S(1)}, bf16[512,384]{1,0:T(8,128)(2,1)S(1)}, u32[]{:S(2)}, u32[]{:S(2)}) collective-permute-start(bf16[512,384]{1,0:T(8,128)(2,1)S(1)} %slice.8), channel_id=1, source_target_pairs={{0,16},{4,20},{8,24},{12,28},{16,0},{20,4},{24,8},{28,12},{1,17},{... | collective-permute-start | bytes 1179656 | tf_op jit(solution)/shard_map/ppermute | solution.py:240
  41.3 9.4 %collective-permute-start.10 = (bf16[512,384]{1,0:T(8,128)(2,1)S(1)}, bf16[512,384]{1,0:T(8,128)(2,1)S(1)}, u32[]{:S(2)}, u32[]{:S(2)}) collective-permute-start(bf16[512,384]{1,0:T(8,128)(2,1)S(1)} %slice.9), channel_id=1, source_target_pairs={{0,8},{4,12},{8,0},{12,4},{16,24},{20,28},{24,16},{28,20},{1,9},{5... | collective-permute-start | bytes 1179656 | tf_op jit(solution)/shard_map/ppermute | solution.py:240
  44.6 6.2 %copy-start = (f32[1,256,768]{2,1,0:T(8,128)S(1)}, f32[1,256,768]{2,1,0:T(8,128)}, u32[]{:S(2)}) copy-start(f32[1,256,768]{2,1,0:T(8,128)} %first_ref.5) | copy-start | bytes 2359300
  44.6 6.2 %copy-start.1 = (f32[1,256,768]{2,1,0:T(8,128)S(1)}, f32[1,256,768]{2,1,0:T(8,128)}, u32[]{:S(2)}) copy-start(f32[1,256,768]{2,1,0:T(8,128)} %second_ref.5) | copy-start | bytes 2359300
  54.9 1.8 %collective-permute-start.17 = (f32[256,384]{1,0:T(8,128)S(1)}, f32[256,384]{1,0:T(8,128)S(1)}, u32[]{:S(2)}, u32[]{:S(2)}) collective-permute-start(f32[256,384]{1,0:T(8,128)S(1)} %product.11), channel_id=1, source_target_pairs={{0,4},{4,0},{8,12},{12,8},{16,20},{20,16},{24,28},{28,24},{1,5},{5... | collective-permute-start | bytes 1179656 | tf_op jit(solution)/shard_map/ppermute | solution.py:240
  55.2 2.1 %collective-permute-start.16 = (f32[256,384]{1,0:T(8,128)S(1)}, f32[256,384]{1,0:T(8,128)S(1)}, u32[]{:S(2)}, u32[]{:S(2)}) collective-permute-start(f32[256,384]{1,0:T(8,128)S(1)} %product.12), channel_id=1, source_target_pairs={{0,4},{4,0},{8,12},{12,8},{16,20},{20,16},{24,28},{28,24},{1,5},{5... | collective-permute-start | bytes 1179656 | tf_op jit(solution)/shard_map/ppermute | solution.py:240
  57.9 1.2 %collective-permute-start.18 = (f32[8,128]{1,0:T(8,128)S(1)}, f32[8,128]{1,0:T(8,128)S(1)}, u32[]{:S(2)}, u32[]{:S(2)}) collective-permute-start(f32[8,128]{1,0:T(8,128)S(1)} %get-tuple-element.50), channel_id=1, source_target_pairs={{0,4},{4,0},{8,12},{12,8},{16,20},{20,16},{24,28},{28,24},{1,5},{5... | collective-permute-start | bytes 12296 | tf_op jit(solution)/shard_map/ppermute | solution.py:240
  59.2 4.9 %collective-permute-start.21 = (f32[8,128]{1,0:T(8,128)S(1)}, f32[8,128]{1,0:T(8,128)S(1)}, u32[]{:S(2)}, u32[]{:S(2)}) collective-permute-start(f32[8,128]{1,0:T(8,128)S(1)} %add.3.refs_0_), channel_id=1, source_target_pairs={{0,24},{4,28},{8,16},{12,20},{16,8},{20,12},{24,0},{28,4},{1,25},{... | collective-permute-start | bytes 12296 | tf_op jit(solution)/shard_map/ppermute | solution.py:240
  59.8 4.3 %collective-permute-start.20 = (f32[8,128]{1,0:T(8,128)S(1)}, f32[8,128]{1,0:T(8,128)S(1)}, u32[]{:S(2)}, u32[]{:S(2)}) collective-permute-start(f32[8,128]{1,0:T(8,128)S(1)} %add.3.refs_0_), channel_id=1, source_target_pairs={{0,16},{4,20},{8,24},{12,28},{16,0},{20,4},{24,8},{28,12},{1,17},{... | collective-permute-start | bytes 12296 | tf_op jit(solution)/shard_map/ppermute | solution.py:240
  61.3 3.6 %collective-permute-start.19 = (f32[8,128]{1,0:T(8,128)S(1)}, f32[8,128]{1,0:T(8,128)S(1)}, u32[]{:S(2)}, u32[]{:S(2)}) collective-permute-start(f32[8,128]{1,0:T(8,128)S(1)} %add.3.refs_0_), channel_id=1, source_target_pairs={{0,8},{4,12},{8,0},{12,4},{16,24},{20,28},{24,16},{28,20},{1,9},{5... | collective-permute-start | bytes 12296 | tf_op jit(solution)/shard_map/ppermute | solution.py:240
  (2 other events, 7.3 us)

commit v10 on v8

--- a/solution.py
+++ b/solution.py
@@ -105,16 +105,25 @@
                 out[...] = packed_rows(routed, expert_row, slot_row, expert, capacity)
 
 
-def pack_kernel(owners, capacity, n_blocks, *refs):
+def pack_kernel(owners, capacity, n_blocks, n_outs, *refs):
     z = lax.axis_index("expert")
-    blocks, outs = refs[:n_blocks], refs[-owners:]
+    blocks, outs = refs[:n_blocks], refs[-n_outs:]
     tokens = blocks[0].shape[0] - TAIL
     for at, block in enumerate(blocks):
         ids = block[tokens:, :tokens].astype(jnp.float32)
         rows = block[:tokens, :]
-        for shift, out in enumerate(outs):
-            expert = lax.rem(z + shift, owners)
-            out[at * capacity : (at + 1) * capacity, :] = packed_rows(rows, ids[0:1], ids[1:2], expert, capacity)
+        span = slice(at * capacity, (at + 1) * capacity)
+        for shift in range(owners):
+            packed = packed_rows(rows, ids[0:1], ids[1:2], lax.rem(z + shift, owners), capacity)
+            for at_out, out in enumerate(outs[shift:] if shift == owners - 1 else outs[shift : shift + 1]):
+                wide = out.shape[1]
+                out[span, :] = packed[:, at_out * wide : (at_out + 1) * wide]
+
+
+def pick_kernel(owners, capacity, *refs):
+    parts, out = refs[:-1], refs[-1]
+    begin = pl.multiple_of(lax.rem(lax.axis_index("expert") + 1, owners) * capacity, capacity)
+    out[...] = jnp.concatenate([part[pl.ds(begin, capacity), :] for part in parts], axis=1)
 
 
 def product_kernel(owners, capacity, columns, first, plan, n_early, *refs):
@@ -132,7 +141,7 @@
             size = refs[parts[0]].shape[1]
             part = refs[parts[column // size]]
             inside = slice(column % size, column % size + wide)
-            begins = [lax.rem(me + owners - shift, owners) * capacity for _, _, shift in packed]
+            begins = [0 if shift is None else lax.rem(me + owners - shift, owners) * capacity for _, _, shift in packed]
             right = [part[pl.ds(pl.multiple_of(begin, capacity), capacity), inside] for begin in begins]
             term = lax.dot_general(left, jnp.concatenate(right), ROWS_FIRST, preferred_element_type=jnp.float32)
             total = term if total is None else total + term
@@ -242,17 +251,29 @@
     def along(array, shift):
         return lax.ppermute(array, "expert", [(d, (d + shift) % owners) for d in range(owners)])
 
-    def pack(*blocks, waits=()):
+    def pack(*blocks, halves=1, waits=()):
         size = len(blocks) * capacity
+        widths = [part] * (owners - 1) + [part // halves] * halves
         return call(
-            functools.partial(pack_kernel, owners, capacity, len(blocks)),
-            [jax.ShapeDtypeStruct((size, part), bf16)] * owners,
+            functools.partial(pack_kernel, owners, capacity, len(blocks), len(widths)),
+            [jax.ShapeDtypeStruct((size, wide), bf16) for wide in widths],
             *blocks,
             *waits,
             spaces=[VMEM] * len(blocks) + [ANY] * len(waits),
             flops=4 * 2 * size * owners * tokens * part,
             name="pack",
         )
+
+    def pick(*parts):
+        shape = jax.ShapeDtypeStruct((capacity, ff), bf16)
+        return across(call(functools.partial(pick_kernel, owners, capacity), shape, *parts, name="pick"), 1)
+
+    def to_sibling(array, shift):
+        pairs = []
+        for d in range(n_dp):
+            for e in range(owners):
+                pairs.append((d * owners + e, (d ^ 1) * owners + (e + shift) % owners))
+        return lax.ppermute(array, ("dp", "expert"), pairs)
 
     def multiply(columns, groups, *early, span=slice(0, ff), waits=()):
         arrays, plan = [], []
@@ -300,8 +321,8 @@
     mid = [mid[0]] + [along(mid[shift], shift) for shift in range(1, owners)]
     late = tick(near[1], near[3], flops=2 * UNIT)
     from_xy = across(after(to_xy, from_x, from_y, seen), 6)
-    far = pack(from_y, from_xy, waits=[late])
-    far = [far[0]] + [along(far[shift], shift) for shift in range(1, owners)]
+    far = pack(from_y, from_xy, halves=2, waits=[late])
+    far = [far[0]] + [along(far[shift], shift) for shift in range(1, owners)] + [far[owners]]
     sent = after(hidden, from_x, from_y, near[2], late)
     by_x, by_y = across(sent, 2), across(sent, 4)
     by_xy = across(by_x[:, : ff // 2], 4), across(by_y[:, ff // 2 :], 2)
@@ -314,15 +335,18 @@
     state_in = down_weight, first_moment, second_moment
     seen = tick(*mid[1:], flops=20 * UNIT)
     groups = [((hidden,), terms(near, 0, 0, 1, 2, 3)), ((by_x,), terms(mid, 0, 0, 1, 2, 3))]
-    total = {side: multiply(side, groups, waits=[seen]) for side in (give, keep)}
+    total = {side: multiply(side, groups, waits=[seen, by_y]) for side in (give, keep)}
+    far[4] = to_sibling(after(far[4], far[1], by_x, by_y, *total.values()), 3)
     seen = tick(far[1], far[2], *total.values(), flops=5 * UNIT)
     groups = [((by_y,), terms(far, 0, 0, 1, 2)), (by_xy, terms(far, 1, 0, 1, 2))]
-    total = {side: multiply(side, groups, early, waits=[seen, *state_in]) for side, early in total.items()}
-    seen = tick(far[3], *total.values(), flops=5 * UNIT)
-    groups = [((by_y,), terms(far, 0, 3)), (by_xy, terms(far, 1, 3))]
-    given = [multiply(give, groups, total[give], span=span, waits=[seen]) for span in spans]
+    given = [multiply(give, groups, total[give], span=span, waits=[seen, *state_in]) for span in spans]
     other = [across(part, 1) for part in given]
-    kept = multiply(keep, groups, after(total[keep], *given))
+    picked = pick(after(by_y, given[0])), pick(*after(by_xy, given[0]))
+    kept = multiply(keep, groups, total[keep], waits=[seen])
+    seen = tick(far[3], far[4], kept, flops=5 * UNIT)
+    groups = [((by_y,), [(far[3], 0, 3)]), (by_xy, [(far[3], 1, 3)])]
+    groups += [((picked[0],), [(far[4], 0, None)]), ((picked[1],), [(far[4], 1, None)])]
+    kept = multiply(keep, groups, kept, waits=[seen])
 
     state = jax.ShapeDtypeStruct((1, half, ff), f32)
     grads, updates, sums = [], [], []

time: 66 us -> 66.2 us (level)
  starting transfers between devices: 27.6 us -> 30.5 us
  waiting for transfers between devices: 27.5 us -> 24.9 us
    ppermute x9, waiting for transfers between devices: 23.3 us -> 19.1 us  [along(): lax.ppermute(array, 'expert', [(d, (d + shift) % owners) for d in range(o...]
    ppermute x13 -> x15, starting transfers between devices: 14.4 us -> 16.2 us  [across(): return lax.ppermute(array, 'dp', [(d, d ^ mask) for d in range(n_dp)])]
    ppermute x0 -> x1, starting transfers between devices: none -> 1.72 us  [to_sibling(): return lax.ppermute(array, ('dp', 'expert'), pairs)]
    ppermute x13 -> x15, waiting for transfers between devices: 4.19 us -> 5.81 us  [across(): return lax.ppermute(array, 'dp', [(d, d ^ mask) for d in range(n_dp)])]
    pallas_call x19 -> x20, Pallas kernels: 9.55 us -> 9.4 us  [call(): pl.pallas_call(kernel, out_shape=out_shape, in_specs=spaces if isinstance...]
  transfers between devices with their start and end apart: 22 -> 25, of which waited for: 9 -> 9; matrix products, arithmetic and copies ran while one was open for 0% -> 0% of each run, Pallas kernels for 9% -> 9%
where the time goes in v10:
time: 66.2 us; the launch traced here: 66 us
  starting transfers between devices  30.5 us (46%)
  waiting for transfers between devices  24.9 us (38%)
  Pallas kernels  9.4 us (14%)
  between operations  0.86 us (1%)
    ppermute x9, waiting for transfers between devices, along(): lax.ppermute(array, 'expert', [(d, (d + shift) % owners) for d in range(o...  19.1 us
    ppermute x15, starting transfers between devices, across(): return lax.ppermute(array, 'dp', [(d, d ^ mask) for d in range(n_dp)])  16.2 us
    ppermute x9, starting transfers between devices, along(): lax.ppermute(array, 'expert', [(d, (d + shift) % owners) for d in range(o...  12.5 us
    pallas_call x20, Pallas kernels, call(): pl.pallas_call(kernel, out_shape=out_shape, in_specs=spaces if isinstance...  9.4 us
    ppermute x15, waiting for transfers between devices, across(): return lax.ppermute(array, 'dp', [(d, d ^ mask) for d in range(n_dp)])  5.81 us
    ppermute x1, starting transfers between devices, to_sibling(): return lax.ppermute(array, ('dp', 'expert'), pairs)  1.72 us
  transfers between devices with their start and end apart: 25, of which 9 were waited for; matrix products, arithmetic and copies ran while one was open for 0% of the time, Pallas kernels for 9%

profile of v10, /device:TPU:0, one launch (start us, length us, event | category | flops | bytes accessed | tf_op | source)
XLA Modules:
  0.0 66.0 jit_solution(5012811744036513609)
XLA Ops:
  0.6 1.6 %cut.1 = (bf16[128,512]{1,0:T(8,128)(2,1)S(1)}, bf16[128,512]{1,0:T(8,128)(2,1)S(1)}, bf16[128,512]{1,0:T(8,128)(2,1)S(1)}, bf16[128,512]{1,0:T(8,128)(2,1)S(1)}...) custom-call(bf16[256,2048]{1,0:T(8,128)(2,1)} %cot_ref.1, ...), custom_call_target="tpu_custom_call" | custom-call | bytes 2411520 | tf_op jit(solution)/shard_map/cut/pallas_call | solution.py:206
  2.3 4.1 %collective-permute-start.2 = (bf16[128,512]{1,0:T(8,128)(2,1)S(1)}, bf16[128,512]{1,0:T(8,128)(2,1)S(1)}, u32[]{:S(2)}, u32[]{:S(2)}) collective-permute-start(bf16[128,512]{1,0:T(8,128)(2,1)S(1)} %get-tuple-element.37), channel_id=1, source_target_pairs={{0,2},{1,3},{2,0},{3,1},{4,6},{5,7},{6,4},{7,5},{8,10},{9,11},{10,... | collective-permute-start | bytes 393224 | tf_op jit(solution)/shard_map/ppermute | solution.py:252
  6.4 1.5 %collective-permute-start = (bf16[272,512]{1,0:T(8,128)(2,1)S(1)}, bf16[272,512]{1,0:T(8,128)(2,1)S(1)}, u32[]{:S(2)}, u32[]{:S(2)}) collective-permute-start(bf16[272,512]{1,0:T(8,128)(2,1)S(1)} %get-tuple-element.35), channel_id=1, source_target_pairs={{0,8},{4,12},{8,0},{12,4},{16,24},{20,28},{24,16},{28,20},{1,9},{5... | collective-permute-start | bytes 835592 | tf_op jit(solution)/shard_map/ppermute | solution.py:249
  7.9 1.5 %collective-permute-start.1 = (bf16[272,512]{1,0:T(8,128)(2,1)S(1)}, bf16[272,512]{1,0:T(8,128)(2,1)S(1)}, u32[]{:S(2)}, u32[]{:S(2)}) collective-permute-start(bf16[272,512]{1,0:T(8,128)(2,1)S(1)} %get-tuple-element.36), channel_id=1, source_target_pairs={{0,16},{4,20},{8,24},{12,28},{16,0},{20,4},{24,8},{28,12},{1,17},{... | collective-permute-start | bytes 835592 | tf_op jit(solution)/shard_map/ppermute | solution.py:249
  9.4 1.6 %collective-permute-start.3 = (bf16[128,512]{1,0:T(8,128)(2,1)S(1)}, bf16[128,512]{1,0:T(8,128)(2,1)S(1)}, u32[]{:S(2)}, u32[]{:S(2)}) collective-permute-start(bf16[128,512]{1,0:T(8,128)(2,1)S(1)} %get-tuple-element.38), channel_id=1, source_target_pairs={{0,1},{1,2},{2,3},{3,0},{4,5},{5,6},{6,7},{7,4},{8,9},{9,10},{10,1... | collective-permute-start | bytes 393224 | tf_op jit(solution)/shard_map/ppermute | solution.py:252
  11.0 2.2 %collective-permute-start.4 = (bf16[128,512]{1,0:T(8,128)(2,1)S(1)}, bf16[128,512]{1,0:T(8,128)(2,1)S(1)}, u32[]{:S(2)}, u32[]{:S(2)}) collective-permute-start(bf16[128,512]{1,0:T(8,128)(2,1)S(1)} %get-tuple-element.39), channel_id=1, source_target_pairs={{0,3},{1,0},{2,1},{3,2},{4,7},{5,4},{6,5},{7,6},{8,11},{9,8},{10,9... | collective-permute-start | bytes 393224 | tf_op jit(solution)/shard_map/ppermute | solution.py:252
  13.2 1.5 %collective-permute-done.2.refs_0_.refs_3_ = bf16[128,512]{1,0:T(8,128)(2,1)S(1)} collective-permute-done((bf16[128,512]{1,0:T(8,128)(2,1)S(1)}, bf16[128,512]{1,0:T(8,128)(2,1)S(1)}, u32[]{:S(2)}, u32[]{:S(2)}) %collective-permute-start.2) | collective-permute-done | bytes 131104 | tf_op jit(solution)/shard_map/ppermute | solution.py:252
  14.7 1.0 %collective-permute-done.1.refs_0_ = bf16[272,512]{1,0:T(8,128)(2,1)S(1)} collective-permute-done((bf16[272,512]{1,0:T(8,128)(2,1)S(1)}, bf16[272,512]{1,0:T(8,128)(2,1)S(1)}, u32[]{:S(2)}, u32[]{:S(2)}) %collective-permute-start.1) | collective-permute-done | bytes 278560 | tf_op jit(solution)/shard_map/ppermute | solution.py:249
  15.7 3.5 %collective-permute-start.6 = (bf16[272,512]{1,0:T(8,128)(2,1)S(1)}, bf16[272,512]{1,0:T(8,128)(2,1)S(1)}, u32[]{:S(2)}, u32[]{:S(2)}) collective-permute-start(bf16[272,512]{1,0:T(8,128)(2,1)S(1)} %get-tuple-element.42), channel_id=1, source_target_pairs={{0,24},{4,28},{8,16},{12,20},{16,8},{20,12},{24,0},{28,4},{1,25},{... | collective-permute-start | bytes 835592 | tf_op jit(solution)/shard_map/ppermute | solution.py:249
  19.6 3.0 %collective-permute-start.14 = (bf16[128,512]{1,0:T(8,128)(2,1)S(1)}, bf16[128,512]{1,0:T(8,128)(2,1)S(1)}, u32[]{:S(2)}, u32[]{:S(2)}) collective-permute-start(bf16[128,512]{1,0:T(8,128)(2,1)S(1)} %get-tuple-element.50), channel_id=1, source_target_pairs={{0,2},{1,3},{2,0},{3,1},{4,6},{5,7},{6,4},{7,5},{8,10},{9,11},{10,... | collective-permute-start | bytes 393224 | tf_op jit(solution)/shard_map/ppermute | solution.py:252
  22.6 0.9 %collective-permute-start.15 = (bf16[128,512]{1,0:T(8,128)(2,1)S(1)}, bf16[128,512]{1,0:T(8,128)(2,1)S(1)}, u32[]{:S(2)}, u32[]{:S(2)}) collective-permute-start(bf16[128,512]{1,0:T(8,128)(2,1)S(1)} %get-tuple-element.51), channel_id=1, source_target_pairs={{0,3},{1,0},{2,1},{3,2},{4,7},{5,4},{6,5},{7,6},{8,11},{9,8},{10,9... | collective-permute-start | bytes 393224 | tf_op jit(solution)/shard_map/ppermute | solution.py:252
  24.8 1.3 %collective-permute-start.8 = (bf16[512,768]{1,0:T(8,128)(2,1)S(1)}, bf16[512,768]{1,0:T(8,128)(2,1)S(1)}, u32[]{:S(2)}, u32[]{:S(2)}) collective-permute-start(bf16[512,768]{1,0:T(8,128)(2,1)S(1)} %bitcast.5), channel_id=1, source_target_pairs={{0,8},{4,12},{8,0},{12,4},{16,24},{20,28},{24,16},{28,20},{1,9},{5... | collective-permute-start | bytes 2359304 | tf_op jit(solution)/shard_map/ppermute | solution.py:249
  27.2 14.0 %collective-permute-done.14.refs_1_.refs_8_ = bf16[128,512]{1,0:T(8,128)(2,1)S(1)} collective-permute-done((bf16[128,512]{1,0:T(8,128)(2,1)S(1)}, bf16[128,512]{1,0:T(8,128)(2,1)S(1)}, u32[]{:S(2)}, u32[]{:S(2)}) %collective-permute-start.14) | collective-permute-done | bytes 131104 | tf_op jit(solution)/shard_map/ppermute | solution.py:252
  41.3 1.3 %collective-permute-start.10 = (bf16[512,384]{1,0:T(8,128)(2,1)S(1)}, bf16[512,384]{1,0:T(8,128)(2,1)S(1)}, u32[]{:S(2)}, u32[]{:S(2)}) collective-permute-start(bf16[512,384]{1,0:T(8,128)(2,1)S(1)} %slice.9), channel_id=1, source_target_pairs={{0,8},{4,12},{8,0},{12,4},{16,24},{20,28},{24,16},{28,20},{1,9},{5... | collective-permute-start | bytes 1179656 | tf_op jit(solution)/shard_map/ppermute | solution.py:249
  42.7 1.6 %collective-permute-start.9 = (bf16[512,384]{1,0:T(8,128)(2,1)S(1)}, bf16[512,384]{1,0:T(8,128)(2,1)S(1)}, u32[]{:S(2)}, u32[]{:S(2)}) collective-permute-start(bf16[512,384]{1,0:T(8,128)(2,1)S(1)} %slice.8), channel_id=1, source_target_pairs={{0,16},{4,20},{8,24},{12,28},{16,0},{20,4},{24,8},{28,12},{1,17},{... | collective-permute-start | bytes 1179656 | tf_op jit(solution)/shard_map/ppermute | solution.py:249
  45.6 1.7 %collective-permute-start.17 = (bf16[256,256]{1,0:T(8,128)(2,1)S(1)}, bf16[256,256]{1,0:T(8,128)(2,1)S(1)}, u32[]{:S(2)}, u32[]{:S(2)}) collective-permute-start(bf16[256,256]{1,0:T(8,128)(2,1)S(1)} %get-tuple-element.54), channel_id=1, source_target_pairs={{0,7},{1,4},{2,5},{3,6},{4,3},{5,0},{6,1},{7,2},{8,15},{9,12},{10,... | collective-permute-start | bytes 393224 | tf_op jit(solution)/shard_map/ppermute | solution.py:276
  47.3 3.6 %collective-permute-done.12.refs_1_.refs_3_ = bf16[256,512]{1,0:T(8,128)(2,1)S(1)} collective-permute-done((bf16[256,512]{1,0:T(8,128)(2,1)S(1)}, bf16[256,512]{1,0:T(8,128)(2,1)S(1)}, u32[]{:S(2)}, u32[]{:S(2)}) %collective-permute-start.12) | collective-permute-done | bytes 262176 | tf_op jit(solution)/shard_map/ppermute | solution.py:252
  50.9 1.4 %collective-permute-done.9.refs_4_.refs_0_.refs_2_ = bf16[512,384]{1,0:T(8,128)(2,1)S(1)} collective-permute-done((bf16[512,384]{1,0:T(8,128)(2,1)S(1)}, bf16[512,384]{1,0:T(8,128)(2,1)S(1)}, u32[]{:S(2)}, u32[]{:S(2)}) %collective-permute-start.9) | collective-permute-done | bytes 393248 | tf_op jit(solution)/shard_map/ppermute | solution.py:249
  57.7 0.8 %collective-permute-done.21 = f32[8,128]{1,0:T(8,128)S(1)} collective-permute-done((f32[8,128]{1,0:T(8,128)S(1)}, f32[8,128]{1,0:T(8,128)S(1)}, u32[]{:S(2)}, u32[]{:S(2)}) %collective-permute-start.21) | collective-permute-done | bytes 4128 | tf_op jit(solution)/shard_map/ppermute | solution.py:249
  58.8 1.7 %collective-permute-start.23 = (f32[8,128]{1,0:T(8,128)S(1)}, f32[8,128]{1,0:T(8,128)S(1)}, u32[]{:S(2)}, u32[]{:S(2)}) collective-permute-start(f32[8,128]{1,0:T(8,128)S(1)} %add.3.refs_0_), channel_id=1, source_target_pairs={{0,16},{4,20},{8,24},{12,28},{16,0},{20,4},{24,8},{28,12},{1,17},{... | collective-permute-start | bytes 12296 | tf_op jit(solution)/shard_map/ppermute | solution.py:249
  60.5 1.4 %collective-permute-start.24 = (f32[8,128]{1,0:T(8,128)S(1)}, f32[8,128]{1,0:T(8,128)S(1)}, u32[]{:S(2)}, u32[]{:S(2)}) collective-permute-start(f32[8,128]{1,0:T(8,128)S(1)} %add.3.refs_0_), channel_id=1, source_target_pairs={{0,24},{4,28},{8,16},{12,20},{16,8},{20,12},{24,0},{28,4},{1,25},{... | collective-permute-start | bytes 12296 | tf_op jit(solution)/shard_map/ppermute | solution.py:249
  62.0 1.4 %moment.1 = (f32[1,256,768]{2,1,0:T(8,128)}, f32[1,256,768]{2,1,0:T(8,128)}) custom-call(f32[256,384]{1,0:T(8,128)S(1)} %get-tuple-element.63.left_ref, f32[256,384]{1,0:T(8,128)S(1)} %get-tuple-element.64.right_ref, f32[1,256,768]{2,1,0:T(8,128)S(1)} %copy-done, f32[1,256,768]{2,1,0:T(8,128)S(1)} %copy-done.1), custom_call_target="tpu_custom_call" | custom-call | bytes 3932160 | tf_op jit(solution)/shard_map/moment/pallas_call | solution.py:206
  63.3 1.7 %collective-permute-done.24.refs_3_ = f32[8,128]{1,0:T(8,128)S(1)} collective-permute-done((f32[8,128]{1,0:T(8,128)S(1)}, f32[8,128]{1,0:T(8,128)S(1)}, u32[]{:S(2)}, u32[]{:S(2)}) %collective-permute-start.24) | collective-permute-done | bytes 4128 | tf_op jit(solution)/shard_map/ppermute | solution.py:249
  65.0 1.0 %weight.1 = f32[1,256,768]{2,1,0:T(8,128)} custom-call(f32[8,128]{1,0:T(8,128)S(1)} %add.3.refs_0_, f32[8,128]{1,0:T(8,128)S(1)} %collective-permute-done.22.refs_1_, f32[8,128]{1,0:T(8,128)S(1)} %collective-permute-done.23.refs_2_, f32[8,128]{1,0:T(8,128)S(1)} %collective-permute-done.24.refs_3_, f32[1,256,768]{2,1,0:T(8,128)S(1)} %copy-done.2, ...), custom_call_target="tpu_custom_call" | custom-call | bytes 2375680 | tf_op jit(solution)/shard_map/weight/pallas_call | solution.py:206
  (57 shorter events, 9.7 us)
Async XLA Ops:
  2.3 12.4 %collective-permute-start.2 = (bf16[128,512]{1,0:T(8,128)(2,1)S(1)}, bf16[128,512]{1,0:T(8,128)(2,1)S(1)}, u32[]{:S(2)}, u32[]{:S(2)}) collective-permute-start(bf16[128,512]{1,0:T(8,128)(2,1)S(1)} %get-tuple-element.37), channel_id=1, source_target_pairs={{0,2},{1,3},{2,0},{3,1},{4,6},{5,7},{6,4},{7,5},{8,10},{9,11},{10,... | collective-permute-start | bytes 393224 | tf_op jit(solution)/shard_map/ppermute | solution.py:252
  6.4 8.3 %collective-permute-start = (bf16[272,512]{1,0:T(8,128)(2,1)S(1)}, bf16[272,512]{1,0:T(8,128)(2,1)S(1)}, u32[]{:S(2)}, u32[]{:S(2)}) collective-permute-start(bf16[272,512]{1,0:T(8,128)(2,1)S(1)} %get-tuple-element.35), channel_id=1, source_target_pairs={{0,8},{4,12},{8,0},{12,4},{16,24},{20,28},{24,16},{28,20},{1,9},{5... | collective-permute-start | bytes 835592 | tf_op jit(solution)/shard_map/ppermute | solution.py:249
  7.9 7.8 %collective-permute-start.1 = (bf16[272,512]{1,0:T(8,128)(2,1)S(1)}, bf16[272,512]{1,0:T(8,128)(2,1)S(1)}, u32[]{:S(2)}, u32[]{:S(2)}) collective-permute-start(bf16[272,512]{1,0:T(8,128)(2,1)S(1)} %get-tuple-element.36), channel_id=1, source_target_pairs={{0,16},{4,20},{8,24},{12,28},{16,0},{20,4},{24,8},{28,12},{1,17},{... | collective-permute-start | bytes 835592 | tf_op jit(solution)/shard_map/ppermute | solution.py:249
  9.4 13.2 %collective-permute-start.3 = (bf16[128,512]{1,0:T(8,128)(2,1)S(1)}, bf16[128,512]{1,0:T(8,128)(2,1)S(1)}, u32[]{:S(2)}, u32[]{:S(2)}) collective-permute-start(bf16[128,512]{1,0:T(8,128)(2,1)S(1)} %get-tuple-element.38), channel_id=1, source_target_pairs={{0,1},{1,2},{2,3},{3,0},{4,5},{5,6},{6,7},{7,4},{8,9},{9,10},{10,1... | collective-permute-start | bytes 393224 | tf_op jit(solution)/shard_map/ppermute | solution.py:252
  11.0 12.5 %collective-permute-start.4 = (bf16[128,512]{1,0:T(8,128)(2,1)S(1)}, bf16[128,512]{1,0:T(8,128)(2,1)S(1)}, u32[]{:S(2)}, u32[]{:S(2)}) collective-permute-start(bf16[128,512]{1,0:T(8,128)(2,1)S(1)} %get-tuple-element.39), channel_id=1, source_target_pairs={{0,3},{1,0},{2,1},{3,2},{4,7},{5,4},{6,5},{7,6},{8,11},{9,8},{10,9... | collective-permute-start | bytes 393224 | tf_op jit(solution)/shard_map/ppermute | solution.py:252
  15.7 9.1 %collective-permute-start.6 = (bf16[272,512]{1,0:T(8,128)(2,1)S(1)}, bf16[272,512]{1,0:T(8,128)(2,1)S(1)}, u32[]{:S(2)}, u32[]{:S(2)}) collective-permute-start(bf16[272,512]{1,0:T(8,128)(2,1)S(1)} %get-tuple-element.42), channel_id=1, source_target_pairs={{0,24},{4,28},{8,16},{12,20},{16,8},{20,12},{24,0},{28,4},{1,25},{... | collective-permute-start | bytes 835592 | tf_op jit(solution)/shard_map/ppermute | solution.py:249
  19.5 7.0 %collective-permute-start.13 = (bf16[128,512]{1,0:T(8,128)(2,1)S(1)}, bf16[128,512]{1,0:T(8,128)(2,1)S(1)}, u32[]{:S(2)}, u32[]{:S(2)}) collective-permute-start(bf16[128,512]{1,0:T(8,128)(2,1)S(1)} %get-tuple-element.49), channel_id=1, source_target_pairs={{0,1},{1,2},{2,3},{3,0},{4,5},{5,6},{6,7},{7,4},{8,9},{9,10},{10,1... | collective-permute-start | bytes 393224 | tf_op jit(solution)/shard_map/ppermute | solution.py:252
  19.6 21.5 %collective-permute-start.14 = (bf16[128,512]{1,0:T(8,128)(2,1)S(1)}, bf16[128,512]{1,0:T(8,128)(2,1)S(1)}, u32[]{:S(2)}, u32[]{:S(2)}) collective-permute-start(bf16[128,512]{1,0:T(8,128)(2,1)S(1)} %get-tuple-element.50), channel_id=1, source_target_pairs={{0,2},{1,3},{2,0},{3,1},{4,6},{5,7},{6,4},{7,5},{8,10},{9,11},{10,... | collective-permute-start | bytes 393224 | tf_op jit(solution)/shard_map/ppermute | solution.py:252
  22.6 18.5 %collective-permute-start.15 = (bf16[128,512]{1,0:T(8,128)(2,1)S(1)}, bf16[128,512]{1,0:T(8,128)(2,1)S(1)}, u32[]{:S(2)}, u32[]{:S(2)}) collective-permute-start(bf16[128,512]{1,0:T(8,128)(2,1)S(1)} %get-tuple-element.51), channel_id=1, source_target_pairs={{0,3},{1,0},{2,1},{3,2},{4,7},{5,4},{6,5},{7,6},{8,11},{9,8},{10,9... | collective-permute-start | bytes 393224 | tf_op jit(solution)/shard_map/ppermute | solution.py:252
  23.8 17.5 %collective-permute-start.5 = (bf16[512,768]{1,0:T(8,128)(2,1)S(1)}, bf16[512,768]{1,0:T(8,128)(2,1)S(1)}, u32[]{:S(2)}, u32[]{:S(2)}) collective-permute-start(bf16[512,768]{1,0:T(8,128)(2,1)S(1)} %bitcast.4), channel_id=1, source_target_pairs={{0,16},{4,20},{8,24},{12,28},{16,0},{20,4},{24,8},{28,12},{1,17},{... | collective-permute-start | bytes 2359304 | tf_op jit(solution)/shard_map/ppermute | solution.py:249
  24.8 17.9 %collective-permute-start.8 = (bf16[512,768]{1,0:T(8,128)(2,1)S(1)}, bf16[512,768]{1,0:T(8,128)(2,1)S(1)}, u32[]{:S(2)}, u32[]{:S(2)}) collective-permute-start(bf16[512,768]{1,0:T(8,128)(2,1)S(1)} %bitcast.5), channel_id=1, source_target_pairs={{0,8},{4,12},{8,0},{12,4},{16,24},{20,28},{24,16},{28,20},{1,9},{5... | collective-permute-start | bytes 2359304 | tf_op jit(solution)/shard_map/ppermute | solution.py:249
  26.6 19.0 %collective-permute-start.11 = (bf16[256,512]{1,0:T(8,128)(2,1)S(1)}, bf16[256,512]{1,0:T(8,128)(2,1)S(1)}, u32[]{:S(2)}, u32[]{:S(2)}) collective-permute-start(bf16[256,512]{1,0:T(8,128)(2,1)S(1)} %get-tuple-element.45), channel_id=1, source_target_pairs={{0,1},{1,2},{2,3},{3,0},{4,5},{5,6},{6,7},{7,4},{8,9},{9,10},{10,1... | collective-permute-start | bytes 786440 | tf_op jit(solution)/shard_map/ppermute | solution.py:252
  41.2 9.7 %collective-permute-start.12 = (bf16[256,512]{1,0:T(8,128)(2,1)S(1)}, bf16[256,512]{1,0:T(8,128)(2,1)S(1)}, u32[]{:S(2)}, u32[]{:S(2)}) collective-permute-start(bf16[256,512]{1,0:T(8,128)(2,1)S(1)} %get-tuple-element.46), channel_id=1, source_target_pairs={{0,2},{1,3},{2,0},{3,1},{4,6},{5,7},{6,4},{7,5},{8,10},{9,11},{10,... | collective-permute-start | bytes 786440 | tf_op jit(solution)/shard_map/ppermute | solution.py:252
  41.2 13.5 %collective-permute-start.7 = (bf16[256,256]{1,0:T(8,128)(2,1)S(1)}, bf16[256,256]{1,0:T(8,128)(2,1)S(1)}, u32[]{:S(2)}, u32[]{:S(2)}) collective-permute-start(bf16[256,256]{1,0:T(8,128)(2,1)S(1)} %get-tuple-element.43), channel_id=1, source_target_pairs={{0,3},{1,0},{2,1},{3,2},{4,7},{5,4},{6,5},{7,6},{8,11},{9,8},{10,9... | collective-permute-start | bytes 393224 | tf_op jit(solution)/shard_map/ppermute | solution.py:252
  41.3 9.6 %collective-permute-start.10 = (bf16[512,384]{1,0:T(8,128)(2,1)S(1)}, bf16[512,384]{1,0:T(8,128)(2,1)S(1)}, u32[]{:S(2)}, u32[]{:S(2)}) collective-permute-start(bf16[512,384]{1,0:T(8,128)(2,1)S(1)} %slice.9), channel_id=1, source_target_pairs={{0,8},{4,12},{8,0},{12,4},{16,24},{20,28},{24,16},{28,20},{1,9},{5... | collective-permute-start | bytes 1179656 | tf_op jit(solution)/shard_map/ppermute | solution.py:249
  42.7 9.6 %collective-permute-start.9 = (bf16[512,384]{1,0:T(8,128)(2,1)S(1)}, bf16[512,384]{1,0:T(8,128)(2,1)S(1)}, u32[]{:S(2)}, u32[]{:S(2)}) collective-permute-start(bf16[512,384]{1,0:T(8,128)(2,1)S(1)} %slice.8), channel_id=1, source_target_pairs={{0,16},{4,20},{8,24},{12,28},{16,0},{20,4},{24,8},{28,12},{1,17},{... | collective-permute-start | bytes 1179656 | tf_op jit(solution)/shard_map/ppermute | solution.py:249
  45.6 9.7 %collective-permute-start.17 = (bf16[256,256]{1,0:T(8,128)(2,1)S(1)}, bf16[256,256]{1,0:T(8,128)(2,1)S(1)}, u32[]{:S(2)}, u32[]{:S(2)}) collective-permute-start(bf16[256,256]{1,0:T(8,128)(2,1)S(1)} %get-tuple-element.54), channel_id=1, source_target_pairs={{0,7},{1,4},{2,5},{3,6},{4,3},{5,0},{6,1},{7,2},{8,15},{9,12},{10,... | collective-permute-start | bytes 393224 | tf_op jit(solution)/shard_map/ppermute | solution.py:276
  52.8 3.1 %collective-permute-start.20 = (f32[256,384]{1,0:T(8,128)S(1)}, f32[256,384]{1,0:T(8,128)S(1)}, u32[]{:S(2)}, u32[]{:S(2)}) collective-permute-start(f32[256,384]{1,0:T(8,128)S(1)} %product.8), channel_id=1, source_target_pairs={{0,4},{4,0},{8,12},{12,8},{16,20},{20,16},{24,28},{28,24},{1,5},{5... | collective-permute-start | bytes 1179656 | tf_op jit(solution)/shard_map/ppermute | solution.py:249
  52.9 2.4 %collective-permute-start.18 = (bf16[128,768]{1,0:T(8,128)(2,1)S(1)}, bf16[128,768]{1,0:T(8,128)(2,1)S(1)}, u32[]{:S(2)}, u32[]{:S(2)}) collective-permute-start(bf16[128,768]{1,0:T(8,128)(2,1)S(1)} %pick.3), channel_id=1, source_target_pairs={{0,4},{4,0},{8,12},{12,8},{16,20},{20,16},{24,28},{28,24},{1,5},{5... | collective-permute-start | bytes 589832 | tf_op jit(solution)/shard_map/ppermute | solution.py:249
  53.4 1.8 %collective-permute-start.16 = (bf16[128,768]{1,0:T(8,128)(2,1)S(1)}, bf16[128,768]{1,0:T(8,128)(2,1)S(1)}, u32[]{:S(2)}, u32[]{:S(2)}) collective-permute-start(bf16[128,768]{1,0:T(8,128)(2,1)S(1)} %pick.2), channel_id=1, source_target_pairs={{0,4},{4,0},{8,12},{12,8},{16,20},{20,16},{24,28},{28,24},{1,5},{5... | collective-permute-start | bytes 589832 | tf_op jit(solution)/shard_map/ppermute | solution.py:249
  54.7 1.9 %collective-permute-start.19 = (f32[256,384]{1,0:T(8,128)S(1)}, f32[256,384]{1,0:T(8,128)S(1)}, u32[]{:S(2)}, u32[]{:S(2)}) collective-permute-start(f32[256,384]{1,0:T(8,128)S(1)} %product.11), channel_id=1, source_target_pairs={{0,4},{4,0},{8,12},{12,8},{16,20},{20,16},{24,28},{28,24},{1,5},{5... | collective-permute-start | bytes 1179656 | tf_op jit(solution)/shard_map/ppermute | solution.py:249
  58.5 4.9 %collective-permute-start.22 = (f32[8,128]{1,0:T(8,128)S(1)}, f32[8,128]{1,0:T(8,128)S(1)}, u32[]{:S(2)}, u32[]{:S(2)}) collective-permute-start(f32[8,128]{1,0:T(8,128)S(1)} %add.3.refs_0_), channel_id=1, source_target_pairs={{0,8},{4,12},{8,0},{12,4},{16,24},{20,28},{24,16},{28,20},{1,9},{5... | collective-permute-start | bytes 12296 | tf_op jit(solution)/shard_map/ppermute | solution.py:249
  58.8 4.6 %collective-permute-start.23 = (f32[8,128]{1,0:T(8,128)S(1)}, f32[8,128]{1,0:T(8,128)S(1)}, u32[]{:S(2)}, u32[]{:S(2)}) collective-permute-start(f32[8,128]{1,0:T(8,128)S(1)} %add.3.refs_0_), channel_id=1, source_target_pairs={{0,16},{4,20},{8,24},{12,28},{16,0},{20,4},{24,8},{28,12},{1,17},{... | collective-permute-start | bytes 12296 | tf_op jit(solution)/shard_map/ppermute | solution.py:249
  60.5 4.5 %collective-permute-start.24 = (f32[8,128]{1,0:T(8,128)S(1)}, f32[8,128]{1,0:T(8,128)S(1)}, u32[]{:S(2)}, u32[]{:S(2)}) collective-permute-start(f32[8,128]{1,0:T(8,128)S(1)} %add.3.refs_0_), channel_id=1, source_target_pairs={{0,24},{4,28},{8,16},{12,20},{16,8},{20,12},{24,0},{28,4},{1,25},{... | collective-permute-start | bytes 12296 | tf_op jit(solution)/shard_map/ppermute | solution.py:249
  (5 other events, 22.6 us)

commit v11 on v9

--- a/solution.py
+++ b/solution.py
@@ -317,12 +317,13 @@
     total = {side: multiply(side, groups, waits=[seen]) for side in (give, keep)}
     seen = tick(far[1], far[3], *total.values(), flops=5 * UNIT)
     groups = [((by_y,), terms(far, 0, 0, 1, 3)), (by_xy, terms(far, 1, 0, 1, 3))]
-    total = {side: multiply(side, groups, early, waits=[seen, *state_in]) for side, early in total.items()}
+    middle = groups
+    total[give] = multiply(give, groups, total[give], waits=[seen, *state_in])
     seen = tick(far[2], *total.values(), flops=5 * UNIT)
     groups = [((by_y,), terms(far, 0, 2)), (by_xy, terms(far, 1, 2))]
     given = [multiply(give, groups, total[give], span=span, waits=[seen]) for span in spans]
     other = [across(part, 1) for part in given]
-    kept = multiply(keep, groups, after(total[keep], *given))
+    kept = multiply(keep, middle + groups, after(total[keep], *given))
 
     state = jax.ShapeDtypeStruct((1, half, ff), f32)
     grads, updates, sums = [], [], []

time: 66.1 us -> 66.1 us (level)
    ppermute x9, waiting for transfers between devices: 9.36 us -> 10.1 us  [along(): lax.ppermute(array, 'expert', [(d, (d + shift) % owners) for d in range(o...]
    pallas_call x19 -> x18, Pallas kernels: 9.55 us -> 9.37 us  [call(): pl.pallas_call(kernel, out_shape=out_shape, in_specs=spaces if isinstance...]
  transfers between devices with their start and end apart: 22 -> 22, of which waited for: 11 -> 10; matrix products, arithmetic and copies ran while one was open for 0% -> 0% of each run, Pallas kernels for 9% -> 9%
where the time goes in v11:
time: 66.1 us; the launch traced here: 65.9 us
  starting transfers between devices  32.1 us (49%)
  waiting for transfers between devices  23.3 us (35%)
  Pallas kernels  9.37 us (14%)
  between operations  0.83 us (1%)
    ppermute x9, starting transfers between devices, along(): lax.ppermute(array, 'expert', [(d, (d + shift) % owners) for d in range(o...  17.5 us
    ppermute x13, starting transfers between devices, across(): return lax.ppermute(array, 'dp', [(d, d ^ mask) for d in range(n_dp)])  14.6 us
    ppermute x13, waiting for transfers between devices, across(): return lax.ppermute(array, 'dp', [(d, d ^ mask) for d in range(n_dp)])  13.3 us
    ppermute x9, waiting for transfers between devices, along(): lax.ppermute(array, 'expert', [(d, (d + shift) % owners) for d in range(o...  10.1 us
    pallas_call x18, Pallas kernels, call(): pl.pallas_call(kernel, out_shape=out_shape, in_specs=spaces if isinstance...  9.37 us
  transfers between devices with their start and end apart: 22, of which 10 were waited for; matrix products, arithmetic and copies ran while one was open for 0% of the time, Pallas kernels for 9%

profile of v11, /device:TPU:0, one launch (start us, length us, event | category | flops | bytes accessed | tf_op | source)
XLA Modules:
  0.0 65.9 jit_solution(17871608596691002808)
XLA Ops:
  0.6 1.6 %cut.1 = (bf16[128,512]{1,0:T(8,128)(2,1)S(1)}, bf16[128,512]{1,0:T(8,128)(2,1)S(1)}, bf16[128,512]{1,0:T(8,128)(2,1)S(1)}, bf16[128,512]{1,0:T(8,128)(2,1)S(1)}...) custom-call(bf16[256,2048]{1,0:T(8,128)(2,1)} %cot_ref.1, ...), custom_call_target="tpu_custom_call" | custom-call | bytes 2411520 | tf_op jit(solution)/shard_map/cut/pallas_call | solution.py:197
  2.3 4.1 %collective-permute-start.2 = (bf16[128,512]{1,0:T(8,128)(2,1)S(1)}, bf16[128,512]{1,0:T(8,128)(2,1)S(1)}, u32[]{:S(2)}, u32[]{:S(2)}) collective-permute-start(bf16[128,512]{1,0:T(8,128)(2,1)S(1)} %get-tuple-element.33), channel_id=1, source_target_pairs={{0,2},{1,3},{2,0},{3,1},{4,6},{5,7},{6,4},{7,5},{8,10},{9,11},{10,... | collective-permute-start | bytes 393224 | tf_op jit(solution)/shard_map/ppermute | solution.py:243
  6.4 1.5 %collective-permute-start = (bf16[272,512]{1,0:T(8,128)(2,1)S(1)}, bf16[272,512]{1,0:T(8,128)(2,1)S(1)}, u32[]{:S(2)}, u32[]{:S(2)}) collective-permute-start(bf16[272,512]{1,0:T(8,128)(2,1)S(1)} %get-tuple-element.31), channel_id=1, source_target_pairs={{0,8},{4,12},{8,0},{12,4},{16,24},{20,28},{24,16},{28,20},{1,9},{5... | collective-permute-start | bytes 835592 | tf_op jit(solution)/shard_map/ppermute | solution.py:240
  7.9 1.5 %collective-permute-start.1 = (bf16[272,512]{1,0:T(8,128)(2,1)S(1)}, bf16[272,512]{1,0:T(8,128)(2,1)S(1)}, u32[]{:S(2)}, u32[]{:S(2)}) collective-permute-start(bf16[272,512]{1,0:T(8,128)(2,1)S(1)} %get-tuple-element.32), channel_id=1, source_target_pairs={{0,16},{4,20},{8,24},{12,28},{16,0},{20,4},{24,8},{28,12},{1,17},{... | collective-permute-start | bytes 835592 | tf_op jit(solution)/shard_map/ppermute | solution.py:240
  9.4 1.6 %collective-permute-start.3 = (bf16[128,512]{1,0:T(8,128)(2,1)S(1)}, bf16[128,512]{1,0:T(8,128)(2,1)S(1)}, u32[]{:S(2)}, u32[]{:S(2)}) collective-permute-start(bf16[128,512]{1,0:T(8,128)(2,1)S(1)} %get-tuple-element.34), channel_id=1, source_target_pairs={{0,1},{1,2},{2,3},{3,0},{4,5},{5,6},{6,7},{7,4},{8,9},{9,10},{10,1... | collective-permute-start | bytes 393224 | tf_op jit(solution)/shard_map/ppermute | solution.py:243
  11.0 2.2 %collective-permute-start.4 = (bf16[128,512]{1,0:T(8,128)(2,1)S(1)}, bf16[128,512]{1,0:T(8,128)(2,1)S(1)}, u32[]{:S(2)}, u32[]{:S(2)}) collective-permute-start(bf16[128,512]{1,0:T(8,128)(2,1)S(1)} %get-tuple-element.35), channel_id=1, source_target_pairs={{0,3},{1,0},{2,1},{3,2},{4,7},{5,4},{6,5},{7,6},{8,11},{9,8},{10,9... | collective-permute-start | bytes 393224 | tf_op jit(solution)/shard_map/ppermute | solution.py:243
  13.2 1.5 %collective-permute-done.2.refs_0_.refs_3_ = bf16[128,512]{1,0:T(8,128)(2,1)S(1)} collective-permute-done((bf16[128,512]{1,0:T(8,128)(2,1)S(1)}, bf16[128,512]{1,0:T(8,128)(2,1)S(1)}, u32[]{:S(2)}, u32[]{:S(2)}) %collective-permute-start.2) | collective-permute-done | bytes 131104 | tf_op jit(solution)/shard_map/ppermute | solution.py:243
  14.7 1.0 %collective-permute-done.1.refs_0_ = bf16[272,512]{1,0:T(8,128)(2,1)S(1)} collective-permute-done((bf16[272,512]{1,0:T(8,128)(2,1)S(1)}, bf16[272,512]{1,0:T(8,128)(2,1)S(1)}, u32[]{:S(2)}, u32[]{:S(2)}) %collective-permute-start.1) | collective-permute-done | bytes 278560 | tf_op jit(solution)/shard_map/ppermute | solution.py:240
  15.7 3.5 %collective-permute-start.6 = (bf16[272,512]{1,0:T(8,128)(2,1)S(1)}, bf16[272,512]{1,0:T(8,128)(2,1)S(1)}, u32[]{:S(2)}, u32[]{:S(2)}) collective-permute-start(bf16[272,512]{1,0:T(8,128)(2,1)S(1)} %get-tuple-element.38), channel_id=1, source_target_pairs={{0,24},{4,28},{8,16},{12,20},{16,8},{20,12},{24,0},{28,4},{1,25},{... | collective-permute-start | bytes 835592 | tf_op jit(solution)/shard_map/ppermute | solution.py:240
  19.6 3.0 %collective-permute-start.14 = (bf16[128,512]{1,0:T(8,128)(2,1)S(1)}, bf16[128,512]{1,0:T(8,128)(2,1)S(1)}, u32[]{:S(2)}, u32[]{:S(2)}) collective-permute-start(bf16[128,512]{1,0:T(8,128)(2,1)S(1)} %get-tuple-element.46), channel_id=1, source_target_pairs={{0,2},{1,3},{2,0},{3,1},{4,6},{5,7},{6,4},{7,5},{8,10},{9,11},{10,... | collective-permute-start | bytes 393224 | tf_op jit(solution)/shard_map/ppermute | solution.py:243
  25.0 1.2 %collective-permute-start.5 = (bf16[512,768]{1,0:T(8,128)(2,1)S(1)}, bf16[512,768]{1,0:T(8,128)(2,1)S(1)}, u32[]{:S(2)}, u32[]{:S(2)}) collective-permute-start(bf16[512,768]{1,0:T(8,128)(2,1)S(1)} %bitcast.5), channel_id=1, source_target_pairs={{0,16},{4,20},{8,24},{12,28},{16,0},{20,4},{24,8},{28,12},{1,17},{... | collective-permute-start | bytes 2359304 | tf_op jit(solution)/shard_map/ppermute | solution.py:240
  26.7 1.2 %collective-permute-start.7 = (bf16[256,512]{1,0:T(8,128)(2,1)S(1)}, bf16[256,512]{1,0:T(8,128)(2,1)S(1)}, u32[]{:S(2)}, u32[]{:S(2)}) collective-permute-start(bf16[256,512]{1,0:T(8,128)(2,1)S(1)} %get-tuple-element.40), channel_id=1, source_target_pairs={{0,1},{1,2},{2,3},{3,0},{4,5},{5,6},{6,7},{7,4},{8,9},{9,10},{10,1... | collective-permute-start | bytes 786440 | tf_op jit(solution)/shard_map/ppermute | solution.py:243
  27.9 5.4 %collective-permute-done.14.refs_1_.refs_8_ = bf16[128,512]{1,0:T(8,128)(2,1)S(1)} collective-permute-done((bf16[128,512]{1,0:T(8,128)(2,1)S(1)}, bf16[128,512]{1,0:T(8,128)(2,1)S(1)}, u32[]{:S(2)}, u32[]{:S(2)}) %collective-permute-start.14) | collective-permute-done | bytes 131104 | tf_op jit(solution)/shard_map/ppermute | solution.py:243
  33.3 1.5 %collective-permute-start.8 = (bf16[256,512]{1,0:T(8,128)(2,1)S(1)}, bf16[256,512]{1,0:T(8,128)(2,1)S(1)}, u32[]{:S(2)}, u32[]{:S(2)}) collective-permute-start(bf16[256,512]{1,0:T(8,128)(2,1)S(1)} %get-tuple-element.41), channel_id=1, source_target_pairs={{0,3},{1,0},{2,1},{3,2},{4,7},{5,4},{6,5},{7,6},{8,11},{9,8},{10,9... | collective-permute-start | bytes 786440 | tf_op jit(solution)/shard_map/ppermute | solution.py:243
  34.8 2.9 %collective-permute-start.12 = (bf16[256,512]{1,0:T(8,128)(2,1)S(1)}, bf16[256,512]{1,0:T(8,128)(2,1)S(1)}, u32[]{:S(2)}, u32[]{:S(2)}) collective-permute-start(bf16[256,512]{1,0:T(8,128)(2,1)S(1)} %get-tuple-element.42), channel_id=1, source_target_pairs={{0,2},{1,3},{2,0},{3,1},{4,6},{5,7},{6,4},{7,5},{8,10},{9,11},{10,... | collective-permute-start | bytes 786440 | tf_op jit(solution)/shard_map/ppermute | solution.py:243
  37.8 3.3 %collective-permute-done.9.refs_5_ = bf16[512,768]{1,0:T(8,128)(2,1)S(1)} collective-permute-done((bf16[512,768]{1,0:T(8,128)(2,1)S(1)}, bf16[512,768]{1,0:T(8,128)(2,1)S(1)}, u32[]{:S(2)}, u32[]{:S(2)}) %collective-permute-start.9) | collective-permute-done | bytes 786464 | tf_op jit(solution)/shard_map/ppermute | solution.py:240
  41.3 2.0 %collective-permute-start.11 = (bf16[512,384]{1,0:T(8,128)(2,1)S(1)}, bf16[512,384]{1,0:T(8,128)(2,1)S(1)}, u32[]{:S(2)}, u32[]{:S(2)}) collective-permute-start(bf16[512,384]{1,0:T(8,128)(2,1)S(1)} %slice.9), channel_id=1, source_target_pairs={{0,8},{4,12},{8,0},{12,4},{16,24},{20,28},{24,16},{28,20},{1,9},{5... | collective-permute-start | bytes 1179656 | tf_op jit(solution)/shard_map/ppermute | solution.py:240
  44.6 4.9 %collective-permute-done.10.refs_4_.refs_2_ = bf16[512,384]{1,0:T(8,128)(2,1)S(1)} collective-permute-done((bf16[512,384]{1,0:T(8,128)(2,1)S(1)}, bf16[512,384]{1,0:T(8,128)(2,1)S(1)}, u32[]{:S(2)}, u32[]{:S(2)}) %collective-permute-start.10) | collective-permute-done | bytes 393248 | tf_op jit(solution)/shard_map/ppermute | solution.py:240
  49.5 1.2 %collective-permute-done.11.refs_5_.refs_3_ = bf16[512,384]{1,0:T(8,128)(2,1)S(1)} collective-permute-done((bf16[512,384]{1,0:T(8,128)(2,1)S(1)}, bf16[512,384]{1,0:T(8,128)(2,1)S(1)}, u32[]{:S(2)}, u32[]{:S(2)}) %collective-permute-start.11) | collective-permute-done | bytes 393248 | tf_op jit(solution)/shard_map/ppermute | solution.py:240
  51.4 3.1 %collective-permute-done.12.refs_0_.refs_1_.refs_6_ = bf16[256,512]{1,0:T(8,128)(2,1)S(1)} collective-permute-done((bf16[256,512]{1,0:T(8,128)(2,1)S(1)}, bf16[256,512]{1,0:T(8,128)(2,1)S(1)}, u32[]{:S(2)}, u32[]{:S(2)}) %collective-permute-start.12) | collective-permute-done | bytes 262176 | tf_op jit(solution)/shard_map/ppermute | solution.py:243
  58.2 1.0 %collective-permute-done.18 = f32[8,128]{1,0:T(8,128)S(1)} collective-permute-done((f32[8,128]{1,0:T(8,128)S(1)}, f32[8,128]{1,0:T(8,128)S(1)}, u32[]{:S(2)}, u32[]{:S(2)}) %collective-permute-start.18) | collective-permute-done | bytes 4128 | tf_op jit(solution)/shard_map/ppermute | solution.py:240
  59.8 1.5 %collective-permute-start.20 = (f32[8,128]{1,0:T(8,128)S(1)}, f32[8,128]{1,0:T(8,128)S(1)}, u32[]{:S(2)}, u32[]{:S(2)}) collective-permute-start(f32[8,128]{1,0:T(8,128)S(1)} %add.3.refs_0_), channel_id=1, source_target_pairs={{0,16},{4,20},{8,24},{12,28},{16,0},{20,4},{24,8},{28,12},{1,17},{... | collective-permute-start | bytes 12296 | tf_op jit(solution)/shard_map/ppermute | solution.py:240
  61.3 1.4 %collective-permute-start.19 = (f32[8,128]{1,0:T(8,128)S(1)}, f32[8,128]{1,0:T(8,128)S(1)}, u32[]{:S(2)}, u32[]{:S(2)}) collective-permute-start(f32[8,128]{1,0:T(8,128)S(1)} %add.3.refs_0_), channel_id=1, source_target_pairs={{0,8},{4,12},{8,0},{12,4},{16,24},{20,28},{24,16},{28,20},{1,9},{5... | collective-permute-start | bytes 12296 | tf_op jit(solution)/shard_map/ppermute | solution.py:240
  62.7 1.4 %moment.1 = (f32[1,256,768]{2,1,0:T(8,128)}, f32[1,256,768]{2,1,0:T(8,128)}) custom-call(f32[256,384]{1,0:T(8,128)S(1)} %get-tuple-element.55.left_ref, f32[256,384]{1,0:T(8,128)S(1)} %get-tuple-element.56.right_ref, f32[1,256,768]{2,1,0:T(8,128)S(1)} %copy-done, f32[1,256,768]{2,1,0:T(8,128)S(1)} %copy-done.1), custom_call_target="tpu_custom_call" | custom-call | bytes 3932160 | tf_op jit(solution)/shard_map/moment/pallas_call | solution.py:197
  (49 shorter events, 11.4 us)
Async XLA Ops:
  2.3 12.4 %collective-permute-start.2 = (bf16[128,512]{1,0:T(8,128)(2,1)S(1)}, bf16[128,512]{1,0:T(8,128)(2,1)S(1)}, u32[]{:S(2)}, u32[]{:S(2)}) collective-permute-start(bf16[128,512]{1,0:T(8,128)(2,1)S(1)} %get-tuple-element.33), channel_id=1, source_target_pairs={{0,2},{1,3},{2,0},{3,1},{4,6},{5,7},{6,4},{7,5},{8,10},{9,11},{10,... | collective-permute-start | bytes 393224 | tf_op jit(solution)/shard_map/ppermute | solution.py:243
  6.4 8.3 %collective-permute-start = (bf16[272,512]{1,0:T(8,128)(2,1)S(1)}, bf16[272,512]{1,0:T(8,128)(2,1)S(1)}, u32[]{:S(2)}, u32[]{:S(2)}) collective-permute-start(bf16[272,512]{1,0:T(8,128)(2,1)S(1)} %get-tuple-element.31), channel_id=1, source_target_pairs={{0,8},{4,12},{8,0},{12,4},{16,24},{20,28},{24,16},{28,20},{1,9},{5... | collective-permute-start | bytes 835592 | tf_op jit(solution)/shard_map/ppermute | solution.py:240
  7.9 7.8 %collective-permute-start.1 = (bf16[272,512]{1,0:T(8,128)(2,1)S(1)}, bf16[272,512]{1,0:T(8,128)(2,1)S(1)}, u32[]{:S(2)}, u32[]{:S(2)}) collective-permute-start(bf16[272,512]{1,0:T(8,128)(2,1)S(1)} %get-tuple-element.32), channel_id=1, source_target_pairs={{0,16},{4,20},{8,24},{12,28},{16,0},{20,4},{24,8},{28,12},{1,17},{... | collective-permute-start | bytes 835592 | tf_op jit(solution)/shard_map/ppermute | solution.py:240
  9.4 13.2 %collective-permute-start.3 = (bf16[128,512]{1,0:T(8,128)(2,1)S(1)}, bf16[128,512]{1,0:T(8,128)(2,1)S(1)}, u32[]{:S(2)}, u32[]{:S(2)}) collective-permute-start(bf16[128,512]{1,0:T(8,128)(2,1)S(1)} %get-tuple-element.34), channel_id=1, source_target_pairs={{0,1},{1,2},{2,3},{3,0},{4,5},{5,6},{6,7},{7,4},{8,9},{9,10},{10,1... | collective-permute-start | bytes 393224 | tf_op jit(solution)/shard_map/ppermute | solution.py:243
  11.0 12.5 %collective-permute-start.4 = (bf16[128,512]{1,0:T(8,128)(2,1)S(1)}, bf16[128,512]{1,0:T(8,128)(2,1)S(1)}, u32[]{:S(2)}, u32[]{:S(2)}) collective-permute-start(bf16[128,512]{1,0:T(8,128)(2,1)S(1)} %get-tuple-element.35), channel_id=1, source_target_pairs={{0,3},{1,0},{2,1},{3,2},{4,7},{5,4},{6,5},{7,6},{8,11},{9,8},{10,9... | collective-permute-start | bytes 393224 | tf_op jit(solution)/shard_map/ppermute | solution.py:243
  15.7 9.3 %collective-permute-start.6 = (bf16[272,512]{1,0:T(8,128)(2,1)S(1)}, bf16[272,512]{1,0:T(8,128)(2,1)S(1)}, u32[]{:S(2)}, u32[]{:S(2)}) collective-permute-start(bf16[272,512]{1,0:T(8,128)(2,1)S(1)} %get-tuple-element.38), channel_id=1, source_target_pairs={{0,24},{4,28},{8,16},{12,20},{16,8},{20,12},{24,0},{28,4},{1,25},{... | collective-permute-start | bytes 835592 | tf_op jit(solution)/shard_map/ppermute | solution.py:240
  19.5 7.1 %collective-permute-start.13 = (bf16[128,512]{1,0:T(8,128)(2,1)S(1)}, bf16[128,512]{1,0:T(8,128)(2,1)S(1)}, u32[]{:S(2)}, u32[]{:S(2)}) collective-permute-start(bf16[128,512]{1,0:T(8,128)(2,1)S(1)} %get-tuple-element.45), channel_id=1, source_target_pairs={{0,1},{1,2},{2,3},{3,0},{4,5},{5,6},{6,7},{7,4},{8,9},{9,10},{10,1... | collective-permute-start | bytes 393224 | tf_op jit(solution)/shard_map/ppermute | solution.py:243
  19.6 13.7 %collective-permute-start.14 = (bf16[128,512]{1,0:T(8,128)(2,1)S(1)}, bf16[128,512]{1,0:T(8,128)(2,1)S(1)}, u32[]{:S(2)}, u32[]{:S(2)}) collective-permute-start(bf16[128,512]{1,0:T(8,128)(2,1)S(1)} %get-tuple-element.46), channel_id=1, source_target_pairs={{0,2},{1,3},{2,0},{3,1},{4,6},{5,7},{6,4},{7,5},{8,10},{9,11},{10,... | collective-permute-start | bytes 393224 | tf_op jit(solution)/shard_map/ppermute | solution.py:243
  22.6 12.2 %collective-permute-start.15 = (bf16[128,512]{1,0:T(8,128)(2,1)S(1)}, bf16[128,512]{1,0:T(8,128)(2,1)S(1)}, u32[]{:S(2)}, u32[]{:S(2)}) collective-permute-start(bf16[128,512]{1,0:T(8,128)(2,1)S(1)} %get-tuple-element.47), channel_id=1, source_target_pairs={{0,3},{1,0},{2,1},{3,2},{4,7},{5,4},{6,5},{7,6},{8,11},{9,8},{10,9... | collective-permute-start | bytes 393224 | tf_op jit(solution)/shard_map/ppermute | solution.py:243
  23.8 17.3 %collective-permute-start.9 = (bf16[512,768]{1,0:T(8,128)(2,1)S(1)}, bf16[512,768]{1,0:T(8,128)(2,1)S(1)}, u32[]{:S(2)}, u32[]{:S(2)}) collective-permute-start(bf16[512,768]{1,0:T(8,128)(2,1)S(1)} %bitcast.4), channel_id=1, source_target_pairs={{0,8},{4,12},{8,0},{12,4},{16,24},{20,28},{24,16},{28,20},{1,9},{5... | collective-permute-start | bytes 2359304 | tf_op jit(solution)/shard_map/ppermute | solution.py:240
  25.0 16.3 %collective-permute-start.5 = (bf16[512,768]{1,0:T(8,128)(2,1)S(1)}, bf16[512,768]{1,0:T(8,128)(2,1)S(1)}, u32[]{:S(2)}, u32[]{:S(2)}) collective-permute-start(bf16[512,768]{1,0:T(8,128)(2,1)S(1)} %bitcast.5), channel_id=1, source_target_pairs={{0,16},{4,20},{8,24},{12,28},{16,0},{20,4},{24,8},{28,12},{1,17},{... | collective-permute-start | bytes 2359304 | tf_op jit(solution)/shard_map/ppermute | solution.py:240
  26.7 17.9 %collective-permute-start.7 = (bf16[256,512]{1,0:T(8,128)(2,1)S(1)}, bf16[256,512]{1,0:T(8,128)(2,1)S(1)}, u32[]{:S(2)}, u32[]{:S(2)}) collective-permute-start(bf16[256,512]{1,0:T(8,128)(2,1)S(1)} %get-tuple-element.40), channel_id=1, source_target_pairs={{0,1},{1,2},{2,3},{3,0},{4,5},{5,6},{6,7},{7,4},{8,9},{9,10},{10,1... | collective-permute-start | bytes 786440 | tf_op jit(solution)/shard_map/ppermute | solution.py:243
  33.3 11.3 %collective-permute-start.8 = (bf16[256,512]{1,0:T(8,128)(2,1)S(1)}, bf16[256,512]{1,0:T(8,128)(2,1)S(1)}, u32[]{:S(2)}, u32[]{:S(2)}) collective-permute-start(bf16[256,512]{1,0:T(8,128)(2,1)S(1)} %get-tuple-element.41), channel_id=1, source_target_pairs={{0,3},{1,0},{2,1},{3,2},{4,7},{5,4},{6,5},{7,6},{8,11},{9,8},{10,9... | collective-permute-start | bytes 786440 | tf_op jit(solution)/shard_map/ppermute | solution.py:243
  34.8 19.7 %collective-permute-start.12 = (bf16[256,512]{1,0:T(8,128)(2,1)S(1)}, bf16[256,512]{1,0:T(8,128)(2,1)S(1)}, u32[]{:S(2)}, u32[]{:S(2)}) collective-permute-start(bf16[256,512]{1,0:T(8,128)(2,1)S(1)} %get-tuple-element.42), channel_id=1, source_target_pairs={{0,2},{1,3},{2,0},{3,1},{4,6},{5,7},{6,4},{7,5},{8,10},{9,11},{10,... | collective-permute-start | bytes 786440 | tf_op jit(solution)/shard_map/ppermute | solution.py:243
  41.1 8.4 %collective-permute-start.10 = (bf16[512,384]{1,0:T(8,128)(2,1)S(1)}, bf16[512,384]{1,0:T(8,128)(2,1)S(1)}, u32[]{:S(2)}, u32[]{:S(2)}) collective-permute-start(bf16[512,384]{1,0:T(8,128)(2,1)S(1)} %slice.8), channel_id=1, source_target_pairs={{0,16},{4,20},{8,24},{12,28},{16,0},{20,4},{24,8},{28,12},{1,17},{... | collective-permute-start | bytes 1179656 | tf_op jit(solution)/shard_map/ppermute | solution.py:240
  41.3 9.4 %collective-permute-start.11 = (bf16[512,384]{1,0:T(8,128)(2,1)S(1)}, bf16[512,384]{1,0:T(8,128)(2,1)S(1)}, u32[]{:S(2)}, u32[]{:S(2)}) collective-permute-start(bf16[512,384]{1,0:T(8,128)(2,1)S(1)} %slice.9), channel_id=1, source_target_pairs={{0,8},{4,12},{8,0},{12,4},{16,24},{20,28},{24,16},{28,20},{1,9},{5... | collective-permute-start | bytes 1179656 | tf_op jit(solution)/shard_map/ppermute | solution.py:240
  44.6 6.2 %copy-start = (f32[1,256,768]{2,1,0:T(8,128)S(1)}, f32[1,256,768]{2,1,0:T(8,128)}, u32[]{:S(2)}) copy-start(f32[1,256,768]{2,1,0:T(8,128)} %first_ref.5) | copy-start | bytes 2359300
  44.6 6.2 %copy-start.1 = (f32[1,256,768]{2,1,0:T(8,128)S(1)}, f32[1,256,768]{2,1,0:T(8,128)}, u32[]{:S(2)}) copy-start(f32[1,256,768]{2,1,0:T(8,128)} %second_ref.5) | copy-start | bytes 2359300
  54.9 1.8 %collective-permute-start.17 = (f32[256,384]{1,0:T(8,128)S(1)}, f32[256,384]{1,0:T(8,128)S(1)}, u32[]{:S(2)}, u32[]{:S(2)}) collective-permute-start(f32[256,384]{1,0:T(8,128)S(1)} %product.9), channel_id=1, source_target_pairs={{0,4},{4,0},{8,12},{12,8},{16,20},{20,16},{24,28},{28,24},{1,5},{5... | collective-permute-start | bytes 1179656 | tf_op jit(solution)/shard_map/ppermute | solution.py:240
  55.2 2.1 %collective-permute-start.16 = (f32[256,384]{1,0:T(8,128)S(1)}, f32[256,384]{1,0:T(8,128)S(1)}, u32[]{:S(2)}, u32[]{:S(2)}) collective-permute-start(f32[256,384]{1,0:T(8,128)S(1)} %product.10), channel_id=1, source_target_pairs={{0,4},{4,0},{8,12},{12,8},{16,20},{20,16},{24,28},{28,24},{1,5},{5... | collective-permute-start | bytes 1179656 | tf_op jit(solution)/shard_map/ppermute | solution.py:240
  58.0 1.2 %collective-permute-start.18 = (f32[8,128]{1,0:T(8,128)S(1)}, f32[8,128]{1,0:T(8,128)S(1)}, u32[]{:S(2)}, u32[]{:S(2)}) collective-permute-start(f32[8,128]{1,0:T(8,128)S(1)} %get-tuple-element.50), channel_id=1, source_target_pairs={{0,4},{4,0},{8,12},{12,8},{16,20},{20,16},{24,28},{28,24},{1,5},{5... | collective-permute-start | bytes 12296 | tf_op jit(solution)/shard_map/ppermute | solution.py:240
  59.2 4.9 %collective-permute-start.21 = (f32[8,128]{1,0:T(8,128)S(1)}, f32[8,128]{1,0:T(8,128)S(1)}, u32[]{:S(2)}, u32[]{:S(2)}) collective-permute-start(f32[8,128]{1,0:T(8,128)S(1)} %add.3.refs_0_), channel_id=1, source_target_pairs={{0,24},{4,28},{8,16},{12,20},{16,8},{20,12},{24,0},{28,4},{1,25},{... | collective-permute-start | bytes 12296 | tf_op jit(solution)/shard_map/ppermute | solution.py:240
  59.8 4.3 %collective-permute-start.20 = (f32[8,128]{1,0:T(8,128)S(1)}, f32[8,128]{1,0:T(8,128)S(1)}, u32[]{:S(2)}, u32[]{:S(2)}) collective-permute-start(f32[8,128]{1,0:T(8,128)S(1)} %add.3.refs_0_), channel_id=1, source_target_pairs={{0,16},{4,20},{8,24},{12,28},{16,0},{20,4},{24,8},{28,12},{1,17},{... | collective-permute-start | bytes 12296 | tf_op jit(solution)/shard_map/ppermute | solution.py:240
  61.3 3.6 %collective-permute-start.19 = (f32[8,128]{1,0:T(8,128)S(1)}, f32[8,128]{1,0:T(8,128)S(1)}, u32[]{:S(2)}, u32[]{:S(2)}) collective-permute-start(f32[8,128]{1,0:T(8,128)S(1)} %add.3.refs_0_), channel_id=1, source_target_pairs={{0,8},{4,12},{8,0},{12,4},{16,24},{20,28},{24,16},{28,20},{1,9},{5... | collective-permute-start | bytes 12296 | tf_op jit(solution)/shard_map/ppermute | solution.py:240
  (2 other events, 7.3 us)
